TPU v7x, 32 devices: a whole 2x2x4 slice. The times are simulated.
32 devices in a mesh: grp: 8 (over y, x, core), seq: 4 (over z).
Axes of the slice: x: 2, y: 2, z: 4, core: 2. Of those that a mesh axis runs over, the one named last changes fastest.
Arguments:
- q_space: bfloat16 [32, 256, 576], P(('grp', 'seq')), may hold values from -96 to 96
- k_space: bfloat16 [32, 256, 576], P(('grp', 'seq')), may hold values from -96 to 96
- v_space: bfloat16 [32, 256, 576], P(('grp', 'seq')), may hold values from -6 to 6
- cot_space: bfloat16 [32, 256, 576], P(('grp', 'seq')), may hold values from -6 to 6
- q_time: bfloat16 [32, 256, 576], P(('grp', 'seq')), may hold values from -96 to 96
- k_time: bfloat16 [32, 256, 576], P(('grp', 'seq')), may hold values from -96 to 96
- v_time: bfloat16 [32, 256, 576], P(('grp', 'seq')), may hold values from -6 to 6
- cot_time: bfloat16 [32, 256, 576], P(('grp', 'seq')), may hold values from -6 to 6
- clip_len: int32 [16], replicated, may hold values from 1 to 4, 32 in all
Outputs:
- grad_q_space: bfloat16 [32, 256, 576], P(('grp', 'seq'))
- grad_k_space: bfloat16 [32, 256, 576], P(('grp', 'seq'))
- grad_v_space: bfloat16 [32, 256, 576], P(('grp', 'seq'))
- grad_q_time: bfloat16 [32, 256, 576], P(('grp', 'seq'))
- grad_k_time: bfloat16 [32, 256, 576], P(('grp', 'seq'))
- grad_v_time: bfloat16 [32, 256, 576], P(('grp', 'seq'))
Inputs may be any that keep to these rules, and one draw needn't show every extreme that they name: `clip_len`: the 16 frame counts sum to 32; some clip has exactly 4 frames.
All inputs are finite; a program needn't handle non-finite values.
Results may differ from a plain program's by a relative error of at most 0.013.
Values may be sent and summed in bfloat16 or wider, within the bound.
No kernel may reach another device: no remote copies, remote signals or barrier semaphores. Data moves between devices by JAX's collectives and lax.ppermute only.
A program may use at most 64 MiB of HBM per device.

v0:
```python
import functools
import math

import jax
import jax.numpy as jnp
from jax import lax
from jax.experimental import pallas as pl
from jax.experimental.pallas import tpu as pltpu
from jax.sharding import PartitionSpec as P

HEADS = 8
HDIM = 72
WIDTH = HEADS * HDIM
SCALING = 1.0 / math.sqrt(HDIM)
CHUNKS = (4, 4)
masked_score = -1e30


def shifted(value, axis, by):
    count = lax.axis_size(axis)
    pairs = [(i, i + by) for i in range(count) if 0 <= i + by < count]
    return lax.ppermute(value, axis, pairs)


def dot(left, right, left_dim, right_dim):
    dims = (((left_dim,), (right_dim,)), ((), ()))
    return lax.dot_general(left, right, dims, preferred_element_type=jnp.float32)


def rounded(value):
    return value.astype(jnp.bfloat16).astype(jnp.float32)


def swapped(value):
    half = value.shape[1] // 2
    if 2 * half == 128:
        return pltpu.roll(value, half, 1)
    return jnp.concatenate([value[:, half:], value[:, :half]], axis=1)


def frame_kernel(q_ref, k_ref, v_ref, g_ref, dq_ref, dk_ref, dv_ref):
    pair = 2 * HDIM
    reach = -(-HDIM // 16) * 16
    row = lax.broadcasted_iota(jnp.int32, (reach, 1), 0)
    for begin in range(0, WIDTH, pair):
        found = [[], [], []]
        for low, own in ((0, 0), (pair - reach, reach - HDIM)):
            span = slice(begin + low, begin + low + reach)
            mask = ((row >= own) & (row < own + HDIM)).astype(jnp.float32).astype(jnp.bfloat16)
            queries, keys = q_ref[0, span, :], k_ref[0, span, :]
            cotangent = g_ref[0, span, :]
            scores = dot(keys * mask, queries, 0, 0) * SCALING
            weight_grad = dot(v_ref[0, span, :] * mask, cotangent, 0, 0)
            raised = jnp.exp(scores - jnp.max(scores, axis=0, keepdims=True))
            weights = raised * (1.0 / jnp.sum(raised, axis=0, keepdims=True))
            weights_low = weights.astype(jnp.bfloat16)
            dots = jnp.sum(weights_low.astype(jnp.float32) * weight_grad, axis=0, keepdims=True)
            score_grad = (weights * (weight_grad - dots)).astype(jnp.bfloat16)
            rows = slice(own, own + HDIM)
            found[0].append(dot(keys, score_grad, 1, 0)[rows] * SCALING)
            found[1].append(dot(queries, score_grad, 1, 1)[rows] * SCALING)
            found[2].append(dot(cotangent, weights_low, 1, 1)[rows])
        for out, parts in zip((dq_ref, dk_ref, dv_ref), found):
            out[0, begin : begin + pair, :] = jnp.concatenate(parts, axis=0).astype(jnp.bfloat16)


def frame_grads(queries, keys, values, cotangent):
    tokens = queries.shape[2]
    shape = jax.ShapeDtypeStruct(queries.shape, jnp.bfloat16)
    return pl.pallas_call(
        frame_kernel,
        out_shape=(shape, shape, shape),
        compiler_params=pltpu.CompilerParams(vmem_limit_bytes=60 * 2**20),
        cost_estimate=pl.CostEstimate(
            flops=12 * tokens * tokens * 256 * HEADS,
            bytes_accessed=14 * tokens * WIDTH,
            transcendentals=tokens * tokens * HEADS,
        ),
        name="space",
    )(queries, keys, values, cotangent)


def split_kernel(rows, n, q_ref, k_ref, v_ref, g_ref, out_ref):
    places = q_ref.shape[2] // n
    for target in range(n):
        lanes = slice(target * places, (target + 1) * places)
        for at, (left, right) in enumerate(((q_ref, g_ref), (k_ref, v_ref))):
            both = [left[0, rows, lanes], right[0, rows, lanes]]
            out_ref[target, at] = jnp.concatenate(both, axis=1)


def split(arrays, rows, n):
    places = arrays[0].shape[2] // n
    shape = (n, 2, rows.stop - rows.start, 2 * places)
    return pl.pallas_call(
        functools.partial(split_kernel, rows, n),
        out_shape=jax.ShapeDtypeStruct(shape, jnp.bfloat16),
        compiler_params=pltpu.CompilerParams(vmem_limit_bytes=32 * 2**20),
        name="pack",
    )(*arrays)


def join_kernel(spans, n, *refs):
    ins, (dq_ref, dk_ref, dv_ref) = refs[: len(spans)], refs[len(spans) :]
    for packed, span in zip(ins, spans):
        count = span.stop - span.start
        half = count // 2
        places = packed.shape[2] // 2

        def gather(rows, lanes):
            return jnp.concatenate([packed[source, rows, lanes] for source in range(n)], axis=1)

        left, right = slice(0, places), slice(places, 2 * places)
        dk_ref[0, span, :] = gather(slice(0, count), left)
        dv_ref[0, span, :] = gather(slice(0, count), right)
        rest = slice(count, count + half)
        dq_ref[0, span.start : span.start + half, :] = gather(rest, left)
        dq_ref[0, span.start + half : span.stop, :] = gather(rest, right)


def join(packed, spans, tokens):
    n = packed[0].shape[0]
    shape = jax.ShapeDtypeStruct((1, WIDTH, tokens), jnp.bfloat16)
    return pl.pallas_call(
        functools.partial(join_kernel, spans, n),
        out_shape=(shape,) * 3,
        compiler_params=pltpu.CompilerParams(vmem_limit_bytes=60 * 2**20),
        name="unpack",
    )(*packed)


def clip_kernel(window, heads, bounds, own_ref, low_ref, high_ref, out_ref, x_ref, y_ref, coef_ref):
    halo = window - 1
    extent = window + 2 * halo
    lanes = out_ref.shape[2]
    places = lanes // 2
    rows = heads * HDIM
    is_left = lax.broadcasted_iota(jnp.int32, (1, lanes), 1) < places
    lowest, highest = bounds[0, halo], bounds[1, halo + window - 1]

    def widen(ref, at, frame):
        x_ref[frame] = ref[at, 0].astype(jnp.float32)
        y_ref[frame] = ref[at, 1].astype(jnp.float32)

    for at in range(window):
        widen(own_ref, at, halo + at)
    for at in range(halo):
        pl.when(at >= lowest)(functools.partial(widen, low_ref, at, at))
        frame = halo + window + at
        pl.when(frame < highest)(functools.partial(widen, high_ref, at, frame))

    def partners(frame):
        first, last = bounds[0, frame], bounds[1, frame]
        return first, last - first, [jnp.minimum(first + t, last - 1) for t in range(window)]

    def weigh(frame, carry):
        first, count, others = partners(frame)
        sums = [[] for _ in range(window)]
        for head in range(heads):
            span = slice(head * HDIM, (head + 1) * HDIM)
            mine = x_ref[frame, span, :]
            for t, other in enumerate(others):
                sums[t].append(jnp.sum(mine * y_ref[other, span, :], axis=0, keepdims=True))
        sums = [jnp.concatenate(parts, axis=0) for parts in sums]
        scores = [
            part * SCALING + jnp.where(t < count, 0.0, masked_score) for t, part in enumerate(sums)
        ]
        peak = functools.reduce(jnp.maximum, scores)
        raised = [jnp.exp(score - peak) for score in scores]
        inverse = 1.0 / functools.reduce(jnp.add, raised)
        weights = [part * inverse for part in raised]
        weights_low = [rounded(part) for part in weights]
        weight_grad = [swapped(part) for part in sums]
        dots = functools.reduce(jnp.add, [w * d for w, d in zip(weights_low, weight_grad)])
        for t in range(window):
            score_grad = rounded(weights[t] * (weight_grad[t] - dots))
            coef_ref[frame, t] = jnp.where(is_left, score_grad, swapped(weights_low[t]))
        return carry

    lax.fori_loop(lowest, highest, weigh, 0)

    def gradients(at, carry):
        frame = halo + at
        first, count, others = partners(frame)
        place = frame - first
        by_key, by_query = [], []
        for head in range(heads):
            span = slice(head * HDIM, (head + 1) * HDIM)
            key_sum, query_sum = None, None
            for t, other in enumerate(others):
                back = coef_ref[other, place, head : head + 1, :]
                back = jnp.where(t < count, back, 0.0)
                ahead = coef_ref[frame, t, head : head + 1, :]
                key_term = back * x_ref[other, span, :]
                query_term = ahead * y_ref[other, span, :]
                key_sum = key_term if t == 0 else key_sum + key_term
                query_sum = query_term if t == 0 else query_sum + query_term
            by_key.append(key_sum * jnp.where(is_left, SCALING, 1.0))
            by_query.append(query_sum * SCALING)
            if head % 2 == 1:
                span = slice((head - 1) * HDIM, (head + 1) * HDIM)
                value = jnp.concatenate(by_key[head - 1 :], axis=0)
                out_ref[at, span, :] = value.astype(jnp.bfloat16)
        half = heads // 2
        folded = [
            jnp.where(is_left, by_query[head], swapped(by_query[head + half]))
            for head in range(half)
        ]
        value = jnp.concatenate(folded, axis=0)
        out_ref[at, rows:, :] = value.astype(jnp.bfloat16)
        return carry

    lax.fori_loop(0, window, gradients, 0)


def clip_grads(bounds, own, low, high):
    window, _, rows, lanes = own.shape
    heads = rows // HDIM
    extent = 3 * window - 2
    vmem = pl.BlockSpec(memory_space=pltpu.VMEM)
    work = extent * window * rows * lanes
    return pl.pallas_call(
        functools.partial(clip_kernel, window, heads),
        out_shape=jax.ShapeDtypeStruct((window, rows + rows // 2, lanes), jnp.bfloat16),
        in_specs=[pl.BlockSpec(memory_space=pltpu.SMEM), vmem, vmem, vmem],
        out_specs=vmem,
        scratch_shapes=[
            pltpu.VMEM((extent, rows, lanes), jnp.float32),
            pltpu.VMEM((extent, rows, lanes), jnp.float32),
            pltpu.VMEM((extent, window, heads, lanes), jnp.float32),
        ],
        compiler_params=pltpu.CompilerParams(vmem_limit_bytes=48 * 2**20),
        cost_estimate=pl.CostEstimate(
            flops=400 * work,
            bytes_accessed=2 * (own.size + low.size + high.size),
            transcendentals=extent * window * heads * lanes,
        ),
        name="clips",
    )(bounds, own, low, high)


def clip_bounds(clip_len, window):
    halo = window - 1
    extent = window + 2 * halo
    start = lax.axis_index("grp") * window - halo
    frames = start + jnp.arange(extent, dtype=jnp.int32)
    order = jnp.arange(clip_len.shape[0])
    ends = jnp.sum(jnp.where(order[:, None] <= order[None, :], clip_len[:, None], 0), axis=0)
    begins = ends - clip_len
    holds = (begins[None, :] <= frames[:, None]) & (frames[:, None] < ends[None, :])
    first = jnp.sum(jnp.where(holds, begins[None, :], 0), axis=1) - start
    last = jnp.sum(jnp.where(holds, ends[None, :], 0), axis=1) - start
    return jnp.stack([first, last]).astype(jnp.int32)


def shards(q_space, k_space, v_space, cot_space, q_time, k_time, v_time, cot_time, clip_len):
    def turned(*arrays):
        return tuple(array.transpose(0, 2, 1) for array in arrays)

    n = lax.axis_size("seq")
    window = q_time.shape[0] * n
    tokens = q_time.shape[1]
    bounds = clip_bounds(clip_len, window)
    time = turned(q_time, k_time, v_time, cot_time)
    spans, back = [], []
    head = 0
    for heads in CHUNKS:
        span = slice(head * HDIM, (head + heads) * HDIM)
        head += heads
        packed = split(time, span, n)
        own = lax.all_to_all(packed, "seq", split_axis=0, concat_axis=0, tiled=True)
        low = shifted(own[1:], "grp", 1)
        high = shifted(own[: window - 1], "grp", -1)
        grads = clip_grads(bounds, own, low, high)
        back.append(lax.all_to_all(grads, "seq", split_axis=0, concat_axis=0, tiled=True))
        spans.append(span)
    space = frame_grads(*turned(q_space, k_space, v_space, cot_space))
    return turned(*space, *join(back, spans, tokens))


def solution(mesh):
    split_spec = P(("grp", "seq"), None, None)
    return jax.shard_map(
        shards,
        mesh=mesh,
        in_specs=(split_spec,) * 8 + (P(),),
        out_specs=(split_spec,) * 6,
        check_vma=False,
    )
```

profile of v0, /device:TPU:2, one launch (start us, length us, event | category | flops | bytes accessed | tf_op | source)
XLA Modules:
  0.0 90.6 jit_solution(1521796581086308090)
XLA Ops:
  0.6 0.0 copy-start
  0.6 1.0 %copy-done = bf16[1,256,576]{1,2,0:T(8,128)(2,1)S(1)} copy-done((bf16[1,256,576]{1,2,0:T(8,128)(2,1)S(1)}, bf16[1,256,576]{1,2,0:T(8,128)(2,1)}, u32[]{:S(2)}) %copy-start) | copy-done | bytes 294936
  1.6 0.0 copy-start.2
  1.6 1.0 %copy-done.2 = bf16[1,256,576]{1,2,0:T(8,128)(2,1)S(1)} copy-done((bf16[1,256,576]{1,2,0:T(8,128)(2,1)S(1)}, bf16[1,256,576]{1,2,0:T(8,128)(2,1)}, u32[]{:S(2)}) %copy-start.2) | copy-done | bytes 294936
  2.6 0.0 copy-start.4
  2.6 1.0 %copy-done.4 = bf16[1,256,576]{1,2,0:T(8,128)(2,1)S(1)} copy-done((bf16[1,256,576]{1,2,0:T(8,128)(2,1)S(1)}, bf16[1,256,576]{1,2,0:T(8,128)(2,1)}, u32[]{:S(2)}) %copy-start.4) | copy-done | bytes 294936
  3.5 0.0 copy-start.6
  3.5 1.0 %copy-done.6 = bf16[1,256,576]{1,2,0:T(8,128)(2,1)S(1)} copy-done((bf16[1,256,576]{1,2,0:T(8,128)(2,1)S(1)}, bf16[1,256,576]{1,2,0:T(8,128)(2,1)}, u32[]{:S(2)}) %copy-start.6) | copy-done | bytes 294936
  4.5 1.1 %pack.3 = bf16[4,2,288,128]{3,2,1,0:T(8,128)(2,1)} custom-call(bf16[1,576,256]{2,1,0:T(8,128)(2,1)S(1)} %bitcast.18, bf16[1,576,256]{2,1,0:T(8,128)(2,1)S(1)} %bitcast.20, bf16[1,576,256]{2,1,0:T(8,128)(2,1)S(1)} %bitcast.22, bf16[1,576,256]{2,1,0:T(8,128)(2,1)S(1)} %bitcast.24), custom_call_target="tpu_custom_call" | custom-call | tf_op jit(solution)/shard_map/pack/pallas_call | solution.py:95
  5.5 0.0 copy-start.1
  5.6 0.0 copy-start.3
  5.6 0.0 copy-start.5
  5.6 0.0 copy-start.7
  5.6 5.0 %all-to-all-start.2 = ((bf16[4,2,288,128]{3,2,1,0:T(8,128)(2,1)}), bf16[4,2,288,128]{3,2,1,0:T(8,128)(2,1)S(1)}, u32[]{:S(2)}, u32[]{:S(2)}) async-start(bf16[4,2,288,128]{3,2,1,0:T(8,128)(2,1)} %pack.3), calls=%async_computation.2 | async-start | bytes 1179648 | tf_op jit(solution)/shard_map/all_to_all | solution.py:271
  10.6 0.0 copy-done.1
  10.6 0.0 copy-done.3
  10.6 0.0 copy-done.5
  10.6 0.0 copy-done.7
  10.6 1.0 %pack.2 = bf16[4,2,288,128]{3,2,1,0:T(8,128)(2,1)} custom-call(bf16[1,576,256]{2,1,0:T(8,128)(2,1)S(1)} %bitcast.19, bf16[1,576,256]{2,1,0:T(8,128)(2,1)S(1)} %bitcast.21, bf16[1,576,256]{2,1,0:T(8,128)(2,1)S(1)} %bitcast.23, bf16[1,576,256]{2,1,0:T(8,128)(2,1)S(1)} %bitcast.25), custom_call_target="tpu_custom_call" | custom-call | tf_op jit(solution)/shard_map/pack/pallas_call | solution.py:95
  11.6 0.0 copy-start.10
  11.6 14.8 %all-to-all-done.2.own_ref = bf16[4,2,288,128]{3,2,1,0:T(8,128)(2,1)S(1)} async-done(((bf16[4,2,288,128]{3,2,1,0:T(8,128)(2,1)}), bf16[4,2,288,128]{3,2,1,0:T(8,128)(2,1)S(1)}, u32[]{:S(2)}, u32[]{:S(2)}) %all-to-all-start.2) | async-done | bytes 589856 | tf_op jit(solution)/shard_map/all_to_all | solution.py:271
  26.5 3.5 %all-to-all-start = ((bf16[4,2,288,128]{3,2,1,0:T(8,128)(2,1)}), bf16[4,2,288,128]{3,2,1,0:T(8,128)(2,1)S(1)}, u32[]{:S(2)}, u32[]{:S(2)}) async-start(bf16[4,2,288,128]{3,2,1,0:T(8,128)(2,1)} %pack.2), calls=%async_computation | async-start | bytes 1179648 | tf_op jit(solution)/shard_map/all_to_all | solution.py:271
  30.0 0.0 copy-done.10
  30.0 0.1 select_reduce_fusion.2
  30.1 0.1 fusion
  30.2 1.9 %collective-permute-start.2 = (bf16[3,2,288,128]{3,2,1,0:T(8,128)(2,1)S(1)}, bf16[3,2,288,128]{3,2,1,0:T(8,128)(2,1)S(1)}, u32[]{:S(2)}, u32[]{:S(2)}) collective-permute-start(bf16[3,2,288,128]{3,2,1,0:T(8,128)(2,1)S(1)} %get-tuple-element.21), channel_id=1, source_target_pairs={{0,4},{4,8},{8,12},{12,16},{16,20},{20,24},{24,28},{1,5},{5,9},{9,... | collective-permute-start | bytes 1327112 | tf_op jit(solution)/shard_map/ppermute | solution.py:22
  32.1 3.6 %collective-permute-start.3 = (bf16[3,2,288,128]{3,2,1,0:T(8,128)(2,1)S(1)}, bf16[3,2,288,128]{3,2,1,0:T(8,128)(2,1)S(1)}, u32[]{:S(2)}, u32[]{:S(2)}) collective-permute-start(bf16[3,2,288,128]{3,2,1,0:T(8,128)(2,1)S(1)} %get-tuple-element.20), channel_id=1, source_target_pairs={{4,0},{8,4},{12,8},{16,12},{20,16},{24,20},{28,24},{5,1},{9,5},{13... | collective-permute-start | bytes 1327112 | tf_op jit(solution)/shard_map/ppermute | solution.py:22
  35.7 0.2 select_reduce_fusion.1
  36.0 3.8 %collective-permute-done.2.low_ref = bf16[3,2,288,128]{3,2,1,0:T(8,128)(2,1)S(1)} collective-permute-done((bf16[3,2,288,128]{3,2,1,0:T(8,128)(2,1)S(1)}, bf16[3,2,288,128]{3,2,1,0:T(8,128)(2,1)S(1)}, u32[]{:S(2)}, u32[]{:S(2)}) %collective-permute-start.2) | collective-permute-done | bytes 442400 | tf_op jit(solution)/shard_map/ppermute | solution.py:22
  39.8 3.7 %collective-permute-done.3.high_ref = bf16[3,2,288,128]{3,2,1,0:T(8,128)(2,1)S(1)} collective-permute-done((bf16[3,2,288,128]{3,2,1,0:T(8,128)(2,1)S(1)}, bf16[3,2,288,128]{3,2,1,0:T(8,128)(2,1)S(1)}, u32[]{:S(2)}, u32[]{:S(2)}) %collective-permute-start.3) | collective-permute-done | bytes 442400 | tf_op jit(solution)/shard_map/ppermute | solution.py:22
  43.5 3.0 %clips.3 = bf16[4,432,128]{2,1,0:T(8,128)(2,1)} custom-call(s32[2,10]{1,0:T(2,128)S(1)} %pad_add_fusion.bounds, bf16[4,2,288,128]{3,2,1,0:T(8,128)(2,1)S(1)} %all-to-all-done.2.own_ref, bf16[3,2,288,128]{3,2,1,0:T(8,128)(2,1)S(1)} %collective-permute-done.2.low_ref, bf16[3,2,288,128]{3,2,1,0:T(8,128)(2,1)S(1)} %collective-permute-done.3.high_ref), custom_call_target="tpu_custom_call" | custom-call | flops 589824000 | bytes 1474560 | tf_op jit(solution)/shard_map/clips/pallas_call | solution.py:222
  46.6 0.0 all-to-all-done.own_ref
  46.6 5.1 %all-to-all-start.3 = ((bf16[4,432,128]{2,1,0:T(8,128)(2,1)}), bf16[4,432,128]{2,1,0:T(8,128)(2,1)S(1)}, u32[]{:S(2)}, u32[]{:S(2)}) async-start(bf16[4,432,128]{2,1,0:T(8,128)(2,1)} %clips.3), calls=%async_computation.3 | async-start | bytes 884736 | tf_op jit(solution)/shard_map/all_to_all | solution.py:275
  51.6 0.1 fusion.1
  51.7 3.2 %collective-permute-start = (bf16[3,2,288,128]{3,2,1,0:T(8,128)(2,1)S(1)}, bf16[3,2,288,128]{3,2,1,0:T(8,128)(2,1)S(1)}, u32[]{:S(2)}, u32[]{:S(2)}) collective-permute-start(bf16[3,2,288,128]{3,2,1,0:T(8,128)(2,1)S(1)} %get-tuple-element.23), channel_id=1, source_target_pairs={{0,4},{4,8},{8,12},{12,16},{16,20},{20,24},{24,28},{1,5},{5,9},{9,... | collective-permute-start | bytes 1327112 | tf_op jit(solution)/shard_map/ppermute | solution.py:22
  55.0 2.3 %collective-permute-start.1 = (bf16[3,2,288,128]{3,2,1,0:T(8,128)(2,1)S(1)}, bf16[3,2,288,128]{3,2,1,0:T(8,128)(2,1)S(1)}, u32[]{:S(2)}, u32[]{:S(2)}) collective-permute-start(bf16[3,2,288,128]{3,2,1,0:T(8,128)(2,1)S(1)} %get-tuple-element.22), channel_id=1, source_target_pairs={{4,0},{8,4},{12,8},{16,12},{20,16},{24,20},{28,24},{5,1},{9,5},{13... | collective-permute-start | bytes 1327112 | tf_op jit(solution)/shard_map/ppermute | solution.py:22
  57.3 4.0 %collective-permute-done.low_ref = bf16[3,2,288,128]{3,2,1,0:T(8,128)(2,1)S(1)} collective-permute-done((bf16[3,2,288,128]{3,2,1,0:T(8,128)(2,1)S(1)}, bf16[3,2,288,128]{3,2,1,0:T(8,128)(2,1)S(1)}, u32[]{:S(2)}, u32[]{:S(2)}) %collective-permute-start) | collective-permute-done | bytes 442400 | tf_op jit(solution)/shard_map/ppermute | solution.py:22
  61.4 3.9 %collective-permute-done.1.high_ref = bf16[3,2,288,128]{3,2,1,0:T(8,128)(2,1)S(1)} collective-permute-done((bf16[3,2,288,128]{3,2,1,0:T(8,128)(2,1)S(1)}, bf16[3,2,288,128]{3,2,1,0:T(8,128)(2,1)S(1)}, u32[]{:S(2)}, u32[]{:S(2)}) %collective-permute-start.1) | collective-permute-done | bytes 442400 | tf_op jit(solution)/shard_map/ppermute | solution.py:22
  65.3 3.0 %clips.2 = bf16[4,432,128]{2,1,0:T(8,128)(2,1)} custom-call(s32[2,10]{1,0:T(2,128)S(1)} %pad_add_fusion.bounds, bf16[4,2,288,128]{3,2,1,0:T(8,128)(2,1)S(1)} %all-to-all-done.own_ref, bf16[3,2,288,128]{3,2,1,0:T(8,128)(2,1)S(1)} %collective-permute-done.low_ref, bf16[3,2,288,128]{3,2,1,0:T(8,128)(2,1)S(1)} %collective-permute-done.1.high_ref), custom_call_target="tpu_custom_call" | custom-call | flops 589824000 | bytes 1474560 | tf_op jit(solution)/shard_map/clips/pallas_call | solution.py:222
  68.3 0.0 all-to-all-done.3.refs_1_
  68.3 0.0 copy-start.8
  68.3 0.7 copy-done.8
  69.1 5.1 %all-to-all-start.1 = ((bf16[4,432,128]{2,1,0:T(8,128)(2,1)}), bf16[4,432,128]{2,1,0:T(8,128)(2,1)S(1)}, u32[]{:S(2)}, u32[]{:S(2)}) async-start(bf16[4,432,128]{2,1,0:T(8,128)(2,1)} %clips.2), calls=%async_computation.1 | async-start | bytes 884736 | tf_op jit(solution)/shard_map/all_to_all | solution.py:275
  74.2 5.5 %space.1 = (bf16[1,576,256]{2,1,0:T(8,128)(2,1)}, bf16[1,576,256]{2,1,0:T(8,128)(2,1)}, bf16[1,576,256]{2,1,0:T(8,128)(2,1)}) custom-call(bf16[1,576,256]{2,1,0:T(8,128)(2,1)} %bitcast.26, bf16[1,576,256]{2,1,0:T(8,128)(2,1)} %bitcast.27, bf16[1,576,256]{2,1,0:T(8,128)(2,1)} %bitcast.28, bf16[1,576,256]{2,1,0:T(8,128)(2,1)} %bitcast.29), custom_call_target="tpu_custom_call" | custom-call | flops 1610612736 | bytes 2064384 | tf_op jit(solution)/shard_map/space/pallas_call | solution.py:70
  79.7 7.9 %all-to-all-done.1.refs_0_ = bf16[4,432,128]{2,1,0:T(8,128)(2,1)S(1)} async-done(((bf16[4,432,128]{2,1,0:T(8,128)(2,1)}), bf16[4,432,128]{2,1,0:T(8,128)(2,1)S(1)}, u32[]{:S(2)}, u32[]{:S(2)}) %all-to-all-start.1) | async-done | bytes 442400 | tf_op jit(solution)/shard_map/all_to_all | solution.py:275
  87.6 0.0 copy-start.9
  87.6 0.8 copy-done.9
  88.3 2.3 %unpack.1 = (bf16[1,576,256]{2,1,0:T(8,128)(2,1)}, bf16[1,576,256]{2,1,0:T(8,128)(2,1)}, bf16[1,576,256]{2,1,0:T(8,128)(2,1)}) custom-call(bf16[4,432,128]{2,1,0:T(8,128)(2,1)} %copy-done.9, bf16[4,432,128]{2,1,0:T(8,128)(2,1)} %copy-done.8), custom_call_target="tpu_custom_call" | custom-call | tf_op jit(solution)/shard_map/unpack/pallas_call | solution.py:124
  (4 shorter events, 0.0 us)
Async XLA Ops:
  0.6 1.0 %copy-start = (bf16[1,256,576]{1,2,0:T(8,128)(2,1)S(1)}, bf16[1,256,576]{1,2,0:T(8,128)(2,1)}, u32[]{:S(2)}) copy-start(bf16[1,256,576]{1,2,0:T(8,128)(2,1)} %param.13) | copy-start | bytes 884740
  1.6 1.0 %copy-start.2 = (bf16[1,256,576]{1,2,0:T(8,128)(2,1)S(1)}, bf16[1,256,576]{1,2,0:T(8,128)(2,1)}, u32[]{:S(2)}) copy-start(bf16[1,256,576]{1,2,0:T(8,128)(2,1)} %param.14) | copy-start | bytes 884740
  2.6 1.0 %copy-start.4 = (bf16[1,256,576]{1,2,0:T(8,128)(2,1)S(1)}, bf16[1,256,576]{1,2,0:T(8,128)(2,1)}, u32[]{:S(2)}) copy-start(bf16[1,256,576]{1,2,0:T(8,128)(2,1)} %param.15) | copy-start | bytes 884740
  3.5 1.0 %copy-start.6 = (bf16[1,256,576]{1,2,0:T(8,128)(2,1)S(1)}, bf16[1,256,576]{1,2,0:T(8,128)(2,1)}, u32[]{:S(2)}) copy-start(bf16[1,256,576]{1,2,0:T(8,128)(2,1)} %param.16) | copy-start | bytes 884740
  5.5 5.0 %copy-start.1 = (bf16[1,256,576]{1,2,0:T(8,128)(2,1)S(1)}, bf16[1,256,576]{1,2,0:T(8,128)(2,1)}, u32[]{:S(2)}) copy-start(bf16[1,256,576]{1,2,0:T(8,128)(2,1)} %param.13) | copy-start | bytes 884740
  5.6 5.0 %copy-start.3 = (bf16[1,256,576]{1,2,0:T(8,128)(2,1)S(1)}, bf16[1,256,576]{1,2,0:T(8,128)(2,1)}, u32[]{:S(2)}) copy-start(bf16[1,256,576]{1,2,0:T(8,128)(2,1)} %param.14) | copy-start | bytes 884740
  5.6 5.0 %copy-start.5 = (bf16[1,256,576]{1,2,0:T(8,128)(2,1)S(1)}, bf16[1,256,576]{1,2,0:T(8,128)(2,1)}, u32[]{:S(2)}) copy-start(bf16[1,256,576]{1,2,0:T(8,128)(2,1)} %param.15) | copy-start | bytes 884740
  5.6 5.0 %copy-start.7 = (bf16[1,256,576]{1,2,0:T(8,128)(2,1)S(1)}, bf16[1,256,576]{1,2,0:T(8,128)(2,1)}, u32[]{:S(2)}) copy-start(bf16[1,256,576]{1,2,0:T(8,128)(2,1)} %param.16) | copy-start | bytes 884740
  5.6 20.9 %all-to-all-start.2 = ((bf16[4,2,288,128]{3,2,1,0:T(8,128)(2,1)}), bf16[4,2,288,128]{3,2,1,0:T(8,128)(2,1)S(1)}, u32[]{:S(2)}, u32[]{:S(2)}) async-start(bf16[4,2,288,128]{3,2,1,0:T(8,128)(2,1)} %pack.3), calls=%async_computation.2 | async-start | bytes 1179648 | tf_op jit(solution)/shard_map/all_to_all | solution.py:271
  11.6 18.3 %copy-start.10 = (s32[16]{0:T(128)S(1)}, s32[16]{0:T(128)}, u32[]{:S(2)}) copy-start(s32[16]{0:T(128)} %param.17) | copy-start | bytes 196
  26.5 20.1 %all-to-all-start = ((bf16[4,2,288,128]{3,2,1,0:T(8,128)(2,1)}), bf16[4,2,288,128]{3,2,1,0:T(8,128)(2,1)S(1)}, u32[]{:S(2)}, u32[]{:S(2)}) async-start(bf16[4,2,288,128]{3,2,1,0:T(8,128)(2,1)} %pack.2), calls=%async_computation | async-start | bytes 1179648 | tf_op jit(solution)/shard_map/all_to_all | solution.py:271
  30.2 9.6 %collective-permute-start.2 = (bf16[3,2,288,128]{3,2,1,0:T(8,128)(2,1)S(1)}, bf16[3,2,288,128]{3,2,1,0:T(8,128)(2,1)S(1)}, u32[]{:S(2)}, u32[]{:S(2)}) collective-permute-start(bf16[3,2,288,128]{3,2,1,0:T(8,128)(2,1)S(1)} %get-tuple-element.21), channel_id=1, source_target_pairs={{0,4},{4,8},{8,12},{12,16},{16,20},{20,24},{24,28},{1,5},{5,9},{9,... | collective-permute-start | bytes 1327112 | tf_op jit(solution)/shard_map/ppermute | solution.py:22
  32.1 11.4 %collective-permute-start.3 = (bf16[3,2,288,128]{3,2,1,0:T(8,128)(2,1)S(1)}, bf16[3,2,288,128]{3,2,1,0:T(8,128)(2,1)S(1)}, u32[]{:S(2)}, u32[]{:S(2)}) collective-permute-start(bf16[3,2,288,128]{3,2,1,0:T(8,128)(2,1)S(1)} %get-tuple-element.20), channel_id=1, source_target_pairs={{4,0},{8,4},{12,8},{16,12},{20,16},{24,20},{28,24},{5,1},{9,5},{13... | collective-permute-start | bytes 1327112 | tf_op jit(solution)/shard_map/ppermute | solution.py:22
  46.6 21.7 %all-to-all-start.3 = ((bf16[4,432,128]{2,1,0:T(8,128)(2,1)}), bf16[4,432,128]{2,1,0:T(8,128)(2,1)S(1)}, u32[]{:S(2)}, u32[]{:S(2)}) async-start(bf16[4,432,128]{2,1,0:T(8,128)(2,1)} %clips.3), calls=%async_computation.3 | async-start | bytes 884736 | tf_op jit(solution)/shard_map/all_to_all | solution.py:275
  51.7 9.6 %collective-permute-start = (bf16[3,2,288,128]{3,2,1,0:T(8,128)(2,1)S(1)}, bf16[3,2,288,128]{3,2,1,0:T(8,128)(2,1)S(1)}, u32[]{:S(2)}, u32[]{:S(2)}) collective-permute-start(bf16[3,2,288,128]{3,2,1,0:T(8,128)(2,1)S(1)} %get-tuple-element.23), channel_id=1, source_target_pairs={{0,4},{4,8},{8,12},{12,16},{16,20},{20,24},{24,28},{1,5},{5,9},{9,... | collective-permute-start | bytes 1327112 | tf_op jit(solution)/shard_map/ppermute | solution.py:22
  55.0 10.3 %collective-permute-start.1 = (bf16[3,2,288,128]{3,2,1,0:T(8,128)(2,1)S(1)}, bf16[3,2,288,128]{3,2,1,0:T(8,128)(2,1)S(1)}, u32[]{:S(2)}, u32[]{:S(2)}) collective-permute-start(bf16[3,2,288,128]{3,2,1,0:T(8,128)(2,1)S(1)} %get-tuple-element.22), channel_id=1, source_target_pairs={{4,0},{8,4},{12,8},{16,12},{20,16},{24,20},{28,24},{5,1},{9,5},{13... | collective-permute-start | bytes 1327112 | tf_op jit(solution)/shard_map/ppermute | solution.py:22
  68.3 0.7 copy-start.8
  69.1 18.5 %all-to-all-start.1 = ((bf16[4,432,128]{2,1,0:T(8,128)(2,1)}), bf16[4,432,128]{2,1,0:T(8,128)(2,1)S(1)}, u32[]{:S(2)}, u32[]{:S(2)}) async-start(bf16[4,432,128]{2,1,0:T(8,128)(2,1)} %clips.2), calls=%async_computation.1 | async-start | bytes 884736 | tf_op jit(solution)/shard_map/all_to_all | solution.py:275
  87.6 0.8 copy-start.9
where the time goes:
time: 91.2 us; the launch traced here: 90.6 us
  waiting for transfers between devices  38.2 us (42%)
  starting transfers between devices  29.8 us (33%)
  Pallas kernels  16 us (18%)
  local copies, waits for them, and re-layouts  5.56 us (6%)
    ppermute x4, waiting for transfers between devices, shifted(): return lax.ppermute(value, axis, pairs)  15.6 us
    all_to_all x2, waiting for transfers between devices, shards(): own = lax.all_to_all(packed, 'seq', split_axis=0, concat_axis=0, tiled=True)  14.8 us
    ppermute x4, starting transfers between devices, shifted(): return lax.ppermute(value, axis, pairs)  11.1 us
    all_to_all x2, starting transfers between devices, shards(): lax.all_to_all(grads, 'seq', split_axis=0, concat_axis=0, tiled=True)  10.1 us
    all_to_all x2, starting transfers between devices, shards(): own = lax.all_to_all(packed, 'seq', split_axis=0, concat_axis=0, tiled=True)  8.49 us
    all_to_all x2, waiting for transfers between devices, shards(): lax.all_to_all(grads, 'seq', split_axis=0, concat_axis=0, tiled=True)  7.87 us
    pallas_call x2, Pallas kernels, clip_grads(): pl.pallas_call(functools.partial(clip_kernel, window, heads), out_shape=j...  6.09 us
    pallas_call x1, Pallas kernels, frame_grads(): pl.pallas_call(frame_kernel, out_shape=(shape, shape, shape), compiler_pa...  5.53 us
  transfers between devices with their start and end apart: 8, of which 6 were waited for; matrix products, arithmetic and copies ran while one was open for 1% of the time, Pallas kernels for 14%

commit v1 on v0

--- a/solution.py
+++ b/solution.py
@@ -12,7 +12,7 @@
 HDIM = 72
 WIDTH = HEADS * HDIM
 SCALING = 1.0 / math.sqrt(HDIM)
-CHUNKS = (4, 4)
+CHUNKS = 2
 masked_score = -1e30
 
 
@@ -80,74 +80,128 @@
     )(queries, keys, values, cotangent)
 
 
-def split_kernel(rows, n, q_ref, k_ref, v_ref, g_ref, out_ref):
+def split_kernel(n, place_ref, q_ref, k_ref, v_ref, g_ref, *refs):
+    outs, held = refs[:n], refs[n]
     places = q_ref.shape[2] // n
     for target in range(n):
         lanes = slice(target * places, (target + 1) * places)
         for at, (left, right) in enumerate(((q_ref, g_ref), (k_ref, v_ref))):
-            both = [left[0, rows, lanes], right[0, rows, lanes]]
-            out_ref[target, at] = jnp.concatenate(both, axis=1)
-
-
-def split(arrays, rows, n):
-    places = arrays[0].shape[2] // n
-    shape = (n, 2, rows.stop - rows.start, 2 * places)
-    return pl.pallas_call(
-        functools.partial(split_kernel, rows, n),
-        out_shape=jax.ShapeDtypeStruct(shape, jnp.bfloat16),
+            held[target, at] = jnp.concatenate([left[0, :, lanes], right[0, :, lanes]], axis=1)
+    for step, out in enumerate(outs):
+        out[...] = held[place_ref[0] ^ step]
+
+
+def split(place, arrays, chunk, rows, n):
+    tokens = arrays[0].shape[2]
+    shape = (2, rows, 2 * tokens // n)
+    block = pl.BlockSpec((1, rows, tokens), lambda i: (0, chunk, 0))
+    return pl.pallas_call(
+        functools.partial(split_kernel, n),
+        grid=(1,),
+        in_specs=[pl.BlockSpec(memory_space=pltpu.SMEM)] + [block] * 4,
+        out_specs=[pl.BlockSpec(shape, lambda i: (0, 0, 0))] * n,
+        out_shape=[jax.ShapeDtypeStruct(shape, jnp.bfloat16)] * n,
+        scratch_shapes=[pltpu.VMEM((n, *shape), jnp.bfloat16)],
+        compiler_params=pltpu.CompilerParams(vmem_limit_bytes=60 * 2**20),
+        name="pack",
+    )(place, *arrays)
+
+
+def exchange(blocks):
+    n = len(blocks)
+    moved = [blocks[0]]
+    for step in range(1, n):
+        moved.append(lax.ppermute(blocks[step], "seq", [(i, i ^ step) for i in range(n)]))
+    return moved
+
+
+def sides_kernel(n, place_ref, *refs):
+    ins, (first_ref, last_ref) = refs[:n], refs[n:]
+    for step, block in enumerate(ins):
+        frame = place_ref[0] ^ step
+
+        @pl.when(frame < n - 1)
+        def _():
+            first_ref[jnp.minimum(frame, n - 2)] = block[...]
+
+        @pl.when(frame > 0)
+        def _():
+            last_ref[jnp.maximum(frame - 1, 0)] = block[...]
+
+
+def sides(place, blocks):
+    n = len(blocks)
+    shape = jax.ShapeDtypeStruct((n - 1, *blocks[0].shape), jnp.bfloat16)
+    vmem = pl.BlockSpec(memory_space=pltpu.VMEM)
+    return pl.pallas_call(
+        functools.partial(sides_kernel, n),
+        in_specs=[pl.BlockSpec(memory_space=pltpu.SMEM)] + [vmem] * n,
+        out_specs=[vmem] * 2,
+        out_shape=[shape] * 2,
         compiler_params=pltpu.CompilerParams(vmem_limit_bytes=32 * 2**20),
-        name="pack",
-    )(*arrays)
-
-
-def join_kernel(spans, n, *refs):
-    ins, (dq_ref, dk_ref, dv_ref) = refs[: len(spans)], refs[len(spans) :]
-    for packed, span in zip(ins, spans):
-        count = span.stop - span.start
-        half = count // 2
-        places = packed.shape[2] // 2
-
-        def gather(rows, lanes):
-            return jnp.concatenate([packed[source, rows, lanes] for source in range(n)], axis=1)
-
-        left, right = slice(0, places), slice(places, 2 * places)
-        dk_ref[0, span, :] = gather(slice(0, count), left)
-        dv_ref[0, span, :] = gather(slice(0, count), right)
-        rest = slice(count, count + half)
-        dq_ref[0, span.start : span.start + half, :] = gather(rest, left)
-        dq_ref[0, span.start + half : span.stop, :] = gather(rest, right)
-
-
-def join(packed, spans, tokens):
-    n = packed[0].shape[0]
+        name="sides",
+    )(place, *blocks)
+
+
+def join_kernel(n, place_ref, *refs):
+    ins, (dq_ref, dk_ref, dv_ref, held) = refs[:n], refs[-4:]
+    for step, block in enumerate(ins):
+        held[place_ref[0] ^ step] = block[...]
+    count = dq_ref.shape[1]
+    half = count // 2
+    places = held.shape[2] // 2
+
+    def gather(rows, lanes):
+        return jnp.concatenate([held[source, rows, lanes] for source in range(n)], axis=1)
+
+    left, right = slice(0, places), slice(places, 2 * places)
+    dk_ref[0] = gather(slice(0, count), left)
+    dv_ref[0] = gather(slice(0, count), right)
+    rest = slice(count, count + half)
+    dq_ref[0, :half, :] = gather(rest, left)
+    dq_ref[0, half:, :] = gather(rest, right)
+
+
+def join(place, blocks, chunk, rows, tokens, earlier):
+    n = len(blocks)
     shape = jax.ShapeDtypeStruct((1, WIDTH, tokens), jnp.bfloat16)
-    return pl.pallas_call(
-        functools.partial(join_kernel, spans, n),
-        out_shape=(shape,) * 3,
-        compiler_params=pltpu.CompilerParams(vmem_limit_bytes=60 * 2**20),
+    vmem = pl.BlockSpec(memory_space=pltpu.VMEM)
+    whole = pl.BlockSpec(memory_space=pl.ANY)
+    earlier = [] if earlier is None else list(earlier)
+    return pl.pallas_call(
+        functools.partial(join_kernel, n),
+        grid=(1,),
+        in_specs=[pl.BlockSpec(memory_space=pltpu.SMEM)] + [vmem] * n + [whole] * len(earlier),
+        out_specs=[pl.BlockSpec((1, rows, tokens), lambda i: (0, chunk, 0))] * 3,
+        out_shape=[shape] * 3,
+        scratch_shapes=[pltpu.VMEM((n, *blocks[0].shape), jnp.bfloat16)],
+        input_output_aliases={1 + n + i: i for i in range(len(earlier))},
+        compiler_params=pltpu.CompilerParams(vmem_limit_bytes=24 * 2**20),
         name="unpack",
-    )(*packed)
-
-
-def clip_kernel(window, heads, bounds, own_ref, low_ref, high_ref, out_ref, x_ref, y_ref, coef_ref):
+    )(place, *blocks, *earlier)
+
+
+def clip_kernel(window, heads, place_ref, bounds, *refs):
+    own, low_ref, high_ref = refs[:window], refs[window], refs[window + 1]
+    outs, (x_ref, y_ref, coef_ref, grad_ref) = refs[window + 2 : 2 * window + 2], refs[-4:]
     halo = window - 1
     extent = window + 2 * halo
-    lanes = out_ref.shape[2]
+    lanes = grad_ref.shape[2]
     places = lanes // 2
     rows = heads * HDIM
     is_left = lax.broadcasted_iota(jnp.int32, (1, lanes), 1) < places
     lowest, highest = bounds[0, halo], bounds[1, halo + window - 1]
 
-    def widen(ref, at, frame):
-        x_ref[frame] = ref[at, 0].astype(jnp.float32)
-        y_ref[frame] = ref[at, 1].astype(jnp.float32)
-
-    for at in range(window):
-        widen(own_ref, at, halo + at)
+    def widen(ref, frame):
+        x_ref[frame] = ref[0].astype(jnp.float32)
+        y_ref[frame] = ref[1].astype(jnp.float32)
+
+    for step, block in enumerate(own):
+        widen(block, halo + (place_ref[0] ^ step))
     for at in range(halo):
-        pl.when(at >= lowest)(functools.partial(widen, low_ref, at, at))
+        pl.when(at >= lowest)(functools.partial(widen, low_ref.at[at], at))
         frame = halo + window + at
-        pl.when(frame < highest)(functools.partial(widen, high_ref, at, frame))
+        pl.when(frame < highest)(functools.partial(widen, high_ref.at[at], frame))
 
     def partners(frame):
         first, last = bounds[0, frame], bounds[1, frame]
@@ -200,43 +254,49 @@
             if head % 2 == 1:
                 span = slice((head - 1) * HDIM, (head + 1) * HDIM)
                 value = jnp.concatenate(by_key[head - 1 :], axis=0)
-                out_ref[at, span, :] = value.astype(jnp.bfloat16)
+                grad_ref[at, span, :] = value.astype(jnp.bfloat16)
         half = heads // 2
         folded = [
             jnp.where(is_left, by_query[head], swapped(by_query[head + half]))
             for head in range(half)
         ]
         value = jnp.concatenate(folded, axis=0)
-        out_ref[at, rows:, :] = value.astype(jnp.bfloat16)
+        grad_ref[at, rows:, :] = value.astype(jnp.bfloat16)
         return carry
 
     lax.fori_loop(0, window, gradients, 0)
-
-
-def clip_grads(bounds, own, low, high):
-    window, _, rows, lanes = own.shape
+    for step, out in enumerate(outs):
+        out[...] = grad_ref[place_ref[0] ^ step]
+
+
+def clip_grads(place, bounds, own, low, high):
+    window = len(own)
+    _, rows, lanes = own[0].shape
     heads = rows // HDIM
     extent = 3 * window - 2
     vmem = pl.BlockSpec(memory_space=pltpu.VMEM)
+    smem = pl.BlockSpec(memory_space=pltpu.SMEM)
     work = extent * window * rows * lanes
+    shape = (rows + rows // 2, lanes)
     return pl.pallas_call(
         functools.partial(clip_kernel, window, heads),
-        out_shape=jax.ShapeDtypeStruct((window, rows + rows // 2, lanes), jnp.bfloat16),
-        in_specs=[pl.BlockSpec(memory_space=pltpu.SMEM), vmem, vmem, vmem],
-        out_specs=vmem,
+        out_shape=[jax.ShapeDtypeStruct(shape, jnp.bfloat16)] * window,
+        in_specs=[smem, smem] + [vmem] * (window + 2),
+        out_specs=[vmem] * window,
         scratch_shapes=[
             pltpu.VMEM((extent, rows, lanes), jnp.float32),
             pltpu.VMEM((extent, rows, lanes), jnp.float32),
             pltpu.VMEM((extent, window, heads, lanes), jnp.float32),
+            pltpu.VMEM((window, *shape), jnp.bfloat16),
         ],
         compiler_params=pltpu.CompilerParams(vmem_limit_bytes=48 * 2**20),
         cost_estimate=pl.CostEstimate(
             flops=400 * work,
-            bytes_accessed=2 * (own.size + low.size + high.size),
+            bytes_accessed=2 * (window * own[0].size + low.size + high.size),
             transcendentals=extent * window * heads * lanes,
         ),
         name="clips",
-    )(bounds, own, low, high)
+    )(place, bounds, *own, low, high)
 
 
 def clip_bounds(clip_len, window):
@@ -261,21 +321,21 @@
     window = q_time.shape[0] * n
     tokens = q_time.shape[1]
     bounds = clip_bounds(clip_len, window)
+    place = lax.axis_index("seq").astype(jnp.int32).reshape(1)
     time = turned(q_time, k_time, v_time, cot_time)
-    spans, back = [], []
-    head = 0
-    for heads in CHUNKS:
-        span = slice(head * HDIM, (head + heads) * HDIM)
-        head += heads
-        packed = split(time, span, n)
-        own = lax.all_to_all(packed, "seq", split_axis=0, concat_axis=0, tiled=True)
-        low = shifted(own[1:], "grp", 1)
-        high = shifted(own[: window - 1], "grp", -1)
-        grads = clip_grads(bounds, own, low, high)
-        back.append(lax.all_to_all(grads, "seq", split_axis=0, concat_axis=0, tiled=True))
-        spans.append(span)
+    rows = WIDTH // CHUNKS
+    back = []
+    for chunk in range(CHUNKS):
+        own = exchange(split(place, time, chunk, rows, n))
+        first, last = sides(place, own)
+        low = shifted(last, "grp", 1)
+        high = shifted(first, "grp", -1)
+        back.append(exchange(clip_grads(place, bounds, own, low, high)))
+    grads = None
+    for chunk, blocks in enumerate(back):
+        grads = join(place, blocks, chunk, rows, tokens, grads)
     space = frame_grads(*turned(q_space, k_space, v_space, cot_space))
-    return turned(*space, *join(back, spans, tokens))
+    return turned(*space, *grads)
 
 
 def solution(mesh):

time: 91.2 us -> 62.6 us (0.69)
  the two profiles are of different devices: /device:TPU:2 before, /device:TPU:12 now
where the time goes in v1:
time: 62.6 us; the launch traced here: 62.1 us
  starting transfers between devices  28 us (45%)
  waiting for transfers between devices  17.2 us (27%)
  Pallas kernels  15.8 us (25%)
  between operations  0.75 us (1%)
    ppermute x12, waiting for transfers between devices, exchange(): lax.ppermute(blocks[step], 'seq', [(i, i ^ step) for i in range(n)])  15.9 us
    ppermute x12, starting transfers between devices, exchange(): lax.ppermute(blocks[step], 'seq', [(i, i ^ step) for i in range(n)])  15.1 us
    ppermute x4, starting transfers between devices, shifted(): return lax.ppermute(value, axis, pairs)  12.9 us
    pallas_call x1, Pallas kernels, frame_grads(): pl.pallas_call(frame_kernel, out_shape=(shape, shape, shape), compiler_pa...  5.53 us
    pallas_call x2, Pallas kernels, split(): pl.pallas_call(functools.partial(split_kernel, n), grid=(1,), in_specs=[p...  4.36 us
    pallas_call x2, Pallas kernels, clip_grads(): pl.pallas_call(functools.partial(clip_kernel, window, heads), out_shape=[...  3.91 us
    pallas_call x2, Pallas kernels, join(): pl.pallas_call(functools.partial(join_kernel, n), grid=(1,), in_specs=[pl...  1.79 us
    ppermute x4, waiting for transfers between devices, shifted(): return lax.ppermute(value, axis, pairs)  1.33 us
  transfers between devices with their start and end apart: 16, of which 9 were waited for; matrix products, arithmetic and copies ran while one was open for 0% of the time, Pallas kernels for 21%

profile of v1, /device:TPU:12, one launch (start us, length us, event | category | flops | bytes accessed | tf_op | source)
XLA Modules:
  0.0 62.1 jit_solution(4860320286501836281)
XLA Ops:
  0.6 2.2 %pack.3 = (bf16[2,288,128]{2,1,0:T(8,128)(2,1)}, bf16[2,288,128]{2,1,0:T(8,128)(2,1)}, bf16[2,288,128]{2,1,0:T(8,128)(2,1)}, bf16[2,288,128]{2,1,0:T(8,128)(2,1)}) custom-call(s32[1]{0:T(128)} %bitcast.7.place_ref, bf16[1,576,256]{2,1,0:T(8,128)(2,1)} %bitcast.19, bf16[1,576,256]{2,1,0:T(8,128)(2,1)} %bitcast.21, bf16[1,576,256]{2,1,0:T(8,128)(2,1)} %bitcast.23, ...), custom_call_target="tpu_custom_call" | custom-call | tf_op jit(solution)/shard_map/pack/pallas_call | solution.py:98
  2.8 1.6 %collective-permute-start.10 = (bf16[2,288,128]{2,1,0:T(8,128)(2,1)}, bf16[2,288,128]{2,1,0:T(8,128)(2,1)S(1)}, u32[]{:S(2)}, u32[]{:S(2)}) collective-permute-start(bf16[2,288,128]{2,1,0:T(8,128)(2,1)} %get-tuple-element.51), channel_id=1, source_target_pairs={{0,3},{1,2},{2,1},{3,0},{4,7},{5,6},{6,5},{7,4},{8,11},{9,10},{10,... | collective-permute-start | bytes 442376 | tf_op jit(solution)/shard_map/ppermute | solution.py:114
  4.4 2.5 %collective-permute-start.8 = (bf16[2,288,128]{2,1,0:T(8,128)(2,1)}, bf16[2,288,128]{2,1,0:T(8,128)(2,1)S(1)}, u32[]{:S(2)}, u32[]{:S(2)}) collective-permute-start(bf16[2,288,128]{2,1,0:T(8,128)(2,1)} %get-tuple-element.49), channel_id=1, source_target_pairs={{0,1},{1,0},{2,3},{3,2},{4,5},{5,4},{6,7},{7,6},{8,9},{9,8},{10,11... | collective-permute-start | bytes 442376 | tf_op jit(solution)/shard_map/ppermute | solution.py:114
  6.8 0.0 copy-start.1
  6.8 0.0 collective-permute-start.9
  6.9 2.2 %pack.2 = (bf16[2,288,128]{2,1,0:T(8,128)(2,1)}, bf16[2,288,128]{2,1,0:T(8,128)(2,1)}, bf16[2,288,128]{2,1,0:T(8,128)(2,1)}, bf16[2,288,128]{2,1,0:T(8,128)(2,1)}) custom-call(s32[1]{0:T(128)} %bitcast.7.place_ref, bf16[1,576,256]{2,1,0:T(8,128)(2,1)} %bitcast.20, bf16[1,576,256]{2,1,0:T(8,128)(2,1)} %bitcast.22, bf16[1,576,256]{2,1,0:T(8,128)(2,1)} %bitcast.24, ...), custom_call_target="tpu_custom_call" | custom-call | tf_op jit(solution)/shard_map/pack/pallas_call | solution.py:98
  9.1 0.0 copy-start.2
  9.1 0.7 %collective-permute-start = (bf16[2,288,128]{2,1,0:T(8,128)(2,1)}, bf16[2,288,128]{2,1,0:T(8,128)(2,1)S(1)}, u32[]{:S(2)}, u32[]{:S(2)}) collective-permute-start(bf16[2,288,128]{2,1,0:T(8,128)(2,1)} %get-tuple-element.39), channel_id=1, source_target_pairs={{0,1},{1,0},{2,3},{3,2},{4,5},{5,4},{6,7},{7,6},{8,9},{9,8},{10,11... | collective-permute-start | bytes 442376 | tf_op jit(solution)/shard_map/ppermute | solution.py:114
  9.8 2.2 %collective-permute-start.1 = (bf16[2,288,128]{2,1,0:T(8,128)(2,1)}, bf16[2,288,128]{2,1,0:T(8,128)(2,1)S(1)}, u32[]{:S(2)}, u32[]{:S(2)}) collective-permute-start(bf16[2,288,128]{2,1,0:T(8,128)(2,1)} %get-tuple-element.40), channel_id=1, source_target_pairs={{0,2},{1,3},{2,0},{3,1},{4,6},{5,7},{6,4},{7,5},{8,10},{9,11},{10,... | collective-permute-start | bytes 442376 | tf_op jit(solution)/shard_map/ppermute | solution.py:114
  12.0 0.0 copy-done.2
  12.0 0.1 select_reduce_fusion.2
  12.1 1.7 %collective-permute-done.10.refs_3_ = bf16[2,288,128]{2,1,0:T(8,128)(2,1)S(1)} collective-permute-done((bf16[2,288,128]{2,1,0:T(8,128)(2,1)}, bf16[2,288,128]{2,1,0:T(8,128)(2,1)S(1)}, u32[]{:S(2)}, u32[]{:S(2)}) %collective-permute-start.10) | collective-permute-done | bytes 147488 | tf_op jit(solution)/shard_map/ppermute | solution.py:114
  13.8 1.0 %collective-permute-start.2 = (bf16[2,288,128]{2,1,0:T(8,128)(2,1)}, bf16[2,288,128]{2,1,0:T(8,128)(2,1)S(1)}, u32[]{:S(2)}, u32[]{:S(2)}) collective-permute-start(bf16[2,288,128]{2,1,0:T(8,128)(2,1)} %get-tuple-element.41), channel_id=1, source_target_pairs={{0,3},{1,2},{2,1},{3,0},{4,7},{5,6},{6,5},{7,4},{8,11},{9,10},{10,... | collective-permute-start | bytes 442376 | tf_op jit(solution)/shard_map/ppermute | solution.py:114
  14.8 0.2 collective-permute-done.8.refs_1_
  14.9 3.4 %collective-permute-done.9.refs_2_ = bf16[2,288,128]{2,1,0:T(8,128)(2,1)S(1)} collective-permute-done((bf16[2,288,128]{2,1,0:T(8,128)(2,1)}, bf16[2,288,128]{2,1,0:T(8,128)(2,1)S(1)}, u32[]{:S(2)}, u32[]{:S(2)}) %collective-permute-start.9) | collective-permute-done | bytes 147488 | tf_op jit(solution)/shard_map/ppermute | solution.py:114
  18.4 0.0 copy-done.1
  18.4 0.0 copy-start
  18.4 0.1 sides.3
  18.5 1.9 %collective-permute-start.11 = (bf16[3,2,288,128]{3,2,1,0:T(8,128)(2,1)S(1)}, bf16[3,2,288,128]{3,2,1,0:T(8,128)(2,1)S(1)}, u32[]{:S(2)}, u32[]{:S(2)}) collective-permute-start(bf16[3,2,288,128]{3,2,1,0:T(8,128)(2,1)S(1)} %get-tuple-element.52), channel_id=1, source_target_pairs={{0,4},{4,8},{8,12},{12,16},{16,20},{20,24},{24,28},{1,5},{5,9},{9,... | collective-permute-start | bytes 1327112 | tf_op jit(solution)/shard_map/ppermute | solution.py:22
  20.4 4.5 %collective-permute-start.12 = (bf16[3,2,288,128]{3,2,1,0:T(8,128)(2,1)S(1)}, bf16[3,2,288,128]{3,2,1,0:T(8,128)(2,1)S(1)}, u32[]{:S(2)}, u32[]{:S(2)}) collective-permute-start(bf16[3,2,288,128]{3,2,1,0:T(8,128)(2,1)S(1)} %get-tuple-element.53), channel_id=1, source_target_pairs={{4,0},{8,4},{12,8},{16,12},{20,16},{24,20},{28,24},{5,1},{9,5},{13... | collective-permute-start | bytes 1327112 | tf_op jit(solution)/shard_map/ppermute | solution.py:22
  25.0 0.2 select_reduce_fusion.1
  25.2 0.0 collective-permute-done.refs_1_
  25.2 2.7 %collective-permute-done.1.refs_2_ = bf16[2,288,128]{2,1,0:T(8,128)(2,1)S(1)} collective-permute-done((bf16[2,288,128]{2,1,0:T(8,128)(2,1)}, bf16[2,288,128]{2,1,0:T(8,128)(2,1)S(1)}, u32[]{:S(2)}, u32[]{:S(2)}) %collective-permute-start.1) | collective-permute-done | bytes 147488 | tf_op jit(solution)/shard_map/ppermute | solution.py:114
  27.9 2.8 %collective-permute-done.2.refs_3_ = bf16[2,288,128]{2,1,0:T(8,128)(2,1)S(1)} collective-permute-done((bf16[2,288,128]{2,1,0:T(8,128)(2,1)}, bf16[2,288,128]{2,1,0:T(8,128)(2,1)S(1)}, u32[]{:S(2)}, u32[]{:S(2)}) %collective-permute-start.2) | collective-permute-done | bytes 147488 | tf_op jit(solution)/shard_map/ppermute | solution.py:114
  30.8 0.0 copy-done
  30.8 0.1 sides.2
  30.9 1.9 %collective-permute-start.3 = (bf16[3,2,288,128]{3,2,1,0:T(8,128)(2,1)S(1)}, bf16[3,2,288,128]{3,2,1,0:T(8,128)(2,1)S(1)}, u32[]{:S(2)}, u32[]{:S(2)}) collective-permute-start(bf16[3,2,288,128]{3,2,1,0:T(8,128)(2,1)S(1)} %get-tuple-element.42), channel_id=1, source_target_pairs={{0,4},{4,8},{8,12},{12,16},{16,20},{20,24},{24,28},{1,5},{5,9},{9,... | collective-permute-start | bytes 1327112 | tf_op jit(solution)/shard_map/ppermute | solution.py:22
  32.8 4.5 %collective-permute-start.4 = (bf16[3,2,288,128]{3,2,1,0:T(8,128)(2,1)S(1)}, bf16[3,2,288,128]{3,2,1,0:T(8,128)(2,1)S(1)}, u32[]{:S(2)}, u32[]{:S(2)}) collective-permute-start(bf16[3,2,288,128]{3,2,1,0:T(8,128)(2,1)S(1)} %get-tuple-element.43), channel_id=1, source_target_pairs={{4,0},{8,4},{12,8},{16,12},{20,16},{24,20},{28,24},{5,1},{9,5},{13... | collective-permute-start | bytes 1327112 | tf_op jit(solution)/shard_map/ppermute | solution.py:22
  37.4 0.0 collective-permute-done.11.refs_4_
  37.4 0.0 collective-permute-done.12.refs_5_
  37.4 2.0 %clips.3 = (bf16[432,128]{1,0:T(8,128)(2,1)S(1)}, bf16[432,128]{1,0:T(8,128)(2,1)S(1)}, bf16[432,128]{1,0:T(8,128)(2,1)S(1)}, bf16[432,128]{1,0:T(8,128)(2,1)S(1)}) custom-call(s32[1]{0:T(128)} %bitcast.7.place_ref, s32[2,10]{1,0:T(2,128)S(1)} %pad_add_fusion.bounds, bf16[2,288,128]{2,1,0:T(8,128)(2,1)S(1)} %copy-done.1, ...), custom_call_target="tpu_custom_call" | custom-call | flops 589824000 | bytes 1474560 | tf_op jit(solution)/shard_map/clips/pallas_call | solution.py:281
  39.4 0.1 collective-permute-start.13
  39.5 3.0 %collective-permute-start.14 = (bf16[432,128]{1,0:T(8,128)(2,1)S(1)}, bf16[432,128]{1,0:T(8,128)(2,1)S(1)}, u32[]{:S(2)}, u32[]{:S(2)}) collective-permute-start(bf16[432,128]{1,0:T(8,128)(2,1)S(1)} %get-tuple-element.56), channel_id=1, source_target_pairs={{0,2},{1,3},{2,0},{3,1},{4,6},{5,7},{6,4},{7,5},{8,10},{9,11},{10,... | collective-permute-start | bytes 331784 | tf_op jit(solution)/shard_map/ppermute | solution.py:114
  42.5 0.5 collective-permute-start.15
  42.9 0.4 collective-permute-done.3.refs_4_
  43.3 0.9 %collective-permute-done.4.refs_5_ = bf16[3,2,288,128]{3,2,1,0:T(8,128)(2,1)S(1)} collective-permute-done((bf16[3,2,288,128]{3,2,1,0:T(8,128)(2,1)S(1)}, bf16[3,2,288,128]{3,2,1,0:T(8,128)(2,1)S(1)}, u32[]{:S(2)}, u32[]{:S(2)}) %collective-permute-start.4) | collective-permute-done | bytes 442400 | tf_op jit(solution)/shard_map/ppermute | solution.py:22
  44.3 2.0 %clips.2 = (bf16[432,128]{1,0:T(8,128)(2,1)S(1)}, bf16[432,128]{1,0:T(8,128)(2,1)S(1)}, bf16[432,128]{1,0:T(8,128)(2,1)S(1)}, bf16[432,128]{1,0:T(8,128)(2,1)S(1)}) custom-call(s32[1]{0:T(128)} %bitcast.7.place_ref, s32[2,10]{1,0:T(2,128)S(1)} %pad_add_fusion.bounds, bf16[2,288,128]{2,1,0:T(8,128)(2,1)S(1)} %copy-done, ...), custom_call_target="tpu_custom_call" | custom-call | flops 589824000 | bytes 1474560 | tf_op jit(solution)/shard_map/clips/pallas_call | solution.py:281
  46.2 0.5 collective-permute-start.5
  46.7 2.6 %collective-permute-start.6 = (bf16[432,128]{1,0:T(8,128)(2,1)S(1)}, bf16[432,128]{1,0:T(8,128)(2,1)S(1)}, u32[]{:S(2)}, u32[]{:S(2)}) collective-permute-start(bf16[432,128]{1,0:T(8,128)(2,1)S(1)} %get-tuple-element.46), channel_id=1, source_target_pairs={{0,2},{1,3},{2,0},{3,1},{4,6},{5,7},{6,4},{7,5},{8,10},{9,11},{10,... | collective-permute-start | bytes 331784 | tf_op jit(solution)/shard_map/ppermute | solution.py:114
  49.3 0.0 collective-permute-done.13.refs_1_
  49.3 0.5 collective-permute-start.7
  49.8 5.5 %space.1 = (bf16[1,576,256]{2,1,0:T(8,128)(2,1)}, bf16[1,576,256]{2,1,0:T(8,128)(2,1)}, bf16[1,576,256]{2,1,0:T(8,128)(2,1)}) custom-call(bf16[1,576,256]{2,1,0:T(8,128)(2,1)} %bitcast.30, bf16[1,576,256]{2,1,0:T(8,128)(2,1)} %bitcast.31, bf16[1,576,256]{2,1,0:T(8,128)(2,1)} %bitcast.32, bf16[1,576,256]{2,1,0:T(8,128)(2,1)} %bitcast.33), custom_call_target="tpu_custom_call" | custom-call | flops 1610612736 | bytes 2064384 | tf_op jit(solution)/shard_map/space/pallas_call | solution.py:70
  55.3 0.0 collective-permute-done.14.refs_2_
  55.3 2.4 %collective-permute-done.15.refs_3_ = bf16[432,128]{1,0:T(8,128)(2,1)S(1)} collective-permute-done((bf16[432,128]{1,0:T(8,128)(2,1)S(1)}, bf16[432,128]{1,0:T(8,128)(2,1)S(1)}, u32[]{:S(2)}, u32[]{:S(2)}) %collective-permute-start.15) | collective-permute-done | bytes 110624 | tf_op jit(solution)/shard_map/ppermute | solution.py:114
  57.7 0.9 %unpack.2 = (bf16[1,576,256]{2,1,0:T(8,128)(2,1)}, bf16[1,576,256]{2,1,0:T(8,128)(2,1)}, bf16[1,576,256]{2,1,0:T(8,128)(2,1)}) custom-call(s32[1]{0:T(128)} %bitcast.7.place_ref, bf16[432,128]{1,0:T(8,128)(2,1)S(1)} %get-tuple-element.54.refs_0_, bf16[432,128]{1,0:T(8,128)(2,1)S(1)} %collective-permute-done.13.refs_1_, ...), custom_call_target="tpu_custom_call" | custom-call | tf_op jit(solution)/shard_map/unpack/pallas_call | solution.py:171
  58.6 0.0 collective-permute-done.5.refs_1_
  58.6 0.0 collective-permute-done.6.refs_2_
  58.6 2.6 %collective-permute-done.7.refs_3_ = bf16[432,128]{1,0:T(8,128)(2,1)S(1)} collective-permute-done((bf16[432,128]{1,0:T(8,128)(2,1)S(1)}, bf16[432,128]{1,0:T(8,128)(2,1)S(1)}, u32[]{:S(2)}, u32[]{:S(2)}) %collective-permute-start.7) | collective-permute-done | bytes 110624 | tf_op jit(solution)/shard_map/ppermute | solution.py:114
  61.2 0.9 %unpack.3 = (bf16[1,576,256]{2,1,0:T(8,128)(2,1)}, bf16[1,576,256]{2,1,0:T(8,128)(2,1)}, bf16[1,576,256]{2,1,0:T(8,128)(2,1)}) custom-call(s32[1]{0:T(128)} %bitcast.7.place_ref, bf16[432,128]{1,0:T(8,128)(2,1)S(1)} %get-tuple-element.44.refs_0_, ...), custom_call_target="tpu_custom_call", output_to_operand_aliasing={{0}: (5, {}), {1}: (6, {}), {2}: (7, {})} | custom-call | tf_op jit(solution)/shard_map/unpack/pallas_call | solution.py:171
  (4 shorter events, 0.0 us)
Async XLA Ops:
  2.8 11.0 %collective-permute-start.10 = (bf16[2,288,128]{2,1,0:T(8,128)(2,1)}, bf16[2,288,128]{2,1,0:T(8,128)(2,1)S(1)}, u32[]{:S(2)}, u32[]{:S(2)}) collective-permute-start(bf16[2,288,128]{2,1,0:T(8,128)(2,1)} %get-tuple-element.51), channel_id=1, source_target_pairs={{0,3},{1,2},{2,1},{3,0},{4,7},{5,6},{6,5},{7,4},{8,11},{9,10},{10,... | collective-permute-start | bytes 442376 | tf_op jit(solution)/shard_map/ppermute | solution.py:114
  4.4 10.6 %collective-permute-start.8 = (bf16[2,288,128]{2,1,0:T(8,128)(2,1)}, bf16[2,288,128]{2,1,0:T(8,128)(2,1)S(1)}, u32[]{:S(2)}, u32[]{:S(2)}) collective-permute-start(bf16[2,288,128]{2,1,0:T(8,128)(2,1)} %get-tuple-element.49), channel_id=1, source_target_pairs={{0,1},{1,0},{2,3},{3,2},{4,5},{5,4},{6,7},{7,6},{8,9},{9,8},{10,11... | collective-permute-start | bytes 442376 | tf_op jit(solution)/shard_map/ppermute | solution.py:114
  6.8 11.5 %copy-start.1 = (bf16[2,288,128]{2,1,0:T(8,128)(2,1)S(1)}, bf16[2,288,128]{2,1,0:T(8,128)(2,1)}, u32[]{:S(2)}) copy-start(bf16[2,288,128]{2,1,0:T(8,128)(2,1)} %get-tuple-element.48.refs_0_) | copy-start | bytes 442372
  6.8 11.5 %collective-permute-start.9 = (bf16[2,288,128]{2,1,0:T(8,128)(2,1)}, bf16[2,288,128]{2,1,0:T(8,128)(2,1)S(1)}, u32[]{:S(2)}, u32[]{:S(2)}) collective-permute-start(bf16[2,288,128]{2,1,0:T(8,128)(2,1)} %get-tuple-element.50), channel_id=1, source_target_pairs={{0,2},{1,3},{2,0},{3,1},{4,6},{5,7},{6,4},{7,5},{8,10},{9,11},{10,... | collective-permute-start | bytes 442376 | tf_op jit(solution)/shard_map/ppermute | solution.py:114
  9.1 3.0 %copy-start.2 = (s32[16]{0:T(128)S(1)}, s32[16]{0:T(128)}, u32[]{:S(2)}) copy-start(s32[16]{0:T(128)} %param.17) | copy-start | bytes 196
  9.1 16.1 %collective-permute-start = (bf16[2,288,128]{2,1,0:T(8,128)(2,1)}, bf16[2,288,128]{2,1,0:T(8,128)(2,1)S(1)}, u32[]{:S(2)}, u32[]{:S(2)}) collective-permute-start(bf16[2,288,128]{2,1,0:T(8,128)(2,1)} %get-tuple-element.39), channel_id=1, source_target_pairs={{0,1},{1,0},{2,3},{3,2},{4,5},{5,4},{6,7},{7,6},{8,9},{9,8},{10,11... | collective-permute-start | bytes 442376 | tf_op jit(solution)/shard_map/ppermute | solution.py:114
  9.8 18.1 %collective-permute-start.1 = (bf16[2,288,128]{2,1,0:T(8,128)(2,1)}, bf16[2,288,128]{2,1,0:T(8,128)(2,1)S(1)}, u32[]{:S(2)}, u32[]{:S(2)}) collective-permute-start(bf16[2,288,128]{2,1,0:T(8,128)(2,1)} %get-tuple-element.40), channel_id=1, source_target_pairs={{0,2},{1,3},{2,0},{3,1},{4,6},{5,7},{6,4},{7,5},{8,10},{9,11},{10,... | collective-permute-start | bytes 442376 | tf_op jit(solution)/shard_map/ppermute | solution.py:114
  13.8 17.0 %collective-permute-start.2 = (bf16[2,288,128]{2,1,0:T(8,128)(2,1)}, bf16[2,288,128]{2,1,0:T(8,128)(2,1)S(1)}, u32[]{:S(2)}, u32[]{:S(2)}) collective-permute-start(bf16[2,288,128]{2,1,0:T(8,128)(2,1)} %get-tuple-element.41), channel_id=1, source_target_pairs={{0,3},{1,2},{2,1},{3,0},{4,7},{5,6},{6,5},{7,4},{8,11},{9,10},{10,... | collective-permute-start | bytes 442376 | tf_op jit(solution)/shard_map/ppermute | solution.py:114
  18.4 12.4 %copy-start = (bf16[2,288,128]{2,1,0:T(8,128)(2,1)S(1)}, bf16[2,288,128]{2,1,0:T(8,128)(2,1)}, u32[]{:S(2)}) copy-start(bf16[2,288,128]{2,1,0:T(8,128)(2,1)} %get-tuple-element.38.refs_0_) | copy-start | bytes 442372
  18.5 18.9 %collective-permute-start.11 = (bf16[3,2,288,128]{3,2,1,0:T(8,128)(2,1)S(1)}, bf16[3,2,288,128]{3,2,1,0:T(8,128)(2,1)S(1)}, u32[]{:S(2)}, u32[]{:S(2)}) collective-permute-start(bf16[3,2,288,128]{3,2,1,0:T(8,128)(2,1)S(1)} %get-tuple-element.52), channel_id=1, source_target_pairs={{0,4},{4,8},{8,12},{12,16},{16,20},{20,24},{24,28},{1,5},{5,9},{9,... | collective-permute-start | bytes 1327112 | tf_op jit(solution)/shard_map/ppermute | solution.py:22
  20.4 17.0 %collective-permute-start.12 = (bf16[3,2,288,128]{3,2,1,0:T(8,128)(2,1)S(1)}, bf16[3,2,288,128]{3,2,1,0:T(8,128)(2,1)S(1)}, u32[]{:S(2)}, u32[]{:S(2)}) collective-permute-start(bf16[3,2,288,128]{3,2,1,0:T(8,128)(2,1)S(1)} %get-tuple-element.53), channel_id=1, source_target_pairs={{4,0},{8,4},{12,8},{16,12},{20,16},{24,20},{28,24},{5,1},{9,5},{13... | collective-permute-start | bytes 1327112 | tf_op jit(solution)/shard_map/ppermute | solution.py:22
  30.9 12.4 %collective-permute-start.3 = (bf16[3,2,288,128]{3,2,1,0:T(8,128)(2,1)S(1)}, bf16[3,2,288,128]{3,2,1,0:T(8,128)(2,1)S(1)}, u32[]{:S(2)}, u32[]{:S(2)}) collective-permute-start(bf16[3,2,288,128]{3,2,1,0:T(8,128)(2,1)S(1)} %get-tuple-element.42), channel_id=1, source_target_pairs={{0,4},{4,8},{8,12},{12,16},{16,20},{20,24},{24,28},{1,5},{5,9},{9,... | collective-permute-start | bytes 1327112 | tf_op jit(solution)/shard_map/ppermute | solution.py:22
  32.8 11.4 %collective-permute-start.4 = (bf16[3,2,288,128]{3,2,1,0:T(8,128)(2,1)S(1)}, bf16[3,2,288,128]{3,2,1,0:T(8,128)(2,1)S(1)}, u32[]{:S(2)}, u32[]{:S(2)}) collective-permute-start(bf16[3,2,288,128]{3,2,1,0:T(8,128)(2,1)S(1)} %get-tuple-element.43), channel_id=1, source_target_pairs={{4,0},{8,4},{12,8},{16,12},{20,16},{24,20},{28,24},{5,1},{9,5},{13... | collective-permute-start | bytes 1327112 | tf_op jit(solution)/shard_map/ppermute | solution.py:22
  39.4 9.9 %collective-permute-start.13 = (bf16[432,128]{1,0:T(8,128)(2,1)S(1)}, bf16[432,128]{1,0:T(8,128)(2,1)S(1)}, u32[]{:S(2)}, u32[]{:S(2)}) collective-permute-start(bf16[432,128]{1,0:T(8,128)(2,1)S(1)} %get-tuple-element.55), channel_id=1, source_target_pairs={{0,1},{1,0},{2,3},{3,2},{4,5},{5,4},{6,7},{7,6},{8,9},{9,8},{10,11... | collective-permute-start | bytes 331784 | tf_op jit(solution)/shard_map/ppermute | solution.py:114
  39.5 15.8 %collective-permute-start.14 = (bf16[432,128]{1,0:T(8,128)(2,1)S(1)}, bf16[432,128]{1,0:T(8,128)(2,1)S(1)}, u32[]{:S(2)}, u32[]{:S(2)}) collective-permute-start(bf16[432,128]{1,0:T(8,128)(2,1)S(1)} %get-tuple-element.56), channel_id=1, source_target_pairs={{0,2},{1,3},{2,0},{3,1},{4,6},{5,7},{6,4},{7,5},{8,10},{9,11},{10,... | collective-permute-start | bytes 331784 | tf_op jit(solution)/shard_map/ppermute | solution.py:114
  42.5 15.3 %collective-permute-start.15 = (bf16[432,128]{1,0:T(8,128)(2,1)S(1)}, bf16[432,128]{1,0:T(8,128)(2,1)S(1)}, u32[]{:S(2)}, u32[]{:S(2)}) collective-permute-start(bf16[432,128]{1,0:T(8,128)(2,1)S(1)} %get-tuple-element.57), channel_id=1, source_target_pairs={{0,3},{1,2},{2,1},{3,0},{4,7},{5,6},{6,5},{7,4},{8,11},{9,10},{10,... | collective-permute-start | bytes 331784 | tf_op jit(solution)/shard_map/ppermute | solution.py:114
  46.2 12.4 %collective-permute-start.5 = (bf16[432,128]{1,0:T(8,128)(2,1)S(1)}, bf16[432,128]{1,0:T(8,128)(2,1)S(1)}, u32[]{:S(2)}, u32[]{:S(2)}) collective-permute-start(bf16[432,128]{1,0:T(8,128)(2,1)S(1)} %get-tuple-element.45), channel_id=1, source_target_pairs={{0,1},{1,0},{2,3},{3,2},{4,5},{5,4},{6,7},{7,6},{8,9},{9,8},{10,11... | collective-permute-start | bytes 331784 | tf_op jit(solution)/shard_map/ppermute | solution.py:114
  46.7 11.9 %collective-permute-start.6 = (bf16[432,128]{1,0:T(8,128)(2,1)S(1)}, bf16[432,128]{1,0:T(8,128)(2,1)S(1)}, u32[]{:S(2)}, u32[]{:S(2)}) collective-permute-start(bf16[432,128]{1,0:T(8,128)(2,1)S(1)} %get-tuple-element.46), channel_id=1, source_target_pairs={{0,2},{1,3},{2,0},{3,1},{4,6},{5,7},{6,4},{7,5},{8,10},{9,11},{10,... | collective-permute-start | bytes 331784 | tf_op jit(solution)/shard_map/ppermute | solution.py:114
  49.3 11.9 %collective-permute-start.7 = (bf16[432,128]{1,0:T(8,128)(2,1)S(1)}, bf16[432,128]{1,0:T(8,128)(2,1)S(1)}, u32[]{:S(2)}, u32[]{:S(2)}) collective-permute-start(bf16[432,128]{1,0:T(8,128)(2,1)S(1)} %get-tuple-element.47), channel_id=1, source_target_pairs={{0,3},{1,2},{2,1},{3,0},{4,7},{5,6},{6,5},{7,4},{8,11},{9,10},{10,... | collective-permute-start | bytes 331784 | tf_op jit(solution)/shard_map/ppermute | solution.py:114

commit v2 on v1

--- a/solution.py
+++ b/solution.py
@@ -12,7 +12,7 @@
 HDIM = 72
 WIDTH = HEADS * HDIM
 SCALING = 1.0 / math.sqrt(HDIM)
-CHUNKS = 2
+CHUNKS = (4, 4)
 masked_score = -1e30
 
 
@@ -80,28 +80,47 @@
     )(queries, keys, values, cotangent)
 
 
-def split_kernel(n, place_ref, q_ref, k_ref, v_ref, g_ref, *refs):
-    outs, held = refs[:n], refs[n]
-    places = q_ref.shape[2] // n
-    for target in range(n):
-        lanes = slice(target * places, (target + 1) * places)
-        for at, (left, right) in enumerate(((q_ref, g_ref), (k_ref, v_ref))):
-            held[target, at] = jnp.concatenate([left[0, :, lanes], right[0, :, lanes]], axis=1)
-    for step, out in enumerate(outs):
-        out[...] = held[place_ref[0] ^ step]
-
-
-def split(place, arrays, chunk, rows, n):
-    tokens = arrays[0].shape[2]
+def split_kernel(n, span, place_ref, *refs):
+    ins, outs, (loaded, held, arrived, left_off) = refs[:4], refs[4 : 4 + n], refs[-4:]
+    loads = [
+        pltpu.make_async_copy(array.at[0, span, :], loaded.at[i], arrived.at[i])
+        for i, array in enumerate(ins)
+    ]
+    for copy in loads:
+        copy.start()
+    places = ins[0].shape[2] // n
+    for at in range(2):
+        loads[2 * at].wait()
+        loads[2 * at + 1].wait()
+        for target in range(n):
+            lanes = slice(target * places, (target + 1) * places)
+            both = [loaded[2 * at, :, lanes], loaded[2 * at + 1, :, lanes]]
+            held[target, at] = jnp.concatenate(both, axis=1)
+    stores = [
+        pltpu.make_async_copy(held.at[place_ref[0] ^ step], out, left_off.at[step])
+        for step, out in enumerate(outs)
+    ]
+    for copy in stores:
+        copy.start()
+    for copy in stores:
+        copy.wait()
+
+
+def split(place, arrays, span, n):
+    rows, tokens = span.stop - span.start, arrays[0].shape[2]
     shape = (2, rows, 2 * tokens // n)
-    block = pl.BlockSpec((1, rows, tokens), lambda i: (0, chunk, 0))
-    return pl.pallas_call(
-        functools.partial(split_kernel, n),
-        grid=(1,),
-        in_specs=[pl.BlockSpec(memory_space=pltpu.SMEM)] + [block] * 4,
-        out_specs=[pl.BlockSpec(shape, lambda i: (0, 0, 0))] * n,
+    hbm = pl.BlockSpec(memory_space=pltpu.HBM)
+    return pl.pallas_call(
+        functools.partial(split_kernel, n, span),
+        in_specs=[pl.BlockSpec(memory_space=pltpu.SMEM)] + [hbm] * 4,
+        out_specs=[hbm] * n,
         out_shape=[jax.ShapeDtypeStruct(shape, jnp.bfloat16)] * n,
-        scratch_shapes=[pltpu.VMEM((n, *shape), jnp.bfloat16)],
+        scratch_shapes=[
+            pltpu.VMEM((4, rows, tokens), jnp.bfloat16),
+            pltpu.VMEM((n, *shape), jnp.bfloat16),
+            pltpu.SemaphoreType.DMA((4,)),
+            pltpu.SemaphoreType.DMA((n,)),
+        ],
         compiler_params=pltpu.CompilerParams(vmem_limit_bytes=60 * 2**20),
         name="pack",
     )(place, *arrays)
@@ -143,11 +162,11 @@
     )(place, *blocks)
 
 
-def join_kernel(n, place_ref, *refs):
-    ins, (dq_ref, dk_ref, dv_ref, held) = refs[:n], refs[-4:]
+def join_kernel(n, span, place_ref, *refs):
+    ins, outs, (held, ready, left_off) = refs[:n], refs[-6:-3], refs[-3:]
     for step, block in enumerate(ins):
         held[place_ref[0] ^ step] = block[...]
-    count = dq_ref.shape[1]
+    count = span.stop - span.start
     half = count // 2
     places = held.shape[2] // 2
 
@@ -155,26 +174,38 @@
         return jnp.concatenate([held[source, rows, lanes] for source in range(n)], axis=1)
 
     left, right = slice(0, places), slice(places, 2 * places)
-    dk_ref[0] = gather(slice(0, count), left)
-    dv_ref[0] = gather(slice(0, count), right)
     rest = slice(count, count + half)
-    dq_ref[0, :half, :] = gather(rest, left)
-    dq_ref[0, half:, :] = gather(rest, right)
-
-
-def join(place, blocks, chunk, rows, tokens, earlier):
+    ready[1] = gather(slice(0, count), left)
+    ready[2] = gather(slice(0, count), right)
+    ready[0, :half, :] = gather(rest, left)
+    ready[0, half:, :] = gather(rest, right)
+    copies = [
+        pltpu.make_async_copy(ready.at[i], out.at[0, span, :], left_off.at[i])
+        for i, out in enumerate(outs)
+    ]
+    for copy in copies:
+        copy.start()
+    for copy in copies:
+        copy.wait()
+
+
+def join(place, blocks, span, tokens, earlier):
     n = len(blocks)
+    rows = span.stop - span.start
     shape = jax.ShapeDtypeStruct((1, WIDTH, tokens), jnp.bfloat16)
     vmem = pl.BlockSpec(memory_space=pltpu.VMEM)
-    whole = pl.BlockSpec(memory_space=pl.ANY)
+    hbm = pl.BlockSpec(memory_space=pltpu.HBM)
     earlier = [] if earlier is None else list(earlier)
     return pl.pallas_call(
-        functools.partial(join_kernel, n),
-        grid=(1,),
-        in_specs=[pl.BlockSpec(memory_space=pltpu.SMEM)] + [vmem] * n + [whole] * len(earlier),
-        out_specs=[pl.BlockSpec((1, rows, tokens), lambda i: (0, chunk, 0))] * 3,
+        functools.partial(join_kernel, n, span),
+        in_specs=[pl.BlockSpec(memory_space=pltpu.SMEM)] + [vmem] * n + [hbm] * len(earlier),
+        out_specs=[hbm] * 3,
         out_shape=[shape] * 3,
-        scratch_shapes=[pltpu.VMEM((n, *blocks[0].shape), jnp.bfloat16)],
+        scratch_shapes=[
+            pltpu.VMEM((n, *blocks[0].shape), jnp.bfloat16),
+            pltpu.VMEM((3, rows, tokens), jnp.bfloat16),
+            pltpu.SemaphoreType.DMA((3,)),
+        ],
         input_output_aliases={1 + n + i: i for i in range(len(earlier))},
         compiler_params=pltpu.CompilerParams(vmem_limit_bytes=24 * 2**20),
         name="unpack",
@@ -322,19 +353,27 @@
     tokens = q_time.shape[1]
     bounds = clip_bounds(clip_len, window)
     place = lax.axis_index("seq").astype(jnp.int32).reshape(1)
-    time = turned(q_time, k_time, v_time, cot_time)
-    rows = WIDTH // CHUNKS
+    time = turned(q_time, cot_time, k_time, v_time)
+    spans = []
+    head = 0
+    for heads in CHUNKS:
+        spans.append(slice(head * HDIM, (head + heads) * HDIM))
+        head += heads
+    space = frame_grads(*turned(q_space, k_space, v_space, cot_space))
     back = []
-    for chunk in range(CHUNKS):
-        own = exchange(split(place, time, chunk, rows, n))
+    own = None
+    for span in spans:
+        packed = list(split(place, time, span, n))
+        if own is not None:
+            packed[2:], own[2] = lax.optimization_barrier((packed[2:], own[2]))
+        own = exchange(packed)
         first, last = sides(place, own)
         low = shifted(last, "grp", 1)
         high = shifted(first, "grp", -1)
         back.append(exchange(clip_grads(place, bounds, own, low, high)))
     grads = None
-    for chunk, blocks in enumerate(back):
-        grads = join(place, blocks, chunk, rows, tokens, grads)
-    space = frame_grads(*turned(q_space, k_space, v_space, cot_space))
+    for span, blocks in zip(spans, back):
+        grads = join(place, blocks, span, tokens, grads)
     return turned(*space, *grads)
 
 

time: 62.6 us -> 63.9 us (1.021)
  the two profiles are of different devices: /device:TPU:12 before, /device:TPU:19 now
where the time goes in v2:
time: 63.9 us; the launch traced here: 63.8 us
  starting transfers between devices  27.4 us (43%)
  waiting for transfers between devices  18.8 us (29%)
  Pallas kernels  16.3 us (26%)
  between operations  0.81 us (1%)
    ppermute x12, starting transfers between devices, exchange(): lax.ppermute(blocks[step], 'seq', [(i, i ^ step) for i in range(n)])  16.3 us
    ppermute x12, waiting for transfers between devices, exchange(): lax.ppermute(blocks[step], 'seq', [(i, i ^ step) for i in range(n)])  13.7 us
    ppermute x4, starting transfers between devices, shifted(): return lax.ppermute(value, axis, pairs)  11.1 us
    pallas_call x1, Pallas kernels, frame_grads(): pl.pallas_call(frame_kernel, out_shape=(shape, shape, shape), compiler_pa...  5.52 us
    ppermute x4, waiting for transfers between devices, shifted(): return lax.ppermute(value, axis, pairs)  5.08 us
    pallas_call x2, Pallas kernels, split(): pl.pallas_call(functools.partial(split_kernel, n, span), in_specs=[pl.Blo...  4.29 us
    pallas_call x2, Pallas kernels, clip_grads(): pl.pallas_call(functools.partial(clip_kernel, window, heads), out_shape=[...  4.26 us
    pallas_call x2, Pallas kernels, join(): pl.pallas_call(functools.partial(join_kernel, n, span), in_specs=[pl.Bloc...  2 us
  transfers between devices with their start and end apart: 16, of which 6 were waited for; matrix products, arithmetic and copies ran while one was open for 0% of the time, Pallas kernels for 21%

profile of v2, /device:TPU:19, one launch (start us, length us, event | category | flops | bytes accessed | tf_op | source)
XLA Modules:
  0.0 63.8 jit_solution(1623671266557883089)
XLA Ops:
  0.6 2.1 %pack.3 = (bf16[2,288,128]{2,1,0:T(8,128)(2,1)}, bf16[2,288,128]{2,1,0:T(8,128)(2,1)}, bf16[2,288,128]{2,1,0:T(8,128)(2,1)}, bf16[2,288,128]{2,1,0:T(8,128)(2,1)}) custom-call(s32[1]{0:T(128)} %bitcast.7.place_ref, bf16[1,576,256]{2,1,0:T(8,128)(2,1)} %bitcast.19, bf16[1,576,256]{2,1,0:T(8,128)(2,1)} %bitcast.21, bf16[1,576,256]{2,1,0:T(8,128)(2,1)} %bitcast.23, ...), custom_call_target="tpu_custom_call" | custom-call | tf_op jit(solution)/shard_map/pack/pallas_call | solution.py:113
  2.8 0.1 collective-permute-start.1
  2.9 2.4 %collective-permute-start.10 = (bf16[2,288,128]{2,1,0:T(8,128)(2,1)}, bf16[2,288,128]{2,1,0:T(8,128)(2,1)S(1)}, u32[]{:S(2)}, u32[]{:S(2)}) collective-permute-start(bf16[2,288,128]{2,1,0:T(8,128)(2,1)} %get-tuple-element.55), channel_id=1, source_target_pairs={{0,3},{1,2},{2,1},{3,0},{4,7},{5,6},{6,5},{7,4},{8,11},{9,10},{10,... | collective-permute-start | bytes 442376 | tf_op jit(solution)/shard_map/ppermute | solution.py:133
  5.3 0.0 copy-start.1
  5.3 1.1 %collective-permute-start.9 = (bf16[2,288,128]{2,1,0:T(8,128)(2,1)}, bf16[2,288,128]{2,1,0:T(8,128)(2,1)S(1)}, u32[]{:S(2)}, u32[]{:S(2)}) collective-permute-start(bf16[2,288,128]{2,1,0:T(8,128)(2,1)} %get-tuple-element.54), channel_id=1, source_target_pairs={{0,1},{1,0},{2,3},{3,2},{4,5},{5,4},{6,7},{7,6},{8,9},{9,8},{10,11... | collective-permute-start | bytes 442376 | tf_op jit(solution)/shard_map/ppermute | solution.py:133
  6.4 2.1 %pack.2 = (bf16[2,288,128]{2,1,0:T(8,128)(2,1)}, bf16[2,288,128]{2,1,0:T(8,128)(2,1)}, bf16[2,288,128]{2,1,0:T(8,128)(2,1)}, bf16[2,288,128]{2,1,0:T(8,128)(2,1)}) custom-call(s32[1]{0:T(128)} %bitcast.7.place_ref, bf16[1,576,256]{2,1,0:T(8,128)(2,1)} %bitcast.20, bf16[1,576,256]{2,1,0:T(8,128)(2,1)} %bitcast.22, bf16[1,576,256]{2,1,0:T(8,128)(2,1)} %bitcast.24, ...), custom_call_target="tpu_custom_call" | custom-call | tf_op jit(solution)/shard_map/pack/pallas_call | solution.py:113
  8.6 0.0 copy-start.2
  8.6 0.5 collective-permute-start
  9.0 0.2 copy-done.2
  9.2 0.1 select_reduce_fusion.2
  9.3 2.3 %collective-permute-done.1.refs_2_ = bf16[2,288,128]{2,1,0:T(8,128)(2,1)S(1)} collective-permute-done((bf16[2,288,128]{2,1,0:T(8,128)(2,1)}, bf16[2,288,128]{2,1,0:T(8,128)(2,1)S(1)}, u32[]{:S(2)}, u32[]{:S(2)}) %collective-permute-start.1) | collective-permute-done | bytes 147488 | tf_op jit(solution)/shard_map/ppermute | solution.py:133
  11.6 3.5 %collective-permute-start.2 = (bf16[2,288,128]{2,1,0:T(8,128)(2,1)}, bf16[2,288,128]{2,1,0:T(8,128)(2,1)S(1)}, u32[]{:S(2)}, u32[]{:S(2)}) collective-permute-start(bf16[2,288,128]{2,1,0:T(8,128)(2,1)} %get-tuple-element.45), channel_id=1, source_target_pairs={{0,2},{1,3},{2,0},{3,1},{4,6},{5,7},{6,4},{7,5},{8,10},{9,11},{10,... | collective-permute-start | bytes 442376 | tf_op jit(solution)/shard_map/ppermute | solution.py:133
  15.1 3.3 %collective-permute-start.3 = (bf16[2,288,128]{2,1,0:T(8,128)(2,1)}, bf16[2,288,128]{2,1,0:T(8,128)(2,1)S(1)}, u32[]{:S(2)}, u32[]{:S(2)}) collective-permute-start(bf16[2,288,128]{2,1,0:T(8,128)(2,1)} %get-tuple-element.46), channel_id=1, source_target_pairs={{0,3},{1,2},{2,1},{3,0},{4,7},{5,6},{6,5},{7,4},{8,11},{9,10},{10,... | collective-permute-start | bytes 442376 | tf_op jit(solution)/shard_map/ppermute | solution.py:133
  18.5 1.8 %collective-permute-done.10.refs_3_ = bf16[2,288,128]{2,1,0:T(8,128)(2,1)S(1)} collective-permute-done((bf16[2,288,128]{2,1,0:T(8,128)(2,1)}, bf16[2,288,128]{2,1,0:T(8,128)(2,1)S(1)}, u32[]{:S(2)}, u32[]{:S(2)}) %collective-permute-start.10) | collective-permute-done | bytes 147488 | tf_op jit(solution)/shard_map/ppermute | solution.py:133
  20.3 0.0 collective-permute-done.9.refs_1_
  20.3 0.0 copy-done.1
  20.3 0.0 copy-start
  20.3 0.1 sides.3
  20.5 3.7 %collective-permute-start.11 = (bf16[3,2,288,128]{3,2,1,0:T(8,128)(2,1)S(1)}, bf16[3,2,288,128]{3,2,1,0:T(8,128)(2,1)S(1)}, u32[]{:S(2)}, u32[]{:S(2)}) collective-permute-start(bf16[3,2,288,128]{3,2,1,0:T(8,128)(2,1)S(1)} %get-tuple-element.56), channel_id=1, source_target_pairs={{0,4},{4,8},{8,12},{12,16},{16,20},{20,24},{24,28},{1,5},{5,9},{9,... | collective-permute-start | bytes 1327112 | tf_op jit(solution)/shard_map/ppermute | solution.py:22
  24.2 1.9 %collective-permute-start.12 = (bf16[3,2,288,128]{3,2,1,0:T(8,128)(2,1)S(1)}, bf16[3,2,288,128]{3,2,1,0:T(8,128)(2,1)S(1)}, u32[]{:S(2)}, u32[]{:S(2)}) collective-permute-start(bf16[3,2,288,128]{3,2,1,0:T(8,128)(2,1)S(1)} %get-tuple-element.57), channel_id=1, source_target_pairs={{4,0},{8,4},{12,8},{16,12},{20,16},{24,20},{28,24},{5,1},{9,5},{13... | collective-permute-start | bytes 1327112 | tf_op jit(solution)/shard_map/ppermute | solution.py:22
  26.1 0.2 select_reduce_fusion.1
  26.3 0.0 collective-permute-done.refs_1_
  26.3 0.0 collective-permute-done.2.refs_2_
  26.3 5.5 %collective-permute-done.3.refs_3_ = bf16[2,288,128]{2,1,0:T(8,128)(2,1)S(1)} collective-permute-done((bf16[2,288,128]{2,1,0:T(8,128)(2,1)}, bf16[2,288,128]{2,1,0:T(8,128)(2,1)S(1)}, u32[]{:S(2)}, u32[]{:S(2)}) %collective-permute-start.3) | collective-permute-done | bytes 147488 | tf_op jit(solution)/shard_map/ppermute | solution.py:133
  31.8 0.0 copy-done
  31.8 0.1 sides.2
  32.0 3.6 %collective-permute-start.4 = (bf16[3,2,288,128]{3,2,1,0:T(8,128)(2,1)S(1)}, bf16[3,2,288,128]{3,2,1,0:T(8,128)(2,1)S(1)}, u32[]{:S(2)}, u32[]{:S(2)}) collective-permute-start(bf16[3,2,288,128]{3,2,1,0:T(8,128)(2,1)S(1)} %get-tuple-element.47), channel_id=1, source_target_pairs={{0,4},{4,8},{8,12},{12,16},{16,20},{20,24},{24,28},{1,5},{5,9},{9,... | collective-permute-start | bytes 1327112 | tf_op jit(solution)/shard_map/ppermute | solution.py:22
  35.5 1.9 %collective-permute-start.5 = (bf16[3,2,288,128]{3,2,1,0:T(8,128)(2,1)S(1)}, bf16[3,2,288,128]{3,2,1,0:T(8,128)(2,1)S(1)}, u32[]{:S(2)}, u32[]{:S(2)}) collective-permute-start(bf16[3,2,288,128]{3,2,1,0:T(8,128)(2,1)S(1)} %get-tuple-element.48), channel_id=1, source_target_pairs={{4,0},{8,4},{12,8},{16,12},{20,16},{24,20},{28,24},{5,1},{9,5},{13... | collective-permute-start | bytes 1327112 | tf_op jit(solution)/shard_map/ppermute | solution.py:22
  37.5 0.0 collective-permute-done.11.refs_4_
  37.5 0.0 collective-permute-done.12.refs_5_
  37.5 2.1 %clips.3 = (bf16[432,128]{1,0:T(8,128)(2,1)S(1)}, bf16[432,128]{1,0:T(8,128)(2,1)S(1)}, bf16[432,128]{1,0:T(8,128)(2,1)S(1)}, bf16[432,128]{1,0:T(8,128)(2,1)S(1)}) custom-call(s32[1]{0:T(128)} %bitcast.7.place_ref, s32[2,10]{1,0:T(2,128)S(1)} %pad_add_fusion.bounds, bf16[2,288,128]{2,1,0:T(8,128)(2,1)S(1)} %copy-done.1, ...), custom_call_target="tpu_custom_call" | custom-call | flops 589824000 | bytes 1474560 | tf_op jit(solution)/shard_map/clips/pallas_call | solution.py:312
  39.7 0.1 collective-permute-start.13
  39.7 0.5 collective-permute-start.14
  40.3 2.1 %collective-permute-start.15 = (bf16[432,128]{1,0:T(8,128)(2,1)S(1)}, bf16[432,128]{1,0:T(8,128)(2,1)S(1)}, u32[]{:S(2)}, u32[]{:S(2)}) collective-permute-start(bf16[432,128]{1,0:T(8,128)(2,1)S(1)} %get-tuple-element.61), channel_id=1, source_target_pairs={{0,3},{1,2},{2,1},{3,0},{4,7},{5,6},{6,5},{7,4},{8,11},{9,10},{10,... | collective-permute-start | bytes 331784 | tf_op jit(solution)/shard_map/ppermute | solution.py:133
  42.4 0.3 collective-permute-done.4.refs_4_
  42.7 4.8 %collective-permute-done.5.refs_5_ = bf16[3,2,288,128]{3,2,1,0:T(8,128)(2,1)S(1)} collective-permute-done((bf16[3,2,288,128]{3,2,1,0:T(8,128)(2,1)S(1)}, bf16[3,2,288,128]{3,2,1,0:T(8,128)(2,1)S(1)}, u32[]{:S(2)}, u32[]{:S(2)}) %collective-permute-start.5) | collective-permute-done | bytes 442400 | tf_op jit(solution)/shard_map/ppermute | solution.py:22
  47.4 2.1 %clips.2 = (bf16[432,128]{1,0:T(8,128)(2,1)S(1)}, bf16[432,128]{1,0:T(8,128)(2,1)S(1)}, bf16[432,128]{1,0:T(8,128)(2,1)S(1)}, bf16[432,128]{1,0:T(8,128)(2,1)S(1)}) custom-call(s32[1]{0:T(128)} %bitcast.7.place_ref, s32[2,10]{1,0:T(2,128)S(1)} %pad_add_fusion.bounds, bf16[2,288,128]{2,1,0:T(8,128)(2,1)S(1)} %copy-done, ...), custom_call_target="tpu_custom_call" | custom-call | flops 589824000 | bytes 1474560 | tf_op jit(solution)/shard_map/clips/pallas_call | solution.py:312
  49.6 0.1 collective-permute-start.6
  49.7 0.2 collective-permute-start.7
  49.9 0.0 collective-permute-done.13.refs_1_
  49.9 2.4 %collective-permute-start.8 = (bf16[432,128]{1,0:T(8,128)(2,1)S(1)}, bf16[432,128]{1,0:T(8,128)(2,1)S(1)}, u32[]{:S(2)}, u32[]{:S(2)}) collective-permute-start(bf16[432,128]{1,0:T(8,128)(2,1)S(1)} %get-tuple-element.52), channel_id=1, source_target_pairs={{0,3},{1,2},{2,1},{3,0},{4,7},{5,6},{6,5},{7,4},{8,11},{9,10},{10,... | collective-permute-start | bytes 331784 | tf_op jit(solution)/shard_map/ppermute | solution.py:133
  52.3 5.5 %space.1 = (bf16[1,576,256]{2,1,0:T(8,128)(2,1)}, bf16[1,576,256]{2,1,0:T(8,128)(2,1)}, bf16[1,576,256]{2,1,0:T(8,128)(2,1)}) custom-call(bf16[1,576,256]{2,1,0:T(8,128)(2,1)} %bitcast.30, bf16[1,576,256]{2,1,0:T(8,128)(2,1)} %bitcast.31, bf16[1,576,256]{2,1,0:T(8,128)(2,1)} %bitcast.32, bf16[1,576,256]{2,1,0:T(8,128)(2,1)} %bitcast.33), custom_call_target="tpu_custom_call" | custom-call | flops 1610612736 | bytes 2064384 | tf_op jit(solution)/shard_map/space/pallas_call | solution.py:70
  57.8 0.0 collective-permute-done.14.refs_2_
  57.8 0.0 collective-permute-done.15.refs_3_
  57.8 1.0 %unpack.2 = (bf16[1,576,256]{2,1,0:T(8,128)(2,1)}, bf16[1,576,256]{2,1,0:T(8,128)(2,1)}, bf16[1,576,256]{2,1,0:T(8,128)(2,1)}) custom-call(s32[1]{0:T(128)} %bitcast.7.place_ref, bf16[432,128]{1,0:T(8,128)(2,1)S(1)} %get-tuple-element.58.refs_0_, bf16[432,128]{1,0:T(8,128)(2,1)S(1)} %collective-permute-done.13.refs_1_, ...), custom_call_target="tpu_custom_call" | custom-call | tf_op jit(solution)/shard_map/unpack/pallas_call | solution.py:199
  58.8 0.0 collective-permute-done.6.refs_1_
  58.9 0.0 collective-permute-done.7.refs_2_
  58.9 4.0 %collective-permute-done.8.refs_3_ = bf16[432,128]{1,0:T(8,128)(2,1)S(1)} collective-permute-done((bf16[432,128]{1,0:T(8,128)(2,1)S(1)}, bf16[432,128]{1,0:T(8,128)(2,1)S(1)}, u32[]{:S(2)}, u32[]{:S(2)}) %collective-permute-start.8) | collective-permute-done | bytes 110624 | tf_op jit(solution)/shard_map/ppermute | solution.py:133
  62.8 1.0 %unpack.3 = (bf16[1,576,256]{2,1,0:T(8,128)(2,1)}, bf16[1,576,256]{2,1,0:T(8,128)(2,1)}, bf16[1,576,256]{2,1,0:T(8,128)(2,1)}) custom-call(s32[1]{0:T(128)} %bitcast.7.place_ref, bf16[432,128]{1,0:T(8,128)(2,1)S(1)} %get-tuple-element.49.refs_0_, ...), custom_call_target="tpu_custom_call", output_to_operand_aliasing={{0}: (5, {}), {1}: (6, {}), {2}: (7, {})} | custom-call | tf_op jit(solution)/shard_map/unpack/pallas_call | solution.py:199
  (4 shorter events, 0.0 us)
Async XLA Ops:
  2.8 8.9 %collective-permute-start.1 = (bf16[2,288,128]{2,1,0:T(8,128)(2,1)}, bf16[2,288,128]{2,1,0:T(8,128)(2,1)S(1)}, u32[]{:S(2)}, u32[]{:S(2)}) collective-permute-start(bf16[2,288,128]{2,1,0:T(8,128)(2,1)} %get-tuple-element.44), channel_id=1, source_target_pairs={{0,2},{1,3},{2,0},{3,1},{4,6},{5,7},{6,4},{7,5},{8,10},{9,11},{10,... | collective-permute-start | bytes 442376 | tf_op jit(solution)/shard_map/ppermute | solution.py:133
  2.9 17.4 %collective-permute-start.10 = (bf16[2,288,128]{2,1,0:T(8,128)(2,1)}, bf16[2,288,128]{2,1,0:T(8,128)(2,1)S(1)}, u32[]{:S(2)}, u32[]{:S(2)}) collective-permute-start(bf16[2,288,128]{2,1,0:T(8,128)(2,1)} %get-tuple-element.55), channel_id=1, source_target_pairs={{0,3},{1,2},{2,1},{3,0},{4,7},{5,6},{6,5},{7,4},{8,11},{9,10},{10,... | collective-permute-start | bytes 442376 | tf_op jit(solution)/shard_map/ppermute | solution.py:133
  5.3 15.0 %copy-start.1 = (bf16[2,288,128]{2,1,0:T(8,128)(2,1)S(1)}, bf16[2,288,128]{2,1,0:T(8,128)(2,1)}, u32[]{:S(2)}) copy-start(bf16[2,288,128]{2,1,0:T(8,128)(2,1)} %get-tuple-element.53.refs_0_) | copy-start | bytes 442372
  5.3 15.0 %collective-permute-start.9 = (bf16[2,288,128]{2,1,0:T(8,128)(2,1)}, bf16[2,288,128]{2,1,0:T(8,128)(2,1)S(1)}, u32[]{:S(2)}, u32[]{:S(2)}) collective-permute-start(bf16[2,288,128]{2,1,0:T(8,128)(2,1)} %get-tuple-element.54), channel_id=1, source_target_pairs={{0,1},{1,0},{2,3},{3,2},{4,5},{5,4},{6,7},{7,6},{8,9},{9,8},{10,11... | collective-permute-start | bytes 442376 | tf_op jit(solution)/shard_map/ppermute | solution.py:133
  8.6 0.7 %copy-start.2 = (s32[16]{0:T(128)S(1)}, s32[16]{0:T(128)}, u32[]{:S(2)}) copy-start(s32[16]{0:T(128)} %param.17) | copy-start | bytes 196
  8.6 17.7 %collective-permute-start = (bf16[2,288,128]{2,1,0:T(8,128)(2,1)}, bf16[2,288,128]{2,1,0:T(8,128)(2,1)S(1)}, u32[]{:S(2)}, u32[]{:S(2)}) collective-permute-start(bf16[2,288,128]{2,1,0:T(8,128)(2,1)} %get-tuple-element.41), channel_id=1, source_target_pairs={{0,1},{1,0},{2,3},{3,2},{4,5},{5,4},{6,7},{7,6},{8,9},{9,8},{10,11... | collective-permute-start | bytes 442376 | tf_op jit(solution)/shard_map/ppermute | solution.py:133
  11.6 14.6 %collective-permute-start.2 = (bf16[2,288,128]{2,1,0:T(8,128)(2,1)}, bf16[2,288,128]{2,1,0:T(8,128)(2,1)S(1)}, u32[]{:S(2)}, u32[]{:S(2)}) collective-permute-start(bf16[2,288,128]{2,1,0:T(8,128)(2,1)} %get-tuple-element.45), channel_id=1, source_target_pairs={{0,2},{1,3},{2,0},{3,1},{4,6},{5,7},{6,4},{7,5},{8,10},{9,11},{10,... | collective-permute-start | bytes 442376 | tf_op jit(solution)/shard_map/ppermute | solution.py:133
  15.1 16.7 %collective-permute-start.3 = (bf16[2,288,128]{2,1,0:T(8,128)(2,1)}, bf16[2,288,128]{2,1,0:T(8,128)(2,1)S(1)}, u32[]{:S(2)}, u32[]{:S(2)}) collective-permute-start(bf16[2,288,128]{2,1,0:T(8,128)(2,1)} %get-tuple-element.46), channel_id=1, source_target_pairs={{0,3},{1,2},{2,1},{3,0},{4,7},{5,6},{6,5},{7,4},{8,11},{9,10},{10,... | collective-permute-start | bytes 442376 | tf_op jit(solution)/shard_map/ppermute | solution.py:133
  20.3 11.5 %copy-start = (bf16[2,288,128]{2,1,0:T(8,128)(2,1)S(1)}, bf16[2,288,128]{2,1,0:T(8,128)(2,1)}, u32[]{:S(2)}) copy-start(bf16[2,288,128]{2,1,0:T(8,128)(2,1)} %get-tuple-element.40.refs_0_) | copy-start | bytes 442372
  20.5 17.0 %collective-permute-start.11 = (bf16[3,2,288,128]{3,2,1,0:T(8,128)(2,1)S(1)}, bf16[3,2,288,128]{3,2,1,0:T(8,128)(2,1)S(1)}, u32[]{:S(2)}, u32[]{:S(2)}) collective-permute-start(bf16[3,2,288,128]{3,2,1,0:T(8,128)(2,1)S(1)} %get-tuple-element.56), channel_id=1, source_target_pairs={{0,4},{4,8},{8,12},{12,16},{16,20},{20,24},{24,28},{1,5},{5,9},{9,... | collective-permute-start | bytes 1327112 | tf_op jit(solution)/shard_map/ppermute | solution.py:22
  24.2 13.3 %collective-permute-start.12 = (bf16[3,2,288,128]{3,2,1,0:T(8,128)(2,1)S(1)}, bf16[3,2,288,128]{3,2,1,0:T(8,128)(2,1)S(1)}, u32[]{:S(2)}, u32[]{:S(2)}) collective-permute-start(bf16[3,2,288,128]{3,2,1,0:T(8,128)(2,1)S(1)} %get-tuple-element.57), channel_id=1, source_target_pairs={{4,0},{8,4},{12,8},{16,12},{20,16},{24,20},{28,24},{5,1},{9,5},{13... | collective-permute-start | bytes 1327112 | tf_op jit(solution)/shard_map/ppermute | solution.py:22
  32.0 10.7 %collective-permute-start.4 = (bf16[3,2,288,128]{3,2,1,0:T(8,128)(2,1)S(1)}, bf16[3,2,288,128]{3,2,1,0:T(8,128)(2,1)S(1)}, u32[]{:S(2)}, u32[]{:S(2)}) collective-permute-start(bf16[3,2,288,128]{3,2,1,0:T(8,128)(2,1)S(1)} %get-tuple-element.47), channel_id=1, source_target_pairs={{0,4},{4,8},{8,12},{12,16},{16,20},{20,24},{24,28},{1,5},{5,9},{9,... | collective-permute-start | bytes 1327112 | tf_op jit(solution)/shard_map/ppermute | solution.py:22
  35.5 11.9 %collective-permute-start.5 = (bf16[3,2,288,128]{3,2,1,0:T(8,128)(2,1)S(1)}, bf16[3,2,288,128]{3,2,1,0:T(8,128)(2,1)S(1)}, u32[]{:S(2)}, u32[]{:S(2)}) collective-permute-start(bf16[3,2,288,128]{3,2,1,0:T(8,128)(2,1)S(1)} %get-tuple-element.48), channel_id=1, source_target_pairs={{4,0},{8,4},{12,8},{16,12},{20,16},{24,20},{28,24},{5,1},{9,5},{13... | collective-permute-start | bytes 1327112 | tf_op jit(solution)/shard_map/ppermute | solution.py:22
  39.7 10.3 %collective-permute-start.13 = (bf16[432,128]{1,0:T(8,128)(2,1)S(1)}, bf16[432,128]{1,0:T(8,128)(2,1)S(1)}, u32[]{:S(2)}, u32[]{:S(2)}) collective-permute-start(bf16[432,128]{1,0:T(8,128)(2,1)S(1)} %get-tuple-element.59), channel_id=1, source_target_pairs={{0,1},{1,0},{2,3},{3,2},{4,5},{5,4},{6,7},{7,6},{8,9},{9,8},{10,11... | collective-permute-start | bytes 331784 | tf_op jit(solution)/shard_map/ppermute | solution.py:133
  39.7 18.1 %collective-permute-start.14 = (bf16[432,128]{1,0:T(8,128)(2,1)S(1)}, bf16[432,128]{1,0:T(8,128)(2,1)S(1)}, u32[]{:S(2)}, u32[]{:S(2)}) collective-permute-start(bf16[432,128]{1,0:T(8,128)(2,1)S(1)} %get-tuple-element.60), channel_id=1, source_target_pairs={{0,2},{1,3},{2,0},{3,1},{4,6},{5,7},{6,4},{7,5},{8,10},{9,11},{10,... | collective-permute-start | bytes 331784 | tf_op jit(solution)/shard_map/ppermute | solution.py:133
  40.3 17.6 %collective-permute-start.15 = (bf16[432,128]{1,0:T(8,128)(2,1)S(1)}, bf16[432,128]{1,0:T(8,128)(2,1)S(1)}, u32[]{:S(2)}, u32[]{:S(2)}) collective-permute-start(bf16[432,128]{1,0:T(8,128)(2,1)S(1)} %get-tuple-element.61), channel_id=1, source_target_pairs={{0,3},{1,2},{2,1},{3,0},{4,7},{5,6},{6,5},{7,4},{8,11},{9,10},{10,... | collective-permute-start | bytes 331784 | tf_op jit(solution)/shard_map/ppermute | solution.py:133
  49.6 9.3 %collective-permute-start.6 = (bf16[432,128]{1,0:T(8,128)(2,1)S(1)}, bf16[432,128]{1,0:T(8,128)(2,1)S(1)}, u32[]{:S(2)}, u32[]{:S(2)}) collective-permute-start(bf16[432,128]{1,0:T(8,128)(2,1)S(1)} %get-tuple-element.50), channel_id=1, source_target_pairs={{0,1},{1,0},{2,3},{3,2},{4,5},{5,4},{6,7},{7,6},{8,9},{9,8},{10,11... | collective-permute-start | bytes 331784 | tf_op jit(solution)/shard_map/ppermute | solution.py:133
  49.7 9.2 %collective-permute-start.7 = (bf16[432,128]{1,0:T(8,128)(2,1)S(1)}, bf16[432,128]{1,0:T(8,128)(2,1)S(1)}, u32[]{:S(2)}, u32[]{:S(2)}) collective-permute-start(bf16[432,128]{1,0:T(8,128)(2,1)S(1)} %get-tuple-element.51), channel_id=1, source_target_pairs={{0,2},{1,3},{2,0},{3,1},{4,6},{5,7},{6,4},{7,5},{8,10},{9,11},{10,... | collective-permute-start | bytes 331784 | tf_op jit(solution)/shard_map/ppermute | solution.py:133
  49.9 12.9 %collective-permute-start.8 = (bf16[432,128]{1,0:T(8,128)(2,1)S(1)}, bf16[432,128]{1,0:T(8,128)(2,1)S(1)}, u32[]{:S(2)}, u32[]{:S(2)}) collective-permute-start(bf16[432,128]{1,0:T(8,128)(2,1)S(1)} %get-tuple-element.52), channel_id=1, source_target_pairs={{0,3},{1,2},{2,1},{3,0},{4,7},{5,6},{6,5},{7,4},{8,11},{9,10},{10,... | collective-permute-start | bytes 331784 | tf_op jit(solution)/shard_map/ppermute | solution.py:133

commit v3 on v2

--- a/solution.py
+++ b/solution.py
@@ -13,13 +13,9 @@
 WIDTH = HEADS * HDIM
 SCALING = 1.0 / math.sqrt(HDIM)
 CHUNKS = (4, 4)
+GATHER_SEQ = True
+GATHER_GRP = True
 masked_score = -1e30
-
-
-def shifted(value, axis, by):
-    count = lax.axis_size(axis)
-    pairs = [(i, i + by) for i in range(count) if 0 <= i + by < count]
-    return lax.ppermute(value, axis, pairs)
 
 
 def dot(left, right, left_dim, right_dim):
@@ -126,26 +122,43 @@
     )(place, *arrays)
 
 
+def swap(block, axis, pairs, gathered):
+    if gathered:
+        return lax.all_gather(block, axis, axis_index_groups=pairs)
+    return lax.ppermute(block, axis, [(i, j) for i, j in pairs] + [(j, i) for i, j in pairs])
+
+
 def exchange(blocks):
     n = len(blocks)
     moved = [blocks[0]]
     for step in range(1, n):
-        moved.append(lax.ppermute(blocks[step], "seq", [(i, i ^ step) for i in range(n)]))
+        pairs = [[i, i ^ step] for i in range(n) if i < i ^ step]
+        moved.append(swap(blocks[step], "seq", pairs, GATHER_SEQ))
     return moved
 
 
+def from_partner(ref, is_second):
+    return ref.at[is_second] if GATHER_SEQ else ref
+
+
+def seq_block(ref, step, place_ref):
+    if step == 0:
+        return ref
+    return from_partner(ref, jnp.int32(place_ref[0] < place_ref[0] ^ step))
+
+
 def sides_kernel(n, place_ref, *refs):
-    ins, (first_ref, last_ref) = refs[:n], refs[n:]
-    for step, block in enumerate(ins):
+    ins, outs = refs[:n], refs[n:]
+    is_odd = place_ref[1]
+    for step, ref in enumerate(ins):
+        block = seq_block(ref, step, place_ref)
         frame = place_ref[0] ^ step
-
-        @pl.when(frame < n - 1)
-        def _():
-            first_ref[jnp.minimum(frame, n - 2)] = block[...]
-
-        @pl.when(frame > 0)
-        def _():
-            last_ref[jnp.maximum(frame - 1, 0)] = block[...]
+        for start, out in enumerate(outs):
+            at = frame - jnp.where(is_odd == start, 1, 0)
+
+            @pl.when((at >= 0) & (at < n - 1))
+            def _():
+                out[jnp.clip(at, 0, n - 2)] = block[...]
 
 
 def sides(place, blocks):
@@ -157,15 +170,26 @@
         in_specs=[pl.BlockSpec(memory_space=pltpu.SMEM)] + [vmem] * n,
         out_specs=[vmem] * 2,
         out_shape=[shape] * 2,
-        compiler_params=pltpu.CompilerParams(vmem_limit_bytes=32 * 2**20),
+        compiler_params=pltpu.CompilerParams(vmem_limit_bytes=60 * 2**20),
         name="sides",
     )(place, *blocks)
 
 
+def neighbours(blocks):
+    count = lax.axis_size("grp")
+    moved = []
+    for start, block in enumerate(blocks):
+        pairs = [[i, (i + 1) % count] for i in range(start, count, 2)]
+        if not GATHER_GRP:
+            pairs = [pair for pair in pairs if pair[0] < pair[1]]
+        moved.append(swap(block, "grp", pairs, GATHER_GRP))
+    return moved
+
+
 def join_kernel(n, span, place_ref, *refs):
     ins, outs, (held, ready, left_off) = refs[:n], refs[-6:-3], refs[-3:]
-    for step, block in enumerate(ins):
-        held[place_ref[0] ^ step] = block[...]
+    for step, ref in enumerate(ins):
+        held[place_ref[0] ^ step] = seq_block(ref, step, place_ref)[...]
     count = span.stop - span.start
     half = count // 2
     places = held.shape[2] // 2
@@ -207,13 +231,13 @@
             pltpu.SemaphoreType.DMA((3,)),
         ],
         input_output_aliases={1 + n + i: i for i in range(len(earlier))},
-        compiler_params=pltpu.CompilerParams(vmem_limit_bytes=24 * 2**20),
+        compiler_params=pltpu.CompilerParams(vmem_limit_bytes=60 * 2**20),
         name="unpack",
     )(place, *blocks, *earlier)
 
 
 def clip_kernel(window, heads, place_ref, bounds, *refs):
-    own, low_ref, high_ref = refs[:window], refs[window], refs[window + 1]
+    own, sides_of = refs[:window], refs[window : window + 2]
     outs, (x_ref, y_ref, coef_ref, grad_ref) = refs[window + 2 : 2 * window + 2], refs[-4:]
     halo = window - 1
     extent = window + 2 * halo
@@ -227,12 +251,16 @@
         x_ref[frame] = ref[0].astype(jnp.float32)
         y_ref[frame] = ref[1].astype(jnp.float32)
 
-    for step, block in enumerate(own):
-        widen(block, halo + (place_ref[0] ^ step))
-    for at in range(halo):
-        pl.when(at >= lowest)(functools.partial(widen, low_ref.at[at], at))
-        frame = halo + window + at
-        pl.when(frame < highest)(functools.partial(widen, high_ref.at[at], frame))
+    for step, ref in enumerate(own):
+        widen(seq_block(ref, step, place_ref), halo + (place_ref[0] ^ step))
+    for start, ref in enumerate(sides_of):
+        is_next = place_ref[1] == start
+        if GATHER_GRP:
+            ref = ref.at[jnp.int32(is_next)]
+        for at in range(halo):
+            frame = at + jnp.where(is_next, halo + window, 0)
+            needed = (frame >= lowest) & (frame < highest)
+            pl.when(needed)(functools.partial(widen, ref.at[at], frame))
 
     def partners(frame):
         first, last = bounds[0, frame], bounds[1, frame]
@@ -300,9 +328,10 @@
         out[...] = grad_ref[place_ref[0] ^ step]
 
 
-def clip_grads(place, bounds, own, low, high):
+def clip_grads(place, bounds, own, beside):
     window = len(own)
     _, rows, lanes = own[0].shape
+    beside = list(beside)
     heads = rows // HDIM
     extent = 3 * window - 2
     vmem = pl.BlockSpec(memory_space=pltpu.VMEM)
@@ -320,14 +349,14 @@
             pltpu.VMEM((extent, window, heads, lanes), jnp.float32),
             pltpu.VMEM((window, *shape), jnp.bfloat16),
         ],
-        compiler_params=pltpu.CompilerParams(vmem_limit_bytes=48 * 2**20),
+        compiler_params=pltpu.CompilerParams(vmem_limit_bytes=60 * 2**20),
         cost_estimate=pl.CostEstimate(
             flops=400 * work,
-            bytes_accessed=2 * (window * own[0].size + low.size + high.size),
+            bytes_accessed=2 * sum(block.size for block in (*own, *beside)),
             transcendentals=extent * window * heads * lanes,
         ),
         name="clips",
-    )(place, bounds, *own, low, high)
+    )(place, bounds, *own, *beside)
 
 
 def clip_bounds(clip_len, window):
@@ -352,7 +381,7 @@
     window = q_time.shape[0] * n
     tokens = q_time.shape[1]
     bounds = clip_bounds(clip_len, window)
-    place = lax.axis_index("seq").astype(jnp.int32).reshape(1)
+    place = jnp.stack([lax.axis_index("seq"), lax.axis_index("grp") % 2]).astype(jnp.int32)
     time = turned(q_time, cot_time, k_time, v_time)
     spans = []
     head = 0
@@ -367,10 +396,8 @@
         if own is not None:
             packed[2:], own[2] = lax.optimization_barrier((packed[2:], own[2]))
         own = exchange(packed)
-        first, last = sides(place, own)
-        low = shifted(last, "grp", 1)
-        high = shifted(first, "grp", -1)
-        back.append(exchange(clip_grads(place, bounds, own, low, high)))
+        beside = neighbours(sides(place, own))
+        back.append(exchange(clip_grads(place, bounds, own, beside)))
     grads = None
     for span, blocks in zip(spans, back):
         grads = join(place, blocks, span, tokens, grads)

time: 63.9 us -> 170 us (2.66)
  the two profiles are of different devices: /device:TPU:19 before, /device:TPU:0 now
where the time goes in v3:
time: 170 us; the launch traced here: 168 us
  blocking collectives  136 us (80%)
  Pallas kernels  29.2 us (17%)
    all_gather x16, blocking collectives, swap(): return lax.all_gather(block, axis, axis_index_groups=pairs)  136 us
    pallas_call x2, Pallas kernels, clip_grads(): pl.pallas_call(functools.partial(clip_kernel, window, heads), out_shape=[...  8.94 us
    pallas_call x2, Pallas kernels, split(): pl.pallas_call(functools.partial(split_kernel, n, span), in_specs=[pl.Blo...  5.62 us
    pallas_call x1, Pallas kernels, frame_grads(): pl.pallas_call(frame_kernel, out_shape=(shape, shape, shape), compiler_pa...  5.53 us
    pallas_call x2, Pallas kernels, sides(): pl.pallas_call(functools.partial(sides_kernel, n), in_specs=[pl.BlockSpec...  4.65 us
    pallas_call x2, Pallas kernels, join(): pl.pallas_call(functools.partial(join_kernel, n, span), in_specs=[pl.Bloc...  4.44 us

profile of v3, /device:TPU:0, one launch (start us, length us, event | category | flops | bytes accessed | tf_op | source)
XLA Modules:
  0.0 168.3 jit_solution(17763434012509091428)
XLA Ops:
  0.6 0.7 pad_add_fusion.1.place_ref
  1.3 2.8 %pack.3 = (bf16[2,288,128]{2,1,0:T(8,128)(2,1)}, bf16[2,288,128]{2,1,0:T(8,128)(2,1)}, bf16[2,288,128]{2,1,0:T(8,128)(2,1)}, bf16[2,288,128]{2,1,0:T(8,128)(2,1)}) custom-call(s32[2]{0:T(128)} %pad_add_fusion.1.place_ref, bf16[1,576,256]{2,1,0:T(8,128)(2,1)} %bitcast.52, bf16[1,576,256]{2,1,0:T(8,128)(2,1)} %bitcast.54, bf16[1,576,256]{2,1,0:T(8,128)(2,1)} %bitcast.56, ...), custom_call_target="tpu_custom_call" | custom-call | tf_op jit(solution)/shard_map/pack/pallas_call | solution.py:109
  4.1 0.0 copy-start.4
  4.1 14.3 %all-gather.1 = bf16[4,288,128]{2,1,0:T(8,128)(2,1)} all-gather(bf16[2,288,128]{2,1,0:T(8,128)(2,1)} %get-tuple-element.44), channel_id=3, replica_groups={{0,2},{1,3},{4,6},{5,7},{8,10},{9,11},{12,14},{13,15},{16,18},{17,19},{..., dimensions={0}, use_global_device_ids=true | all-gather | bytes 442368 | tf_op jit(solution)/shard_map/all_gather | solution.py:127
  18.4 0.0 copy-done.4
  18.4 0.0 copy-start.2
  18.4 6.0 %all-gather.9 = bf16[4,288,128]{2,1,0:T(8,128)(2,1)} all-gather(bf16[2,288,128]{2,1,0:T(8,128)(2,1)S(1)} %copy-done.4), channel_id=11, replica_groups={{0,1},{2,3},{4,5},{6,7},{8,9},{10,11},{12,13},{14,15},{16,17},{18,19},{..., dimensions={0}, use_global_device_ids=true | all-gather | bytes 442368 | tf_op jit(solution)/shard_map/all_gather | solution.py:127
  24.5 0.0 copy-done.2
  24.5 7.8 %all-gather.10 = bf16[4,288,128]{2,1,0:T(8,128)(2,1)} all-gather(bf16[2,288,128]{2,1,0:T(8,128)(2,1)S(1)} %copy-done.2), channel_id=12, replica_groups={{0,3},{1,2},{4,7},{5,6},{8,11},{9,10},{12,15},{13,14},{16,19},{17,18},{..., dimensions={0}, use_global_device_ids=true | all-gather | bytes 442368 | tf_op jit(solution)/shard_map/all_gather | solution.py:127
  32.3 2.3 %sides.3 = (bf16[3,2,288,128]{3,2,1,0:T(8,128)(2,1)}, bf16[3,2,288,128]{3,2,1,0:T(8,128)(2,1)}) custom-call(s32[2]{0:T(128)} %pad_add_fusion.1.place_ref, bf16[2,288,128]{2,1,0:T(8,128)(2,1)} %get-tuple-element.53.refs_0_, bf16[2,2,288,128]{3,2,1,0:T(8,128)(2,1)} %bitcast.42, bf16[2,2,288,128]{3,2,1,0:T(8,128)(2,1)} %bitcast.40, ...), custom_call_target="tpu_custom_call" | custom-call | tf_op jit(solution)/shard_map/sides/pallas_call | solution.py:168
  34.6 0.0 copy-start
  34.6 6.9 %all-gather.11 = bf16[6,2,288,128]{3,2,1,0:T(8,128)(2,1)} all-gather(bf16[3,2,288,128]{3,2,1,0:T(8,128)(2,1)} %get-tuple-element.56), channel_id=13, replica_groups={{0,4},{8,12},{16,20},{24,28},{1,5},{9,13},{17,21},{25,29},{2,6},{10,14}..., dimensions={0}, use_global_device_ids=true | all-gather | bytes 1327104 | tf_op jit(solution)/shard_map/all_gather | solution.py:127
  41.5 0.0 copy-done
  41.5 13.6 %all-gather.12 = bf16[6,2,288,128]{3,2,1,0:T(8,128)(2,1)} all-gather(bf16[3,2,288,128]{3,2,1,0:T(8,128)(2,1)S(1)} %copy-done), channel_id=14, replica_groups={{4,8},{12,16},{20,24},{28,0},{5,9},{13,17},{21,25},{29,1},{6,10},{14,18..., dimensions={0}, use_global_device_ids=true | all-gather | bytes 1327104 | tf_op jit(solution)/shard_map/all_gather | solution.py:127
  55.1 0.0 copy-start.10
  55.1 0.7 copy-done.10
  55.8 0.1 select_reduce_fusion.2
  55.9 0.2 select_reduce_fusion.1
  56.1 0.6 pad_add_fusion.bounds
  56.7 4.5 %clips.3 = (bf16[432,128]{1,0:T(8,128)(2,1)}, bf16[432,128]{1,0:T(8,128)(2,1)}, bf16[432,128]{1,0:T(8,128)(2,1)}, bf16[432,128]{1,0:T(8,128)(2,1)}) custom-call(s32[2]{0:T(128)} %pad_add_fusion.1.place_ref, s32[2,10]{1,0:T(2,128)} %pad_add_fusion.bounds, bf16[2,288,128]{2,1,0:T(8,128)(2,1)} %get-tuple-element.53.refs_0_, bf16[2,2,288,128]{3,2,1,0:T(8,128)(2,1)} %bitcast.43, ...), custom_call_target="tpu_custom_call" | custom-call | flops 589824000 | bytes 2801664 | tf_op jit(solution)/shard_map/clips/pallas_call | solution.py:341
  61.1 0.0 copy-start.9
  61.1 6.5 %all-gather.13 = bf16[864,128]{1,0:T(8,128)(2,1)} all-gather(bf16[432,128]{1,0:T(8,128)(2,1)} %get-tuple-element.59), channel_id=15, replica_groups={{0,1},{2,3},{4,5},{6,7},{8,9},{10,11},{12,13},{14,15},{16,17},{18,19},{..., dimensions={0}, use_global_device_ids=true | all-gather | bytes 331776 | tf_op jit(solution)/shard_map/all_gather | solution.py:127
  67.6 0.0 copy-done.9
  67.6 0.0 copy-start.7
  67.6 8.2 %all-gather.14 = bf16[864,128]{1,0:T(8,128)(2,1)} all-gather(bf16[432,128]{1,0:T(8,128)(2,1)S(1)} %copy-done.9), channel_id=16, replica_groups={{0,2},{1,3},{4,6},{5,7},{8,10},{9,11},{12,14},{13,15},{16,18},{17,19},{..., dimensions={0}, use_global_device_ids=true | all-gather | bytes 331776 | tf_op jit(solution)/shard_map/all_gather | solution.py:127
  75.8 0.0 copy-done.7
  75.8 7.3 %all-gather.15 = bf16[864,128]{1,0:T(8,128)(2,1)} all-gather(bf16[432,128]{1,0:T(8,128)(2,1)S(1)} %copy-done.7), channel_id=17, replica_groups={{0,3},{1,2},{4,7},{5,6},{8,11},{9,10},{12,15},{13,14},{16,19},{17,18},{..., dimensions={0}, use_global_device_ids=true | all-gather | bytes 331776 | tf_op jit(solution)/shard_map/all_gather | solution.py:127
  83.1 2.2 %unpack.2 = (bf16[1,576,256]{2,1,0:T(8,128)(2,1)}, bf16[1,576,256]{2,1,0:T(8,128)(2,1)}, bf16[1,576,256]{2,1,0:T(8,128)(2,1)}) custom-call(s32[2]{0:T(128)} %pad_add_fusion.1.place_ref, bf16[432,128]{1,0:T(8,128)(2,1)} %get-tuple-element.58.refs_0_, bf16[2,432,128]{2,1,0:T(8,128)(2,1)} %bitcast.63, bf16[2,432,128]{2,1,0:T(8,128)(2,1)} %bitcast.64, ...), custom_call_target="tpu_custom_call" | custom-call | tf_op jit(solution)/shard_map/unpack/pallas_call | solution.py:223
  85.4 2.8 %pack.2 = (bf16[2,288,128]{2,1,0:T(8,128)(2,1)}, bf16[2,288,128]{2,1,0:T(8,128)(2,1)}, bf16[2,288,128]{2,1,0:T(8,128)(2,1)}, bf16[2,288,128]{2,1,0:T(8,128)(2,1)}) custom-call(s32[2]{0:T(128)} %pad_add_fusion.1.place_ref, bf16[1,576,256]{2,1,0:T(8,128)(2,1)} %bitcast.53, bf16[1,576,256]{2,1,0:T(8,128)(2,1)} %bitcast.55, bf16[1,576,256]{2,1,0:T(8,128)(2,1)} %bitcast.57, ...), custom_call_target="tpu_custom_call" | custom-call | tf_op jit(solution)/shard_map/pack/pallas_call | solution.py:109
  88.2 0.0 copy-start.5
  88.2 9.1 %all-gather.2 = bf16[4,288,128]{2,1,0:T(8,128)(2,1)} all-gather(bf16[2,288,128]{2,1,0:T(8,128)(2,1)} %get-tuple-element.45), channel_id=4, replica_groups={{0,2},{1,3},{4,6},{5,7},{8,10},{9,11},{12,14},{13,15},{16,18},{17,19},{..., dimensions={0}, use_global_device_ids=true | all-gather | bytes 442368 | tf_op jit(solution)/shard_map/all_gather | solution.py:127
  97.3 0.0 copy-done.5
  97.3 0.0 copy-start.3
  97.3 8.9 %all-gather.3 = bf16[4,288,128]{2,1,0:T(8,128)(2,1)} all-gather(bf16[2,288,128]{2,1,0:T(8,128)(2,1)S(1)} %copy-done.5), channel_id=5, replica_groups={{0,3},{1,2},{4,7},{5,6},{8,11},{9,10},{12,15},{13,14},{16,19},{17,18},{..., dimensions={0}, use_global_device_ids=true | all-gather | bytes 442368 | tf_op jit(solution)/shard_map/all_gather | solution.py:127
  106.2 0.0 copy-done.3
  106.2 5.9 %all-gather = bf16[4,288,128]{2,1,0:T(8,128)(2,1)} all-gather(bf16[2,288,128]{2,1,0:T(8,128)(2,1)S(1)} %copy-done.3), channel_id=2, replica_groups={{0,1},{2,3},{4,5},{6,7},{8,9},{10,11},{12,13},{14,15},{16,17},{18,19},{..., dimensions={0}, use_global_device_ids=true | all-gather | bytes 442368 | tf_op jit(solution)/shard_map/all_gather | solution.py:127
  112.1 2.3 %sides.2 = (bf16[3,2,288,128]{3,2,1,0:T(8,128)(2,1)}, bf16[3,2,288,128]{3,2,1,0:T(8,128)(2,1)}) custom-call(s32[2]{0:T(128)} %pad_add_fusion.1.place_ref, bf16[2,288,128]{2,1,0:T(8,128)(2,1)} %get-tuple-element.40.refs_0_, bf16[2,2,288,128]{3,2,1,0:T(8,128)(2,1)} %bitcast.50, bf16[2,2,288,128]{3,2,1,0:T(8,128)(2,1)} %bitcast.46, ...), custom_call_target="tpu_custom_call" | custom-call | tf_op jit(solution)/shard_map/sides/pallas_call | solution.py:168
  114.5 0.0 copy-start.1
  114.5 6.9 %all-gather.4 = bf16[6,2,288,128]{3,2,1,0:T(8,128)(2,1)} all-gather(bf16[3,2,288,128]{3,2,1,0:T(8,128)(2,1)} %get-tuple-element.47), channel_id=6, replica_groups={{0,4},{8,12},{16,20},{24,28},{1,5},{9,13},{17,21},{25,29},{2,6},{10,14}..., dimensions={0}, use_global_device_ids=true | all-gather | bytes 1327104 | tf_op jit(solution)/shard_map/all_gather | solution.py:127
  121.3 0.0 copy-done.1
  121.3 13.8 %all-gather.5 = bf16[6,2,288,128]{3,2,1,0:T(8,128)(2,1)} all-gather(bf16[3,2,288,128]{3,2,1,0:T(8,128)(2,1)S(1)} %copy-done.1), channel_id=7, replica_groups={{4,8},{12,16},{20,24},{28,0},{5,9},{13,17},{21,25},{29,1},{6,10},{14,18..., dimensions={0}, use_global_device_ids=true | all-gather | bytes 1327104 | tf_op jit(solution)/shard_map/all_gather | solution.py:127
  135.2 4.5 %clips.2 = (bf16[432,128]{1,0:T(8,128)(2,1)}, bf16[432,128]{1,0:T(8,128)(2,1)}, bf16[432,128]{1,0:T(8,128)(2,1)}, bf16[432,128]{1,0:T(8,128)(2,1)}) custom-call(s32[2]{0:T(128)} %pad_add_fusion.1.place_ref, s32[2,10]{1,0:T(2,128)} %pad_add_fusion.bounds, bf16[2,288,128]{2,1,0:T(8,128)(2,1)} %get-tuple-element.40.refs_0_, bf16[2,2,288,128]{3,2,1,0:T(8,128)(2,1)} %bitcast.51, ...), custom_call_target="tpu_custom_call" | custom-call | flops 589824000 | bytes 2801664 | tf_op jit(solution)/shard_map/clips/pallas_call | solution.py:341
  139.6 0.0 copy-start.8
  139.7 5.9 %all-gather.6 = bf16[864,128]{1,0:T(8,128)(2,1)} all-gather(bf16[432,128]{1,0:T(8,128)(2,1)} %get-tuple-element.50), channel_id=8, replica_groups={{0,1},{2,3},{4,5},{6,7},{8,9},{10,11},{12,13},{14,15},{16,17},{18,19},{..., dimensions={0}, use_global_device_ids=true | all-gather | bytes 331776 | tf_op jit(solution)/shard_map/all_gather | solution.py:127
  145.5 0.0 copy-done.8
  145.5 0.0 copy-start.6
  145.5 7.7 %all-gather.7 = bf16[864,128]{1,0:T(8,128)(2,1)} all-gather(bf16[432,128]{1,0:T(8,128)(2,1)S(1)} %copy-done.8), channel_id=9, replica_groups={{0,2},{1,3},{4,6},{5,7},{8,10},{9,11},{12,14},{13,15},{16,18},{17,19},{..., dimensions={0}, use_global_device_ids=true | all-gather | bytes 331776 | tf_op jit(solution)/shard_map/all_gather | solution.py:127
  153.3 0.0 copy-done.6
  153.3 7.3 %all-gather.8 = bf16[864,128]{1,0:T(8,128)(2,1)} all-gather(bf16[432,128]{1,0:T(8,128)(2,1)S(1)} %copy-done.6), channel_id=10, replica_groups={{0,3},{1,2},{4,7},{5,6},{8,11},{9,10},{12,15},{13,14},{16,19},{17,18},{..., dimensions={0}, use_global_device_ids=true | all-gather | bytes 331776 | tf_op jit(solution)/shard_map/all_gather | solution.py:127
  160.6 2.2 %unpack.3 = (bf16[1,576,256]{2,1,0:T(8,128)(2,1)}, bf16[1,576,256]{2,1,0:T(8,128)(2,1)}, bf16[1,576,256]{2,1,0:T(8,128)(2,1)}) custom-call(s32[2]{0:T(128)} %pad_add_fusion.1.place_ref, bf16[432,128]{1,0:T(8,128)(2,1)} %get-tuple-element.49.refs_0_, bf16[2,432,128]{2,1,0:T(8,128)(2,1)} %bitcast.60, ...), custom_call_target="tpu_custom_call", output_to_operand_aliasing={{0}: (5, {}), {1}: (6, {}), {2}: (7, {})} | custom-call | tf_op jit(solution)/shard_map/unpack/pallas_call | solution.py:223
  162.8 5.5 %space.1 = (bf16[1,576,256]{2,1,0:T(8,128)(2,1)}, bf16[1,576,256]{2,1,0:T(8,128)(2,1)}, bf16[1,576,256]{2,1,0:T(8,128)(2,1)}) custom-call(bf16[1,576,256]{2,1,0:T(8,128)(2,1)} %bitcast.69, bf16[1,576,256]{2,1,0:T(8,128)(2,1)} %bitcast.70, bf16[1,576,256]{2,1,0:T(8,128)(2,1)} %bitcast.71, bf16[1,576,256]{2,1,0:T(8,128)(2,1)} %bitcast.72), custom_call_target="tpu_custom_call" | custom-call | flops 1610612736 | bytes 2064384 | tf_op jit(solution)/shard_map/space/pallas_call | solution.py:66
  (3 shorter events, 0.0 us)
Async XLA Ops:
  4.1 14.3 %copy-start.4 = (bf16[2,288,128]{2,1,0:T(8,128)(2,1)S(1)}, bf16[2,288,128]{2,1,0:T(8,128)(2,1)}, u32[]{:S(2)}) copy-start(bf16[2,288,128]{2,1,0:T(8,128)(2,1)} %get-tuple-element.54) | copy-start | bytes 442372
  18.4 6.1 %copy-start.2 = (bf16[2,288,128]{2,1,0:T(8,128)(2,1)S(1)}, bf16[2,288,128]{2,1,0:T(8,128)(2,1)}, u32[]{:S(2)}) copy-start(bf16[2,288,128]{2,1,0:T(8,128)(2,1)} %get-tuple-element.55) | copy-start | bytes 442372
  34.6 6.9 %copy-start = (bf16[3,2,288,128]{3,2,1,0:T(8,128)(2,1)S(1)}, bf16[3,2,288,128]{3,2,1,0:T(8,128)(2,1)}, u32[]{:S(2)}) copy-start(bf16[3,2,288,128]{3,2,1,0:T(8,128)(2,1)} %get-tuple-element.57) | copy-start | bytes 1327108
  55.1 0.7 copy-start.10
  61.1 6.5 %copy-start.9 = (bf16[432,128]{1,0:T(8,128)(2,1)S(1)}, bf16[432,128]{1,0:T(8,128)(2,1)}, u32[]{:S(2)}) copy-start(bf16[432,128]{1,0:T(8,128)(2,1)} %get-tuple-element.60) | copy-start | bytes 331780
  67.6 8.2 %copy-start.7 = (bf16[432,128]{1,0:T(8,128)(2,1)S(1)}, bf16[432,128]{1,0:T(8,128)(2,1)}, u32[]{:S(2)}) copy-start(bf16[432,128]{1,0:T(8,128)(2,1)} %get-tuple-element.61) | copy-start | bytes 331780
  88.2 9.1 %copy-start.5 = (bf16[2,288,128]{2,1,0:T(8,128)(2,1)S(1)}, bf16[2,288,128]{2,1,0:T(8,128)(2,1)}, u32[]{:S(2)}) copy-start(bf16[2,288,128]{2,1,0:T(8,128)(2,1)} %get-tuple-element.46) | copy-start | bytes 442372
  97.3 8.9 %copy-start.3 = (bf16[2,288,128]{2,1,0:T(8,128)(2,1)S(1)}, bf16[2,288,128]{2,1,0:T(8,128)(2,1)}, u32[]{:S(2)}) copy-start(bf16[2,288,128]{2,1,0:T(8,128)(2,1)} %get-tuple-element.41) | copy-start | bytes 442372
  114.5 6.9 %copy-start.1 = (bf16[3,2,288,128]{3,2,1,0:T(8,128)(2,1)S(1)}, bf16[3,2,288,128]{3,2,1,0:T(8,128)(2,1)}, u32[]{:S(2)}) copy-start(bf16[3,2,288,128]{3,2,1,0:T(8,128)(2,1)} %get-tuple-element.48) | copy-start | bytes 1327108
  139.6 5.9 %copy-start.8 = (bf16[432,128]{1,0:T(8,128)(2,1)S(1)}, bf16[432,128]{1,0:T(8,128)(2,1)}, u32[]{:S(2)}) copy-start(bf16[432,128]{1,0:T(8,128)(2,1)} %get-tuple-element.51) | copy-start | bytes 331780
  145.5 7.7 %copy-start.6 = (bf16[432,128]{1,0:T(8,128)(2,1)S(1)}, bf16[432,128]{1,0:T(8,128)(2,1)}, u32[]{:S(2)}) copy-start(bf16[432,128]{1,0:T(8,128)(2,1)} %get-tuple-element.52) | copy-start | bytes 331780

commit v4 on v3

--- a/solution.py
+++ b/solution.py
@@ -13,8 +13,6 @@
 WIDTH = HEADS * HDIM
 SCALING = 1.0 / math.sqrt(HDIM)
 CHUNKS = (4, 4)
-GATHER_SEQ = True
-GATHER_GRP = True
 masked_score = -1e30
 
 
@@ -122,9 +120,7 @@
     )(place, *arrays)
 
 
-def swap(block, axis, pairs, gathered):
-    if gathered:
-        return lax.all_gather(block, axis, axis_index_groups=pairs)
+def swap(block, axis, pairs):
     return lax.ppermute(block, axis, [(i, j) for i, j in pairs] + [(j, i) for i, j in pairs])
 
 
@@ -133,32 +129,21 @@
     moved = [blocks[0]]
     for step in range(1, n):
         pairs = [[i, i ^ step] for i in range(n) if i < i ^ step]
-        moved.append(swap(blocks[step], "seq", pairs, GATHER_SEQ))
+        moved.append(swap(blocks[step], "seq", pairs))
     return moved
-
-
-def from_partner(ref, is_second):
-    return ref.at[is_second] if GATHER_SEQ else ref
-
-
-def seq_block(ref, step, place_ref):
-    if step == 0:
-        return ref
-    return from_partner(ref, jnp.int32(place_ref[0] < place_ref[0] ^ step))
 
 
 def sides_kernel(n, place_ref, *refs):
     ins, outs = refs[:n], refs[n:]
     is_odd = place_ref[1]
     for step, ref in enumerate(ins):
-        block = seq_block(ref, step, place_ref)
         frame = place_ref[0] ^ step
         for start, out in enumerate(outs):
             at = frame - jnp.where(is_odd == start, 1, 0)
 
             @pl.when((at >= 0) & (at < n - 1))
             def _():
-                out[jnp.clip(at, 0, n - 2)] = block[...]
+                out[jnp.clip(at, 0, n - 2)] = ref[...]
 
 
 def sides(place, blocks):
@@ -170,7 +155,7 @@
         in_specs=[pl.BlockSpec(memory_space=pltpu.SMEM)] + [vmem] * n,
         out_specs=[vmem] * 2,
         out_shape=[shape] * 2,
-        compiler_params=pltpu.CompilerParams(vmem_limit_bytes=60 * 2**20),
+        compiler_params=pltpu.CompilerParams(vmem_limit_bytes=24 * 2**20),
         name="sides",
     )(place, *blocks)
 
@@ -179,17 +164,14 @@
     count = lax.axis_size("grp")
     moved = []
     for start, block in enumerate(blocks):
-        pairs = [[i, (i + 1) % count] for i in range(start, count, 2)]
-        if not GATHER_GRP:
-            pairs = [pair for pair in pairs if pair[0] < pair[1]]
-        moved.append(swap(block, "grp", pairs, GATHER_GRP))
+        moved.append(swap(block, "grp", [(i, i + 1) for i in range(start, count - 1, 2)]))
     return moved
 
 
 def join_kernel(n, span, place_ref, *refs):
     ins, outs, (held, ready, left_off) = refs[:n], refs[-6:-3], refs[-3:]
     for step, ref in enumerate(ins):
-        held[place_ref[0] ^ step] = seq_block(ref, step, place_ref)[...]
+        held[place_ref[0] ^ step] = ref[...]
     count = span.stop - span.start
     half = count // 2
     places = held.shape[2] // 2
@@ -231,7 +213,7 @@
             pltpu.SemaphoreType.DMA((3,)),
         ],
         input_output_aliases={1 + n + i: i for i in range(len(earlier))},
-        compiler_params=pltpu.CompilerParams(vmem_limit_bytes=60 * 2**20),
+        compiler_params=pltpu.CompilerParams(vmem_limit_bytes=24 * 2**20),
         name="unpack",
     )(place, *blocks, *earlier)
 
@@ -252,11 +234,9 @@
         y_ref[frame] = ref[1].astype(jnp.float32)
 
     for step, ref in enumerate(own):
-        widen(seq_block(ref, step, place_ref), halo + (place_ref[0] ^ step))
+        widen(ref, halo + (place_ref[0] ^ step))
     for start, ref in enumerate(sides_of):
         is_next = place_ref[1] == start
-        if GATHER_GRP:
-            ref = ref.at[jnp.int32(is_next)]
         for at in range(halo):
             frame = at + jnp.where(is_next, halo + window, 0)
             needed = (frame >= lowest) & (frame < highest)
@@ -349,7 +329,7 @@
             pltpu.VMEM((extent, window, heads, lanes), jnp.float32),
             pltpu.VMEM((window, *shape), jnp.bfloat16),
         ],
-        compiler_params=pltpu.CompilerParams(vmem_limit_bytes=60 * 2**20),
+        compiler_params=pltpu.CompilerParams(vmem_limit_bytes=48 * 2**20),
         cost_estimate=pl.CostEstimate(
             flops=400 * work,
             bytes_accessed=2 * sum(block.size for block in (*own, *beside)),
@@ -390,12 +370,8 @@
         head += heads
     space = frame_grads(*turned(q_space, k_space, v_space, cot_space))
     back = []
-    own = None
     for span in spans:
-        packed = list(split(place, time, span, n))
-        if own is not None:
-            packed[2:], own[2] = lax.optimization_barrier((packed[2:], own[2]))
-        own = exchange(packed)
+        own = exchange(split(place, time, span, n))
         beside = neighbours(sides(place, own))
         back.append(exchange(clip_grads(place, bounds, own, beside)))
     grads = None

time: 170 us -> 64 us (0.38)
  the two profiles are of different devices: /device:TPU:0 before, /device:TPU:11 now
where the time goes in v4:
time: 64 us; the launch traced here: 63.8 us
  starting transfers between devices  24.5 us (38%)
  Pallas kernels  19.7 us (31%)
  waiting for transfers between devices  17.8 us (28%)
  other arithmetic  0.93 us (1%)
  between operations  0.79 us (1%)
    ppermute x16, starting transfers between devices, swap(): lax.ppermute(block, axis, [(i, j) for i, j in pairs] + [(j, i) for i, j i...  24.5 us
    ppermute x16, waiting for transfers between devices, swap(): lax.ppermute(block, axis, [(i, j) for i, j in pairs] + [(j, i) for i, j i...  17.8 us
    pallas_call x2, Pallas kernels, split(): pl.pallas_call(functools.partial(split_kernel, n, span), in_specs=[pl.Blo...  5.76 us
    pallas_call x1, Pallas kernels, frame_grads(): pl.pallas_call(frame_kernel, out_shape=(shape, shape, shape), compiler_pa...  5.53 us
    pallas_call x2, Pallas kernels, clip_grads(): pl.pallas_call(functools.partial(clip_kernel, window, heads), out_shape=[...  3.94 us
    pallas_call x2, Pallas kernels, join(): pl.pallas_call(functools.partial(join_kernel, n, span), in_specs=[pl.Bloc...  3.08 us
    pallas_call x2, Pallas kernels, sides(): pl.pallas_call(functools.partial(sides_kernel, n), in_specs=[pl.BlockSpec...  1.36 us
  transfers between devices with their start and end apart: 16, of which 5 were waited for; matrix products, arithmetic and copies ran while one was open for 0% of the time, Pallas kernels for 24%

profile of v4, /device:TPU:11, one launch (start us, length us, event | category | flops | bytes accessed | tf_op | source)
XLA Modules:
  0.0 63.8 jit_solution(5614368710256247120)
XLA Ops:
  0.6 0.6 %pad_add_fusion.1.place_ref = s32[2]{0:T(128)} fusion(s32[1]{0:T(128)} %bitcast.8, s32[1]{0:T(128)} %bitcast.7), kind=kLoop, calls=%fused_computation.6 | loop fusion | flops 2 | bytes 16 | tf_op jit(solution)/shard_map/stack | solution.py:364
  1.3 2.8 %pack.3 = (bf16[2,288,128]{2,1,0:T(8,128)(2,1)}, bf16[2,288,128]{2,1,0:T(8,128)(2,1)}, bf16[2,288,128]{2,1,0:T(8,128)(2,1)}, bf16[2,288,128]{2,1,0:T(8,128)(2,1)}) custom-call(s32[2]{0:T(128)} %pad_add_fusion.1.place_ref, bf16[1,576,256]{2,1,0:T(8,128)(2,1)} %bitcast.20, bf16[1,576,256]{2,1,0:T(8,128)(2,1)} %bitcast.22, bf16[1,576,256]{2,1,0:T(8,128)(2,1)} %bitcast.24, ...), custom_call_target="tpu_custom_call" | custom-call | tf_op jit(solution)/shard_map/pack/pallas_call | solution.py:107
  4.1 1.4 %collective-permute-start.10 = (bf16[2,288,128]{2,1,0:T(8,128)(2,1)}, bf16[2,288,128]{2,1,0:T(8,128)(2,1)S(1)}, u32[]{:S(2)}, u32[]{:S(2)}) collective-permute-start(bf16[2,288,128]{2,1,0:T(8,128)(2,1)} %get-tuple-element.51), channel_id=1, source_target_pairs={{0,3},{1,2},{3,0},{2,1},{4,7},{5,6},{7,4},{6,5},{8,11},{9,10},{11,... | collective-permute-start | bytes 442376 | tf_op jit(solution)/shard_map/ppermute | solution.py:124
  5.5 2.2 %collective-permute-start.8 = (bf16[2,288,128]{2,1,0:T(8,128)(2,1)}, bf16[2,288,128]{2,1,0:T(8,128)(2,1)S(1)}, u32[]{:S(2)}, u32[]{:S(2)}) collective-permute-start(bf16[2,288,128]{2,1,0:T(8,128)(2,1)} %get-tuple-element.49), channel_id=1, source_target_pairs={{0,1},{2,3},{1,0},{3,2},{4,5},{6,7},{5,4},{7,6},{8,9},{10,11},{9,8... | collective-permute-start | bytes 442376 | tf_op jit(solution)/shard_map/ppermute | solution.py:124
  7.7 0.0 copy-start.1
  7.7 0.0 collective-permute-start.9
  7.7 2.9 %pack.2 = (bf16[2,288,128]{2,1,0:T(8,128)(2,1)}, bf16[2,288,128]{2,1,0:T(8,128)(2,1)}, bf16[2,288,128]{2,1,0:T(8,128)(2,1)}, bf16[2,288,128]{2,1,0:T(8,128)(2,1)}) custom-call(s32[2]{0:T(128)} %pad_add_fusion.1.place_ref, bf16[1,576,256]{2,1,0:T(8,128)(2,1)} %bitcast.21, bf16[1,576,256]{2,1,0:T(8,128)(2,1)} %bitcast.23, bf16[1,576,256]{2,1,0:T(8,128)(2,1)} %bitcast.25, ...), custom_call_target="tpu_custom_call" | custom-call | tf_op jit(solution)/shard_map/pack/pallas_call | solution.py:107
  10.6 0.0 copy-start.3
  10.6 0.3 collective-permute-start
  10.9 2.1 %collective-permute-start.1 = (bf16[2,288,128]{2,1,0:T(8,128)(2,1)}, bf16[2,288,128]{2,1,0:T(8,128)(2,1)S(1)}, u32[]{:S(2)}, u32[]{:S(2)}) collective-permute-start(bf16[2,288,128]{2,1,0:T(8,128)(2,1)} %get-tuple-element.40), channel_id=1, source_target_pairs={{0,2},{1,3},{2,0},{3,1},{4,6},{5,7},{6,4},{7,5},{8,10},{9,11},{10,... | collective-permute-start | bytes 442376 | tf_op jit(solution)/shard_map/ppermute | solution.py:124
  13.0 0.0 copy-done.3
  13.0 0.1 select_reduce_fusion.2
  13.1 0.0 collective-permute-done.10.refs_3_
  13.1 0.4 collective-permute-start.2
  13.5 0.0 copy-start.2
  13.5 0.9 %collective-permute-done.8.refs_1_ = bf16[2,288,128]{2,1,0:T(8,128)(2,1)S(1)} collective-permute-done((bf16[2,288,128]{2,1,0:T(8,128)(2,1)}, bf16[2,288,128]{2,1,0:T(8,128)(2,1)S(1)}, u32[]{:S(2)}, u32[]{:S(2)}) %collective-permute-start.8) | collective-permute-done | bytes 147488 | tf_op jit(solution)/shard_map/ppermute | solution.py:124
  14.4 2.1 %collective-permute-done.9.refs_2_ = bf16[2,288,128]{2,1,0:T(8,128)(2,1)S(1)} collective-permute-done((bf16[2,288,128]{2,1,0:T(8,128)(2,1)}, bf16[2,288,128]{2,1,0:T(8,128)(2,1)S(1)}, u32[]{:S(2)}, u32[]{:S(2)}) %collective-permute-start.9) | collective-permute-done | bytes 147488 | tf_op jit(solution)/shard_map/ppermute | solution.py:124
  16.5 0.0 copy-done.1
  16.5 0.0 copy-done.2
  16.5 0.0 copy-start
  16.5 0.7 %sides.3 = (bf16[3,2,288,128]{3,2,1,0:T(8,128)(2,1)S(1)}, bf16[3,2,288,128]{3,2,1,0:T(8,128)(2,1)S(1)}) custom-call(s32[2]{0:T(128)S(1)} %copy-done.2, bf16[2,288,128]{2,1,0:T(8,128)(2,1)S(1)} %copy-done.1, bf16[2,288,128]{2,1,0:T(8,128)(2,1)S(1)} %collective-permute-done.8.refs_1_, bf16[2,288,128]{2,1,0:T(8,128)(2,1)S(1)} %collective-permute-done.9.refs_2_, ...), custom_call_target="tpu_custom_call" | custom-call | tf_op jit(solution)/shard_map/sides/pallas_call | solution.py:153
  17.2 4.0 %collective-permute-start.11 = (bf16[3,2,288,128]{3,2,1,0:T(8,128)(2,1)S(1)}, bf16[3,2,288,128]{3,2,1,0:T(8,128)(2,1)S(1)}, u32[]{:S(2)}, u32[]{:S(2)}) collective-permute-start(bf16[3,2,288,128]{3,2,1,0:T(8,128)(2,1)S(1)} %get-tuple-element.52), channel_id=1, source_target_pairs={{0,4},{8,12},{16,20},{24,28},{4,0},{12,8},{20,16},{28,24},{1,5},{9... | collective-permute-start | bytes 1327112 | tf_op jit(solution)/shard_map/ppermute | solution.py:124
  21.2 3.0 %collective-permute-start.12 = (bf16[3,2,288,128]{3,2,1,0:T(8,128)(2,1)S(1)}, bf16[3,2,288,128]{3,2,1,0:T(8,128)(2,1)S(1)}, u32[]{:S(2)}, u32[]{:S(2)}) collective-permute-start(bf16[3,2,288,128]{3,2,1,0:T(8,128)(2,1)S(1)} %get-tuple-element.53), channel_id=1, source_target_pairs={{4,8},{12,16},{20,24},{8,4},{16,12},{24,20},{5,9},{13,17},{21,25},... | collective-permute-start | bytes 1327112 | tf_op jit(solution)/shard_map/ppermute | solution.py:124
  24.2 0.2 select_reduce_fusion.1
  24.4 0.0 collective-permute-done.refs_1_
  24.4 0.0 collective-permute-done.1.refs_2_
  24.4 7.0 %collective-permute-done.2.refs_3_ = bf16[2,288,128]{2,1,0:T(8,128)(2,1)S(1)} collective-permute-done((bf16[2,288,128]{2,1,0:T(8,128)(2,1)}, bf16[2,288,128]{2,1,0:T(8,128)(2,1)S(1)}, u32[]{:S(2)}, u32[]{:S(2)}) %collective-permute-start.2) | collective-permute-done | bytes 147488 | tf_op jit(solution)/shard_map/ppermute | solution.py:124
  31.5 0.0 copy-done
  31.5 0.7 %sides.2 = (bf16[3,2,288,128]{3,2,1,0:T(8,128)(2,1)S(1)}, bf16[3,2,288,128]{3,2,1,0:T(8,128)(2,1)S(1)}) custom-call(s32[2]{0:T(128)S(1)} %copy-done.2, bf16[2,288,128]{2,1,0:T(8,128)(2,1)S(1)} %copy-done, bf16[2,288,128]{2,1,0:T(8,128)(2,1)S(1)} %collective-permute-done.refs_1_, bf16[2,288,128]{2,1,0:T(8,128)(2,1)S(1)} %collective-permute-done.1.refs_2_, ...), custom_call_target="tpu_custom_call" | custom-call | tf_op jit(solution)/shard_map/sides/pallas_call | solution.py:153
  32.1 1.4 %collective-permute-start.3 = (bf16[3,2,288,128]{3,2,1,0:T(8,128)(2,1)S(1)}, bf16[3,2,288,128]{3,2,1,0:T(8,128)(2,1)S(1)}, u32[]{:S(2)}, u32[]{:S(2)}) collective-permute-start(bf16[3,2,288,128]{3,2,1,0:T(8,128)(2,1)S(1)} %get-tuple-element.42), channel_id=1, source_target_pairs={{0,4},{8,12},{16,20},{24,28},{4,0},{12,8},{20,16},{28,24},{1,5},{9... | collective-permute-start | bytes 1327112 | tf_op jit(solution)/shard_map/ppermute | solution.py:124
  33.6 3.0 %collective-permute-start.4 = (bf16[3,2,288,128]{3,2,1,0:T(8,128)(2,1)S(1)}, bf16[3,2,288,128]{3,2,1,0:T(8,128)(2,1)S(1)}, u32[]{:S(2)}, u32[]{:S(2)}) collective-permute-start(bf16[3,2,288,128]{3,2,1,0:T(8,128)(2,1)S(1)} %get-tuple-element.43), channel_id=1, source_target_pairs={{4,8},{12,16},{20,24},{8,4},{16,12},{24,20},{5,9},{13,17},{21,25},... | collective-permute-start | bytes 1327112 | tf_op jit(solution)/shard_map/ppermute | solution.py:124
  36.6 0.0 collective-permute-done.11.refs_4_
  36.6 0.0 collective-permute-done.12.refs_5_
  36.6 2.0 %clips.3 = (bf16[432,128]{1,0:T(8,128)(2,1)S(1)}, bf16[432,128]{1,0:T(8,128)(2,1)S(1)}, bf16[432,128]{1,0:T(8,128)(2,1)S(1)}, bf16[432,128]{1,0:T(8,128)(2,1)S(1)}) custom-call(s32[2]{0:T(128)S(1)} %copy-done.2, s32[2,10]{1,0:T(2,128)S(1)} %pad_add_fusion.bounds, bf16[2,288,128]{2,1,0:T(8,128)(2,1)S(1)} %copy-done.1, ...), custom_call_target="tpu_custom_call" | custom-call | flops 589824000 | bytes 1474560 | tf_op jit(solution)/shard_map/clips/pallas_call | solution.py:321
  38.6 2.7 %collective-permute-start.13 = (bf16[432,128]{1,0:T(8,128)(2,1)S(1)}, bf16[432,128]{1,0:T(8,128)(2,1)S(1)}, u32[]{:S(2)}, u32[]{:S(2)}) collective-permute-start(bf16[432,128]{1,0:T(8,128)(2,1)S(1)} %get-tuple-element.55), channel_id=1, source_target_pairs={{0,1},{2,3},{1,0},{3,2},{4,5},{6,7},{5,4},{7,6},{8,9},{10,11},{9,8... | collective-permute-start | bytes 331784 | tf_op jit(solution)/shard_map/ppermute | solution.py:124
  41.3 0.1 collective-permute-start.14
  41.5 1.1 %collective-permute-start.15 = (bf16[432,128]{1,0:T(8,128)(2,1)S(1)}, bf16[432,128]{1,0:T(8,128)(2,1)S(1)}, u32[]{:S(2)}, u32[]{:S(2)}) collective-permute-start(bf16[432,128]{1,0:T(8,128)(2,1)S(1)} %get-tuple-element.57), channel_id=1, source_target_pairs={{0,3},{1,2},{3,0},{2,1},{4,7},{5,6},{7,4},{6,5},{8,11},{9,10},{11,... | collective-permute-start | bytes 331784 | tf_op jit(solution)/shard_map/ppermute | solution.py:124
  42.6 0.0 collective-permute-done.3.refs_4_
  42.6 5.6 %collective-permute-done.4.refs_5_ = bf16[3,2,288,128]{3,2,1,0:T(8,128)(2,1)S(1)} collective-permute-done((bf16[3,2,288,128]{3,2,1,0:T(8,128)(2,1)S(1)}, bf16[3,2,288,128]{3,2,1,0:T(8,128)(2,1)S(1)}, u32[]{:S(2)}, u32[]{:S(2)}) %collective-permute-start.4) | collective-permute-done | bytes 442400 | tf_op jit(solution)/shard_map/ppermute | solution.py:124
  48.2 2.0 %clips.2 = (bf16[432,128]{1,0:T(8,128)(2,1)S(1)}, bf16[432,128]{1,0:T(8,128)(2,1)S(1)}, bf16[432,128]{1,0:T(8,128)(2,1)S(1)}, bf16[432,128]{1,0:T(8,128)(2,1)S(1)}) custom-call(s32[2]{0:T(128)S(1)} %copy-done.2, s32[2,10]{1,0:T(2,128)S(1)} %pad_add_fusion.bounds, bf16[2,288,128]{2,1,0:T(8,128)(2,1)S(1)} %copy-done, ...), custom_call_target="tpu_custom_call" | custom-call | flops 589824000 | bytes 1474560 | tf_op jit(solution)/shard_map/clips/pallas_call | solution.py:321
  50.2 0.4 collective-permute-start.5
  50.6 2.1 %collective-permute-start.6 = (bf16[432,128]{1,0:T(8,128)(2,1)S(1)}, bf16[432,128]{1,0:T(8,128)(2,1)S(1)}, u32[]{:S(2)}, u32[]{:S(2)}) collective-permute-start(bf16[432,128]{1,0:T(8,128)(2,1)S(1)} %get-tuple-element.46), channel_id=1, source_target_pairs={{0,2},{1,3},{2,0},{3,1},{4,6},{5,7},{6,4},{7,5},{8,10},{9,11},{10,... | collective-permute-start | bytes 331784 | tf_op jit(solution)/shard_map/ppermute | solution.py:124
  52.7 0.0 collective-permute-done.13.refs_1_
  52.7 0.2 collective-permute-start.7
  52.9 5.5 %space.1 = (bf16[1,576,256]{2,1,0:T(8,128)(2,1)}, bf16[1,576,256]{2,1,0:T(8,128)(2,1)}, bf16[1,576,256]{2,1,0:T(8,128)(2,1)}) custom-call(bf16[1,576,256]{2,1,0:T(8,128)(2,1)} %bitcast.31, bf16[1,576,256]{2,1,0:T(8,128)(2,1)} %bitcast.32, bf16[1,576,256]{2,1,0:T(8,128)(2,1)} %bitcast.33, bf16[1,576,256]{2,1,0:T(8,128)(2,1)} %bitcast.34), custom_call_target="tpu_custom_call" | custom-call | flops 1610612736 | bytes 2064384 | tf_op jit(solution)/shard_map/space/pallas_call | solution.py:64
  58.4 0.0 collective-permute-done.14.refs_2_
  58.4 0.0 collective-permute-done.15.refs_3_
  58.4 1.5 %unpack.2 = (bf16[1,576,256]{2,1,0:T(8,128)(2,1)}, bf16[1,576,256]{2,1,0:T(8,128)(2,1)}, bf16[1,576,256]{2,1,0:T(8,128)(2,1)}) custom-call(s32[2]{0:T(128)S(1)} %copy-done.2, bf16[432,128]{1,0:T(8,128)(2,1)S(1)} %get-tuple-element.54.refs_0_, bf16[432,128]{1,0:T(8,128)(2,1)S(1)} %collective-permute-done.13.refs_1_, ...), custom_call_target="tpu_custom_call" | custom-call | tf_op jit(solution)/shard_map/unpack/pallas_call | solution.py:205
  60.0 0.0 collective-permute-done.5.refs_1_
  60.0 0.0 collective-permute-done.6.refs_2_
  60.0 2.2 %collective-permute-done.7.refs_3_ = bf16[432,128]{1,0:T(8,128)(2,1)S(1)} collective-permute-done((bf16[432,128]{1,0:T(8,128)(2,1)S(1)}, bf16[432,128]{1,0:T(8,128)(2,1)S(1)}, u32[]{:S(2)}, u32[]{:S(2)}) %collective-permute-start.7) | collective-permute-done | bytes 110624 | tf_op jit(solution)/shard_map/ppermute | solution.py:124
  62.2 1.5 %unpack.3 = (bf16[1,576,256]{2,1,0:T(8,128)(2,1)}, bf16[1,576,256]{2,1,0:T(8,128)(2,1)}, bf16[1,576,256]{2,1,0:T(8,128)(2,1)}) custom-call(s32[2]{0:T(128)S(1)} %copy-done.2, bf16[432,128]{1,0:T(8,128)(2,1)S(1)} %get-tuple-element.44.refs_0_, ...), custom_call_target="tpu_custom_call", output_to_operand_aliasing={{0}: (5, {}), {1}: (6, {}), {2}: (7, {})} | custom-call | tf_op jit(solution)/shard_map/unpack/pallas_call | solution.py:205
  (4 shorter events, 0.0 us)
Async XLA Ops:
  4.1 9.0 %collective-permute-start.10 = (bf16[2,288,128]{2,1,0:T(8,128)(2,1)}, bf16[2,288,128]{2,1,0:T(8,128)(2,1)S(1)}, u32[]{:S(2)}, u32[]{:S(2)}) collective-permute-start(bf16[2,288,128]{2,1,0:T(8,128)(2,1)} %get-tuple-element.51), channel_id=1, source_target_pairs={{0,3},{1,2},{3,0},{2,1},{4,7},{5,6},{7,4},{6,5},{8,11},{9,10},{11,... | collective-permute-start | bytes 442376 | tf_op jit(solution)/shard_map/ppermute | solution.py:124
  5.5 8.9 %collective-permute-start.8 = (bf16[2,288,128]{2,1,0:T(8,128)(2,1)}, bf16[2,288,128]{2,1,0:T(8,128)(2,1)S(1)}, u32[]{:S(2)}, u32[]{:S(2)}) collective-permute-start(bf16[2,288,128]{2,1,0:T(8,128)(2,1)} %get-tuple-element.49), channel_id=1, source_target_pairs={{0,1},{2,3},{1,0},{3,2},{4,5},{6,7},{5,4},{7,6},{8,9},{10,11},{9,8... | collective-permute-start | bytes 442376 | tf_op jit(solution)/shard_map/ppermute | solution.py:124
  7.7 8.8 %copy-start.1 = (bf16[2,288,128]{2,1,0:T(8,128)(2,1)S(1)}, bf16[2,288,128]{2,1,0:T(8,128)(2,1)}, u32[]{:S(2)}) copy-start(bf16[2,288,128]{2,1,0:T(8,128)(2,1)} %get-tuple-element.48.refs_0_) | copy-start | bytes 442372
  7.7 8.8 %collective-permute-start.9 = (bf16[2,288,128]{2,1,0:T(8,128)(2,1)}, bf16[2,288,128]{2,1,0:T(8,128)(2,1)S(1)}, u32[]{:S(2)}, u32[]{:S(2)}) collective-permute-start(bf16[2,288,128]{2,1,0:T(8,128)(2,1)} %get-tuple-element.50), channel_id=1, source_target_pairs={{0,2},{1,3},{2,0},{3,1},{4,6},{5,7},{6,4},{7,5},{8,10},{9,11},{10,... | collective-permute-start | bytes 442376 | tf_op jit(solution)/shard_map/ppermute | solution.py:124
  10.6 2.4 %copy-start.3 = (s32[16]{0:T(128)S(1)}, s32[16]{0:T(128)}, u32[]{:S(2)}) copy-start(s32[16]{0:T(128)} %param.17) | copy-start | bytes 196
  10.6 13.8 %collective-permute-start = (bf16[2,288,128]{2,1,0:T(8,128)(2,1)}, bf16[2,288,128]{2,1,0:T(8,128)(2,1)S(1)}, u32[]{:S(2)}, u32[]{:S(2)}) collective-permute-start(bf16[2,288,128]{2,1,0:T(8,128)(2,1)} %get-tuple-element.39), channel_id=1, source_target_pairs={{0,1},{2,3},{1,0},{3,2},{4,5},{6,7},{5,4},{7,6},{8,9},{10,11},{9,8... | collective-permute-start | bytes 442376 | tf_op jit(solution)/shard_map/ppermute | solution.py:124
  10.9 13.5 %collective-permute-start.1 = (bf16[2,288,128]{2,1,0:T(8,128)(2,1)}, bf16[2,288,128]{2,1,0:T(8,128)(2,1)S(1)}, u32[]{:S(2)}, u32[]{:S(2)}) collective-permute-start(bf16[2,288,128]{2,1,0:T(8,128)(2,1)} %get-tuple-element.40), channel_id=1, source_target_pairs={{0,2},{1,3},{2,0},{3,1},{4,6},{5,7},{6,4},{7,5},{8,10},{9,11},{10,... | collective-permute-start | bytes 442376 | tf_op jit(solution)/shard_map/ppermute | solution.py:124
  13.1 18.4 %collective-permute-start.2 = (bf16[2,288,128]{2,1,0:T(8,128)(2,1)}, bf16[2,288,128]{2,1,0:T(8,128)(2,1)S(1)}, u32[]{:S(2)}, u32[]{:S(2)}) collective-permute-start(bf16[2,288,128]{2,1,0:T(8,128)(2,1)} %get-tuple-element.41), channel_id=1, source_target_pairs={{0,3},{1,2},{3,0},{2,1},{4,7},{5,6},{7,4},{6,5},{8,11},{9,10},{11,... | collective-permute-start | bytes 442376 | tf_op jit(solution)/shard_map/ppermute | solution.py:124
  13.5 3.0 %copy-start.2 = (s32[2]{0:T(128)S(1)}, s32[2]{0:T(128)}, u32[]{:S(2)}) copy-start(s32[2]{0:T(128)} %pad_add_fusion.1.place_ref) | copy-start | bytes 28
  16.5 15.0 %copy-start = (bf16[2,288,128]{2,1,0:T(8,128)(2,1)S(1)}, bf16[2,288,128]{2,1,0:T(8,128)(2,1)}, u32[]{:S(2)}) copy-start(bf16[2,288,128]{2,1,0:T(8,128)(2,1)} %get-tuple-element.38.refs_0_) | copy-start | bytes 442372
  17.2 19.5 %collective-permute-start.11 = (bf16[3,2,288,128]{3,2,1,0:T(8,128)(2,1)S(1)}, bf16[3,2,288,128]{3,2,1,0:T(8,128)(2,1)S(1)}, u32[]{:S(2)}, u32[]{:S(2)}) collective-permute-start(bf16[3,2,288,128]{3,2,1,0:T(8,128)(2,1)S(1)} %get-tuple-element.52), channel_id=1, source_target_pairs={{0,4},{8,12},{16,20},{24,28},{4,0},{12,8},{20,16},{28,24},{1,5},{9... | collective-permute-start | bytes 1327112 | tf_op jit(solution)/shard_map/ppermute | solution.py:124
  21.2 15.5 %collective-permute-start.12 = (bf16[3,2,288,128]{3,2,1,0:T(8,128)(2,1)S(1)}, bf16[3,2,288,128]{3,2,1,0:T(8,128)(2,1)S(1)}, u32[]{:S(2)}, u32[]{:S(2)}) collective-permute-start(bf16[3,2,288,128]{3,2,1,0:T(8,128)(2,1)S(1)} %get-tuple-element.53), channel_id=1, source_target_pairs={{4,8},{12,16},{20,24},{8,4},{16,12},{24,20},{5,9},{13,17},{21,25},... | collective-permute-start | bytes 1327112 | tf_op jit(solution)/shard_map/ppermute | solution.py:124
  32.1 10.5 %collective-permute-start.3 = (bf16[3,2,288,128]{3,2,1,0:T(8,128)(2,1)S(1)}, bf16[3,2,288,128]{3,2,1,0:T(8,128)(2,1)S(1)}, u32[]{:S(2)}, u32[]{:S(2)}) collective-permute-start(bf16[3,2,288,128]{3,2,1,0:T(8,128)(2,1)S(1)} %get-tuple-element.42), channel_id=1, source_target_pairs={{0,4},{8,12},{16,20},{24,28},{4,0},{12,8},{20,16},{28,24},{1,5},{9... | collective-permute-start | bytes 1327112 | tf_op jit(solution)/shard_map/ppermute | solution.py:124
  33.6 14.6 %collective-permute-start.4 = (bf16[3,2,288,128]{3,2,1,0:T(8,128)(2,1)S(1)}, bf16[3,2,288,128]{3,2,1,0:T(8,128)(2,1)S(1)}, u32[]{:S(2)}, u32[]{:S(2)}) collective-permute-start(bf16[3,2,288,128]{3,2,1,0:T(8,128)(2,1)S(1)} %get-tuple-element.43), channel_id=1, source_target_pairs={{4,8},{12,16},{20,24},{8,4},{16,12},{24,20},{5,9},{13,17},{21,25},... | collective-permute-start | bytes 1327112 | tf_op jit(solution)/shard_map/ppermute | solution.py:124
  38.6 14.1 %collective-permute-start.13 = (bf16[432,128]{1,0:T(8,128)(2,1)S(1)}, bf16[432,128]{1,0:T(8,128)(2,1)S(1)}, u32[]{:S(2)}, u32[]{:S(2)}) collective-permute-start(bf16[432,128]{1,0:T(8,128)(2,1)S(1)} %get-tuple-element.55), channel_id=1, source_target_pairs={{0,1},{2,3},{1,0},{3,2},{4,5},{6,7},{5,4},{7,6},{8,9},{10,11},{9,8... | collective-permute-start | bytes 331784 | tf_op jit(solution)/shard_map/ppermute | solution.py:124
  41.3 17.1 %collective-permute-start.14 = (bf16[432,128]{1,0:T(8,128)(2,1)S(1)}, bf16[432,128]{1,0:T(8,128)(2,1)S(1)}, u32[]{:S(2)}, u32[]{:S(2)}) collective-permute-start(bf16[432,128]{1,0:T(8,128)(2,1)S(1)} %get-tuple-element.56), channel_id=1, source_target_pairs={{0,2},{1,3},{2,0},{3,1},{4,6},{5,7},{6,4},{7,5},{8,10},{9,11},{10,... | collective-permute-start | bytes 331784 | tf_op jit(solution)/shard_map/ppermute | solution.py:124
  41.5 17.0 %collective-permute-start.15 = (bf16[432,128]{1,0:T(8,128)(2,1)S(1)}, bf16[432,128]{1,0:T(8,128)(2,1)S(1)}, u32[]{:S(2)}, u32[]{:S(2)}) collective-permute-start(bf16[432,128]{1,0:T(8,128)(2,1)S(1)} %get-tuple-element.57), channel_id=1, source_target_pairs={{0,3},{1,2},{3,0},{2,1},{4,7},{5,6},{7,4},{6,5},{8,11},{9,10},{11,... | collective-permute-start | bytes 331784 | tf_op jit(solution)/shard_map/ppermute | solution.py:124
  50.2 9.8 %collective-permute-start.5 = (bf16[432,128]{1,0:T(8,128)(2,1)S(1)}, bf16[432,128]{1,0:T(8,128)(2,1)S(1)}, u32[]{:S(2)}, u32[]{:S(2)}) collective-permute-start(bf16[432,128]{1,0:T(8,128)(2,1)S(1)} %get-tuple-element.45), channel_id=1, source_target_pairs={{0,1},{2,3},{1,0},{3,2},{4,5},{6,7},{5,4},{7,6},{8,9},{10,11},{9,8... | collective-permute-start | bytes 331784 | tf_op jit(solution)/shard_map/ppermute | solution.py:124
  50.6 9.4 %collective-permute-start.6 = (bf16[432,128]{1,0:T(8,128)(2,1)S(1)}, bf16[432,128]{1,0:T(8,128)(2,1)S(1)}, u32[]{:S(2)}, u32[]{:S(2)}) collective-permute-start(bf16[432,128]{1,0:T(8,128)(2,1)S(1)} %get-tuple-element.46), channel_id=1, source_target_pairs={{0,2},{1,3},{2,0},{3,1},{4,6},{5,7},{6,4},{7,5},{8,10},{9,11},{10,... | collective-permute-start | bytes 331784 | tf_op jit(solution)/shard_map/ppermute | solution.py:124
  52.7 9.5 %collective-permute-start.7 = (bf16[432,128]{1,0:T(8,128)(2,1)S(1)}, bf16[432,128]{1,0:T(8,128)(2,1)S(1)}, u32[]{:S(2)}, u32[]{:S(2)}) collective-permute-start(bf16[432,128]{1,0:T(8,128)(2,1)S(1)} %get-tuple-element.47), channel_id=1, source_target_pairs={{0,3},{1,2},{3,0},{2,1},{4,7},{5,6},{7,4},{6,5},{8,11},{9,10},{11,... | collective-permute-start | bytes 331784 | tf_op jit(solution)/shard_map/ppermute | solution.py:124

commit v5 on v4

--- a/solution.py
+++ b/solution.py
@@ -12,7 +12,7 @@
 HDIM = 72
 WIDTH = HEADS * HDIM
 SCALING = 1.0 / math.sqrt(HDIM)
-CHUNKS = (4, 4)
+CHUNKS = (2, 4, 2)
 masked_score = -1e30
 
 
@@ -74,7 +74,7 @@
     )(queries, keys, values, cotangent)
 
 
-def split_kernel(n, span, place_ref, *refs):
+def split_kernel(n, span, *refs):
     ins, outs, (loaded, held, arrived, left_off) = refs[:4], refs[4 : 4 + n], refs[-4:]
     loads = [
         pltpu.make_async_copy(array.at[0, span, :], loaded.at[i], arrived.at[i])
@@ -91,7 +91,7 @@
             both = [loaded[2 * at, :, lanes], loaded[2 * at + 1, :, lanes]]
             held[target, at] = jnp.concatenate(both, axis=1)
     stores = [
-        pltpu.make_async_copy(held.at[place_ref[0] ^ step], out, left_off.at[step])
+        pltpu.make_async_copy(held.at[(lax.axis_index("seq") ^ step)], out, left_off.at[step])
         for step, out in enumerate(outs)
     ]
     for copy in stores:
@@ -100,13 +100,13 @@
         copy.wait()
 
 
-def split(place, arrays, span, n):
+def split(arrays, span, n):
     rows, tokens = span.stop - span.start, arrays[0].shape[2]
     shape = (2, rows, 2 * tokens // n)
     hbm = pl.BlockSpec(memory_space=pltpu.HBM)
     return pl.pallas_call(
         functools.partial(split_kernel, n, span),
-        in_specs=[pl.BlockSpec(memory_space=pltpu.SMEM)] + [hbm] * 4,
+        in_specs=[hbm] * 4,
         out_specs=[hbm] * n,
         out_shape=[jax.ShapeDtypeStruct(shape, jnp.bfloat16)] * n,
         scratch_shapes=[
@@ -117,7 +117,7 @@
         ],
         compiler_params=pltpu.CompilerParams(vmem_limit_bytes=60 * 2**20),
         name="pack",
-    )(place, *arrays)
+    )(*arrays)
 
 
 def swap(block, axis, pairs):
@@ -133,11 +133,11 @@
     return moved
 
 
-def sides_kernel(n, place_ref, *refs):
+def sides_kernel(n, *refs):
     ins, outs = refs[:n], refs[n:]
-    is_odd = place_ref[1]
+    is_odd = lax.axis_index("grp") & 1
     for step, ref in enumerate(ins):
-        frame = place_ref[0] ^ step
+        frame = (lax.axis_index("seq") ^ step)
         for start, out in enumerate(outs):
             at = frame - jnp.where(is_odd == start, 1, 0)
 
@@ -146,18 +146,18 @@
                 out[jnp.clip(at, 0, n - 2)] = ref[...]
 
 
-def sides(place, blocks):
+def sides(blocks):
     n = len(blocks)
     shape = jax.ShapeDtypeStruct((n - 1, *blocks[0].shape), jnp.bfloat16)
     vmem = pl.BlockSpec(memory_space=pltpu.VMEM)
     return pl.pallas_call(
         functools.partial(sides_kernel, n),
-        in_specs=[pl.BlockSpec(memory_space=pltpu.SMEM)] + [vmem] * n,
+        in_specs=[vmem] * n,
         out_specs=[vmem] * 2,
         out_shape=[shape] * 2,
         compiler_params=pltpu.CompilerParams(vmem_limit_bytes=24 * 2**20),
         name="sides",
-    )(place, *blocks)
+    )(*blocks)
 
 
 def neighbours(blocks):
@@ -168,10 +168,10 @@
     return moved
 
 
-def join_kernel(n, span, place_ref, *refs):
+def join_kernel(n, span, *refs):
     ins, outs, (held, ready, left_off) = refs[:n], refs[-6:-3], refs[-3:]
     for step, ref in enumerate(ins):
-        held[place_ref[0] ^ step] = ref[...]
+        held[(lax.axis_index("seq") ^ step)] = ref[...]
     count = span.stop - span.start
     half = count // 2
     places = held.shape[2] // 2
@@ -195,7 +195,7 @@
         copy.wait()
 
 
-def join(place, blocks, span, tokens, earlier):
+def join(blocks, span, tokens, earlier):
     n = len(blocks)
     rows = span.stop - span.start
     shape = jax.ShapeDtypeStruct((1, WIDTH, tokens), jnp.bfloat16)
@@ -204,7 +204,7 @@
     earlier = [] if earlier is None else list(earlier)
     return pl.pallas_call(
         functools.partial(join_kernel, n, span),
-        in_specs=[pl.BlockSpec(memory_space=pltpu.SMEM)] + [vmem] * n + [hbm] * len(earlier),
+        in_specs=[vmem] * n + [hbm] * len(earlier),
         out_specs=[hbm] * 3,
         out_shape=[shape] * 3,
         scratch_shapes=[
@@ -212,13 +212,13 @@
             pltpu.VMEM((3, rows, tokens), jnp.bfloat16),
             pltpu.SemaphoreType.DMA((3,)),
         ],
-        input_output_aliases={1 + n + i: i for i in range(len(earlier))},
+        input_output_aliases={n + i: i for i in range(len(earlier))},
         compiler_params=pltpu.CompilerParams(vmem_limit_bytes=24 * 2**20),
         name="unpack",
-    )(place, *blocks, *earlier)
-
-
-def clip_kernel(window, heads, place_ref, bounds, *refs):
+    )(*blocks, *earlier)
+
+
+def clip_kernel(window, heads, bounds, *refs):
     own, sides_of = refs[:window], refs[window : window + 2]
     outs, (x_ref, y_ref, coef_ref, grad_ref) = refs[window + 2 : 2 * window + 2], refs[-4:]
     halo = window - 1
@@ -234,9 +234,9 @@
         y_ref[frame] = ref[1].astype(jnp.float32)
 
     for step, ref in enumerate(own):
-        widen(ref, halo + (place_ref[0] ^ step))
+        widen(ref, halo + ((lax.axis_index("seq") ^ step)))
     for start, ref in enumerate(sides_of):
-        is_next = place_ref[1] == start
+        is_next = (lax.axis_index("grp") & 1) == start
         for at in range(halo):
             frame = at + jnp.where(is_next, halo + window, 0)
             needed = (frame >= lowest) & (frame < highest)
@@ -305,10 +305,10 @@
 
     lax.fori_loop(0, window, gradients, 0)
     for step, out in enumerate(outs):
-        out[...] = grad_ref[place_ref[0] ^ step]
-
-
-def clip_grads(place, bounds, own, beside):
+        out[...] = grad_ref[(lax.axis_index("seq") ^ step)]
+
+
+def clip_grads(bounds, own, beside):
     window = len(own)
     _, rows, lanes = own[0].shape
     beside = list(beside)
@@ -321,7 +321,7 @@
     return pl.pallas_call(
         functools.partial(clip_kernel, window, heads),
         out_shape=[jax.ShapeDtypeStruct(shape, jnp.bfloat16)] * window,
-        in_specs=[smem, smem] + [vmem] * (window + 2),
+        in_specs=[smem] + [vmem] * (window + 2),
         out_specs=[vmem] * window,
         scratch_shapes=[
             pltpu.VMEM((extent, rows, lanes), jnp.float32),
@@ -336,7 +336,7 @@
             transcendentals=extent * window * heads * lanes,
         ),
         name="clips",
-    )(place, bounds, *own, *beside)
+    )(bounds, *own, *beside)
 
 
 def clip_bounds(clip_len, window):
@@ -361,22 +361,39 @@
     window = q_time.shape[0] * n
     tokens = q_time.shape[1]
     bounds = clip_bounds(clip_len, window)
-    place = jnp.stack([lax.axis_index("seq"), lax.axis_index("grp") % 2]).astype(jnp.int32)
     time = turned(q_time, cot_time, k_time, v_time)
     spans = []
     head = 0
     for heads in CHUNKS:
         spans.append(slice(head * HDIM, (head + heads) * HDIM))
         head += heads
-    space = frame_grads(*turned(q_space, k_space, v_space, cot_space))
-    back = []
-    for span in spans:
-        own = exchange(split(place, time, span, n))
-        beside = neighbours(sides(place, own))
-        back.append(exchange(clip_grads(place, bounds, own, beside)))
-    grads = None
-    for span, blocks in zip(spans, back):
-        grads = join(place, blocks, span, tokens, grads)
+    space_in = turned(q_space, k_space, v_space, cot_space)
+    packed = [split(time, span, n) for span in spans]
+
+    def gated(values, *earlier):
+        return lax.optimization_barrier((values, *earlier))
+
+    back, grads, own, beside = [], None, [], []
+    own.append(exchange(packed[0]))
+    own.append(exchange(packed[1]))
+    ends = sides(own[0])
+    space_in, ends = gated(space_in, ends)
+    beside.append(neighbours(ends))
+    space = frame_grads(*space_in)
+    packed[2], space, beside[0], own[1][1] = gated(packed[2], space, beside[0], own[1][1])
+    own.append(exchange(packed[2]))
+    own[1], own[2][1] = gated(own[1], own[2][1])
+    ends, beside[0] = gated(sides(own[1]), beside[0])
+    beside.append(neighbours(ends))
+    back.append(exchange(clip_grads(bounds, own[0], beside[0])))
+    ends, beside[1], back[0][1] = gated(sides(own[2]), beside[1], back[0][1])
+    beside.append(neighbours(ends))
+    back.append(exchange(clip_grads(bounds, own[1], beside[1])))
+    grads = join(back[0], spans[0], tokens, grads)
+    beside[2], grads = gated(beside[2], grads)
+    back.append(exchange(clip_grads(bounds, own[2], beside[2])))
+    grads = join(back[1], spans[1], tokens, grads)
+    grads = join(back[2], spans[2], tokens, grads)
     return turned(*space, *grads)
 
 

time: 64 us -> 72.8 us (1.14)
  the two profiles are of different devices: /device:TPU:11 before, /device:TPU:19 now
where the time goes in v5:
time: 72.8 us; the launch traced here: 72.3 us
  starting transfers between devices  33.3 us (46%)
  Pallas kernels  20.2 us (28%)
  waiting for transfers between devices  17.6 us (24%)
  between operations  0.9 us (1%)
    ppermute x24, starting transfers between devices, swap(): lax.ppermute(block, axis, [(i, j) for i, j in pairs] + [(j, i) for i, j i...  33.3 us
    ppermute x24, waiting for transfers between devices, swap(): lax.ppermute(block, axis, [(i, j) for i, j in pairs] + [(j, i) for i, j i...  17.6 us
    pallas_call x3, Pallas kernels, split(): pl.pallas_call(functools.partial(split_kernel, n, span), in_specs=[hbm] *...  6.03 us
    pallas_call x1, Pallas kernels, frame_grads(): pl.pallas_call(frame_kernel, out_shape=(shape, shape, shape), compiler_pa...  5.57 us
    pallas_call x3, Pallas kernels, clip_grads(): pl.pallas_call(functools.partial(clip_kernel, window, heads), out_shape=[...  5.54 us
    pallas_call x3, Pallas kernels, join(): pl.pallas_call(functools.partial(join_kernel, n, span), in_specs=[vmem] *...  2.72 us
  transfers between devices with their start and end apart: 24, of which 8 were waited for; matrix products, arithmetic and copies ran while one was open for 0% of the time, Pallas kernels for 24%

profile of v5, /device:TPU:19, one launch (start us, length us, event | category | flops | bytes accessed | tf_op | source)
XLA Modules:
  0.0 72.3 jit_solution(5785141423183486142)
XLA Ops:
  0.6 1.9 %pack.4 = (bf16[2,144,128]{2,1,0:T(8,128)(2,1)}, bf16[2,144,128]{2,1,0:T(8,128)(2,1)}, bf16[2,144,128]{2,1,0:T(8,128)(2,1)}, bf16[2,144,128]{2,1,0:T(8,128)(2,1)}) custom-call(bf16[1,576,256]{2,1,0:T(8,128)(2,1)} %bitcast.18, bf16[1,576,256]{2,1,0:T(8,128)(2,1)} %bitcast.21, bf16[1,576,256]{2,1,0:T(8,128)(2,1)} %bitcast.24, bf16[1,576,256]{2,1,0:T(8,128)(2,1)} %bitcast.27), custom_call_target="tpu_custom_call" | custom-call | tf_op jit(solution)/shard_map/pack/pallas_call | solution.py:107
  2.6 1.4 %collective-permute-start = (bf16[2,144,128]{2,1,0:T(8,128)(2,1)}, bf16[2,144,128]{2,1,0:T(8,128)(2,1)S(1)}, u32[]{:S(2)}, u32[]{:S(2)}) collective-permute-start(bf16[2,144,128]{2,1,0:T(8,128)(2,1)} %get-tuple-element.88), channel_id=1, source_target_pairs={{0,1},{2,3},{1,0},{3,2},{4,5},{6,7},{5,4},{7,6},{8,9},{10,11},{9,8... | collective-permute-start | bytes 221192 | tf_op jit(solution)/shard_map/ppermute | solution.py:124
  3.9 0.1 collective-permute-start.1
  4.0 1.3 %collective-permute-start.2 = (bf16[2,144,128]{2,1,0:T(8,128)(2,1)}, bf16[2,144,128]{2,1,0:T(8,128)(2,1)S(1)}, u32[]{:S(2)}, u32[]{:S(2)}) collective-permute-start(bf16[2,144,128]{2,1,0:T(8,128)(2,1)} %get-tuple-element.90), channel_id=1, source_target_pairs={{0,3},{1,2},{3,0},{2,1},{4,7},{5,6},{7,4},{6,5},{8,11},{9,10},{11,... | collective-permute-start | bytes 221192 | tf_op jit(solution)/shard_map/ppermute | solution.py:124
  5.3 2.1 %pack.5 = (bf16[2,288,128]{2,1,0:T(8,128)(2,1)}, bf16[2,288,128]{2,1,0:T(8,128)(2,1)}, bf16[2,288,128]{2,1,0:T(8,128)(2,1)}, bf16[2,288,128]{2,1,0:T(8,128)(2,1)}) custom-call(bf16[1,576,256]{2,1,0:T(8,128)(2,1)} %bitcast.19, bf16[1,576,256]{2,1,0:T(8,128)(2,1)} %bitcast.22, bf16[1,576,256]{2,1,0:T(8,128)(2,1)} %bitcast.25, bf16[1,576,256]{2,1,0:T(8,128)(2,1)} %bitcast.28), custom_call_target="tpu_custom_call" | custom-call | tf_op jit(solution)/shard_map/pack/pallas_call | solution.py:107
  7.4 2.3 %collective-permute-start.5 = (bf16[2,288,128]{2,1,0:T(8,128)(2,1)}, bf16[2,288,128]{2,1,0:T(8,128)(2,1)S(1)}, u32[]{:S(2)}, u32[]{:S(2)}) collective-permute-start(bf16[2,288,128]{2,1,0:T(8,128)(2,1)} %get-tuple-element.102), channel_id=1, source_target_pairs={{0,1},{2,3},{1,0},{3,2},{4,5},{6,7},{5,4},{7,6},{8,9},{10,11},{9,8... | collective-permute-start | bytes 442376 | tf_op jit(solution)/shard_map/ppermute | solution.py:124
  9.7 0.0 collective-permute-start.6
  9.7 2.0 %pack.3 = (bf16[2,144,128]{2,1,0:T(8,128)(2,1)}, bf16[2,144,128]{2,1,0:T(8,128)(2,1)}, bf16[2,144,128]{2,1,0:T(8,128)(2,1)}, bf16[2,144,128]{2,1,0:T(8,128)(2,1)}) custom-call(bf16[1,576,256]{2,1,0:T(8,128)(2,1)} %bitcast.20, bf16[1,576,256]{2,1,0:T(8,128)(2,1)} %bitcast.23, bf16[1,576,256]{2,1,0:T(8,128)(2,1)} %bitcast.26, bf16[1,576,256]{2,1,0:T(8,128)(2,1)} %bitcast.29), custom_call_target="tpu_custom_call" | custom-call | tf_op jit(solution)/shard_map/pack/pallas_call | solution.py:107
  11.7 0.0 collective-permute-done.refs_1_
  11.7 1.3 %collective-permute-start.7 = (bf16[2,288,128]{2,1,0:T(8,128)(2,1)S(1)}, bf16[2,288,128]{2,1,0:T(8,128)(2,1)S(1)}, u32[]{:S(2)}, u32[]{:S(2)}) collective-permute-start(bf16[2,288,128]{2,1,0:T(8,128)(2,1)S(1)} %copy-done.3), channel_id=1, source_target_pairs={{0,3},{1,2},{3,0},{2,1},{4,7},{5,6},{7,4},{6,5},{8,11},{9,10},{11,... | collective-permute-start | bytes 442376 | tf_op jit(solution)/shard_map/ppermute | solution.py:124
  13.0 0.0 collective-permute-done.1.refs_2_
  13.0 0.0 collective-permute-done.2.refs_3_
  13.0 0.1 sides.3
  13.1 0.0 copy-start.7
  13.1 2.1 %collective-permute-start.3 = (bf16[3,2,144,128]{3,2,1,0:T(8,128)(2,1)S(1)}, bf16[3,2,144,128]{3,2,1,0:T(8,128)(2,1)S(1)}, u32[]{:S(2)}, u32[]{:S(2)}) collective-permute-start(bf16[3,2,144,128]{3,2,1,0:T(8,128)(2,1)S(1)} %get-tuple-element.100), channel_id=1, source_target_pairs={{0,4},{8,12},{16,20},{24,28},{4,0},{12,8},{20,16},{28,24},{1,5},{9... | collective-permute-start | bytes 663560 | tf_op jit(solution)/shard_map/ppermute | solution.py:124
  15.3 3.0 %collective-permute-start.4 = (bf16[3,2,144,128]{3,2,1,0:T(8,128)(2,1)S(1)}, bf16[3,2,144,128]{3,2,1,0:T(8,128)(2,1)S(1)}, u32[]{:S(2)}, u32[]{:S(2)}) collective-permute-start(bf16[3,2,144,128]{3,2,1,0:T(8,128)(2,1)S(1)} %get-tuple-element.101), channel_id=1, source_target_pairs={{4,8},{12,16},{20,24},{8,4},{16,12},{24,20},{5,9},{13,17},{21,25},... | collective-permute-start | bytes 663560 | tf_op jit(solution)/shard_map/ppermute | solution.py:124
  18.3 0.1 select_reduce_fusion.2
  18.4 0.0 copy-start
  18.4 5.6 %space.1 = (bf16[1,576,256]{2,1,0:T(8,128)(2,1)}, bf16[1,576,256]{2,1,0:T(8,128)(2,1)}, bf16[1,576,256]{2,1,0:T(8,128)(2,1)}) custom-call(bf16[1,576,256]{2,1,0:T(8,128)(2,1)} %bitcast.33, bf16[1,576,256]{2,1,0:T(8,128)(2,1)} %bitcast.34, bf16[1,576,256]{2,1,0:T(8,128)(2,1)} %bitcast.35, bf16[1,576,256]{2,1,0:T(8,128)(2,1)} %bitcast.36), custom_call_target="tpu_custom_call" | custom-call | flops 1610612736 | bytes 2064384 | tf_op jit(solution)/shard_map/space/pallas_call | solution.py:64
  24.0 0.0 collective-permute-done.5.refs_1_
  24.0 0.0 collective-permute-done.3.refs_4_
  24.0 1.2 %collective-permute-done.4.refs_5_ = bf16[3,2,144,128]{3,2,1,0:T(8,128)(2,1)S(1)} collective-permute-done((bf16[3,2,144,128]{3,2,1,0:T(8,128)(2,1)S(1)}, bf16[3,2,144,128]{3,2,1,0:T(8,128)(2,1)S(1)}, u32[]{:S(2)}, u32[]{:S(2)}) %collective-permute-start.4) | collective-permute-done | bytes 221216 | tf_op jit(solution)/shard_map/ppermute | solution.py:124
  25.2 2.5 %collective-permute-start.8 = (bf16[2,144,128]{2,1,0:T(8,128)(2,1)S(1)}, bf16[2,144,128]{2,1,0:T(8,128)(2,1)S(1)}, u32[]{:S(2)}, u32[]{:S(2)}) collective-permute-start(bf16[2,144,128]{2,1,0:T(8,128)(2,1)S(1)} %copy-done.6), channel_id=1, source_target_pairs={{0,1},{2,3},{1,0},{3,2},{4,5},{6,7},{5,4},{7,6},{8,9},{10,11},{9,8... | collective-permute-start | bytes 221192 | tf_op jit(solution)/shard_map/ppermute | solution.py:124
  27.7 0.0 collective-permute-done.6.refs_2_
  27.7 0.0 collective-permute-done.7.refs_3_
  27.7 1.7 %collective-permute-done.8.refs_1_ = bf16[2,144,128]{2,1,0:T(8,128)(2,1)S(1)} collective-permute-done((bf16[2,144,128]{2,1,0:T(8,128)(2,1)S(1)}, bf16[2,144,128]{2,1,0:T(8,128)(2,1)S(1)}, u32[]{:S(2)}, u32[]{:S(2)}) %collective-permute-start.8) | collective-permute-done | bytes 73760 | tf_op jit(solution)/shard_map/ppermute | solution.py:124
  29.5 0.1 sides.5
  29.6 0.1 collective-permute-start.11
  29.7 4.2 %collective-permute-start.12 = (bf16[3,2,288,128]{3,2,1,0:T(8,128)(2,1)S(1)}, bf16[3,2,288,128]{3,2,1,0:T(8,128)(2,1)S(1)}, u32[]{:S(2)}, u32[]{:S(2)}) collective-permute-start(bf16[3,2,288,128]{3,2,1,0:T(8,128)(2,1)S(1)} %get-tuple-element.126), channel_id=1, source_target_pairs={{4,8},{12,16},{20,24},{8,4},{16,12},{24,20},{5,9},{13,17},{21,25},... | collective-permute-start | bytes 1327112 | tf_op jit(solution)/shard_map/ppermute | solution.py:124
  33.9 0.2 select_reduce_fusion.1
  34.1 0.1 collective-permute-start.10
  34.2 3.8 %collective-permute-start.9 = (bf16[2,144,128]{2,1,0:T(8,128)(2,1)S(1)}, bf16[2,144,128]{2,1,0:T(8,128)(2,1)S(1)}, u32[]{:S(2)}, u32[]{:S(2)}) collective-permute-start(bf16[2,144,128]{2,1,0:T(8,128)(2,1)S(1)} %copy-done.4), channel_id=1, source_target_pairs={{0,2},{1,3},{2,0},{3,1},{4,6},{5,7},{6,4},{7,5},{8,10},{9,11},{10,... | collective-permute-start | bytes 221192 | tf_op jit(solution)/shard_map/ppermute | solution.py:124
  38.0 1.7 %clips.3 = (bf16[216,128]{1,0:T(8,128)(2,1)S(1)}, bf16[216,128]{1,0:T(8,128)(2,1)S(1)}, bf16[216,128]{1,0:T(8,128)(2,1)S(1)}, bf16[216,128]{1,0:T(8,128)(2,1)S(1)}) custom-call(s32[2,10]{1,0:T(2,128)S(1)} %pad_add_fusion.bounds, bf16[2,144,128]{2,1,0:T(8,128)(2,1)S(1)} %copy-done.2, bf16[2,144,128]{2,1,0:T(8,128)(2,1)S(1)} %collective-permute-done.refs_1_, ...), custom_call_target="tpu_custom_call" | custom-call | flops 294912000 | bytes 737280 | tf_op jit(solution)/shard_map/clips/pallas_call | solution.py:321
  39.7 0.1 collective-permute-start.13
  39.8 1.5 %collective-permute-done.10.refs_3_ = bf16[2,144,128]{2,1,0:T(8,128)(2,1)S(1)} collective-permute-done((bf16[2,144,128]{2,1,0:T(8,128)(2,1)S(1)}, bf16[2,144,128]{2,1,0:T(8,128)(2,1)S(1)}, u32[]{:S(2)}, u32[]{:S(2)}) %collective-permute-start.10) | collective-permute-done | bytes 73760 | tf_op jit(solution)/shard_map/ppermute | solution.py:124
  41.3 0.0 collective-permute-done.9.refs_2_
  41.3 0.1 sides.4
  41.4 1.4 %collective-permute-done.13.refs_1_ = bf16[216,128]{1,0:T(8,128)(2,1)S(1)} collective-permute-done((bf16[216,128]{1,0:T(8,128)(2,1)S(1)}, bf16[216,128]{1,0:T(8,128)(2,1)S(1)}, u32[]{:S(2)}, u32[]{:S(2)}) %collective-permute-start.13) | collective-permute-done | bytes 55328 | tf_op jit(solution)/shard_map/ppermute | solution.py:124
  42.8 0.0 collective-permute-done.11.refs_4_
  42.8 1.6 %collective-permute-done.12.refs_5_ = bf16[3,2,288,128]{3,2,1,0:T(8,128)(2,1)S(1)} collective-permute-done((bf16[3,2,288,128]{3,2,1,0:T(8,128)(2,1)S(1)}, bf16[3,2,288,128]{3,2,1,0:T(8,128)(2,1)S(1)}, u32[]{:S(2)}, u32[]{:S(2)}) %collective-permute-start.12) | collective-permute-done | bytes 442400 | tf_op jit(solution)/shard_map/ppermute | solution.py:124
  44.4 0.0 collective-permute-start.14
  44.4 3.1 %collective-permute-start.15 = (bf16[3,2,144,128]{3,2,1,0:T(8,128)(2,1)S(1)}, bf16[3,2,144,128]{3,2,1,0:T(8,128)(2,1)S(1)}, u32[]{:S(2)}, u32[]{:S(2)}) collective-permute-start(bf16[3,2,144,128]{3,2,1,0:T(8,128)(2,1)S(1)} %get-tuple-element.131), channel_id=1, source_target_pairs={{4,8},{12,16},{20,24},{8,4},{16,12},{24,20},{5,9},{13,17},{21,25},... | collective-permute-start | bytes 663560 | tf_op jit(solution)/shard_map/ppermute | solution.py:124
  47.5 0.3 collective-permute-start.16
  47.8 2.4 %collective-permute-start.17 = (bf16[216,128]{1,0:T(8,128)(2,1)S(1)}, bf16[216,128]{1,0:T(8,128)(2,1)S(1)}, u32[]{:S(2)}, u32[]{:S(2)}) collective-permute-start(bf16[216,128]{1,0:T(8,128)(2,1)S(1)} %get-tuple-element.135), channel_id=1, source_target_pairs={{0,3},{1,2},{3,0},{2,1},{4,7},{5,6},{7,4},{6,5},{8,11},{9,10},{11,... | collective-permute-start | bytes 165896 | tf_op jit(solution)/shard_map/ppermute | solution.py:124
  50.2 2.1 %clips.5 = (bf16[432,128]{1,0:T(8,128)(2,1)S(1)}, bf16[432,128]{1,0:T(8,128)(2,1)S(1)}, bf16[432,128]{1,0:T(8,128)(2,1)S(1)}, bf16[432,128]{1,0:T(8,128)(2,1)S(1)}) custom-call(s32[2,10]{1,0:T(2,128)S(1)} %pad_add_fusion.bounds, bf16[2,288,128]{2,1,0:T(8,128)(2,1)S(1)} %copy-done, bf16[2,288,128]{2,1,0:T(8,128)(2,1)S(1)} %collective-permute-done.5.refs_1_, ...), custom_call_target="tpu_custom_call" | custom-call | flops 589824000 | bytes 1474560 | tf_op jit(solution)/shard_map/clips/pallas_call | solution.py:321
  52.4 1.0 %collective-permute-start.21 = (bf16[432,128]{1,0:T(8,128)(2,1)S(1)}, bf16[432,128]{1,0:T(8,128)(2,1)S(1)}, u32[]{:S(2)}, u32[]{:S(2)}) collective-permute-start(bf16[432,128]{1,0:T(8,128)(2,1)S(1)} %get-tuple-element.148), channel_id=1, source_target_pairs={{0,1},{2,3},{1,0},{3,2},{4,5},{6,7},{5,4},{7,6},{8,9},{10,11},{9,8... | collective-permute-start | bytes 331784 | tf_op jit(solution)/shard_map/ppermute | solution.py:124
  53.4 0.0 collective-permute-done.16.refs_2_
  53.4 0.4 collective-permute-start.22
  53.8 1.9 %collective-permute-done.17.refs_3_ = bf16[216,128]{1,0:T(8,128)(2,1)S(1)} collective-permute-done((bf16[216,128]{1,0:T(8,128)(2,1)S(1)}, bf16[216,128]{1,0:T(8,128)(2,1)S(1)}, u32[]{:S(2)}, u32[]{:S(2)}) %collective-permute-start.17) | collective-permute-done | bytes 55328 | tf_op jit(solution)/shard_map/ppermute | solution.py:124
  55.7 1.2 %collective-permute-start.23 = (bf16[432,128]{1,0:T(8,128)(2,1)S(1)}, bf16[432,128]{1,0:T(8,128)(2,1)S(1)}, u32[]{:S(2)}, u32[]{:S(2)}) collective-permute-start(bf16[432,128]{1,0:T(8,128)(2,1)S(1)} %get-tuple-element.150), channel_id=1, source_target_pairs={{0,3},{1,2},{3,0},{2,1},{4,7},{5,6},{7,4},{6,5},{8,11},{9,10},{11,... | collective-permute-start | bytes 331784 | tf_op jit(solution)/shard_map/ppermute | solution.py:124
  56.9 0.9 %unpack.3 = (bf16[1,576,256]{2,1,0:T(8,128)(2,1)}, bf16[1,576,256]{2,1,0:T(8,128)(2,1)}, bf16[1,576,256]{2,1,0:T(8,128)(2,1)}) custom-call(bf16[216,128]{1,0:T(8,128)(2,1)S(1)} %get-tuple-element.132.refs_0_, bf16[216,128]{1,0:T(8,128)(2,1)S(1)} %collective-permute-done.13.refs_1_, bf16[216,128]{1,0:T(8,128)(2,1)S(1)} %collective-permute-done.16.refs_2_, ...), custom_call_target="tpu_custom_call" | custom-call | tf_op jit(solution)/shard_map/unpack/pallas_call | solution.py:205
  57.8 0.0 collective-permute-done.14.refs_4_
  57.8 0.0 collective-permute-done.15.refs_5_
  57.8 1.7 %clips.4 = (bf16[216,128]{1,0:T(8,128)(2,1)S(1)}, bf16[216,128]{1,0:T(8,128)(2,1)S(1)}, bf16[216,128]{1,0:T(8,128)(2,1)S(1)}, bf16[216,128]{1,0:T(8,128)(2,1)S(1)}) custom-call(s32[2,10]{1,0:T(2,128)S(1)} %pad_add_fusion.bounds, bf16[2,144,128]{2,1,0:T(8,128)(2,1)S(1)} %copy-done.1, bf16[2,144,128]{2,1,0:T(8,128)(2,1)S(1)} %collective-permute-done.8.refs_1_, ...), custom_call_target="tpu_custom_call" | custom-call | flops 294912000 | bytes 737280 | tf_op jit(solution)/shard_map/clips/pallas_call | solution.py:321
  59.5 0.1 collective-permute-start.18
  59.6 1.4 %collective-permute-start.19 = (bf16[216,128]{1,0:T(8,128)(2,1)S(1)}, bf16[216,128]{1,0:T(8,128)(2,1)S(1)}, u32[]{:S(2)}, u32[]{:S(2)}) collective-permute-start(bf16[216,128]{1,0:T(8,128)(2,1)S(1)} %get-tuple-element.143), channel_id=1, source_target_pairs={{0,2},{1,3},{2,0},{3,1},{4,6},{5,7},{6,4},{7,5},{8,10},{9,11},{10,... | collective-permute-start | bytes 165896 | tf_op jit(solution)/shard_map/ppermute | solution.py:124
  61.0 0.0 collective-permute-done.21.refs_1_
  61.0 1.2 %collective-permute-start.20 = (bf16[216,128]{1,0:T(8,128)(2,1)S(1)}, bf16[216,128]{1,0:T(8,128)(2,1)S(1)}, u32[]{:S(2)}, u32[]{:S(2)}) collective-permute-start(bf16[216,128]{1,0:T(8,128)(2,1)S(1)} %get-tuple-element.144), channel_id=1, source_target_pairs={{0,3},{1,2},{3,0},{2,1},{4,7},{5,6},{7,4},{6,5},{8,11},{9,10},{11,... | collective-permute-start | bytes 165896 | tf_op jit(solution)/shard_map/ppermute | solution.py:124
  62.2 0.0 collective-permute-done.22.refs_2_
  62.2 6.8 %collective-permute-done.23.refs_3_ = bf16[432,128]{1,0:T(8,128)(2,1)S(1)} collective-permute-done((bf16[432,128]{1,0:T(8,128)(2,1)S(1)}, bf16[432,128]{1,0:T(8,128)(2,1)S(1)}, u32[]{:S(2)}, u32[]{:S(2)}) %collective-permute-start.23) | collective-permute-done | bytes 110624 | tf_op jit(solution)/shard_map/ppermute | solution.py:124
  69.1 1.0 %unpack.4 = (bf16[1,576,256]{2,1,0:T(8,128)(2,1)}, bf16[1,576,256]{2,1,0:T(8,128)(2,1)}, bf16[1,576,256]{2,1,0:T(8,128)(2,1)}) custom-call(bf16[432,128]{1,0:T(8,128)(2,1)S(1)} %get-tuple-element.147.refs_0_, bf16[432,128]{1,0:T(8,128)(2,1)S(1)} %collective-permute-done.21.refs_1_, ...), custom_call_target="tpu_custom_call", output_to_operand_aliasing={{0}: (4, {}), {1}: (5, {}), {2}: (6, {})} | custom-call | tf_op jit(solution)/shard_map/unpack/pallas_call | solution.py:205
  70.1 0.0 collective-permute-done.18.refs_1_
  70.1 1.3 %collective-permute-done.20.refs_3_ = bf16[216,128]{1,0:T(8,128)(2,1)S(1)} collective-permute-done((bf16[216,128]{1,0:T(8,128)(2,1)S(1)}, bf16[216,128]{1,0:T(8,128)(2,1)S(1)}, u32[]{:S(2)}, u32[]{:S(2)}) %collective-permute-start.20) | collective-permute-done | bytes 55328 | tf_op jit(solution)/shard_map/ppermute | solution.py:124
  71.4 0.9 %unpack.5 = (bf16[1,576,256]{2,1,0:T(8,128)(2,1)}, bf16[1,576,256]{2,1,0:T(8,128)(2,1)}, bf16[1,576,256]{2,1,0:T(8,128)(2,1)}) custom-call(bf16[216,128]{1,0:T(8,128)(2,1)S(1)} %get-tuple-element.141.refs_0_, bf16[216,128]{1,0:T(8,128)(2,1)S(1)} %collective-permute-done.18.refs_1_, ...), custom_call_target="tpu_custom_call", output_to_operand_aliasing={{0}: (4, {}), {1}: (5, {}), {2}: (6, {})} | custom-call | tf_op jit(solution)/shard_map/unpack/pallas_call | solution.py:205
  (19 shorter events, 0.1 us)
Async XLA Ops:
  2.6 9.1 %collective-permute-start = (bf16[2,144,128]{2,1,0:T(8,128)(2,1)}, bf16[2,144,128]{2,1,0:T(8,128)(2,1)S(1)}, u32[]{:S(2)}, u32[]{:S(2)}) collective-permute-start(bf16[2,144,128]{2,1,0:T(8,128)(2,1)} %get-tuple-element.88), channel_id=1, source_target_pairs={{0,1},{2,3},{1,0},{3,2},{4,5},{6,7},{5,4},{7,6},{8,9},{10,11},{9,8... | collective-permute-start | bytes 221192 | tf_op jit(solution)/shard_map/ppermute | solution.py:124
  3.9 9.1 %collective-permute-start.1 = (bf16[2,144,128]{2,1,0:T(8,128)(2,1)}, bf16[2,144,128]{2,1,0:T(8,128)(2,1)S(1)}, u32[]{:S(2)}, u32[]{:S(2)}) collective-permute-start(bf16[2,144,128]{2,1,0:T(8,128)(2,1)} %get-tuple-element.89), channel_id=1, source_target_pairs={{0,2},{1,3},{2,0},{3,1},{4,6},{5,7},{6,4},{7,5},{8,10},{9,11},{10,... | collective-permute-start | bytes 221192 | tf_op jit(solution)/shard_map/ppermute | solution.py:124
  4.0 9.0 %collective-permute-start.2 = (bf16[2,144,128]{2,1,0:T(8,128)(2,1)}, bf16[2,144,128]{2,1,0:T(8,128)(2,1)S(1)}, u32[]{:S(2)}, u32[]{:S(2)}) collective-permute-start(bf16[2,144,128]{2,1,0:T(8,128)(2,1)} %get-tuple-element.90), channel_id=1, source_target_pairs={{0,3},{1,2},{3,0},{2,1},{4,7},{5,6},{7,4},{6,5},{8,11},{9,10},{11,... | collective-permute-start | bytes 221192 | tf_op jit(solution)/shard_map/ppermute | solution.py:124
  7.4 16.6 %collective-permute-start.5 = (bf16[2,288,128]{2,1,0:T(8,128)(2,1)}, bf16[2,288,128]{2,1,0:T(8,128)(2,1)S(1)}, u32[]{:S(2)}, u32[]{:S(2)}) collective-permute-start(bf16[2,288,128]{2,1,0:T(8,128)(2,1)} %get-tuple-element.102), channel_id=1, source_target_pairs={{0,1},{2,3},{1,0},{3,2},{4,5},{6,7},{5,4},{7,6},{8,9},{10,11},{9,8... | collective-permute-start | bytes 442376 | tf_op jit(solution)/shard_map/ppermute | solution.py:124
  9.7 2.0 %copy-start.3 = (bf16[2,288,128]{2,1,0:T(8,128)(2,1)S(1)}, bf16[2,288,128]{2,1,0:T(8,128)(2,1)}, u32[]{:S(2)}) copy-start(bf16[2,288,128]{2,1,0:T(8,128)(2,1)} %get-tuple-element.110) | copy-start | bytes 442372
  9.7 3.3 %copy-start.2 = (bf16[2,144,128]{2,1,0:T(8,128)(2,1)S(1)}, bf16[2,144,128]{2,1,0:T(8,128)(2,1)}, u32[]{:S(2)}) copy-start(bf16[2,144,128]{2,1,0:T(8,128)(2,1)} %get-tuple-element.87.refs_0_) | copy-start | bytes 221188
  9.7 18.0 %collective-permute-start.6 = (bf16[2,288,128]{2,1,0:T(8,128)(2,1)}, bf16[2,288,128]{2,1,0:T(8,128)(2,1)S(1)}, u32[]{:S(2)}, u32[]{:S(2)}) collective-permute-start(bf16[2,288,128]{2,1,0:T(8,128)(2,1)} %get-tuple-element.109), channel_id=1, source_target_pairs={{0,2},{1,3},{2,0},{3,1},{4,6},{5,7},{6,4},{7,5},{8,10},{9,11},{10,... | collective-permute-start | bytes 442376 | tf_op jit(solution)/shard_map/ppermute | solution.py:124
  11.7 16.0 %collective-permute-start.7 = (bf16[2,288,128]{2,1,0:T(8,128)(2,1)S(1)}, bf16[2,288,128]{2,1,0:T(8,128)(2,1)S(1)}, u32[]{:S(2)}, u32[]{:S(2)}) collective-permute-start(bf16[2,288,128]{2,1,0:T(8,128)(2,1)S(1)} %copy-done.3), channel_id=1, source_target_pairs={{0,3},{1,2},{3,0},{2,1},{4,7},{5,6},{7,4},{6,5},{8,11},{9,10},{11,... | collective-permute-start | bytes 442376 | tf_op jit(solution)/shard_map/ppermute | solution.py:124
  13.1 5.2 %copy-start.7 = (s32[16]{0:T(128)S(1)}, s32[16]{0:T(128)}, u32[]{:S(2)}) copy-start(s32[16]{0:T(128)} %param.17) | copy-start | bytes 196
  13.1 10.9 %collective-permute-start.3 = (bf16[3,2,144,128]{3,2,1,0:T(8,128)(2,1)S(1)}, bf16[3,2,144,128]{3,2,1,0:T(8,128)(2,1)S(1)}, u32[]{:S(2)}, u32[]{:S(2)}) collective-permute-start(bf16[3,2,144,128]{3,2,1,0:T(8,128)(2,1)S(1)} %get-tuple-element.100), channel_id=1, source_target_pairs={{0,4},{8,12},{16,20},{24,28},{4,0},{12,8},{20,16},{28,24},{1,5},{9... | collective-permute-start | bytes 663560 | tf_op jit(solution)/shard_map/ppermute | solution.py:124
  15.3 9.9 %collective-permute-start.4 = (bf16[3,2,144,128]{3,2,1,0:T(8,128)(2,1)S(1)}, bf16[3,2,144,128]{3,2,1,0:T(8,128)(2,1)S(1)}, u32[]{:S(2)}, u32[]{:S(2)}) collective-permute-start(bf16[3,2,144,128]{3,2,1,0:T(8,128)(2,1)S(1)} %get-tuple-element.101), channel_id=1, source_target_pairs={{4,8},{12,16},{20,24},{8,4},{16,12},{24,20},{5,9},{13,17},{21,25},... | collective-permute-start | bytes 663560 | tf_op jit(solution)/shard_map/ppermute | solution.py:124
  18.4 6.8 %copy-start.6 = (bf16[2,144,128]{2,1,0:T(8,128)(2,1)S(1)}, bf16[2,144,128]{2,1,0:T(8,128)(2,1)}, u32[]{:S(2)}) copy-start(bf16[2,144,128]{2,1,0:T(8,128)(2,1)} %get-tuple-element.111) | copy-start | bytes 221188
  18.4 11.1 %copy-start = (bf16[2,288,128]{2,1,0:T(8,128)(2,1)S(1)}, bf16[2,288,128]{2,1,0:T(8,128)(2,1)}, u32[]{:S(2)}) copy-start(bf16[2,288,128]{2,1,0:T(8,128)(2,1)} %get-tuple-element.117.refs_0_) | copy-start | bytes 442372
  25.2 4.3 %collective-permute-start.8 = (bf16[2,144,128]{2,1,0:T(8,128)(2,1)S(1)}, bf16[2,144,128]{2,1,0:T(8,128)(2,1)S(1)}, u32[]{:S(2)}, u32[]{:S(2)}) collective-permute-start(bf16[2,144,128]{2,1,0:T(8,128)(2,1)S(1)} %copy-done.6), channel_id=1, source_target_pairs={{0,1},{2,3},{1,0},{3,2},{4,5},{6,7},{5,4},{7,6},{8,9},{10,11},{9,8... | collective-permute-start | bytes 221192 | tf_op jit(solution)/shard_map/ppermute | solution.py:124
  29.5 4.6 %copy-start.5 = (bf16[2,144,128]{2,1,0:T(8,128)(2,1)S(1)}, bf16[2,144,128]{2,1,0:T(8,128)(2,1)}, u32[]{:S(2)}) copy-start(bf16[2,144,128]{2,1,0:T(8,128)(2,1)} %get-tuple-element.114) | copy-start | bytes 221188
  29.5 4.7 %copy-start.4 = (bf16[2,144,128]{2,1,0:T(8,128)(2,1)S(1)}, bf16[2,144,128]{2,1,0:T(8,128)(2,1)}, u32[]{:S(2)}) copy-start(bf16[2,144,128]{2,1,0:T(8,128)(2,1)} %get-tuple-element.113) | copy-start | bytes 221188
  29.6 13.2 %collective-permute-start.11 = (bf16[3,2,288,128]{3,2,1,0:T(8,128)(2,1)S(1)}, bf16[3,2,288,128]{3,2,1,0:T(8,128)(2,1)S(1)}, u32[]{:S(2)}, u32[]{:S(2)}) collective-permute-start(bf16[3,2,288,128]{3,2,1,0:T(8,128)(2,1)S(1)} %get-tuple-element.125), channel_id=1, source_target_pairs={{0,4},{8,12},{16,20},{24,28},{4,0},{12,8},{20,16},{28,24},{1,5},{9... | collective-permute-start | bytes 1327112 | tf_op jit(solution)/shard_map/ppermute | solution.py:124
  29.7 14.7 %collective-permute-start.12 = (bf16[3,2,288,128]{3,2,1,0:T(8,128)(2,1)S(1)}, bf16[3,2,288,128]{3,2,1,0:T(8,128)(2,1)S(1)}, u32[]{:S(2)}, u32[]{:S(2)}) collective-permute-start(bf16[3,2,288,128]{3,2,1,0:T(8,128)(2,1)S(1)} %get-tuple-element.126), channel_id=1, source_target_pairs={{4,8},{12,16},{20,24},{8,4},{16,12},{24,20},{5,9},{13,17},{21,25},... | collective-permute-start | bytes 1327112 | tf_op jit(solution)/shard_map/ppermute | solution.py:124
  34.1 7.2 %copy-start.1 = (bf16[2,144,128]{2,1,0:T(8,128)(2,1)S(1)}, bf16[2,144,128]{2,1,0:T(8,128)(2,1)}, u32[]{:S(2)}) copy-start(bf16[2,144,128]{2,1,0:T(8,128)(2,1)} %get-tuple-element.106.refs_0_) | copy-start | bytes 221188
  34.1 7.2 %collective-permute-start.10 = (bf16[2,144,128]{2,1,0:T(8,128)(2,1)S(1)}, bf16[2,144,128]{2,1,0:T(8,128)(2,1)S(1)}, u32[]{:S(2)}, u32[]{:S(2)}) collective-permute-start(bf16[2,144,128]{2,1,0:T(8,128)(2,1)S(1)} %copy-done.5), channel_id=1, source_target_pairs={{0,3},{1,2},{3,0},{2,1},{4,7},{5,6},{7,4},{6,5},{8,11},{9,10},{11,... | collective-permute-start | bytes 221192 | tf_op jit(solution)/shard_map/ppermute | solution.py:124
  34.2 7.1 %collective-permute-start.9 = (bf16[2,144,128]{2,1,0:T(8,128)(2,1)S(1)}, bf16[2,144,128]{2,1,0:T(8,128)(2,1)S(1)}, u32[]{:S(2)}, u32[]{:S(2)}) collective-permute-start(bf16[2,144,128]{2,1,0:T(8,128)(2,1)S(1)} %copy-done.4), channel_id=1, source_target_pairs={{0,2},{1,3},{2,0},{3,1},{4,6},{5,7},{6,4},{7,5},{8,10},{9,11},{10,... | collective-permute-start | bytes 221192 | tf_op jit(solution)/shard_map/ppermute | solution.py:124
  39.7 3.1 %collective-permute-start.13 = (bf16[216,128]{1,0:T(8,128)(2,1)S(1)}, bf16[216,128]{1,0:T(8,128)(2,1)S(1)}, u32[]{:S(2)}, u32[]{:S(2)}) collective-permute-start(bf16[216,128]{1,0:T(8,128)(2,1)S(1)} %get-tuple-element.129), channel_id=1, source_target_pairs={{0,1},{2,3},{1,0},{3,2},{4,5},{6,7},{5,4},{7,6},{8,9},{10,11},{9,8... | collective-permute-start | bytes 165896 | tf_op jit(solution)/shard_map/ppermute | solution.py:124
  44.4 13.3 %collective-permute-start.14 = (bf16[3,2,144,128]{3,2,1,0:T(8,128)(2,1)S(1)}, bf16[3,2,144,128]{3,2,1,0:T(8,128)(2,1)S(1)}, u32[]{:S(2)}, u32[]{:S(2)}) collective-permute-start(bf16[3,2,144,128]{3,2,1,0:T(8,128)(2,1)S(1)} %get-tuple-element.130), channel_id=1, source_target_pairs={{0,4},{8,12},{16,20},{24,28},{4,0},{12,8},{20,16},{28,24},{1,5},{9... | collective-permute-start | bytes 663560 | tf_op jit(solution)/shard_map/ppermute | solution.py:124
  44.4 13.4 %collective-permute-start.15 = (bf16[3,2,144,128]{3,2,1,0:T(8,128)(2,1)S(1)}, bf16[3,2,144,128]{3,2,1,0:T(8,128)(2,1)S(1)}, u32[]{:S(2)}, u32[]{:S(2)}) collective-permute-start(bf16[3,2,144,128]{3,2,1,0:T(8,128)(2,1)S(1)} %get-tuple-element.131), channel_id=1, source_target_pairs={{4,8},{12,16},{20,24},{8,4},{16,12},{24,20},{5,9},{13,17},{21,25},... | collective-permute-start | bytes 663560 | tf_op jit(solution)/shard_map/ppermute | solution.py:124
  47.5 5.8 %collective-permute-start.16 = (bf16[216,128]{1,0:T(8,128)(2,1)S(1)}, bf16[216,128]{1,0:T(8,128)(2,1)S(1)}, u32[]{:S(2)}, u32[]{:S(2)}) collective-permute-start(bf16[216,128]{1,0:T(8,128)(2,1)S(1)} %get-tuple-element.134), channel_id=1, source_target_pairs={{0,2},{1,3},{2,0},{3,1},{4,6},{5,7},{6,4},{7,5},{8,10},{9,11},{10,... | collective-permute-start | bytes 165896 | tf_op jit(solution)/shard_map/ppermute | solution.py:124
  47.8 7.9 %collective-permute-start.17 = (bf16[216,128]{1,0:T(8,128)(2,1)S(1)}, bf16[216,128]{1,0:T(8,128)(2,1)S(1)}, u32[]{:S(2)}, u32[]{:S(2)}) collective-permute-start(bf16[216,128]{1,0:T(8,128)(2,1)S(1)} %get-tuple-element.135), channel_id=1, source_target_pairs={{0,3},{1,2},{3,0},{2,1},{4,7},{5,6},{7,4},{6,5},{8,11},{9,10},{11,... | collective-permute-start | bytes 165896 | tf_op jit(solution)/shard_map/ppermute | solution.py:124
  52.4 8.6 %collective-permute-start.21 = (bf16[432,128]{1,0:T(8,128)(2,1)S(1)}, bf16[432,128]{1,0:T(8,128)(2,1)S(1)}, u32[]{:S(2)}, u32[]{:S(2)}) collective-permute-start(bf16[432,128]{1,0:T(8,128)(2,1)S(1)} %get-tuple-element.148), channel_id=1, source_target_pairs={{0,1},{2,3},{1,0},{3,2},{4,5},{6,7},{5,4},{7,6},{8,9},{10,11},{9,8... | collective-permute-start | bytes 331784 | tf_op jit(solution)/shard_map/ppermute | solution.py:124
  53.4 8.8 %collective-permute-start.22 = (bf16[432,128]{1,0:T(8,128)(2,1)S(1)}, bf16[432,128]{1,0:T(8,128)(2,1)S(1)}, u32[]{:S(2)}, u32[]{:S(2)}) collective-permute-start(bf16[432,128]{1,0:T(8,128)(2,1)S(1)} %get-tuple-element.149), channel_id=1, source_target_pairs={{0,2},{1,3},{2,0},{3,1},{4,6},{5,7},{6,4},{7,5},{8,10},{9,11},{10,... | collective-permute-start | bytes 331784 | tf_op jit(solution)/shard_map/ppermute | solution.py:124
  55.7 13.3 %collective-permute-start.23 = (bf16[432,128]{1,0:T(8,128)(2,1)S(1)}, bf16[432,128]{1,0:T(8,128)(2,1)S(1)}, u32[]{:S(2)}, u32[]{:S(2)}) collective-permute-start(bf16[432,128]{1,0:T(8,128)(2,1)S(1)} %get-tuple-element.150), channel_id=1, source_target_pairs={{0,3},{1,2},{3,0},{2,1},{4,7},{5,6},{7,4},{6,5},{8,11},{9,10},{11,... | collective-permute-start | bytes 331784 | tf_op jit(solution)/shard_map/ppermute | solution.py:124
  59.5 10.6 %collective-permute-start.18 = (bf16[216,128]{1,0:T(8,128)(2,1)S(1)}, bf16[216,128]{1,0:T(8,128)(2,1)S(1)}, u32[]{:S(2)}, u32[]{:S(2)}) collective-permute-start(bf16[216,128]{1,0:T(8,128)(2,1)S(1)} %get-tuple-element.142), channel_id=1, source_target_pairs={{0,1},{2,3},{1,0},{3,2},{4,5},{6,7},{5,4},{7,6},{8,9},{10,11},{9,8... | collective-permute-start | bytes 165896 | tf_op jit(solution)/shard_map/ppermute | solution.py:124
  59.6 10.5 %collective-permute-start.19 = (bf16[216,128]{1,0:T(8,128)(2,1)S(1)}, bf16[216,128]{1,0:T(8,128)(2,1)S(1)}, u32[]{:S(2)}, u32[]{:S(2)}) collective-permute-start(bf16[216,128]{1,0:T(8,128)(2,1)S(1)} %get-tuple-element.143), channel_id=1, source_target_pairs={{0,2},{1,3},{2,0},{3,1},{4,6},{5,7},{6,4},{7,5},{8,10},{9,11},{10,... | collective-permute-start | bytes 165896 | tf_op jit(solution)/shard_map/ppermute | solution.py:124
  61.0 10.4 %collective-permute-start.20 = (bf16[216,128]{1,0:T(8,128)(2,1)S(1)}, bf16[216,128]{1,0:T(8,128)(2,1)S(1)}, u32[]{:S(2)}, u32[]{:S(2)}) collective-permute-start(bf16[216,128]{1,0:T(8,128)(2,1)S(1)} %get-tuple-element.144), channel_id=1, source_target_pairs={{0,3},{1,2},{3,0},{2,1},{4,7},{5,6},{7,4},{6,5},{8,11},{9,10},{11,... | collective-permute-start | bytes 165896 | tf_op jit(solution)/shard_map/ppermute | solution.py:124

commit v6 on v5

--- a/solution.py
+++ b/solution.py
@@ -12,7 +12,7 @@
 HDIM = 72
 WIDTH = HEADS * HDIM
 SCALING = 1.0 / math.sqrt(HDIM)
-CHUNKS = (2, 4, 2)
+CHUNKS = (4, 4)
 masked_score = -1e30
 
 
@@ -83,19 +83,18 @@
     for copy in loads:
         copy.start()
     places = ins[0].shape[2] // n
+    stores = []
     for at in range(2):
         loads[2 * at].wait()
         loads[2 * at + 1].wait()
         for target in range(n):
             lanes = slice(target * places, (target + 1) * places)
             both = [loaded[2 * at, :, lanes], loaded[2 * at + 1, :, lanes]]
-            held[target, at] = jnp.concatenate(both, axis=1)
-    stores = [
-        pltpu.make_async_copy(held.at[(lax.axis_index("seq") ^ step)], out, left_off.at[step])
-        for step, out in enumerate(outs)
-    ]
-    for copy in stores:
-        copy.start()
+            held[at, target] = jnp.concatenate(both, axis=1)
+        for step, out in enumerate(outs):
+            block = held.at[at, lax.axis_index("seq") ^ step]
+            stores.append(pltpu.make_async_copy(block, out.at[at], left_off.at[at, step]))
+            stores[-1].start()
     for copy in stores:
         copy.wait()
 
@@ -111,9 +110,9 @@
         out_shape=[jax.ShapeDtypeStruct(shape, jnp.bfloat16)] * n,
         scratch_shapes=[
             pltpu.VMEM((4, rows, tokens), jnp.bfloat16),
-            pltpu.VMEM((n, *shape), jnp.bfloat16),
+            pltpu.VMEM((2, n, *shape[1:]), jnp.bfloat16),
             pltpu.SemaphoreType.DMA((4,)),
-            pltpu.SemaphoreType.DMA((n,)),
+            pltpu.SemaphoreType.DMA((2, n)),
         ],
         compiler_params=pltpu.CompilerParams(vmem_limit_bytes=60 * 2**20),
         name="pack",
@@ -126,10 +125,10 @@
 
 def exchange(blocks):
     n = len(blocks)
-    moved = [blocks[0]]
-    for step in range(1, n):
+    moved = list(blocks)
+    for step in reversed(range(1, n)):
         pairs = [[i, i ^ step] for i in range(n) if i < i ^ step]
-        moved.append(swap(blocks[step], "seq", pairs))
+        moved[step] = swap(blocks[step], "seq", pairs)
     return moved
 
 
@@ -162,9 +161,9 @@
 
 def neighbours(blocks):
     count = lax.axis_size("grp")
-    moved = []
-    for start, block in enumerate(blocks):
-        moved.append(swap(block, "grp", [(i, i + 1) for i in range(start, count - 1, 2)]))
+    moved = list(blocks)
+    for start in (1, 0):
+        moved[start] = swap(blocks[start], "grp", [(i, i + 1) for i in range(start, count - 1, 2)])
     return moved
 
 
@@ -218,23 +217,27 @@
     )(*blocks, *earlier)
 
 
-def clip_kernel(window, heads, bounds, *refs):
+def clip_kernel(window, heads, given_bounds, *refs):
     own, sides_of = refs[:window], refs[window : window + 2]
-    outs, (x_ref, y_ref, coef_ref, grad_ref) = refs[window + 2 : 2 * window + 2], refs[-4:]
+    outs, (x_ref, y_ref, coef_ref, grad_ref) = refs[window + 2 : 2 * window + 2], refs[-6:-2]
+    bounds, arrived = refs[-2:]
+    copy = pltpu.make_async_copy(given_bounds, bounds, arrived)
+    copy.start()
     halo = window - 1
     extent = window + 2 * halo
     lanes = grad_ref.shape[2]
     places = lanes // 2
     rows = heads * HDIM
     is_left = lax.broadcasted_iota(jnp.int32, (1, lanes), 1) < places
-    lowest, highest = bounds[0, halo], bounds[1, halo + window - 1]
 
     def widen(ref, frame):
         x_ref[frame] = ref[0].astype(jnp.float32)
         y_ref[frame] = ref[1].astype(jnp.float32)
 
     for step, ref in enumerate(own):
-        widen(ref, halo + ((lax.axis_index("seq") ^ step)))
+        widen(ref, halo + (lax.axis_index("seq") ^ step))
+    copy.wait()
+    lowest, highest = bounds[0, halo], bounds[1, halo + window - 1]
     for start, ref in enumerate(sides_of):
         is_next = (lax.axis_index("grp") & 1) == start
         for at in range(halo):
@@ -315,19 +318,20 @@
     heads = rows // HDIM
     extent = 3 * window - 2
     vmem = pl.BlockSpec(memory_space=pltpu.VMEM)
-    smem = pl.BlockSpec(memory_space=pltpu.SMEM)
     work = extent * window * rows * lanes
     shape = (rows + rows // 2, lanes)
     return pl.pallas_call(
         functools.partial(clip_kernel, window, heads),
         out_shape=[jax.ShapeDtypeStruct(shape, jnp.bfloat16)] * window,
-        in_specs=[smem] + [vmem] * (window + 2),
+        in_specs=[pl.BlockSpec(memory_space=pl.ANY)] + [vmem] * (window + 2),
         out_specs=[vmem] * window,
         scratch_shapes=[
             pltpu.VMEM((extent, rows, lanes), jnp.float32),
             pltpu.VMEM((extent, rows, lanes), jnp.float32),
             pltpu.VMEM((extent, window, heads, lanes), jnp.float32),
             pltpu.VMEM((window, *shape), jnp.bfloat16),
+            pltpu.SMEM(bounds.shape, jnp.int32),
+            pltpu.SemaphoreType.DMA,
         ],
         compiler_params=pltpu.CompilerParams(vmem_limit_bytes=48 * 2**20),
         cost_estimate=pl.CostEstimate(
@@ -373,27 +377,18 @@
     def gated(values, *earlier):
         return lax.optimization_barrier((values, *earlier))
 
-    back, grads, own, beside = [], None, [], []
-    own.append(exchange(packed[0]))
-    own.append(exchange(packed[1]))
+    own = [exchange(blocks) for blocks in packed]
     ends = sides(own[0])
     space_in, ends = gated(space_in, ends)
-    beside.append(neighbours(ends))
+    beside = [neighbours(ends)]
     space = frame_grads(*space_in)
-    packed[2], space, beside[0], own[1][1] = gated(packed[2], space, beside[0], own[1][1])
-    own.append(exchange(packed[2]))
-    own[1], own[2][1] = gated(own[1], own[2][1])
-    ends, beside[0] = gated(sides(own[1]), beside[0])
-    beside.append(neighbours(ends))
-    back.append(exchange(clip_grads(bounds, own[0], beside[0])))
-    ends, beside[1], back[0][1] = gated(sides(own[2]), beside[1], back[0][1])
-    beside.append(neighbours(ends))
-    back.append(exchange(clip_grads(bounds, own[1], beside[1])))
-    grads = join(back[0], spans[0], tokens, grads)
-    beside[2], grads = gated(beside[2], grads)
-    back.append(exchange(clip_grads(bounds, own[2], beside[2])))
-    grads = join(back[1], spans[1], tokens, grads)
-    grads = join(back[2], spans[2], tokens, grads)
+    own[1], space = gated(own[1], space)
+    beside.append(neighbours(sides(own[1])))
+    back, grads = [], None
+    for blocks, near in zip(own, beside):
+        back.append(exchange(clip_grads(bounds, blocks, near)))
+    for span, blocks in zip(spans, back):
+        grads = join(blocks, span, tokens, grads)
     return turned(*space, *grads)
 
 

time: 72.8 us -> 67.5 us (0.927)
  the two profiles are of different devices: /device:TPU:19 before, /device:TPU:11 now
where the time goes in v6:
time: 67.5 us; the launch traced here: 67.4 us
  starting transfers between devices  28 us (41%)
  waiting for transfers between devices  21.2 us (31%)
  Pallas kernels  16.5 us (24%)
  between operations  0.79 us (1%)
    ppermute x16, starting transfers between devices, swap(): lax.ppermute(block, axis, [(i, j) for i, j in pairs] + [(j, i) for i, j i...  28 us
    ppermute x16, waiting for transfers between devices, swap(): lax.ppermute(block, axis, [(i, j) for i, j in pairs] + [(j, i) for i, j i...  21.2 us
    pallas_call x1, Pallas kernels, frame_grads(): pl.pallas_call(frame_kernel, out_shape=(shape, shape, shape), compiler_pa...  5.53 us
    pallas_call x2, Pallas kernels, clip_grads(): pl.pallas_call(functools.partial(clip_kernel, window, heads), out_shape=[...  4.51 us
    pallas_call x2, Pallas kernels, split(): pl.pallas_call(functools.partial(split_kernel, n, span), in_specs=[hbm] *...  4.16 us
    pallas_call x2, Pallas kernels, join(): pl.pallas_call(functools.partial(join_kernel, n, span), in_specs=[vmem] *...  2.01 us
  transfers between devices with their start and end apart: 16, of which 6 were waited for; matrix products, arithmetic and copies ran while one was open for 0% of the time, Pallas kernels for 20%

profile of v6, /device:TPU:11, one launch (start us, length us, event | category | flops | bytes accessed | tf_op | source)
XLA Modules:
  0.0 67.4 jit_solution(11185542632333832910)
XLA Ops:
  0.6 2.1 %pack.3 = (bf16[2,288,128]{2,1,0:T(8,128)(2,1)}, bf16[2,288,128]{2,1,0:T(8,128)(2,1)}, bf16[2,288,128]{2,1,0:T(8,128)(2,1)}, bf16[2,288,128]{2,1,0:T(8,128)(2,1)}) custom-call(bf16[1,576,256]{2,1,0:T(8,128)(2,1)} %bitcast.18, bf16[1,576,256]{2,1,0:T(8,128)(2,1)} %bitcast.20, bf16[1,576,256]{2,1,0:T(8,128)(2,1)} %bitcast.22, bf16[1,576,256]{2,1,0:T(8,128)(2,1)} %bitcast.24), custom_call_target="tpu_custom_call" | custom-call | tf_op jit(solution)/shard_map/pack/pallas_call | solution.py:106
  2.7 0.2 collective-permute-start.3
  2.9 2.3 %collective-permute-start.4 = (bf16[2,288,128]{2,1,0:T(8,128)(2,1)}, bf16[2,288,128]{2,1,0:T(8,128)(2,1)S(1)}, u32[]{:S(2)}, u32[]{:S(2)}) collective-permute-start(bf16[2,288,128]{2,1,0:T(8,128)(2,1)} %get-tuple-element.54), channel_id=1, source_target_pairs={{0,2},{1,3},{2,0},{3,1},{4,6},{5,7},{6,4},{7,5},{8,10},{9,11},{10,... | collective-permute-start | bytes 442376 | tf_op jit(solution)/shard_map/ppermute | solution.py:123
  5.3 0.0 copy-start.1
  5.3 0.2 collective-permute-start.5
  5.4 2.1 %pack.2 = (bf16[2,288,128]{2,1,0:T(8,128)(2,1)}, bf16[2,288,128]{2,1,0:T(8,128)(2,1)}, bf16[2,288,128]{2,1,0:T(8,128)(2,1)}, bf16[2,288,128]{2,1,0:T(8,128)(2,1)}) custom-call(bf16[1,576,256]{2,1,0:T(8,128)(2,1)} %bitcast.19, bf16[1,576,256]{2,1,0:T(8,128)(2,1)} %bitcast.21, bf16[1,576,256]{2,1,0:T(8,128)(2,1)} %bitcast.23, bf16[1,576,256]{2,1,0:T(8,128)(2,1)} %bitcast.25), custom_call_target="tpu_custom_call" | custom-call | tf_op jit(solution)/shard_map/pack/pallas_call | solution.py:106
  7.5 1.2 %collective-permute-start = (bf16[2,288,128]{2,1,0:T(8,128)(2,1)}, bf16[2,288,128]{2,1,0:T(8,128)(2,1)S(1)}, u32[]{:S(2)}, u32[]{:S(2)}) collective-permute-start(bf16[2,288,128]{2,1,0:T(8,128)(2,1)} %get-tuple-element.49), channel_id=1, source_target_pairs={{0,1},{2,3},{1,0},{3,2},{4,5},{6,7},{5,4},{7,6},{8,9},{10,11},{9,8... | collective-permute-start | bytes 442376 | tf_op jit(solution)/shard_map/ppermute | solution.py:123
  8.8 2.1 %collective-permute-start.1 = (bf16[2,288,128]{2,1,0:T(8,128)(2,1)}, bf16[2,288,128]{2,1,0:T(8,128)(2,1)S(1)}, u32[]{:S(2)}, u32[]{:S(2)}) collective-permute-start(bf16[2,288,128]{2,1,0:T(8,128)(2,1)} %get-tuple-element.50), channel_id=1, source_target_pairs={{0,2},{1,3},{2,0},{3,1},{4,6},{5,7},{6,4},{7,5},{8,10},{9,11},{10,... | collective-permute-start | bytes 442376 | tf_op jit(solution)/shard_map/ppermute | solution.py:123
  10.9 0.0 copy-start.2
  10.9 0.7 copy-done.2
  11.5 0.1 select_reduce_fusion.2
  11.6 0.2 select_reduce_fusion.1
  11.8 0.0 collective-permute-done.3.refs_1_
  11.8 0.3 collective-permute-start.2
  12.1 0.0 collective-permute-done.4.refs_2_
  12.1 6.1 %collective-permute-done.5.refs_3_ = bf16[2,288,128]{2,1,0:T(8,128)(2,1)S(1)} collective-permute-done((bf16[2,288,128]{2,1,0:T(8,128)(2,1)}, bf16[2,288,128]{2,1,0:T(8,128)(2,1)S(1)}, u32[]{:S(2)}, u32[]{:S(2)}) %collective-permute-start.5) | collective-permute-done | bytes 147488 | tf_op jit(solution)/shard_map/ppermute | solution.py:123
  18.2 0.0 copy-done.1
  18.2 0.1 sides.2
  18.3 0.0 copy-start
  18.3 9.6 %collective-permute-start.11 = (bf16[3,2,288,128]{3,2,1,0:T(8,128)(2,1)S(1)}, bf16[3,2,288,128]{3,2,1,0:T(8,128)(2,1)S(1)}, u32[]{:S(2)}, u32[]{:S(2)}) collective-permute-start(bf16[3,2,288,128]{3,2,1,0:T(8,128)(2,1)S(1)} %get-tuple-element.78), channel_id=1, source_target_pairs={{0,4},{8,12},{16,20},{24,28},{4,0},{12,8},{20,16},{28,24},{1,5},{9... | collective-permute-start | bytes 1327112 | tf_op jit(solution)/shard_map/ppermute | solution.py:123
  27.9 3.0 %collective-permute-start.12 = (bf16[3,2,288,128]{3,2,1,0:T(8,128)(2,1)S(1)}, bf16[3,2,288,128]{3,2,1,0:T(8,128)(2,1)S(1)}, u32[]{:S(2)}, u32[]{:S(2)}) collective-permute-start(bf16[3,2,288,128]{3,2,1,0:T(8,128)(2,1)S(1)} %get-tuple-element.79), channel_id=1, source_target_pairs={{4,8},{12,16},{20,24},{8,4},{16,12},{24,20},{5,9},{13,17},{21,25},... | collective-permute-start | bytes 1327112 | tf_op jit(solution)/shard_map/ppermute | solution.py:123
  31.0 5.5 %space.1 = (bf16[1,576,256]{2,1,0:T(8,128)(2,1)}, bf16[1,576,256]{2,1,0:T(8,128)(2,1)}, bf16[1,576,256]{2,1,0:T(8,128)(2,1)}) custom-call(bf16[1,576,256]{2,1,0:T(8,128)(2,1)} %bitcast.29, bf16[1,576,256]{2,1,0:T(8,128)(2,1)} %bitcast.30, bf16[1,576,256]{2,1,0:T(8,128)(2,1)} %bitcast.31, bf16[1,576,256]{2,1,0:T(8,128)(2,1)} %bitcast.32), custom_call_target="tpu_custom_call" | custom-call | flops 1610612736 | bytes 2064384 | tf_op jit(solution)/shard_map/space/pallas_call | solution.py:64
  36.5 0.0 collective-permute-done.refs_1_
  36.5 0.0 collective-permute-done.1.refs_2_
  36.5 0.0 collective-permute-done.2.refs_3_
  36.5 0.0 copy-done
  36.5 0.1 sides.3
  36.7 0.1 collective-permute-start.6
  36.8 3.5 %collective-permute-start.7 = (bf16[3,2,288,128]{3,2,1,0:T(8,128)(2,1)S(1)}, bf16[3,2,288,128]{3,2,1,0:T(8,128)(2,1)S(1)}, u32[]{:S(2)}, u32[]{:S(2)}) collective-permute-start(bf16[3,2,288,128]{3,2,1,0:T(8,128)(2,1)S(1)} %get-tuple-element.73), channel_id=1, source_target_pairs={{4,8},{12,16},{20,24},{8,4},{16,12},{24,20},{5,9},{13,17},{21,25},... | collective-permute-start | bytes 1327112 | tf_op jit(solution)/shard_map/ppermute | solution.py:123
  40.3 0.0 collective-permute-done.11.refs_4_
  40.3 2.8 %collective-permute-done.12.refs_5_ = bf16[3,2,288,128]{3,2,1,0:T(8,128)(2,1)S(1)} collective-permute-done((bf16[3,2,288,128]{3,2,1,0:T(8,128)(2,1)S(1)}, bf16[3,2,288,128]{3,2,1,0:T(8,128)(2,1)S(1)}, u32[]{:S(2)}, u32[]{:S(2)}) %collective-permute-start.12) | collective-permute-done | bytes 442400 | tf_op jit(solution)/shard_map/ppermute | solution.py:123
  43.1 2.3 %clips.3 = (bf16[432,128]{1,0:T(8,128)(2,1)S(1)}, bf16[432,128]{1,0:T(8,128)(2,1)S(1)}, bf16[432,128]{1,0:T(8,128)(2,1)S(1)}, bf16[432,128]{1,0:T(8,128)(2,1)S(1)}) custom-call(s32[2,10]{1,0:T(2,128)S(1)} %pad_add_fusion.given_bounds, bf16[2,288,128]{2,1,0:T(8,128)(2,1)S(1)} %copy-done.1, bf16[2,288,128]{2,1,0:T(8,128)(2,1)S(1)} %collective-permute-done.3.refs_1_, ...), custom_call_target="tpu_custom_call" | custom-call | flops 589824000 | bytes 1474560 | tf_op jit(solution)/shard_map/clips/pallas_call | solution.py:323
  45.4 0.1 collective-permute-start.13
  45.5 2.3 %collective-permute-start.14 = (bf16[432,128]{1,0:T(8,128)(2,1)S(1)}, bf16[432,128]{1,0:T(8,128)(2,1)S(1)}, u32[]{:S(2)}, u32[]{:S(2)}) collective-permute-start(bf16[432,128]{1,0:T(8,128)(2,1)S(1)} %get-tuple-element.82), channel_id=1, source_target_pairs={{0,2},{1,3},{2,0},{3,1},{4,6},{5,7},{6,4},{7,5},{8,10},{9,11},{10,... | collective-permute-start | bytes 331784 | tf_op jit(solution)/shard_map/ppermute | solution.py:123
  47.8 0.3 collective-permute-start.15
  48.1 0.0 collective-permute-done.6.refs_4_
  48.1 3.9 %collective-permute-done.7.refs_5_ = bf16[3,2,288,128]{3,2,1,0:T(8,128)(2,1)S(1)} collective-permute-done((bf16[3,2,288,128]{3,2,1,0:T(8,128)(2,1)S(1)}, bf16[3,2,288,128]{3,2,1,0:T(8,128)(2,1)S(1)}, u32[]{:S(2)}, u32[]{:S(2)}) %collective-permute-start.7) | collective-permute-done | bytes 442400 | tf_op jit(solution)/shard_map/ppermute | solution.py:123
  52.1 2.3 %clips.2 = (bf16[432,128]{1,0:T(8,128)(2,1)S(1)}, bf16[432,128]{1,0:T(8,128)(2,1)S(1)}, bf16[432,128]{1,0:T(8,128)(2,1)S(1)}, bf16[432,128]{1,0:T(8,128)(2,1)S(1)}) custom-call(s32[2,10]{1,0:T(2,128)S(1)} %pad_add_fusion.given_bounds, bf16[2,288,128]{2,1,0:T(8,128)(2,1)S(1)} %copy-done, bf16[2,288,128]{2,1,0:T(8,128)(2,1)S(1)} %collective-permute-done.refs_1_, ...), custom_call_target="tpu_custom_call" | custom-call | flops 589824000 | bytes 1474560 | tf_op jit(solution)/shard_map/clips/pallas_call | solution.py:323
  54.3 0.1 collective-permute-start.8
  54.4 2.3 %collective-permute-start.9 = (bf16[432,128]{1,0:T(8,128)(2,1)S(1)}, bf16[432,128]{1,0:T(8,128)(2,1)S(1)}, u32[]{:S(2)}, u32[]{:S(2)}) collective-permute-start(bf16[432,128]{1,0:T(8,128)(2,1)S(1)} %get-tuple-element.76), channel_id=1, source_target_pairs={{0,2},{1,3},{2,0},{3,1},{4,6},{5,7},{6,4},{7,5},{8,10},{9,11},{10,... | collective-permute-start | bytes 331784 | tf_op jit(solution)/shard_map/ppermute | solution.py:123
  56.7 0.0 collective-permute-done.13.refs_1_
  56.7 0.3 collective-permute-start.10
  57.0 0.0 collective-permute-done.14.refs_2_
  57.0 0.0 collective-permute-done.15.refs_3_
  57.1 1.0 %unpack.2 = (bf16[1,576,256]{2,1,0:T(8,128)(2,1)}, bf16[1,576,256]{2,1,0:T(8,128)(2,1)}, bf16[1,576,256]{2,1,0:T(8,128)(2,1)}) custom-call(bf16[432,128]{1,0:T(8,128)(2,1)S(1)} %get-tuple-element.80.refs_0_, bf16[432,128]{1,0:T(8,128)(2,1)S(1)} %collective-permute-done.13.refs_1_, bf16[432,128]{1,0:T(8,128)(2,1)S(1)} %collective-permute-done.14.refs_2_, ...), custom_call_target="tpu_custom_call" | custom-call | tf_op jit(solution)/shard_map/unpack/pallas_call | solution.py:204
  58.1 1.5 %collective-permute-done.8.refs_1_ = bf16[432,128]{1,0:T(8,128)(2,1)S(1)} collective-permute-done((bf16[432,128]{1,0:T(8,128)(2,1)S(1)}, bf16[432,128]{1,0:T(8,128)(2,1)S(1)}, u32[]{:S(2)}, u32[]{:S(2)}) %collective-permute-start.8) | collective-permute-done | bytes 110624 | tf_op jit(solution)/shard_map/ppermute | solution.py:123
  59.5 4.0 %collective-permute-done.9.refs_2_ = bf16[432,128]{1,0:T(8,128)(2,1)S(1)} collective-permute-done((bf16[432,128]{1,0:T(8,128)(2,1)S(1)}, bf16[432,128]{1,0:T(8,128)(2,1)S(1)}, u32[]{:S(2)}, u32[]{:S(2)}) %collective-permute-start.9) | collective-permute-done | bytes 110624 | tf_op jit(solution)/shard_map/ppermute | solution.py:123
  63.5 2.8 %collective-permute-done.10.refs_3_ = bf16[432,128]{1,0:T(8,128)(2,1)S(1)} collective-permute-done((bf16[432,128]{1,0:T(8,128)(2,1)S(1)}, bf16[432,128]{1,0:T(8,128)(2,1)S(1)}, u32[]{:S(2)}, u32[]{:S(2)}) %collective-permute-start.10) | collective-permute-done | bytes 110624 | tf_op jit(solution)/shard_map/ppermute | solution.py:123
  66.4 1.0 %unpack.3 = (bf16[1,576,256]{2,1,0:T(8,128)(2,1)}, bf16[1,576,256]{2,1,0:T(8,128)(2,1)}, bf16[1,576,256]{2,1,0:T(8,128)(2,1)}) custom-call(bf16[432,128]{1,0:T(8,128)(2,1)S(1)} %get-tuple-element.74.refs_0_, bf16[432,128]{1,0:T(8,128)(2,1)S(1)} %collective-permute-done.8.refs_1_, ...), custom_call_target="tpu_custom_call", output_to_operand_aliasing={{0}: (4, {}), {1}: (5, {}), {2}: (6, {})} | custom-call | tf_op jit(solution)/shard_map/unpack/pallas_call | solution.py:204
  (4 shorter events, 0.0 us)
Async XLA Ops:
  2.7 9.1 %collective-permute-start.3 = (bf16[2,288,128]{2,1,0:T(8,128)(2,1)}, bf16[2,288,128]{2,1,0:T(8,128)(2,1)S(1)}, u32[]{:S(2)}, u32[]{:S(2)}) collective-permute-start(bf16[2,288,128]{2,1,0:T(8,128)(2,1)} %get-tuple-element.53), channel_id=1, source_target_pairs={{0,1},{2,3},{1,0},{3,2},{4,5},{6,7},{5,4},{7,6},{8,9},{10,11},{9,8... | collective-permute-start | bytes 442376 | tf_op jit(solution)/shard_map/ppermute | solution.py:123
  2.9 9.1 %collective-permute-start.4 = (bf16[2,288,128]{2,1,0:T(8,128)(2,1)}, bf16[2,288,128]{2,1,0:T(8,128)(2,1)S(1)}, u32[]{:S(2)}, u32[]{:S(2)}) collective-permute-start(bf16[2,288,128]{2,1,0:T(8,128)(2,1)} %get-tuple-element.54), channel_id=1, source_target_pairs={{0,2},{1,3},{2,0},{3,1},{4,6},{5,7},{6,4},{7,5},{8,10},{9,11},{10,... | collective-permute-start | bytes 442376 | tf_op jit(solution)/shard_map/ppermute | solution.py:123
  5.3 12.9 %copy-start.1 = (bf16[2,288,128]{2,1,0:T(8,128)(2,1)S(1)}, bf16[2,288,128]{2,1,0:T(8,128)(2,1)}, u32[]{:S(2)}) copy-start(bf16[2,288,128]{2,1,0:T(8,128)(2,1)} %get-tuple-element.52.refs_0_) | copy-start | bytes 442372
  5.3 12.9 %collective-permute-start.5 = (bf16[2,288,128]{2,1,0:T(8,128)(2,1)}, bf16[2,288,128]{2,1,0:T(8,128)(2,1)S(1)}, u32[]{:S(2)}, u32[]{:S(2)}) collective-permute-start(bf16[2,288,128]{2,1,0:T(8,128)(2,1)} %get-tuple-element.55), channel_id=1, source_target_pairs={{0,3},{1,2},{3,0},{2,1},{4,7},{5,6},{7,4},{6,5},{8,11},{9,10},{11,... | collective-permute-start | bytes 442376 | tf_op jit(solution)/shard_map/ppermute | solution.py:123
  7.5 29.0 %collective-permute-start = (bf16[2,288,128]{2,1,0:T(8,128)(2,1)}, bf16[2,288,128]{2,1,0:T(8,128)(2,1)S(1)}, u32[]{:S(2)}, u32[]{:S(2)}) collective-permute-start(bf16[2,288,128]{2,1,0:T(8,128)(2,1)} %get-tuple-element.49), channel_id=1, source_target_pairs={{0,1},{2,3},{1,0},{3,2},{4,5},{6,7},{5,4},{7,6},{8,9},{10,11},{9,8... | collective-permute-start | bytes 442376 | tf_op jit(solution)/shard_map/ppermute | solution.py:123
  8.8 27.7 %collective-permute-start.1 = (bf16[2,288,128]{2,1,0:T(8,128)(2,1)}, bf16[2,288,128]{2,1,0:T(8,128)(2,1)S(1)}, u32[]{:S(2)}, u32[]{:S(2)}) collective-permute-start(bf16[2,288,128]{2,1,0:T(8,128)(2,1)} %get-tuple-element.50), channel_id=1, source_target_pairs={{0,2},{1,3},{2,0},{3,1},{4,6},{5,7},{6,4},{7,5},{8,10},{9,11},{10,... | collective-permute-start | bytes 442376 | tf_op jit(solution)/shard_map/ppermute | solution.py:123
  10.9 0.7 copy-start.2
  11.8 24.7 %collective-permute-start.2 = (bf16[2,288,128]{2,1,0:T(8,128)(2,1)}, bf16[2,288,128]{2,1,0:T(8,128)(2,1)S(1)}, u32[]{:S(2)}, u32[]{:S(2)}) collective-permute-start(bf16[2,288,128]{2,1,0:T(8,128)(2,1)} %get-tuple-element.51), channel_id=1, source_target_pairs={{0,3},{1,2},{3,0},{2,1},{4,7},{5,6},{7,4},{6,5},{8,11},{9,10},{11,... | collective-permute-start | bytes 442376 | tf_op jit(solution)/shard_map/ppermute | solution.py:123
  18.3 18.2 %copy-start = (bf16[2,288,128]{2,1,0:T(8,128)(2,1)S(1)}, bf16[2,288,128]{2,1,0:T(8,128)(2,1)}, u32[]{:S(2)}) copy-start(bf16[2,288,128]{2,1,0:T(8,128)(2,1)} %get-tuple-element.68.refs_0_) | copy-start | bytes 442372
  18.3 22.0 %collective-permute-start.11 = (bf16[3,2,288,128]{3,2,1,0:T(8,128)(2,1)S(1)}, bf16[3,2,288,128]{3,2,1,0:T(8,128)(2,1)S(1)}, u32[]{:S(2)}, u32[]{:S(2)}) collective-permute-start(bf16[3,2,288,128]{3,2,1,0:T(8,128)(2,1)S(1)} %get-tuple-element.78), channel_id=1, source_target_pairs={{0,4},{8,12},{16,20},{24,28},{4,0},{12,8},{20,16},{28,24},{1,5},{9... | collective-permute-start | bytes 1327112 | tf_op jit(solution)/shard_map/ppermute | solution.py:123
  27.9 15.2 %collective-permute-start.12 = (bf16[3,2,288,128]{3,2,1,0:T(8,128)(2,1)S(1)}, bf16[3,2,288,128]{3,2,1,0:T(8,128)(2,1)S(1)}, u32[]{:S(2)}, u32[]{:S(2)}) collective-permute-start(bf16[3,2,288,128]{3,2,1,0:T(8,128)(2,1)S(1)} %get-tuple-element.79), channel_id=1, source_target_pairs={{4,8},{12,16},{20,24},{8,4},{16,12},{24,20},{5,9},{13,17},{21,25},... | collective-permute-start | bytes 1327112 | tf_op jit(solution)/shard_map/ppermute | solution.py:123
  36.7 11.4 %collective-permute-start.6 = (bf16[3,2,288,128]{3,2,1,0:T(8,128)(2,1)S(1)}, bf16[3,2,288,128]{3,2,1,0:T(8,128)(2,1)S(1)}, u32[]{:S(2)}, u32[]{:S(2)}) collective-permute-start(bf16[3,2,288,128]{3,2,1,0:T(8,128)(2,1)S(1)} %get-tuple-element.72), channel_id=1, source_target_pairs={{0,4},{8,12},{16,20},{24,28},{4,0},{12,8},{20,16},{28,24},{1,5},{9... | collective-permute-start | bytes 1327112 | tf_op jit(solution)/shard_map/ppermute | solution.py:123
  36.8 15.3 %collective-permute-start.7 = (bf16[3,2,288,128]{3,2,1,0:T(8,128)(2,1)S(1)}, bf16[3,2,288,128]{3,2,1,0:T(8,128)(2,1)S(1)}, u32[]{:S(2)}, u32[]{:S(2)}) collective-permute-start(bf16[3,2,288,128]{3,2,1,0:T(8,128)(2,1)S(1)} %get-tuple-element.73), channel_id=1, source_target_pairs={{4,8},{12,16},{20,24},{8,4},{16,12},{24,20},{5,9},{13,17},{21,25},... | collective-permute-start | bytes 1327112 | tf_op jit(solution)/shard_map/ppermute | solution.py:123
  45.4 11.3 %collective-permute-start.13 = (bf16[432,128]{1,0:T(8,128)(2,1)S(1)}, bf16[432,128]{1,0:T(8,128)(2,1)S(1)}, u32[]{:S(2)}, u32[]{:S(2)}) collective-permute-start(bf16[432,128]{1,0:T(8,128)(2,1)S(1)} %get-tuple-element.81), channel_id=1, source_target_pairs={{0,1},{2,3},{1,0},{3,2},{4,5},{6,7},{5,4},{7,6},{8,9},{10,11},{9,8... | collective-permute-start | bytes 331784 | tf_op jit(solution)/shard_map/ppermute | solution.py:123
  45.5 11.6 %collective-permute-start.14 = (bf16[432,128]{1,0:T(8,128)(2,1)S(1)}, bf16[432,128]{1,0:T(8,128)(2,1)S(1)}, u32[]{:S(2)}, u32[]{:S(2)}) collective-permute-start(bf16[432,128]{1,0:T(8,128)(2,1)S(1)} %get-tuple-element.82), channel_id=1, source_target_pairs={{0,2},{1,3},{2,0},{3,1},{4,6},{5,7},{6,4},{7,5},{8,10},{9,11},{10,... | collective-permute-start | bytes 331784 | tf_op jit(solution)/shard_map/ppermute | solution.py:123
  47.8 9.3 %collective-permute-start.15 = (bf16[432,128]{1,0:T(8,128)(2,1)S(1)}, bf16[432,128]{1,0:T(8,128)(2,1)S(1)}, u32[]{:S(2)}, u32[]{:S(2)}) collective-permute-start(bf16[432,128]{1,0:T(8,128)(2,1)S(1)} %get-tuple-element.83), channel_id=1, source_target_pairs={{0,3},{1,2},{3,0},{2,1},{4,7},{5,6},{7,4},{6,5},{8,11},{9,10},{11,... | collective-permute-start | bytes 331784 | tf_op jit(solution)/shard_map/ppermute | solution.py:123
  54.3 5.2 %collective-permute-start.8 = (bf16[432,128]{1,0:T(8,128)(2,1)S(1)}, bf16[432,128]{1,0:T(8,128)(2,1)S(1)}, u32[]{:S(2)}, u32[]{:S(2)}) collective-permute-start(bf16[432,128]{1,0:T(8,128)(2,1)S(1)} %get-tuple-element.75), channel_id=1, source_target_pairs={{0,1},{2,3},{1,0},{3,2},{4,5},{6,7},{5,4},{7,6},{8,9},{10,11},{9,8... | collective-permute-start | bytes 331784 | tf_op jit(solution)/shard_map/ppermute | solution.py:123
  54.4 9.1 %collective-permute-start.9 = (bf16[432,128]{1,0:T(8,128)(2,1)S(1)}, bf16[432,128]{1,0:T(8,128)(2,1)S(1)}, u32[]{:S(2)}, u32[]{:S(2)}) collective-permute-start(bf16[432,128]{1,0:T(8,128)(2,1)S(1)} %get-tuple-element.76), channel_id=1, source_target_pairs={{0,2},{1,3},{2,0},{3,1},{4,6},{5,7},{6,4},{7,5},{8,10},{9,11},{10,... | collective-permute-start | bytes 331784 | tf_op jit(solution)/shard_map/ppermute | solution.py:123
  56.7 9.7 %collective-permute-start.10 = (bf16[432,128]{1,0:T(8,128)(2,1)S(1)}, bf16[432,128]{1,0:T(8,128)(2,1)S(1)}, u32[]{:S(2)}, u32[]{:S(2)}) collective-permute-start(bf16[432,128]{1,0:T(8,128)(2,1)S(1)} %get-tuple-element.77), channel_id=1, source_target_pairs={{0,3},{1,2},{3,0},{2,1},{4,7},{5,6},{7,4},{6,5},{8,11},{9,10},{11,... | collective-permute-start | bytes 331784 | tf_op jit(solution)/shard_map/ppermute | solution.py:123

commit v7 on v6

--- a/solution.py
+++ b/solution.py
@@ -372,18 +372,16 @@
         spans.append(slice(head * HDIM, (head + heads) * HDIM))
         head += heads
     space_in = turned(q_space, k_space, v_space, cot_space)
-    packed = [split(time, span, n) for span in spans]
+    packed = [list(split(time, span, n)) for span in spans]
 
     def gated(values, *earlier):
         return lax.optimization_barrier((values, *earlier))
 
-    own = [exchange(blocks) for blocks in packed]
-    ends = sides(own[0])
-    space_in, ends = gated(space_in, ends)
-    beside = [neighbours(ends)]
+    own = [exchange(packed[0])]
     space = frame_grads(*space_in)
-    own[1], space = gated(own[1], space)
-    beside.append(neighbours(sides(own[1])))
+    packed[1][2:], own[0][2], space = gated(packed[1][2:], own[0][2], space)
+    own.append(exchange(packed[1]))
+    beside = [neighbours(sides(blocks)) for blocks in own]
     back, grads = [], None
     for blocks, near in zip(own, beside):
         back.append(exchange(clip_grads(bounds, blocks, near)))

time: 67.5 us -> 62.1 us (0.920)
  the two profiles are of different devices: /device:TPU:11 before, /device:TPU:19 now
where the time goes in v7:
time: 62.1 us; the launch traced here: 61.9 us
  waiting for transfers between devices  25.9 us (42%)
  starting transfers between devices  19.1 us (31%)
  Pallas kernels  15.8 us (25%)
  between operations  0.78 us (1%)
    ppermute x16, waiting for transfers between devices, swap(): lax.ppermute(block, axis, [(i, j) for i, j in pairs] + [(j, i) for i, j i...  25.9 us
    ppermute x16, starting transfers between devices, swap(): lax.ppermute(block, axis, [(i, j) for i, j in pairs] + [(j, i) for i, j i...  19.1 us
    pallas_call x1, Pallas kernels, frame_grads(): pl.pallas_call(frame_kernel, out_shape=(shape, shape, shape), compiler_pa...  5.58 us
    pallas_call x2, Pallas kernels, split(): pl.pallas_call(functools.partial(split_kernel, n, span), in_specs=[hbm] *...  4.17 us
    pallas_call x2, Pallas kernels, clip_grads(): pl.pallas_call(functools.partial(clip_kernel, window, heads), out_shape=[...  3.8 us
    pallas_call x2, Pallas kernels, join(): pl.pallas_call(functools.partial(join_kernel, n, span), in_specs=[vmem] *...  2.01 us
  transfers between devices with their start and end apart: 16, of which 7 were waited for; matrix products, arithmetic and copies ran while one was open for 0% of the time, Pallas kernels for 21%

profile of v7, /device:TPU:19, one launch (start us, length us, event | category | flops | bytes accessed | tf_op | source)
XLA Modules:
  0.0 61.9 jit_solution(7996945987982462722)
XLA Ops:
  0.6 2.1 %pack.3 = (bf16[2,288,128]{2,1,0:T(8,128)(2,1)}, bf16[2,288,128]{2,1,0:T(8,128)(2,1)}, bf16[2,288,128]{2,1,0:T(8,128)(2,1)}, bf16[2,288,128]{2,1,0:T(8,128)(2,1)}) custom-call(bf16[1,576,256]{2,1,0:T(8,128)(2,1)} %bitcast.18, bf16[1,576,256]{2,1,0:T(8,128)(2,1)} %bitcast.20, bf16[1,576,256]{2,1,0:T(8,128)(2,1)} %bitcast.22, bf16[1,576,256]{2,1,0:T(8,128)(2,1)} %bitcast.24), custom_call_target="tpu_custom_call" | custom-call | tf_op jit(solution)/shard_map/pack/pallas_call | solution.py:106
  2.7 0.1 collective-permute-start
  2.9 1.3 %collective-permute-start.9 = (bf16[2,288,128]{2,1,0:T(8,128)(2,1)}, bf16[2,288,128]{2,1,0:T(8,128)(2,1)S(1)}, u32[]{:S(2)}, u32[]{:S(2)}) collective-permute-start(bf16[2,288,128]{2,1,0:T(8,128)(2,1)} %get-tuple-element.61), channel_id=1, source_target_pairs={{0,1},{2,3},{1,0},{3,2},{4,5},{6,7},{5,4},{7,6},{8,9},{10,11},{9,8... | collective-permute-start | bytes 442376 | tf_op jit(solution)/shard_map/ppermute | solution.py:123
  4.2 1.3 %collective-permute-start.10 = (bf16[2,288,128]{2,1,0:T(8,128)(2,1)}, bf16[2,288,128]{2,1,0:T(8,128)(2,1)S(1)}, u32[]{:S(2)}, u32[]{:S(2)}) collective-permute-start(bf16[2,288,128]{2,1,0:T(8,128)(2,1)} %get-tuple-element.63), channel_id=1, source_target_pairs={{0,3},{1,2},{3,0},{2,1},{4,7},{5,6},{7,4},{6,5},{8,11},{9,10},{11,... | collective-permute-start | bytes 442376 | tf_op jit(solution)/shard_map/ppermute | solution.py:123
  5.4 2.1 %pack.2 = (bf16[2,288,128]{2,1,0:T(8,128)(2,1)}, bf16[2,288,128]{2,1,0:T(8,128)(2,1)}, bf16[2,288,128]{2,1,0:T(8,128)(2,1)}, bf16[2,288,128]{2,1,0:T(8,128)(2,1)}) custom-call(bf16[1,576,256]{2,1,0:T(8,128)(2,1)} %bitcast.19, bf16[1,576,256]{2,1,0:T(8,128)(2,1)} %bitcast.21, bf16[1,576,256]{2,1,0:T(8,128)(2,1)} %bitcast.23, bf16[1,576,256]{2,1,0:T(8,128)(2,1)} %bitcast.25), custom_call_target="tpu_custom_call" | custom-call | tf_op jit(solution)/shard_map/pack/pallas_call | solution.py:106
  7.5 2.3 %collective-permute-start.1 = (bf16[2,288,128]{2,1,0:T(8,128)(2,1)}, bf16[2,288,128]{2,1,0:T(8,128)(2,1)S(1)}, u32[]{:S(2)}, u32[]{:S(2)}) collective-permute-start(bf16[2,288,128]{2,1,0:T(8,128)(2,1)} %get-tuple-element.51), channel_id=1, source_target_pairs={{0,1},{2,3},{1,0},{3,2},{4,5},{6,7},{5,4},{7,6},{8,9},{10,11},{9,8... | collective-permute-start | bytes 442376 | tf_op jit(solution)/shard_map/ppermute | solution.py:123
  9.8 0.0 copy-start.4
  9.8 0.0 copy-start.3
  9.8 0.0 copy-start.2
  9.8 0.0 copy-start.1
  9.8 5.6 %space.1 = (bf16[1,576,256]{2,1,0:T(8,128)(2,1)}, bf16[1,576,256]{2,1,0:T(8,128)(2,1)}, bf16[1,576,256]{2,1,0:T(8,128)(2,1)}) custom-call(bf16[1,576,256]{2,1,0:T(8,128)(2,1)} %bitcast.29, bf16[1,576,256]{2,1,0:T(8,128)(2,1)} %bitcast.30, bf16[1,576,256]{2,1,0:T(8,128)(2,1)} %bitcast.31, bf16[1,576,256]{2,1,0:T(8,128)(2,1)} %bitcast.32), custom_call_target="tpu_custom_call" | custom-call | flops 1610612736 | bytes 2064384 | tf_op jit(solution)/shard_map/space/pallas_call | solution.py:64
  15.4 0.0 copy-done.4
  15.4 0.1 select_reduce_fusion.2
  15.5 0.0 collective-permute-done.refs_2_
  15.5 0.0 copy-done.3
  15.5 0.1 collective-permute-start.2
  15.6 0.0 copy-done.2
  15.6 1.2 %collective-permute-start.3 = (bf16[2,288,128]{2,1,0:T(8,128)(2,1)S(1)}, bf16[2,288,128]{2,1,0:T(8,128)(2,1)S(1)}, u32[]{:S(2)}, u32[]{:S(2)}) collective-permute-start(bf16[2,288,128]{2,1,0:T(8,128)(2,1)S(1)} %copy-done.2), channel_id=1, source_target_pairs={{0,3},{1,2},{3,0},{2,1},{4,7},{5,6},{7,4},{6,5},{8,11},{9,10},{11,... | collective-permute-start | bytes 442376 | tf_op jit(solution)/shard_map/ppermute | solution.py:123
  16.8 0.0 collective-permute-done.9.refs_1_
  16.8 2.4 %collective-permute-done.10.refs_3_ = bf16[2,288,128]{2,1,0:T(8,128)(2,1)S(1)} collective-permute-done((bf16[2,288,128]{2,1,0:T(8,128)(2,1)}, bf16[2,288,128]{2,1,0:T(8,128)(2,1)S(1)}, u32[]{:S(2)}, u32[]{:S(2)}) %collective-permute-start.10) | collective-permute-done | bytes 147488 | tf_op jit(solution)/shard_map/ppermute | solution.py:123
  19.2 0.0 copy-done.1
  19.2 0.0 copy-start
  19.2 0.1 sides.3
  19.3 0.7 %collective-permute-start.11 = (bf16[3,2,288,128]{3,2,1,0:T(8,128)(2,1)S(1)}, bf16[3,2,288,128]{3,2,1,0:T(8,128)(2,1)S(1)}, u32[]{:S(2)}, u32[]{:S(2)}) collective-permute-start(bf16[3,2,288,128]{3,2,1,0:T(8,128)(2,1)S(1)} %get-tuple-element.64), channel_id=1, source_target_pairs={{0,4},{8,12},{16,20},{24,28},{4,0},{12,8},{20,16},{28,24},{1,5},{9... | collective-permute-start | bytes 1327112 | tf_op jit(solution)/shard_map/ppermute | solution.py:123
  20.1 3.0 %collective-permute-start.12 = (bf16[3,2,288,128]{3,2,1,0:T(8,128)(2,1)S(1)}, bf16[3,2,288,128]{3,2,1,0:T(8,128)(2,1)S(1)}, u32[]{:S(2)}, u32[]{:S(2)}) collective-permute-start(bf16[3,2,288,128]{3,2,1,0:T(8,128)(2,1)S(1)} %get-tuple-element.65), channel_id=1, source_target_pairs={{4,8},{12,16},{20,24},{8,4},{16,12},{24,20},{5,9},{13,17},{21,25},... | collective-permute-start | bytes 1327112 | tf_op jit(solution)/shard_map/ppermute | solution.py:123
  23.1 0.2 select_reduce_fusion.1
  23.3 0.0 collective-permute-done.1.refs_1_
  23.3 1.4 %collective-permute-done.2.refs_2_ = bf16[2,288,128]{2,1,0:T(8,128)(2,1)S(1)} collective-permute-done((bf16[2,288,128]{2,1,0:T(8,128)(2,1)S(1)}, bf16[2,288,128]{2,1,0:T(8,128)(2,1)S(1)}, u32[]{:S(2)}, u32[]{:S(2)}) %collective-permute-start.2) | collective-permute-done | bytes 147488 | tf_op jit(solution)/shard_map/ppermute | solution.py:123
  24.7 7.1 %collective-permute-done.3.refs_3_ = bf16[2,288,128]{2,1,0:T(8,128)(2,1)S(1)} collective-permute-done((bf16[2,288,128]{2,1,0:T(8,128)(2,1)S(1)}, bf16[2,288,128]{2,1,0:T(8,128)(2,1)S(1)}, u32[]{:S(2)}, u32[]{:S(2)}) %collective-permute-start.3) | collective-permute-done | bytes 147488 | tf_op jit(solution)/shard_map/ppermute | solution.py:123
  31.8 0.0 copy-done
  31.8 0.1 sides.2
  31.9 0.6 %collective-permute-start.4 = (bf16[3,2,288,128]{3,2,1,0:T(8,128)(2,1)S(1)}, bf16[3,2,288,128]{3,2,1,0:T(8,128)(2,1)S(1)}, u32[]{:S(2)}, u32[]{:S(2)}) collective-permute-start(bf16[3,2,288,128]{3,2,1,0:T(8,128)(2,1)S(1)} %get-tuple-element.54), channel_id=1, source_target_pairs={{0,4},{8,12},{16,20},{24,28},{4,0},{12,8},{20,16},{28,24},{1,5},{9... | collective-permute-start | bytes 1327112 | tf_op jit(solution)/shard_map/ppermute | solution.py:123
  32.5 3.0 %collective-permute-start.5 = (bf16[3,2,288,128]{3,2,1,0:T(8,128)(2,1)S(1)}, bf16[3,2,288,128]{3,2,1,0:T(8,128)(2,1)S(1)}, u32[]{:S(2)}, u32[]{:S(2)}) collective-permute-start(bf16[3,2,288,128]{3,2,1,0:T(8,128)(2,1)S(1)} %get-tuple-element.55), channel_id=1, source_target_pairs={{4,8},{12,16},{20,24},{8,4},{16,12},{24,20},{5,9},{13,17},{21,25},... | collective-permute-start | bytes 1327112 | tf_op jit(solution)/shard_map/ppermute | solution.py:123
  35.6 0.0 collective-permute-done.11.refs_4_
  35.6 0.0 collective-permute-done.12.refs_5_
  35.6 1.9 %clips.3 = (bf16[432,128]{1,0:T(8,128)(2,1)S(1)}, bf16[432,128]{1,0:T(8,128)(2,1)S(1)}, bf16[432,128]{1,0:T(8,128)(2,1)S(1)}, bf16[432,128]{1,0:T(8,128)(2,1)S(1)}) custom-call(s32[2,10]{1,0:T(2,128)S(1)} %pad_add_fusion.given_bounds, bf16[2,288,128]{2,1,0:T(8,128)(2,1)S(1)} %copy-done.1, bf16[2,288,128]{2,1,0:T(8,128)(2,1)S(1)} %collective-permute-done.9.refs_1_, ...), custom_call_target="tpu_custom_call" | custom-call | flops 589824000 | bytes 1474560 | tf_op jit(solution)/shard_map/clips/pallas_call | solution.py:323
  37.5 1.2 %collective-permute-start.13 = (bf16[432,128]{1,0:T(8,128)(2,1)S(1)}, bf16[432,128]{1,0:T(8,128)(2,1)S(1)}, u32[]{:S(2)}, u32[]{:S(2)}) collective-permute-start(bf16[432,128]{1,0:T(8,128)(2,1)S(1)} %get-tuple-element.67), channel_id=1, source_target_pairs={{0,1},{2,3},{1,0},{3,2},{4,5},{6,7},{5,4},{7,6},{8,9},{10,11},{9,8... | collective-permute-start | bytes 331784 | tf_op jit(solution)/shard_map/ppermute | solution.py:123
  38.8 0.0 collective-permute-start.14
  38.8 1.5 %collective-permute-start.15 = (bf16[432,128]{1,0:T(8,128)(2,1)S(1)}, bf16[432,128]{1,0:T(8,128)(2,1)S(1)}, u32[]{:S(2)}, u32[]{:S(2)}) collective-permute-start(bf16[432,128]{1,0:T(8,128)(2,1)S(1)} %get-tuple-element.69), channel_id=1, source_target_pairs={{0,3},{1,2},{3,0},{2,1},{4,7},{5,6},{7,4},{6,5},{8,11},{9,10},{11,... | collective-permute-start | bytes 331784 | tf_op jit(solution)/shard_map/ppermute | solution.py:123
  40.2 0.0 collective-permute-done.4.refs_4_
  40.3 6.9 %collective-permute-done.5.refs_5_ = bf16[3,2,288,128]{3,2,1,0:T(8,128)(2,1)S(1)} collective-permute-done((bf16[3,2,288,128]{3,2,1,0:T(8,128)(2,1)S(1)}, bf16[3,2,288,128]{3,2,1,0:T(8,128)(2,1)S(1)}, u32[]{:S(2)}, u32[]{:S(2)}) %collective-permute-start.5) | collective-permute-done | bytes 442400 | tf_op jit(solution)/shard_map/ppermute | solution.py:123
  47.2 1.9 %clips.2 = (bf16[432,128]{1,0:T(8,128)(2,1)S(1)}, bf16[432,128]{1,0:T(8,128)(2,1)S(1)}, bf16[432,128]{1,0:T(8,128)(2,1)S(1)}, bf16[432,128]{1,0:T(8,128)(2,1)S(1)}) custom-call(s32[2,10]{1,0:T(2,128)S(1)} %pad_add_fusion.given_bounds, bf16[2,288,128]{2,1,0:T(8,128)(2,1)S(1)} %copy-done, bf16[2,288,128]{2,1,0:T(8,128)(2,1)S(1)} %collective-permute-done.1.refs_1_, ...), custom_call_target="tpu_custom_call" | custom-call | flops 589824000 | bytes 1474560 | tf_op jit(solution)/shard_map/clips/pallas_call | solution.py:323
  49.1 0.1 collective-permute-start.6
  49.2 0.4 collective-permute-start.7
  49.6 0.0 collective-permute-done.13.refs_1_
  49.6 2.2 %collective-permute-start.8 = (bf16[432,128]{1,0:T(8,128)(2,1)S(1)}, bf16[432,128]{1,0:T(8,128)(2,1)S(1)}, u32[]{:S(2)}, u32[]{:S(2)}) collective-permute-start(bf16[432,128]{1,0:T(8,128)(2,1)S(1)} %get-tuple-element.59), channel_id=1, source_target_pairs={{0,3},{1,2},{3,0},{2,1},{4,7},{5,6},{7,4},{6,5},{8,11},{9,10},{11,... | collective-permute-start | bytes 331784 | tf_op jit(solution)/shard_map/ppermute | solution.py:123
  51.8 0.0 collective-permute-done.14.refs_2_
  51.8 0.0 collective-permute-done.15.refs_3_
  51.8 1.0 %unpack.2 = (bf16[1,576,256]{2,1,0:T(8,128)(2,1)}, bf16[1,576,256]{2,1,0:T(8,128)(2,1)}, bf16[1,576,256]{2,1,0:T(8,128)(2,1)}) custom-call(bf16[432,128]{1,0:T(8,128)(2,1)S(1)} %get-tuple-element.66.refs_0_, bf16[432,128]{1,0:T(8,128)(2,1)S(1)} %collective-permute-done.13.refs_1_, bf16[432,128]{1,0:T(8,128)(2,1)S(1)} %collective-permute-done.14.refs_2_, ...), custom_call_target="tpu_custom_call" | custom-call | tf_op jit(solution)/shard_map/unpack/pallas_call | solution.py:204
  52.8 1.2 %collective-permute-done.6.refs_1_ = bf16[432,128]{1,0:T(8,128)(2,1)S(1)} collective-permute-done((bf16[432,128]{1,0:T(8,128)(2,1)S(1)}, bf16[432,128]{1,0:T(8,128)(2,1)S(1)}, u32[]{:S(2)}, u32[]{:S(2)}) %collective-permute-start.6) | collective-permute-done | bytes 110624 | tf_op jit(solution)/shard_map/ppermute | solution.py:123
  54.0 1.1 %collective-permute-done.7.refs_2_ = bf16[432,128]{1,0:T(8,128)(2,1)S(1)} collective-permute-done((bf16[432,128]{1,0:T(8,128)(2,1)S(1)}, bf16[432,128]{1,0:T(8,128)(2,1)S(1)}, u32[]{:S(2)}, u32[]{:S(2)}) %collective-permute-start.7) | collective-permute-done | bytes 110624 | tf_op jit(solution)/shard_map/ppermute | solution.py:123
  55.1 5.8 %collective-permute-done.8.refs_3_ = bf16[432,128]{1,0:T(8,128)(2,1)S(1)} collective-permute-done((bf16[432,128]{1,0:T(8,128)(2,1)S(1)}, bf16[432,128]{1,0:T(8,128)(2,1)S(1)}, u32[]{:S(2)}, u32[]{:S(2)}) %collective-permute-start.8) | collective-permute-done | bytes 110624 | tf_op jit(solution)/shard_map/ppermute | solution.py:123
  60.8 1.0 %unpack.3 = (bf16[1,576,256]{2,1,0:T(8,128)(2,1)}, bf16[1,576,256]{2,1,0:T(8,128)(2,1)}, bf16[1,576,256]{2,1,0:T(8,128)(2,1)}) custom-call(bf16[432,128]{1,0:T(8,128)(2,1)S(1)} %get-tuple-element.56.refs_0_, bf16[432,128]{1,0:T(8,128)(2,1)S(1)} %collective-permute-done.6.refs_1_, ...), custom_call_target="tpu_custom_call", output_to_operand_aliasing={{0}: (4, {}), {1}: (5, {}), {2}: (6, {})} | custom-call | tf_op jit(solution)/shard_map/unpack/pallas_call | solution.py:204
  (4 shorter events, 0.0 us)
Async XLA Ops:
  2.7 12.8 %collective-permute-start = (bf16[2,288,128]{2,1,0:T(8,128)(2,1)}, bf16[2,288,128]{2,1,0:T(8,128)(2,1)S(1)}, u32[]{:S(2)}, u32[]{:S(2)}) collective-permute-start(bf16[2,288,128]{2,1,0:T(8,128)(2,1)} %get-tuple-element.43), channel_id=1, source_target_pairs={{0,2},{1,3},{2,0},{3,1},{4,6},{5,7},{6,4},{7,5},{8,10},{9,11},{10,... | collective-permute-start | bytes 442376 | tf_op jit(solution)/shard_map/ppermute | solution.py:123
  2.9 13.9 %collective-permute-start.9 = (bf16[2,288,128]{2,1,0:T(8,128)(2,1)}, bf16[2,288,128]{2,1,0:T(8,128)(2,1)S(1)}, u32[]{:S(2)}, u32[]{:S(2)}) collective-permute-start(bf16[2,288,128]{2,1,0:T(8,128)(2,1)} %get-tuple-element.61), channel_id=1, source_target_pairs={{0,1},{2,3},{1,0},{3,2},{4,5},{6,7},{5,4},{7,6},{8,9},{10,11},{9,8... | collective-permute-start | bytes 442376 | tf_op jit(solution)/shard_map/ppermute | solution.py:123
  4.2 15.0 %collective-permute-start.10 = (bf16[2,288,128]{2,1,0:T(8,128)(2,1)}, bf16[2,288,128]{2,1,0:T(8,128)(2,1)S(1)}, u32[]{:S(2)}, u32[]{:S(2)}) collective-permute-start(bf16[2,288,128]{2,1,0:T(8,128)(2,1)} %get-tuple-element.63), channel_id=1, source_target_pairs={{0,3},{1,2},{3,0},{2,1},{4,7},{5,6},{7,4},{6,5},{8,11},{9,10},{11,... | collective-permute-start | bytes 442376 | tf_op jit(solution)/shard_map/ppermute | solution.py:123
  7.5 15.7 %collective-permute-start.1 = (bf16[2,288,128]{2,1,0:T(8,128)(2,1)}, bf16[2,288,128]{2,1,0:T(8,128)(2,1)S(1)}, u32[]{:S(2)}, u32[]{:S(2)}) collective-permute-start(bf16[2,288,128]{2,1,0:T(8,128)(2,1)} %get-tuple-element.51), channel_id=1, source_target_pairs={{0,1},{2,3},{1,0},{3,2},{4,5},{6,7},{5,4},{7,6},{8,9},{10,11},{9,8... | collective-permute-start | bytes 442376 | tf_op jit(solution)/shard_map/ppermute | solution.py:123
  9.8 5.6 %copy-start.4 = (s32[16]{0:T(128)S(1)}, s32[16]{0:T(128)}, u32[]{:S(2)}) copy-start(s32[16]{0:T(128)} %param.17) | copy-start | bytes 196
  9.8 5.7 %copy-start.3 = (bf16[2,288,128]{2,1,0:T(8,128)(2,1)S(1)}, bf16[2,288,128]{2,1,0:T(8,128)(2,1)}, u32[]{:S(2)}) copy-start(bf16[2,288,128]{2,1,0:T(8,128)(2,1)} %get-tuple-element.52) | copy-start | bytes 442372
  9.8 5.8 %copy-start.2 = (bf16[2,288,128]{2,1,0:T(8,128)(2,1)S(1)}, bf16[2,288,128]{2,1,0:T(8,128)(2,1)}, u32[]{:S(2)}) copy-start(bf16[2,288,128]{2,1,0:T(8,128)(2,1)} %get-tuple-element.53) | copy-start | bytes 442372
  9.8 9.4 %copy-start.1 = (bf16[2,288,128]{2,1,0:T(8,128)(2,1)S(1)}, bf16[2,288,128]{2,1,0:T(8,128)(2,1)}, u32[]{:S(2)}) copy-start(bf16[2,288,128]{2,1,0:T(8,128)(2,1)} %get-tuple-element.60.refs_0_) | copy-start | bytes 442372
  15.5 9.2 %collective-permute-start.2 = (bf16[2,288,128]{2,1,0:T(8,128)(2,1)S(1)}, bf16[2,288,128]{2,1,0:T(8,128)(2,1)S(1)}, u32[]{:S(2)}, u32[]{:S(2)}) collective-permute-start(bf16[2,288,128]{2,1,0:T(8,128)(2,1)S(1)} %copy-done.3), channel_id=1, source_target_pairs={{0,2},{1,3},{2,0},{3,1},{4,6},{5,7},{6,4},{7,5},{8,10},{9,11},{10,... | collective-permute-start | bytes 442376 | tf_op jit(solution)/shard_map/ppermute | solution.py:123
  15.6 16.2 %collective-permute-start.3 = (bf16[2,288,128]{2,1,0:T(8,128)(2,1)S(1)}, bf16[2,288,128]{2,1,0:T(8,128)(2,1)S(1)}, u32[]{:S(2)}, u32[]{:S(2)}) collective-permute-start(bf16[2,288,128]{2,1,0:T(8,128)(2,1)S(1)} %copy-done.2), channel_id=1, source_target_pairs={{0,3},{1,2},{3,0},{2,1},{4,7},{5,6},{7,4},{6,5},{8,11},{9,10},{11,... | collective-permute-start | bytes 442376 | tf_op jit(solution)/shard_map/ppermute | solution.py:123
  19.2 12.6 %copy-start = (bf16[2,288,128]{2,1,0:T(8,128)(2,1)S(1)}, bf16[2,288,128]{2,1,0:T(8,128)(2,1)}, u32[]{:S(2)}) copy-start(bf16[2,288,128]{2,1,0:T(8,128)(2,1)} %get-tuple-element.50.refs_0_) | copy-start | bytes 442372
  19.3 16.3 %collective-permute-start.11 = (bf16[3,2,288,128]{3,2,1,0:T(8,128)(2,1)S(1)}, bf16[3,2,288,128]{3,2,1,0:T(8,128)(2,1)S(1)}, u32[]{:S(2)}, u32[]{:S(2)}) collective-permute-start(bf16[3,2,288,128]{3,2,1,0:T(8,128)(2,1)S(1)} %get-tuple-element.64), channel_id=1, source_target_pairs={{0,4},{8,12},{16,20},{24,28},{4,0},{12,8},{20,16},{28,24},{1,5},{9... | collective-permute-start | bytes 1327112 | tf_op jit(solution)/shard_map/ppermute | solution.py:123
  20.1 15.5 %collective-permute-start.12 = (bf16[3,2,288,128]{3,2,1,0:T(8,128)(2,1)S(1)}, bf16[3,2,288,128]{3,2,1,0:T(8,128)(2,1)S(1)}, u32[]{:S(2)}, u32[]{:S(2)}) collective-permute-start(bf16[3,2,288,128]{3,2,1,0:T(8,128)(2,1)S(1)} %get-tuple-element.65), channel_id=1, source_target_pairs={{4,8},{12,16},{20,24},{8,4},{16,12},{24,20},{5,9},{13,17},{21,25},... | collective-permute-start | bytes 1327112 | tf_op jit(solution)/shard_map/ppermute | solution.py:123
  31.9 8.3 %collective-permute-start.4 = (bf16[3,2,288,128]{3,2,1,0:T(8,128)(2,1)S(1)}, bf16[3,2,288,128]{3,2,1,0:T(8,128)(2,1)S(1)}, u32[]{:S(2)}, u32[]{:S(2)}) collective-permute-start(bf16[3,2,288,128]{3,2,1,0:T(8,128)(2,1)S(1)} %get-tuple-element.54), channel_id=1, source_target_pairs={{0,4},{8,12},{16,20},{24,28},{4,0},{12,8},{20,16},{28,24},{1,5},{9... | collective-permute-start | bytes 1327112 | tf_op jit(solution)/shard_map/ppermute | solution.py:123
  32.5 14.6 %collective-permute-start.5 = (bf16[3,2,288,128]{3,2,1,0:T(8,128)(2,1)S(1)}, bf16[3,2,288,128]{3,2,1,0:T(8,128)(2,1)S(1)}, u32[]{:S(2)}, u32[]{:S(2)}) collective-permute-start(bf16[3,2,288,128]{3,2,1,0:T(8,128)(2,1)S(1)} %get-tuple-element.55), channel_id=1, source_target_pairs={{4,8},{12,16},{20,24},{8,4},{16,12},{24,20},{5,9},{13,17},{21,25},... | collective-permute-start | bytes 1327112 | tf_op jit(solution)/shard_map/ppermute | solution.py:123
  37.5 12.1 %collective-permute-start.13 = (bf16[432,128]{1,0:T(8,128)(2,1)S(1)}, bf16[432,128]{1,0:T(8,128)(2,1)S(1)}, u32[]{:S(2)}, u32[]{:S(2)}) collective-permute-start(bf16[432,128]{1,0:T(8,128)(2,1)S(1)} %get-tuple-element.67), channel_id=1, source_target_pairs={{0,1},{2,3},{1,0},{3,2},{4,5},{6,7},{5,4},{7,6},{8,9},{10,11},{9,8... | collective-permute-start | bytes 331784 | tf_op jit(solution)/shard_map/ppermute | solution.py:123
  38.8 13.0 %collective-permute-start.14 = (bf16[432,128]{1,0:T(8,128)(2,1)S(1)}, bf16[432,128]{1,0:T(8,128)(2,1)S(1)}, u32[]{:S(2)}, u32[]{:S(2)}) collective-permute-start(bf16[432,128]{1,0:T(8,128)(2,1)S(1)} %get-tuple-element.68), channel_id=1, source_target_pairs={{0,2},{1,3},{2,0},{3,1},{4,6},{5,7},{6,4},{7,5},{8,10},{9,11},{10,... | collective-permute-start | bytes 331784 | tf_op jit(solution)/shard_map/ppermute | solution.py:123
  38.8 13.0 %collective-permute-start.15 = (bf16[432,128]{1,0:T(8,128)(2,1)S(1)}, bf16[432,128]{1,0:T(8,128)(2,1)S(1)}, u32[]{:S(2)}, u32[]{:S(2)}) collective-permute-start(bf16[432,128]{1,0:T(8,128)(2,1)S(1)} %get-tuple-element.69), channel_id=1, source_target_pairs={{0,3},{1,2},{3,0},{2,1},{4,7},{5,6},{7,4},{6,5},{8,11},{9,10},{11,... | collective-permute-start | bytes 331784 | tf_op jit(solution)/shard_map/ppermute | solution.py:123
  49.1 4.9 %collective-permute-start.6 = (bf16[432,128]{1,0:T(8,128)(2,1)S(1)}, bf16[432,128]{1,0:T(8,128)(2,1)S(1)}, u32[]{:S(2)}, u32[]{:S(2)}) collective-permute-start(bf16[432,128]{1,0:T(8,128)(2,1)S(1)} %get-tuple-element.57), channel_id=1, source_target_pairs={{0,1},{2,3},{1,0},{3,2},{4,5},{6,7},{5,4},{7,6},{8,9},{10,11},{9,8... | collective-permute-start | bytes 331784 | tf_op jit(solution)/shard_map/ppermute | solution.py:123
  49.2 5.9 %collective-permute-start.7 = (bf16[432,128]{1,0:T(8,128)(2,1)S(1)}, bf16[432,128]{1,0:T(8,128)(2,1)S(1)}, u32[]{:S(2)}, u32[]{:S(2)}) collective-permute-start(bf16[432,128]{1,0:T(8,128)(2,1)S(1)} %get-tuple-element.58), channel_id=1, source_target_pairs={{0,2},{1,3},{2,0},{3,1},{4,6},{5,7},{6,4},{7,5},{8,10},{9,11},{10,... | collective-permute-start | bytes 331784 | tf_op jit(solution)/shard_map/ppermute | solution.py:123
  49.6 11.3 %collective-permute-start.8 = (bf16[432,128]{1,0:T(8,128)(2,1)S(1)}, bf16[432,128]{1,0:T(8,128)(2,1)S(1)}, u32[]{:S(2)}, u32[]{:S(2)}) collective-permute-start(bf16[432,128]{1,0:T(8,128)(2,1)S(1)} %get-tuple-element.59), channel_id=1, source_target_pairs={{0,3},{1,2},{3,0},{2,1},{4,7},{5,6},{7,4},{6,5},{8,11},{9,10},{11,... | collective-permute-start | bytes 331784 | tf_op jit(solution)/shard_map/ppermute | solution.py:123

commit v8 on v7

--- a/solution.py
+++ b/solution.py
@@ -13,6 +13,7 @@
 WIDTH = HEADS * HDIM
 SCALING = 1.0 / math.sqrt(HDIM)
 CHUNKS = (4, 4)
+PARTS = 2
 masked_score = -1e30
 
 
@@ -76,25 +77,32 @@
 
 def split_kernel(n, span, *refs):
     ins, outs, (loaded, held, arrived, left_off) = refs[:4], refs[4 : 4 + n], refs[-4:]
-    loads = [
-        pltpu.make_async_copy(array.at[0, span, :], loaded.at[i], arrived.at[i])
-        for i, array in enumerate(ins)
-    ]
-    for copy in loads:
-        copy.start()
+    count = (span.stop - span.start) // PARTS
     places = ins[0].shape[2] // n
-    stores = []
-    for at in range(2):
-        loads[2 * at].wait()
-        loads[2 * at + 1].wait()
-        for target in range(n):
-            lanes = slice(target * places, (target + 1) * places)
-            both = [loaded[2 * at, :, lanes], loaded[2 * at + 1, :, lanes]]
-            held[at, target] = jnp.concatenate(both, axis=1)
-        for step, out in enumerate(outs):
-            block = held.at[at, lax.axis_index("seq") ^ step]
-            stores.append(pltpu.make_async_copy(block, out.at[at], left_off.at[at, step]))
-            stores[-1].start()
+    loads, stores = [], []
+    for part in range(PARTS):
+        rows = slice(part * count, (part + 1) * count)
+        given = slice(span.start + rows.start, span.start + rows.stop)
+        for i, array in enumerate(ins):
+            copy = pltpu.make_async_copy(
+                array.at[0, given, :], loaded.at[i, rows, :], arrived.at[part, i]
+            )
+            copy.start()
+            loads.append(copy)
+    for part in range(PARTS):
+        rows = slice(part * count, (part + 1) * count)
+        for at in range(2):
+            for i in (2 * at, 2 * at + 1):
+                loads[4 * part + i].wait()
+            for target in range(n):
+                lanes = slice(target * places, (target + 1) * places)
+                both = [loaded[2 * at, rows, lanes], loaded[2 * at + 1, rows, lanes]]
+                held[at, target, rows, :] = jnp.concatenate(both, axis=1)
+            for step, out in enumerate(outs):
+                block = held.at[at, lax.axis_index("seq") ^ step, rows, :]
+                copy = pltpu.make_async_copy(block, out.at[at, rows, :], left_off.at[part, at, step])
+                copy.start()
+                stores.append(copy)
     for copy in stores:
         copy.wait()
 
@@ -111,8 +119,8 @@
         scratch_shapes=[
             pltpu.VMEM((4, rows, tokens), jnp.bfloat16),
             pltpu.VMEM((2, n, *shape[1:]), jnp.bfloat16),
-            pltpu.SemaphoreType.DMA((4,)),
-            pltpu.SemaphoreType.DMA((2, n)),
+            pltpu.SemaphoreType.DMA((PARTS, 4)),
+            pltpu.SemaphoreType.DMA((PARTS, 2, n)),
         ],
         compiler_params=pltpu.CompilerParams(vmem_limit_bytes=60 * 2**20),
         name="pack",
@@ -137,7 +145,7 @@
     is_odd = lax.axis_index("grp") & 1
     for step, ref in enumerate(ins):
         frame = (lax.axis_index("seq") ^ step)
-        for start, out in enumerate(outs):
+        for start, out in zip((1, 0), outs):
             at = frame - jnp.where(is_odd == start, 1, 0)
 
             @pl.when((at >= 0) & (at < n - 1))
@@ -159,24 +167,27 @@
     )(*blocks)
 
 
+def gated(values, *earlier):
+    return lax.optimization_barrier((values, *earlier))
+
+
 def neighbours(blocks):
     count = lax.axis_size("grp")
-    moved = list(blocks)
-    for start in (1, 0):
-        moved[start] = swap(blocks[start], "grp", [(i, i + 1) for i in range(start, count - 1, 2)])
-    return moved
-
-
-def join_kernel(n, span, *refs):
-    ins, outs, (held, ready, left_off) = refs[:n], refs[-6:-3], refs[-3:]
+    pairs = [[(i, i + 1) for i in range(start, count - 1, 2)] for start in (1, 0)]
+    return [swap(block, "grp", links) for block, links in zip(blocks, pairs)]
+
+
+def join_kernel(near, far, span, *refs):
+    ins, outs, (held, ready, left_off) = refs[:near], refs[-6:-3], refs[-3:]
+    place = lax.axis_index("seq")
     for step, ref in enumerate(ins):
-        held[(lax.axis_index("seq") ^ step)] = ref[...]
+        held[(place ^ step) & (near - 1)] = ref[...]
     count = span.stop - span.start
     half = count // 2
     places = held.shape[2] // 2
 
     def gather(rows, lanes):
-        return jnp.concatenate([held[source, rows, lanes] for source in range(n)], axis=1)
+        return jnp.concatenate([held[source, rows, lanes] for source in range(near)], axis=1)
 
     left, right = slice(0, places), slice(places, 2 * places)
     rest = slice(count, count + half)
@@ -184,8 +195,10 @@
     ready[2] = gather(slice(0, count), right)
     ready[0, :half, :] = gather(rest, left)
     ready[0, half:, :] = gather(rest, right)
+    width = near * places
+    tokens = pl.ds(pl.multiple_of((place // near ^ far) * width, width), width)
     copies = [
-        pltpu.make_async_copy(ready.at[i], out.at[0, span, :], left_off.at[i])
+        pltpu.make_async_copy(ready.at[i], out.at[0, span, tokens], left_off.at[i])
         for i, out in enumerate(outs)
     ]
     for copy in copies:
@@ -194,24 +207,25 @@
         copy.wait()
 
 
-def join(blocks, span, tokens, earlier):
-    n = len(blocks)
+def join(blocks, span, tokens, far, earlier):
+    near = len(blocks) // 2
+    blocks = blocks[near:] if far else blocks[:near]
     rows = span.stop - span.start
     shape = jax.ShapeDtypeStruct((1, WIDTH, tokens), jnp.bfloat16)
     vmem = pl.BlockSpec(memory_space=pltpu.VMEM)
     hbm = pl.BlockSpec(memory_space=pltpu.HBM)
     earlier = [] if earlier is None else list(earlier)
     return pl.pallas_call(
-        functools.partial(join_kernel, n, span),
-        in_specs=[vmem] * n + [hbm] * len(earlier),
+        functools.partial(join_kernel, near, far, span),
+        in_specs=[vmem] * near + [hbm] * len(earlier),
         out_specs=[hbm] * 3,
         out_shape=[shape] * 3,
         scratch_shapes=[
-            pltpu.VMEM((n, *blocks[0].shape), jnp.bfloat16),
-            pltpu.VMEM((3, rows, tokens), jnp.bfloat16),
+            pltpu.VMEM((near, *blocks[0].shape), jnp.bfloat16),
+            pltpu.VMEM((3, rows, tokens // 2), jnp.bfloat16),
             pltpu.SemaphoreType.DMA((3,)),
         ],
-        input_output_aliases={n + i: i for i in range(len(earlier))},
+        input_output_aliases={near + i: i for i in range(len(earlier))},
         compiler_params=pltpu.CompilerParams(vmem_limit_bytes=24 * 2**20),
         name="unpack",
     )(*blocks, *earlier)
@@ -238,7 +252,7 @@
         widen(ref, halo + (lax.axis_index("seq") ^ step))
     copy.wait()
     lowest, highest = bounds[0, halo], bounds[1, halo + window - 1]
-    for start, ref in enumerate(sides_of):
+    for start, ref in zip((1, 0), sides_of):
         is_next = (lax.axis_index("grp") & 1) == start
         for at in range(halo):
             frame = at + jnp.where(is_next, halo + window, 0)
@@ -374,9 +388,6 @@
     space_in = turned(q_space, k_space, v_space, cot_space)
     packed = [list(split(time, span, n)) for span in spans]
 
-    def gated(values, *earlier):
-        return lax.optimization_barrier((values, *earlier))
-
     own = [exchange(packed[0])]
     space = frame_grads(*space_in)
     packed[1][2:], own[0][2], space = gated(packed[1][2:], own[0][2], space)
@@ -386,7 +397,8 @@
     for blocks, near in zip(own, beside):
         back.append(exchange(clip_grads(bounds, blocks, near)))
     for span, blocks in zip(spans, back):
-        grads = join(blocks, span, tokens, grads)
+        for far in (1, 0):
+            grads = join(blocks, span, tokens, far, grads)
     return turned(*space, *grads)
 
 

time: 62.1 us -> 61.9 us (level)
  the two profiles are of different devices: /device:TPU:19 before, /device:TPU:0 now
where the time goes in v8:
time: 61.9 us; the launch traced here: 61.6 us
  starting transfers between devices  27.2 us (44%)
  Pallas kernels  17.9 us (29%)
  waiting for transfers between devices  15.4 us (25%)
  between operations  0.81 us (1%)
    ppermute x16, starting transfers between devices, swap(): lax.ppermute(block, axis, [(i, j) for i, j in pairs] + [(j, i) for i, j i...  27.2 us
    ppermute x16, waiting for transfers between devices, swap(): lax.ppermute(block, axis, [(i, j) for i, j in pairs] + [(j, i) for i, j i...  15.4 us
    pallas_call x1, Pallas kernels, frame_grads(): pl.pallas_call(frame_kernel, out_shape=(shape, shape, shape), compiler_pa...  5.59 us
    pallas_call x2, Pallas kernels, split(): pl.pallas_call(functools.partial(split_kernel, n, span), in_specs=[hbm] *...  4.46 us
    pallas_call x2, Pallas kernels, clip_grads(): pl.pallas_call(functools.partial(clip_kernel, window, heads), out_shape=[...  4.16 us
    pallas_call x4, Pallas kernels, join(): pl.pallas_call(functools.partial(join_kernel, near, far, span), in_specs=...  3.44 us
  transfers between devices with their start and end apart: 16, of which 4 were waited for; matrix products, arithmetic and copies ran while one was open for 0% of the time, Pallas kernels for 24%

profile of v8, /device:TPU:0, one launch (start us, length us, event | category | flops | bytes accessed | tf_op | source)
XLA Modules:
  0.0 61.6 jit_solution(12178828089674728672)
XLA Ops:
  0.6 2.2 %pack.3 = (bf16[2,288,128]{2,1,0:T(8,128)(2,1)}, bf16[2,288,128]{2,1,0:T(8,128)(2,1)}, bf16[2,288,128]{2,1,0:T(8,128)(2,1)}, bf16[2,288,128]{2,1,0:T(8,128)(2,1)}) custom-call(bf16[1,576,256]{2,1,0:T(8,128)(2,1)} %bitcast.21, bf16[1,576,256]{2,1,0:T(8,128)(2,1)} %bitcast.23, bf16[1,576,256]{2,1,0:T(8,128)(2,1)} %bitcast.25, bf16[1,576,256]{2,1,0:T(8,128)(2,1)} %bitcast.27), custom_call_target="tpu_custom_call" | custom-call | tf_op jit(solution)/shard_map/pack/pallas_call | solution.py:114
  2.9 4.1 %collective-permute-start = (bf16[2,288,128]{2,1,0:T(8,128)(2,1)}, bf16[2,288,128]{2,1,0:T(8,128)(2,1)S(1)}, u32[]{:S(2)}, u32[]{:S(2)}) collective-permute-start(bf16[2,288,128]{2,1,0:T(8,128)(2,1)} %get-tuple-element.49), channel_id=1, source_target_pairs={{0,2},{1,3},{2,0},{3,1},{4,6},{5,7},{6,4},{7,5},{8,10},{9,11},{10,... | collective-permute-start | bytes 442376 | tf_op jit(solution)/shard_map/ppermute | solution.py:131
  7.0 1.6 %collective-permute-start.9 = (bf16[2,288,128]{2,1,0:T(8,128)(2,1)}, bf16[2,288,128]{2,1,0:T(8,128)(2,1)S(1)}, u32[]{:S(2)}, u32[]{:S(2)}) collective-permute-start(bf16[2,288,128]{2,1,0:T(8,128)(2,1)} %get-tuple-element.67), channel_id=1, source_target_pairs={{0,1},{2,3},{1,0},{3,2},{4,5},{6,7},{5,4},{7,6},{8,9},{10,11},{9,8... | collective-permute-start | bytes 442376 | tf_op jit(solution)/shard_map/ppermute | solution.py:131
  8.6 0.0 collective-permute-start.10
  8.6 2.2 %pack.2 = (bf16[2,288,128]{2,1,0:T(8,128)(2,1)}, bf16[2,288,128]{2,1,0:T(8,128)(2,1)}, bf16[2,288,128]{2,1,0:T(8,128)(2,1)}, bf16[2,288,128]{2,1,0:T(8,128)(2,1)}) custom-call(bf16[1,576,256]{2,1,0:T(8,128)(2,1)} %bitcast.22, bf16[1,576,256]{2,1,0:T(8,128)(2,1)} %bitcast.24, bf16[1,576,256]{2,1,0:T(8,128)(2,1)} %bitcast.26, bf16[1,576,256]{2,1,0:T(8,128)(2,1)} %bitcast.28), custom_call_target="tpu_custom_call" | custom-call | tf_op jit(solution)/shard_map/pack/pallas_call | solution.py:114
  10.8 1.0 %collective-permute-start.1 = (bf16[2,288,128]{2,1,0:T(8,128)(2,1)}, bf16[2,288,128]{2,1,0:T(8,128)(2,1)S(1)}, u32[]{:S(2)}, u32[]{:S(2)}) collective-permute-start(bf16[2,288,128]{2,1,0:T(8,128)(2,1)} %get-tuple-element.57), channel_id=1, source_target_pairs={{0,1},{2,3},{1,0},{3,2},{4,5},{6,7},{5,4},{7,6},{8,9},{10,11},{9,8... | collective-permute-start | bytes 442376 | tf_op jit(solution)/shard_map/ppermute | solution.py:131
  11.8 0.0 copy-start.4
  11.8 0.0 copy-start.3
  11.8 0.0 copy-start.2
  11.8 0.0 copy-start.1
  11.8 5.6 %space.1 = (bf16[1,576,256]{2,1,0:T(8,128)(2,1)}, bf16[1,576,256]{2,1,0:T(8,128)(2,1)}, bf16[1,576,256]{2,1,0:T(8,128)(2,1)}) custom-call(bf16[1,576,256]{2,1,0:T(8,128)(2,1)} %bitcast.29, bf16[1,576,256]{2,1,0:T(8,128)(2,1)} %bitcast.30, bf16[1,576,256]{2,1,0:T(8,128)(2,1)} %bitcast.31, bf16[1,576,256]{2,1,0:T(8,128)(2,1)} %bitcast.32), custom_call_target="tpu_custom_call" | custom-call | flops 1610612736 | bytes 2064384 | tf_op jit(solution)/shard_map/space/pallas_call | solution.py:65
  17.3 0.0 copy-done.4
  17.4 0.1 select_reduce_fusion.2
  17.4 0.0 collective-permute-done.refs_2_
  17.4 0.0 copy-done.3
  17.4 3.5 %collective-permute-start.2 = (bf16[2,288,128]{2,1,0:T(8,128)(2,1)S(1)}, bf16[2,288,128]{2,1,0:T(8,128)(2,1)S(1)}, u32[]{:S(2)}, u32[]{:S(2)}) collective-permute-start(bf16[2,288,128]{2,1,0:T(8,128)(2,1)S(1)} %copy-done.3), channel_id=1, source_target_pairs={{0,2},{1,3},{2,0},{3,1},{4,6},{5,7},{6,4},{7,5},{8,10},{9,11},{10,... | collective-permute-start | bytes 442376 | tf_op jit(solution)/shard_map/ppermute | solution.py:131
  21.0 0.0 copy-done.2
  21.0 0.0 collective-permute-start.3
  21.0 0.0 collective-permute-done.9.refs_1_
  21.0 0.0 collective-permute-done.10.refs_3_
  21.0 0.0 copy-done.1
  21.1 0.0 copy-start
  21.1 0.1 sides.3
  21.2 0.7 %collective-permute-start.11 = (bf16[3,2,288,128]{3,2,1,0:T(8,128)(2,1)S(1)}, bf16[3,2,288,128]{3,2,1,0:T(8,128)(2,1)S(1)}, u32[]{:S(2)}, u32[]{:S(2)}) collective-permute-start(bf16[3,2,288,128]{3,2,1,0:T(8,128)(2,1)S(1)} %get-tuple-element.70), channel_id=1, source_target_pairs={{4,8},{12,16},{20,24},{8,4},{16,12},{24,20},{5,9},{13,17},{21,25},... | collective-permute-start | bytes 1327112 | tf_op jit(solution)/shard_map/ppermute | solution.py:131
  21.9 3.1 %collective-permute-start.12 = (bf16[3,2,288,128]{3,2,1,0:T(8,128)(2,1)S(1)}, bf16[3,2,288,128]{3,2,1,0:T(8,128)(2,1)S(1)}, u32[]{:S(2)}, u32[]{:S(2)}) collective-permute-start(bf16[3,2,288,128]{3,2,1,0:T(8,128)(2,1)S(1)} %get-tuple-element.71), channel_id=1, source_target_pairs={{0,4},{8,12},{16,20},{24,28},{4,0},{12,8},{20,16},{28,24},{1,5},{9... | collective-permute-start | bytes 1327112 | tf_op jit(solution)/shard_map/ppermute | solution.py:131
  25.0 0.2 select_reduce_fusion.1
  25.2 0.0 collective-permute-done.1.refs_1_
  25.2 5.9 %collective-permute-done.2.refs_2_ = bf16[2,288,128]{2,1,0:T(8,128)(2,1)S(1)} collective-permute-done((bf16[2,288,128]{2,1,0:T(8,128)(2,1)S(1)}, bf16[2,288,128]{2,1,0:T(8,128)(2,1)S(1)}, u32[]{:S(2)}, u32[]{:S(2)}) %collective-permute-start.2) | collective-permute-done | bytes 147488 | tf_op jit(solution)/shard_map/ppermute | solution.py:131
  31.1 0.0 collective-permute-done.3.refs_3_
  31.1 0.0 copy-done
  31.1 0.1 sides.2
  31.3 0.7 %collective-permute-start.4 = (bf16[3,2,288,128]{3,2,1,0:T(8,128)(2,1)S(1)}, bf16[3,2,288,128]{3,2,1,0:T(8,128)(2,1)S(1)}, u32[]{:S(2)}, u32[]{:S(2)}) collective-permute-start(bf16[3,2,288,128]{3,2,1,0:T(8,128)(2,1)S(1)} %get-tuple-element.60), channel_id=1, source_target_pairs={{4,8},{12,16},{20,24},{8,4},{16,12},{24,20},{5,9},{13,17},{21,25},... | collective-permute-start | bytes 1327112 | tf_op jit(solution)/shard_map/ppermute | solution.py:131
  32.0 2.9 %collective-permute-start.5 = (bf16[3,2,288,128]{3,2,1,0:T(8,128)(2,1)S(1)}, bf16[3,2,288,128]{3,2,1,0:T(8,128)(2,1)S(1)}, u32[]{:S(2)}, u32[]{:S(2)}) collective-permute-start(bf16[3,2,288,128]{3,2,1,0:T(8,128)(2,1)S(1)} %get-tuple-element.61), channel_id=1, source_target_pairs={{0,4},{8,12},{16,20},{24,28},{4,0},{12,8},{20,16},{28,24},{1,5},{9... | collective-permute-start | bytes 1327112 | tf_op jit(solution)/shard_map/ppermute | solution.py:131
  34.9 0.0 collective-permute-done.11.refs_4_
  34.9 0.0 collective-permute-done.12.refs_5_
  34.9 2.1 %clips.3 = (bf16[432,128]{1,0:T(8,128)(2,1)S(1)}, bf16[432,128]{1,0:T(8,128)(2,1)S(1)}, bf16[432,128]{1,0:T(8,128)(2,1)S(1)}, bf16[432,128]{1,0:T(8,128)(2,1)S(1)}) custom-call(s32[2,10]{1,0:T(2,128)S(1)} %pad_add_fusion.given_bounds, bf16[2,288,128]{2,1,0:T(8,128)(2,1)S(1)} %copy-done.1, bf16[2,288,128]{2,1,0:T(8,128)(2,1)S(1)} %collective-permute-done.9.refs_1_, ...), custom_call_target="tpu_custom_call" | custom-call | flops 589824000 | bytes 1474560 | tf_op jit(solution)/shard_map/clips/pallas_call | solution.py:337
  37.0 4.8 %collective-permute-start.14 = (bf16[432,128]{1,0:T(8,128)(2,1)S(1)}, bf16[432,128]{1,0:T(8,128)(2,1)S(1)}, u32[]{:S(2)}, u32[]{:S(2)}) collective-permute-start(bf16[432,128]{1,0:T(8,128)(2,1)S(1)} %get-tuple-element.74), channel_id=1, source_target_pairs={{0,2},{1,3},{2,0},{3,1},{4,6},{5,7},{6,4},{7,5},{8,10},{9,11},{10,... | collective-permute-start | bytes 331784 | tf_op jit(solution)/shard_map/ppermute | solution.py:131
  41.8 0.0 collective-permute-start.13
  41.8 1.5 %collective-permute-start.15 = (bf16[432,128]{1,0:T(8,128)(2,1)S(1)}, bf16[432,128]{1,0:T(8,128)(2,1)S(1)}, u32[]{:S(2)}, u32[]{:S(2)}) collective-permute-start(bf16[432,128]{1,0:T(8,128)(2,1)S(1)} %get-tuple-element.75), channel_id=1, source_target_pairs={{0,3},{1,2},{3,0},{2,1},{4,7},{5,6},{7,4},{6,5},{8,11},{9,10},{11,... | collective-permute-start | bytes 331784 | tf_op jit(solution)/shard_map/ppermute | solution.py:131
  43.3 0.0 collective-permute-done.4.refs_4_
  43.3 0.0 collective-permute-done.5.refs_5_
  43.3 2.1 %clips.2 = (bf16[432,128]{1,0:T(8,128)(2,1)S(1)}, bf16[432,128]{1,0:T(8,128)(2,1)S(1)}, bf16[432,128]{1,0:T(8,128)(2,1)S(1)}, bf16[432,128]{1,0:T(8,128)(2,1)S(1)}) custom-call(s32[2,10]{1,0:T(2,128)S(1)} %pad_add_fusion.given_bounds, bf16[2,288,128]{2,1,0:T(8,128)(2,1)S(1)} %copy-done, bf16[2,288,128]{2,1,0:T(8,128)(2,1)S(1)} %collective-permute-done.1.refs_1_, ...), custom_call_target="tpu_custom_call" | custom-call | flops 589824000 | bytes 1474560 | tf_op jit(solution)/shard_map/clips/pallas_call | solution.py:337
  45.4 2.0 %collective-permute-start.7 = (bf16[432,128]{1,0:T(8,128)(2,1)S(1)}, bf16[432,128]{1,0:T(8,128)(2,1)S(1)}, u32[]{:S(2)}, u32[]{:S(2)}) collective-permute-start(bf16[432,128]{1,0:T(8,128)(2,1)S(1)} %get-tuple-element.64), channel_id=1, source_target_pairs={{0,2},{1,3},{2,0},{3,1},{4,6},{5,7},{6,4},{7,5},{8,10},{9,11},{10,... | collective-permute-start | bytes 331784 | tf_op jit(solution)/shard_map/ppermute | solution.py:131
  47.4 0.9 %collective-permute-start.8 = (bf16[432,128]{1,0:T(8,128)(2,1)S(1)}, bf16[432,128]{1,0:T(8,128)(2,1)S(1)}, u32[]{:S(2)}, u32[]{:S(2)}) collective-permute-start(bf16[432,128]{1,0:T(8,128)(2,1)S(1)} %get-tuple-element.65), channel_id=1, source_target_pairs={{0,3},{1,2},{3,0},{2,1},{4,7},{5,6},{7,4},{6,5},{8,11},{9,10},{11,... | collective-permute-start | bytes 331784 | tf_op jit(solution)/shard_map/ppermute | solution.py:131
  48.3 0.3 collective-permute-done.14.refs_0_
  48.6 0.4 collective-permute-start.6
  49.0 1.5 %collective-permute-done.15.refs_1_ = bf16[432,128]{1,0:T(8,128)(2,1)S(1)} collective-permute-done((bf16[432,128]{1,0:T(8,128)(2,1)S(1)}, bf16[432,128]{1,0:T(8,128)(2,1)S(1)}, u32[]{:S(2)}, u32[]{:S(2)}) %collective-permute-start.15) | collective-permute-done | bytes 110624 | tf_op jit(solution)/shard_map/ppermute | solution.py:131
  50.5 0.9 %unpack.4 = (bf16[1,576,256]{2,1,0:T(8,128)(2,1)}, bf16[1,576,256]{2,1,0:T(8,128)(2,1)}, bf16[1,576,256]{2,1,0:T(8,128)(2,1)}) custom-call(bf16[432,128]{1,0:T(8,128)(2,1)S(1)} %collective-permute-done.14.refs_0_, bf16[432,128]{1,0:T(8,128)(2,1)S(1)} %collective-permute-done.15.refs_1_), custom_call_target="tpu_custom_call" | custom-call | tf_op jit(solution)/shard_map/unpack/pallas_call | solution.py:218
  51.3 0.0 collective-permute-done.13.refs_1_
  51.3 0.9 %unpack.5 = (bf16[1,576,256]{2,1,0:T(8,128)(2,1)}, bf16[1,576,256]{2,1,0:T(8,128)(2,1)}, bf16[1,576,256]{2,1,0:T(8,128)(2,1)}) custom-call(bf16[432,128]{1,0:T(8,128)(2,1)S(1)} %get-tuple-element.72.refs_0_, bf16[432,128]{1,0:T(8,128)(2,1)S(1)} %collective-permute-done.13.refs_1_, ...), custom_call_target="tpu_custom_call", output_to_operand_aliasing={{0}: (2, {}), {1}: (3, {}), {2}: (4, {})} | custom-call | tf_op jit(solution)/shard_map/unpack/pallas_call | solution.py:218
  52.2 7.7 %collective-permute-done.7.refs_0_ = bf16[432,128]{1,0:T(8,128)(2,1)S(1)} collective-permute-done((bf16[432,128]{1,0:T(8,128)(2,1)S(1)}, bf16[432,128]{1,0:T(8,128)(2,1)S(1)}, u32[]{:S(2)}, u32[]{:S(2)}) %collective-permute-start.7) | collective-permute-done | bytes 110624 | tf_op jit(solution)/shard_map/ppermute | solution.py:131
  59.9 0.0 collective-permute-done.8.refs_1_
  59.9 0.9 %unpack.6 = (bf16[1,576,256]{2,1,0:T(8,128)(2,1)}, bf16[1,576,256]{2,1,0:T(8,128)(2,1)}, bf16[1,576,256]{2,1,0:T(8,128)(2,1)}) custom-call(bf16[432,128]{1,0:T(8,128)(2,1)S(1)} %collective-permute-done.7.refs_0_, bf16[432,128]{1,0:T(8,128)(2,1)S(1)} %collective-permute-done.8.refs_1_, ...), custom_call_target="tpu_custom_call", output_to_operand_aliasing={{0}: (2, {}), {1}: (3, {}), {2}: (4, {})} | custom-call | tf_op jit(solution)/shard_map/unpack/pallas_call | solution.py:218
  60.8 0.0 collective-permute-done.6.refs_1_
  60.8 0.9 %unpack.7 = (bf16[1,576,256]{2,1,0:T(8,128)(2,1)}, bf16[1,576,256]{2,1,0:T(8,128)(2,1)}, bf16[1,576,256]{2,1,0:T(8,128)(2,1)}) custom-call(bf16[432,128]{1,0:T(8,128)(2,1)S(1)} %get-tuple-element.62.refs_0_, bf16[432,128]{1,0:T(8,128)(2,1)S(1)} %collective-permute-done.6.refs_1_, ...), custom_call_target="tpu_custom_call", output_to_operand_aliasing={{0}: (2, {}), {1}: (3, {}), {2}: (4, {})} | custom-call | tf_op jit(solution)/shard_map/unpack/pallas_call | solution.py:218
  (4 shorter events, 0.0 us)
Async XLA Ops:
  2.9 14.6 %collective-permute-start = (bf16[2,288,128]{2,1,0:T(8,128)(2,1)}, bf16[2,288,128]{2,1,0:T(8,128)(2,1)S(1)}, u32[]{:S(2)}, u32[]{:S(2)}) collective-permute-start(bf16[2,288,128]{2,1,0:T(8,128)(2,1)} %get-tuple-element.49), channel_id=1, source_target_pairs={{0,2},{1,3},{2,0},{3,1},{4,6},{5,7},{6,4},{7,5},{8,10},{9,11},{10,... | collective-permute-start | bytes 442376 | tf_op jit(solution)/shard_map/ppermute | solution.py:131
  7.0 14.0 %collective-permute-start.9 = (bf16[2,288,128]{2,1,0:T(8,128)(2,1)}, bf16[2,288,128]{2,1,0:T(8,128)(2,1)S(1)}, u32[]{:S(2)}, u32[]{:S(2)}) collective-permute-start(bf16[2,288,128]{2,1,0:T(8,128)(2,1)} %get-tuple-element.67), channel_id=1, source_target_pairs={{0,1},{2,3},{1,0},{3,2},{4,5},{6,7},{5,4},{7,6},{8,9},{10,11},{9,8... | collective-permute-start | bytes 442376 | tf_op jit(solution)/shard_map/ppermute | solution.py:131
  8.6 12.5 %collective-permute-start.10 = (bf16[2,288,128]{2,1,0:T(8,128)(2,1)}, bf16[2,288,128]{2,1,0:T(8,128)(2,1)S(1)}, u32[]{:S(2)}, u32[]{:S(2)}) collective-permute-start(bf16[2,288,128]{2,1,0:T(8,128)(2,1)} %get-tuple-element.69), channel_id=1, source_target_pairs={{0,3},{1,2},{3,0},{2,1},{4,7},{5,6},{7,4},{6,5},{8,11},{9,10},{11,... | collective-permute-start | bytes 442376 | tf_op jit(solution)/shard_map/ppermute | solution.py:131
  10.8 14.4 %collective-permute-start.1 = (bf16[2,288,128]{2,1,0:T(8,128)(2,1)}, bf16[2,288,128]{2,1,0:T(8,128)(2,1)S(1)}, u32[]{:S(2)}, u32[]{:S(2)}) collective-permute-start(bf16[2,288,128]{2,1,0:T(8,128)(2,1)} %get-tuple-element.57), channel_id=1, source_target_pairs={{0,1},{2,3},{1,0},{3,2},{4,5},{6,7},{5,4},{7,6},{8,9},{10,11},{9,8... | collective-permute-start | bytes 442376 | tf_op jit(solution)/shard_map/ppermute | solution.py:131
  11.8 5.6 %copy-start.4 = (s32[16]{0:T(128)S(1)}, s32[16]{0:T(128)}, u32[]{:S(2)}) copy-start(s32[16]{0:T(128)} %param.17) | copy-start | bytes 196
  11.8 5.7 %copy-start.3 = (bf16[2,288,128]{2,1,0:T(8,128)(2,1)S(1)}, bf16[2,288,128]{2,1,0:T(8,128)(2,1)}, u32[]{:S(2)}) copy-start(bf16[2,288,128]{2,1,0:T(8,128)(2,1)} %get-tuple-element.58) | copy-start | bytes 442372
  11.8 9.2 %copy-start.2 = (bf16[2,288,128]{2,1,0:T(8,128)(2,1)S(1)}, bf16[2,288,128]{2,1,0:T(8,128)(2,1)}, u32[]{:S(2)}) copy-start(bf16[2,288,128]{2,1,0:T(8,128)(2,1)} %get-tuple-element.59) | copy-start | bytes 442372
  11.8 9.3 %copy-start.1 = (bf16[2,288,128]{2,1,0:T(8,128)(2,1)S(1)}, bf16[2,288,128]{2,1,0:T(8,128)(2,1)}, u32[]{:S(2)}) copy-start(bf16[2,288,128]{2,1,0:T(8,128)(2,1)} %get-tuple-element.66.refs_0_) | copy-start | bytes 442372
  17.4 13.7 %collective-permute-start.2 = (bf16[2,288,128]{2,1,0:T(8,128)(2,1)S(1)}, bf16[2,288,128]{2,1,0:T(8,128)(2,1)S(1)}, u32[]{:S(2)}, u32[]{:S(2)}) collective-permute-start(bf16[2,288,128]{2,1,0:T(8,128)(2,1)S(1)} %copy-done.3), channel_id=1, source_target_pairs={{0,2},{1,3},{2,0},{3,1},{4,6},{5,7},{6,4},{7,5},{8,10},{9,11},{10,... | collective-permute-start | bytes 442376 | tf_op jit(solution)/shard_map/ppermute | solution.py:131
  21.0 10.1 %collective-permute-start.3 = (bf16[2,288,128]{2,1,0:T(8,128)(2,1)S(1)}, bf16[2,288,128]{2,1,0:T(8,128)(2,1)S(1)}, u32[]{:S(2)}, u32[]{:S(2)}) collective-permute-start(bf16[2,288,128]{2,1,0:T(8,128)(2,1)S(1)} %copy-done.2), channel_id=1, source_target_pairs={{0,3},{1,2},{3,0},{2,1},{4,7},{5,6},{7,4},{6,5},{8,11},{9,10},{11,... | collective-permute-start | bytes 442376 | tf_op jit(solution)/shard_map/ppermute | solution.py:131
  21.1 10.1 %copy-start = (bf16[2,288,128]{2,1,0:T(8,128)(2,1)S(1)}, bf16[2,288,128]{2,1,0:T(8,128)(2,1)}, u32[]{:S(2)}) copy-start(bf16[2,288,128]{2,1,0:T(8,128)(2,1)} %get-tuple-element.56.refs_0_) | copy-start | bytes 442372
  21.2 13.7 %collective-permute-start.11 = (bf16[3,2,288,128]{3,2,1,0:T(8,128)(2,1)S(1)}, bf16[3,2,288,128]{3,2,1,0:T(8,128)(2,1)S(1)}, u32[]{:S(2)}, u32[]{:S(2)}) collective-permute-start(bf16[3,2,288,128]{3,2,1,0:T(8,128)(2,1)S(1)} %get-tuple-element.70), channel_id=1, source_target_pairs={{4,8},{12,16},{20,24},{8,4},{16,12},{24,20},{5,9},{13,17},{21,25},... | collective-permute-start | bytes 1327112 | tf_op jit(solution)/shard_map/ppermute | solution.py:131
  21.9 13.0 %collective-permute-start.12 = (bf16[3,2,288,128]{3,2,1,0:T(8,128)(2,1)S(1)}, bf16[3,2,288,128]{3,2,1,0:T(8,128)(2,1)S(1)}, u32[]{:S(2)}, u32[]{:S(2)}) collective-permute-start(bf16[3,2,288,128]{3,2,1,0:T(8,128)(2,1)S(1)} %get-tuple-element.71), channel_id=1, source_target_pairs={{0,4},{8,12},{16,20},{24,28},{4,0},{12,8},{20,16},{28,24},{1,5},{9... | collective-permute-start | bytes 1327112 | tf_op jit(solution)/shard_map/ppermute | solution.py:131
  31.3 12.1 %collective-permute-start.4 = (bf16[3,2,288,128]{3,2,1,0:T(8,128)(2,1)S(1)}, bf16[3,2,288,128]{3,2,1,0:T(8,128)(2,1)S(1)}, u32[]{:S(2)}, u32[]{:S(2)}) collective-permute-start(bf16[3,2,288,128]{3,2,1,0:T(8,128)(2,1)S(1)} %get-tuple-element.60), channel_id=1, source_target_pairs={{4,8},{12,16},{20,24},{8,4},{16,12},{24,20},{5,9},{13,17},{21,25},... | collective-permute-start | bytes 1327112 | tf_op jit(solution)/shard_map/ppermute | solution.py:131
  32.0 11.4 %collective-permute-start.5 = (bf16[3,2,288,128]{3,2,1,0:T(8,128)(2,1)S(1)}, bf16[3,2,288,128]{3,2,1,0:T(8,128)(2,1)S(1)}, u32[]{:S(2)}, u32[]{:S(2)}) collective-permute-start(bf16[3,2,288,128]{3,2,1,0:T(8,128)(2,1)S(1)} %get-tuple-element.61), channel_id=1, source_target_pairs={{0,4},{8,12},{16,20},{24,28},{4,0},{12,8},{20,16},{28,24},{1,5},{9... | collective-permute-start | bytes 1327112 | tf_op jit(solution)/shard_map/ppermute | solution.py:131
  37.0 11.6 %collective-permute-start.14 = (bf16[432,128]{1,0:T(8,128)(2,1)S(1)}, bf16[432,128]{1,0:T(8,128)(2,1)S(1)}, u32[]{:S(2)}, u32[]{:S(2)}) collective-permute-start(bf16[432,128]{1,0:T(8,128)(2,1)S(1)} %get-tuple-element.74), channel_id=1, source_target_pairs={{0,2},{1,3},{2,0},{3,1},{4,6},{5,7},{6,4},{7,5},{8,10},{9,11},{10,... | collective-permute-start | bytes 331784 | tf_op jit(solution)/shard_map/ppermute | solution.py:131
  41.8 9.6 %collective-permute-start.13 = (bf16[432,128]{1,0:T(8,128)(2,1)S(1)}, bf16[432,128]{1,0:T(8,128)(2,1)S(1)}, u32[]{:S(2)}, u32[]{:S(2)}) collective-permute-start(bf16[432,128]{1,0:T(8,128)(2,1)S(1)} %get-tuple-element.73), channel_id=1, source_target_pairs={{0,1},{2,3},{1,0},{3,2},{4,5},{6,7},{5,4},{7,6},{8,9},{10,11},{9,8... | collective-permute-start | bytes 331784 | tf_op jit(solution)/shard_map/ppermute | solution.py:131
  41.8 8.7 %collective-permute-start.15 = (bf16[432,128]{1,0:T(8,128)(2,1)S(1)}, bf16[432,128]{1,0:T(8,128)(2,1)S(1)}, u32[]{:S(2)}, u32[]{:S(2)}) collective-permute-start(bf16[432,128]{1,0:T(8,128)(2,1)S(1)} %get-tuple-element.75), channel_id=1, source_target_pairs={{0,3},{1,2},{3,0},{2,1},{4,7},{5,6},{7,4},{6,5},{8,11},{9,10},{11,... | collective-permute-start | bytes 331784 | tf_op jit(solution)/shard_map/ppermute | solution.py:131
  45.4 14.5 %collective-permute-start.7 = (bf16[432,128]{1,0:T(8,128)(2,1)S(1)}, bf16[432,128]{1,0:T(8,128)(2,1)S(1)}, u32[]{:S(2)}, u32[]{:S(2)}) collective-permute-start(bf16[432,128]{1,0:T(8,128)(2,1)S(1)} %get-tuple-element.64), channel_id=1, source_target_pairs={{0,2},{1,3},{2,0},{3,1},{4,6},{5,7},{6,4},{7,5},{8,10},{9,11},{10,... | collective-permute-start | bytes 331784 | tf_op jit(solution)/shard_map/ppermute | solution.py:131
  47.4 12.5 %collective-permute-start.8 = (bf16[432,128]{1,0:T(8,128)(2,1)S(1)}, bf16[432,128]{1,0:T(8,128)(2,1)S(1)}, u32[]{:S(2)}, u32[]{:S(2)}) collective-permute-start(bf16[432,128]{1,0:T(8,128)(2,1)S(1)} %get-tuple-element.65), channel_id=1, source_target_pairs={{0,3},{1,2},{3,0},{2,1},{4,7},{5,6},{7,4},{6,5},{8,11},{9,10},{11,... | collective-permute-start | bytes 331784 | tf_op jit(solution)/shard_map/ppermute | solution.py:131
  48.6 12.2 %collective-permute-start.6 = (bf16[432,128]{1,0:T(8,128)(2,1)S(1)}, bf16[432,128]{1,0:T(8,128)(2,1)S(1)}, u32[]{:S(2)}, u32[]{:S(2)}) collective-permute-start(bf16[432,128]{1,0:T(8,128)(2,1)S(1)} %get-tuple-element.63), channel_id=1, source_target_pairs={{0,1},{2,3},{1,0},{3,2},{4,5},{6,7},{5,4},{7,6},{8,9},{10,11},{9,8... | collective-permute-start | bytes 331784 | tf_op jit(solution)/shard_map/ppermute | solution.py:131

commit v9 on v8

--- a/solution.py
+++ b/solution.py
@@ -357,14 +357,214 @@
     )(bounds, *own, *beside)
 
 
-def clip_bounds(clip_len, window):
-    halo = window - 1
-    extent = window + 2 * halo
-    start = lax.axis_index("grp") * window - halo
-    frames = start + jnp.arange(extent, dtype=jnp.int32)
+def transposed_groups(tiles):
+    count = len(tiles)
+    size = tiles[0].shape[1] // count
+    group = lax.broadcasted_iota(jnp.int32, (1, tiles[0].shape[1]), 1) // size
+    step = count // 2
+    while step:
+        upper = (group & step) != 0
+        moved = list(tiles)
+        for a in range(count):
+            if not a & step:
+                low, high = tiles[a], tiles[a | step]
+                moved[a] = jnp.where(upper, pltpu.roll(high, step * size, 1), low)
+                moved[a | step] = jnp.where(upper, high, pltpu.roll(low, (count - step) * size, 1))
+        tiles = moved
+        step //= 2
+    return tiles
+
+
+def deal_kernel(q_ref, g_ref, k_ref, v_ref, out_ref, wide, turned):
+    for i, ref in enumerate((q_ref, g_ref, k_ref, v_ref)):
+        wide[i] = ref[0].astype(jnp.float32)
+    groups = 2 * HEADS
+
+    def rows_of(step, carry):
+        begin = pl.multiple_of(step * 8, 8)
+        for pair in range(2):
+            for tile in range(wide.shape[2] // 128):
+                lanes = slice(tile * 128, (tile + 1) * 128)
+                parts = [
+                    wide[2 * pair + i, pl.ds(head * HDIM + begin, 8), lanes]
+                    for head in range(HEADS)
+                    for i in range(2)
+                ]
+                for d, part in enumerate(transposed_groups(parts)):
+                    turned[tile * groups + d, pl.ds(pair * HDIM + begin, 8), :] = part
+        return carry
+
+    lax.fori_loop(0, HDIM // 8, rows_of, 0)
+    for target in range(out_ref.shape[0]):
+        out_ref[target] = turned[target].astype(jnp.bfloat16)
+
+
+def deal(arrays, count):
+    shape = (count, 2 * HDIM, 128)
+    return pl.pallas_call(
+        deal_kernel,
+        out_shape=jax.ShapeDtypeStruct(shape, jnp.bfloat16),
+        scratch_shapes=[
+            pltpu.VMEM((4, *arrays[0].shape[1:]), jnp.float32),
+            pltpu.VMEM(shape, jnp.float32),
+        ],
+        compiler_params=pltpu.CompilerParams(vmem_limit_bytes=60 * 2**20),
+        name="pack",
+    )(*arrays)
+
+
+FOLD = 40
+
+
+def all_frames_kernel(slots, given_bounds, in_ref, out_ref, both, sums_ref, bias_ref, coef_ref, bounds, arrived):
+    copy = pltpu.make_async_copy(given_bounds, bounds, arrived)
+    copy.start()
+    count = in_ref.shape[0]
+    for frame in range(count):
+        both[frame] = in_ref[frame].astype(jnp.float32)
+    copy.wait()
+    lane = lax.broadcasted_iota(jnp.int32, (1, 128), 1)
+    is_left = (lane & 8) == 0
+    x_rows, y_rows = slice(0, HDIM), slice(HDIM, 2 * HDIM)
+    together = 4
+
+    def partners(frame):
+        first, last = bounds[0, frame], bounds[1, frame]
+        return first, last - first, [jnp.minimum(first + t, last - 1) for t in range(slots)]
+
+    def products(step, carry):
+        for i in range(together):
+            frame = step * together + i
+            first, size, others = partners(frame)
+            mine = both[frame, x_rows, :]
+            for t, other in enumerate(others):
+                total = jnp.sum(mine * both[other, y_rows, :], axis=0, keepdims=True)
+                sums_ref[t, pl.ds(frame, 1), :] = total
+                bias = jnp.where(t < size, 0.0, masked_score)
+                bias_ref[t, pl.ds(frame, 1), :] = jnp.full((1, 128), bias, jnp.float32)
+        return carry
+
+    lax.fori_loop(0, count // together, products, 0)
+    sums = [sums_ref[t] for t in range(slots)]
+    scores = [sums[t] * SCALING + bias_ref[t] for t in range(slots)]
+    peak = functools.reduce(jnp.maximum, scores)
+    raised = [jnp.exp(score - peak) for score in scores]
+    inverse = 1.0 / functools.reduce(jnp.add, raised)
+    weights = [part * inverse for part in raised]
+    weights_low = [rounded(part) for part in weights]
+    weight_grad = [pltpu.roll(part, 120, 1) for part in sums]
+    dots = functools.reduce(jnp.add, [w * d for w, d in zip(weights_low, weight_grad)])
+    for t in range(slots):
+        score_grad = rounded(weights[t] * (weight_grad[t] - dots))
+        coef_ref[t] = jnp.where(is_left, score_grad, pltpu.roll(weights_low[t], 8, 1))
+
+    def gradients(step, carry):
+        for i in range(together):
+            frame = step * together + i
+            first, size, others = partners(frame)
+            key_sum, query_sum = None, None
+            for t, other in enumerate(others):
+                back = coef_ref[frame - first, pl.ds(other, 1), :]
+                back = jnp.where(t < size, back, 0.0)
+                key_term = back * both[other, x_rows, :]
+                query_term = coef_ref[t, pl.ds(frame, 1), :] * both[other, y_rows, :]
+                key_sum = key_term if t == 0 else key_sum + key_term
+                query_sum = query_term if t == 0 else query_sum + query_term
+            query_sum = query_sum * SCALING
+            rest = pltpu.roll(query_sum[FOLD:], 8, 1)
+            rest = jnp.concatenate([rest, jnp.zeros((2 * FOLD - HDIM, 128), jnp.float32)], axis=0)
+            folded = jnp.where(is_left, query_sum[:FOLD], rest)
+            value = jnp.concatenate([key_sum * jnp.where(is_left, SCALING, 1.0), folded], axis=0)
+            out_ref[frame] = value.astype(jnp.bfloat16)
+        return carry
+
+    lax.fori_loop(0, count // together, gradients, 0)
+
+
+def all_frames_grads(bounds, blocks, slots):
+    count = blocks.shape[0]
+    rows = pltpu.VMEM((slots, count, 128), jnp.float32)
+    return pl.pallas_call(
+        functools.partial(all_frames_kernel, slots),
+        out_shape=jax.ShapeDtypeStruct((count, HDIM + FOLD, 128), jnp.bfloat16),
+        in_specs=[pl.BlockSpec(memory_space=pl.ANY), pl.BlockSpec(memory_space=pltpu.VMEM)],
+        out_specs=pl.BlockSpec(memory_space=pltpu.VMEM),
+        scratch_shapes=[
+            pltpu.VMEM(blocks.shape, jnp.float32),
+            rows,
+            rows,
+            rows,
+            pltpu.SMEM(bounds.shape, jnp.int32),
+            pltpu.SemaphoreType.DMA,
+        ],
+        compiler_params=pltpu.CompilerParams(vmem_limit_bytes=48 * 2**20),
+        name="clips",
+    )(bounds, blocks)
+
+
+def collect_kernel(in_ref, dq_ref, dk_ref, dv_ref, wide, turned):
+    count = in_ref.shape[0]
+    groups = 2 * HEADS
+    for source in range(count):
+        wide[source] = in_ref[source].astype(jnp.float32)
+    lane = lax.broadcasted_iota(jnp.int32, (1, 128), 1)
+    is_left = (lane & 8) == 0
+    for begin in range(0, HDIM, 8):
+        for tile in range(count // groups):
+            lanes = slice(tile * 128, (tile + 1) * 128)
+            parts = [wide[tile * groups + d, begin : begin + 8, :] for d in range(groups)]
+            for s, part in enumerate(transposed_groups(parts)):
+                row = s // 2 * HDIM + begin
+                turned[1 + s % 2, row : row + 8, lanes] = part
+        parts = []
+        row = HDIM + begin % FOLD
+        for d in range(groups):
+            low, high = wide[d, row : row + 8, :], wide[groups + d, row : row + 8, :]
+            if begin < FOLD:
+                high = pltpu.roll(high, 8, 1)
+            else:
+                low = pltpu.roll(low, 120, 1)
+            parts.append(jnp.where(is_left, low, high))
+        for s, part in enumerate(transposed_groups(parts)):
+            row = s // 2 * HDIM + begin
+            turned[0, row : row + 8, s % 2 * 128 : (s % 2 + 1) * 128] = part
+    for i, out in enumerate((dq_ref, dk_ref, dv_ref)):
+        out[0] = turned[i].astype(jnp.bfloat16)
+
+
+def collect(blocks, tokens):
+    shape = jax.ShapeDtypeStruct((1, WIDTH, tokens), jnp.bfloat16)
+    return pl.pallas_call(
+        collect_kernel,
+        out_shape=[shape] * 3,
+        scratch_shapes=[
+            pltpu.VMEM(blocks.shape, jnp.float32),
+            pltpu.VMEM((3, WIDTH, tokens), jnp.float32),
+        ],
+        compiler_params=pltpu.CompilerParams(vmem_limit_bytes=60 * 2**20),
+        name="unpack",
+    )(blocks)
+
+
+def all_frames(time, clip_len, slots):
+    axes = ("grp", "seq")
+    count = lax.axis_size("grp") * lax.axis_size("seq")
+    begins, ends = clip_edges(clip_len)
+    bounds = clip_bounds(begins, ends, 0, count)
+    blocks = lax.all_to_all(deal(time, count), axes, split_axis=0, concat_axis=0, tiled=True)
+    grads = all_frames_grads(bounds, blocks, slots)
+    grads = lax.all_to_all(grads, axes, split_axis=0, concat_axis=0, tiled=True)
+    return collect(grads, time[0].shape[2])
+
+
+def clip_edges(clip_len):
     order = jnp.arange(clip_len.shape[0])
     ends = jnp.sum(jnp.where(order[:, None] <= order[None, :], clip_len[:, None], 0), axis=0)
-    begins = ends - clip_len
+    return ends - clip_len, ends
+
+
+def clip_bounds(begins, ends, start, count):
+    frames = start + jnp.arange(count, dtype=jnp.int32)
     holds = (begins[None, :] <= frames[:, None]) & (frames[:, None] < ends[None, :])
     first = jnp.sum(jnp.where(holds, begins[None, :], 0), axis=1) - start
     last = jnp.sum(jnp.where(holds, ends[None, :], 0), axis=1) - start
@@ -378,14 +578,20 @@
     n = lax.axis_size("seq")
     window = q_time.shape[0] * n
     tokens = q_time.shape[1]
-    bounds = clip_bounds(clip_len, window)
     time = turned(q_time, cot_time, k_time, v_time)
+    space_in = turned(q_space, k_space, v_space, cot_space)
+    if tokens * 2 * HEADS == 128 * n * lax.axis_size("grp"):
+        grads = all_frames(time, clip_len, window)
+        return turned(*frame_grads(*space_in), *grads)
+    halo = window - 1
+    begins, ends = clip_edges(clip_len)
+    start = lax.axis_index("grp") * window - halo
+    bounds = clip_bounds(begins, ends, start, window + 2 * halo)
     spans = []
     head = 0
     for heads in CHUNKS:
         spans.append(slice(head * HDIM, (head + heads) * HDIM))
         head += heads
-    space_in = turned(q_space, k_space, v_space, cot_space)
     packed = [list(split(time, span, n)) for span in spans]
 
     own = [exchange(packed[0])]

time: 61.9 us -> 82.5 us (1.33); the launches traced: 61.6 us -> 81.1 us
  waiting for transfers between devices: 15.4 us -> 44.4 us
  starting transfers between devices: 27.2 us -> 11.8 us
  Pallas kernels: 17.9 us -> 23.1 us
  local copies, waits for them, and re-layouts: 0.02 us -> 0.94 us
    all_to_all x0 -> x2, waiting for transfers between devices: none -> 44.4 us  [the longest x1 27.6 us: all_frames(): lax.all_to_all(deal(time, count), axes, split_axis=0, concat_axis=0, tile...]
    ppermute x16 -> x0, starting transfers between devices: 27.2 us -> none  [swap(): lax.ppermute(block, axis, [(i, j) for i, j in pairs] + [(j, i) for i, j i...]
    ppermute x16 -> x0, waiting for transfers between devices: 15.4 us -> none  [swap(): lax.ppermute(block, axis, [(i, j) for i, j in pairs] + [(j, i) for i, j i...]
    all_to_all x0 -> x2, starting transfers between devices: none -> 11.8 us  [the longest x1 7.3 us: all_frames(): lax.all_to_all(deal(time, count), axes, split_axis=0, concat_axis=0, tile...]
    pallas_call x10 -> x3, Pallas kernels: 12.3 us -> 17.6 us  [the longest x1 7.43 us: collect(): pl.pallas_call(collect_kernel, out_shape=[shape] * 3, scratch_shapes=[plt...]
    unnamed x10 -> x4, local copies, waits for them, and re-layouts: 0.02 us -> 0.94 us
  transfers between devices with their start and end apart: 16 -> 2, of which waited for: 4 -> 2; matrix products, arithmetic and copies ran while one was open for 0% -> 0% of each run, Pallas kernels for 24% -> 7%
where the time goes in v9:
time: 82.5 us; the launch traced here: 81.1 us
  waiting for transfers between devices  44.4 us (54%)
  Pallas kernels  23.1 us (28%)
  starting transfers between devices  11.8 us (14%)
  local copies, waits for them, and re-layouts  0.94 us (1%)
    all_to_all x1, waiting for transfers between devices, all_frames(): lax.all_to_all(deal(time, count), axes, split_axis=0, concat_axis=0, tile...  27.6 us
    all_to_all x1, waiting for transfers between devices, all_frames(): grads = lax.all_to_all(grads, axes, split_axis=0, concat_axis=0, tiled=True)  16.8 us
    pallas_call x1, Pallas kernels, collect(): pl.pallas_call(collect_kernel, out_shape=[shape] * 3, scratch_shapes=[plt...  7.43 us
    all_to_all x1, starting transfers between devices, all_frames(): lax.all_to_all(deal(time, count), axes, split_axis=0, concat_axis=0, tile...  7.3 us
    pallas_call x1, Pallas kernels, deal(): pl.pallas_call(deal_kernel, out_shape=jax.ShapeDtypeStruct(shape, jnp.bfl...  6.93 us
    pallas_call x1, Pallas kernels, frame_grads(): pl.pallas_call(frame_kernel, out_shape=(shape, shape, shape), compiler_pa...  5.53 us
    all_to_all x1, starting transfers between devices, all_frames(): grads = lax.all_to_all(grads, axes, split_axis=0, concat_axis=0, tiled=True)  4.5 us
    pallas_call x1, Pallas kernels, all_frames_grads(): pl.pallas_call(functools.partial(all_frames_kernel, slots), out_shape=jax...  3.18 us
  transfers between devices with their start and end apart: 2, of which 2 were waited for; matrix products, arithmetic and copies ran while one was open for 0% of the time, Pallas kernels for 7%

profile of v9, /device:TPU:0, one launch (start us, length us, event | category | flops | bytes accessed | tf_op | source)
XLA Modules:
  0.0 81.1 jit_solution(7622205672567972050)
XLA Ops:
  0.6 6.9 %pack.1 = bf16[32,144,128]{2,1,0:T(8,128)(2,1)} custom-call(bf16[1,576,256]{2,1,0:T(8,128)(2,1)} %bitcast.16, bf16[1,576,256]{2,1,0:T(8,128)(2,1)} %bitcast.17, bf16[1,576,256]{2,1,0:T(8,128)(2,1)} %bitcast.18, bf16[1,576,256]{2,1,0:T(8,128)(2,1)} %bitcast.19), custom_call_target="tpu_custom_call" | custom-call | tf_op jit(solution)/shard_map/pack/pallas_call | solution.py:404
  7.6 0.0 copy-start.1
  7.6 7.3 %all-to-all-start = ((bf16[32,144,128]{2,1,0:T(8,128)(2,1)}), bf16[32,144,128]{2,1,0:T(8,128)(2,1)S(1)}, u32[]{:S(2)}, u32[]{:S(2)}) async-start(bf16[32,144,128]{2,1,0:T(8,128)(2,1)} %pack.1), calls=%async_computation | async-start | bytes 2359296 | tf_op jit(solution)/shard_map/all_to_all | solution.py:554
  14.9 0.0 copy-done.1
  14.9 0.1 select_reduce_fusion.2
  15.0 0.1 select_reduce_fusion.1
  15.1 27.6 %all-to-all-done.in_ref = bf16[32,144,128]{2,1,0:T(8,128)(2,1)S(1)} async-done(((bf16[32,144,128]{2,1,0:T(8,128)(2,1)}), bf16[32,144,128]{2,1,0:T(8,128)(2,1)S(1)}, u32[]{:S(2)}, u32[]{:S(2)}) %all-to-all-start) | async-done | bytes 1179680 | tf_op jit(solution)/shard_map/all_to_all | solution.py:554
  42.7 3.2 %clips.1 = bf16[32,112,128]{2,1,0:T(8,128)(2,1)} custom-call(s32[2,32]{1,0:T(2,128)S(1)} %pad_add_fusion.given_bounds, bf16[32,144,128]{2,1,0:T(8,128)(2,1)S(1)} %all-to-all-done.in_ref), custom_call_target="tpu_custom_call" | custom-call | tf_op jit(solution)/shard_map/clips/pallas_call | solution.py:487
  45.8 4.5 %all-to-all-start.1 = ((bf16[32,112,128]{2,1,0:T(8,128)(2,1)}), bf16[32,112,128]{2,1,0:T(8,128)(2,1)S(1)}, u32[]{:S(2)}, u32[]{:S(2)}) async-start(bf16[32,112,128]{2,1,0:T(8,128)(2,1)} %clips.1), calls=%async_computation.1 | async-start | bytes 1835008 | tf_op jit(solution)/shard_map/all_to_all | solution.py:556
  50.4 5.5 %space.1 = (bf16[1,576,256]{2,1,0:T(8,128)(2,1)}, bf16[1,576,256]{2,1,0:T(8,128)(2,1)}, bf16[1,576,256]{2,1,0:T(8,128)(2,1)}) custom-call(bf16[1,576,256]{2,1,0:T(8,128)(2,1)} %bitcast.22, bf16[1,576,256]{2,1,0:T(8,128)(2,1)} %bitcast.23, bf16[1,576,256]{2,1,0:T(8,128)(2,1)} %bitcast.24, bf16[1,576,256]{2,1,0:T(8,128)(2,1)} %bitcast.25), custom_call_target="tpu_custom_call" | custom-call | flops 1610612736 | bytes 2064384 | tf_op jit(solution)/shard_map/space/pallas_call | solution.py:65
  55.9 16.8 %all-to-all-done.1.in_ref = bf16[32,112,128]{2,1,0:T(8,128)(2,1)S(1)} async-done(((bf16[32,112,128]{2,1,0:T(8,128)(2,1)}), bf16[32,112,128]{2,1,0:T(8,128)(2,1)S(1)}, u32[]{:S(2)}, u32[]{:S(2)}) %all-to-all-start.1) | async-done | bytes 917536 | tf_op jit(solution)/shard_map/all_to_all | solution.py:556
  72.7 0.0 copy-start
  72.7 0.9 %copy-done = bf16[32,112,128]{2,1,0:T(8,128)(2,1)} copy-done((bf16[32,112,128]{2,1,0:T(8,128)(2,1)}, bf16[32,112,128]{2,1,0:T(8,128)(2,1)S(1)}, u32[]{:S(2)}) %copy-start) | copy-done | bytes 917528
  73.6 7.4 %unpack.1 = (bf16[1,576,256]{2,1,0:T(8,128)(2,1)}, bf16[1,576,256]{2,1,0:T(8,128)(2,1)}, bf16[1,576,256]{2,1,0:T(8,128)(2,1)}) custom-call(bf16[32,112,128]{2,1,0:T(8,128)(2,1)} %copy-done), custom_call_target="tpu_custom_call" | custom-call | tf_op jit(solution)/shard_map/unpack/pallas_call | solution.py:537
  (2 shorter events, 0.0 us)
Async XLA Ops:
  7.6 7.3 %copy-start.1 = (s32[16]{0:T(128)S(1)}, s32[16]{0:T(128)}, u32[]{:S(2)}) copy-start(s32[16]{0:T(128)} %param.17) | copy-start | bytes 196
  7.6 35.1 %all-to-all-start = ((bf16[32,144,128]{2,1,0:T(8,128)(2,1)}), bf16[32,144,128]{2,1,0:T(8,128)(2,1)S(1)}, u32[]{:S(2)}, u32[]{:S(2)}) async-start(bf16[32,144,128]{2,1,0:T(8,128)(2,1)} %pack.1), calls=%async_computation | async-start | bytes 2359296 | tf_op jit(solution)/shard_map/all_to_all | solution.py:554
  45.8 26.8 %all-to-all-start.1 = ((bf16[32,112,128]{2,1,0:T(8,128)(2,1)}), bf16[32,112,128]{2,1,0:T(8,128)(2,1)S(1)}, u32[]{:S(2)}, u32[]{:S(2)}) async-start(bf16[32,112,128]{2,1,0:T(8,128)(2,1)} %clips.1), calls=%async_computation.1 | async-start | bytes 1835008 | tf_op jit(solution)/shard_map/all_to_all | solution.py:556
  72.7 0.9 %copy-start = (bf16[32,112,128]{2,1,0:T(8,128)(2,1)}, bf16[32,112,128]{2,1,0:T(8,128)(2,1)S(1)}, u32[]{:S(2)}) copy-start(bf16[32,112,128]{2,1,0:T(8,128)(2,1)S(1)} %all-to-all-done.1.in_ref) | copy-start | bytes 2752516

commit v10 on v8

--- a/solution.py
+++ b/solution.py
@@ -13,7 +13,7 @@
 WIDTH = HEADS * HDIM
 SCALING = 1.0 / math.sqrt(HDIM)
 CHUNKS = (4, 4)
-PARTS = 2
+PARTS = 1
 masked_score = -1e30
 
 
@@ -171,23 +171,25 @@
     return lax.optimization_barrier((values, *earlier))
 
 
-def neighbours(blocks):
+def neighbours(block, start):
     count = lax.axis_size("grp")
-    pairs = [[(i, i + 1) for i in range(start, count - 1, 2)] for start in (1, 0)]
-    return [swap(block, "grp", links) for block, links in zip(blocks, pairs)]
-
-
-def join_kernel(near, far, span, *refs):
-    ins, outs, (held, ready, left_off) = refs[:near], refs[-6:-3], refs[-3:]
-    place = lax.axis_index("seq")
-    for step, ref in enumerate(ins):
-        held[(place ^ step) & (near - 1)] = ref[...]
+    return swap(block, "grp", [(i, i + 1) for i in range(start, count - 1, 2)])
+
+
+def far_first(n):
+    return [*range(n // 2, n), *range(n // 2)]
+
+
+def join_kernel(n, span, *refs):
+    ins, outs, (held, ready, left_off) = refs[:n], refs[-6:-3], refs[-3:]
+    for step, ref in zip(far_first(n), ins):
+        held[lax.axis_index("seq") ^ step] = ref[...]
     count = span.stop - span.start
     half = count // 2
     places = held.shape[2] // 2
 
     def gather(rows, lanes):
-        return jnp.concatenate([held[source, rows, lanes] for source in range(near)], axis=1)
+        return jnp.concatenate([held[source, rows, lanes] for source in range(n)], axis=1)
 
     left, right = slice(0, places), slice(places, 2 * places)
     rest = slice(count, count + half)
@@ -195,10 +197,8 @@
     ready[2] = gather(slice(0, count), right)
     ready[0, :half, :] = gather(rest, left)
     ready[0, half:, :] = gather(rest, right)
-    width = near * places
-    tokens = pl.ds(pl.multiple_of((place // near ^ far) * width, width), width)
     copies = [
-        pltpu.make_async_copy(ready.at[i], out.at[0, span, tokens], left_off.at[i])
+        pltpu.make_async_copy(ready.at[i], out.at[0, span, :], left_off.at[i])
         for i, out in enumerate(outs)
     ]
     for copy in copies:
@@ -207,33 +207,33 @@
         copy.wait()
 
 
-def join(blocks, span, tokens, far, earlier):
-    near = len(blocks) // 2
-    blocks = blocks[near:] if far else blocks[:near]
+def join(blocks, span, tokens, earlier):
+    n = len(blocks)
     rows = span.stop - span.start
     shape = jax.ShapeDtypeStruct((1, WIDTH, tokens), jnp.bfloat16)
     vmem = pl.BlockSpec(memory_space=pltpu.VMEM)
     hbm = pl.BlockSpec(memory_space=pltpu.HBM)
     earlier = [] if earlier is None else list(earlier)
     return pl.pallas_call(
-        functools.partial(join_kernel, near, far, span),
-        in_specs=[vmem] * near + [hbm] * len(earlier),
+        functools.partial(join_kernel, n, span),
+        in_specs=[vmem] * n + [hbm] * len(earlier),
         out_specs=[hbm] * 3,
         out_shape=[shape] * 3,
         scratch_shapes=[
-            pltpu.VMEM((near, *blocks[0].shape), jnp.bfloat16),
-            pltpu.VMEM((3, rows, tokens // 2), jnp.bfloat16),
+            pltpu.VMEM((n, *blocks[0].shape), jnp.bfloat16),
+            pltpu.VMEM((3, rows, tokens), jnp.bfloat16),
             pltpu.SemaphoreType.DMA((3,)),
         ],
-        input_output_aliases={near + i: i for i in range(len(earlier))},
+        input_output_aliases={n + i: i for i in range(len(earlier))},
         compiler_params=pltpu.CompilerParams(vmem_limit_bytes=24 * 2**20),
         name="unpack",
-    )(*blocks, *earlier)
+    )(*(blocks[step] for step in far_first(n)), *earlier)
 
 
 def clip_kernel(window, heads, given_bounds, *refs):
     own, sides_of = refs[:window], refs[window : window + 2]
-    outs, (x_ref, y_ref, coef_ref, grad_ref) = refs[window + 2 : 2 * window + 2], refs[-6:-2]
+    outs, (x_ref, y_ref) = refs[window + 2 : 2 * window + 2], refs[-8:-6]
+    sums_ref, score_ref, coef_ref, grad_ref = refs[-6:-2]
     bounds, arrived = refs[-2:]
     copy = pltpu.make_async_copy(given_bounds, bounds, arrived)
     copy.start()
@@ -263,7 +263,7 @@
         first, last = bounds[0, frame], bounds[1, frame]
         return first, last - first, [jnp.minimum(first + t, last - 1) for t in range(window)]
 
-    def weigh(frame, carry):
+    def products(frame, carry):
         first, count, others = partners(frame)
         sums = [[] for _ in range(window)]
         for head in range(heads):
@@ -271,23 +271,27 @@
             mine = x_ref[frame, span, :]
             for t, other in enumerate(others):
                 sums[t].append(jnp.sum(mine * y_ref[other, span, :], axis=0, keepdims=True))
-        sums = [jnp.concatenate(parts, axis=0) for parts in sums]
-        scores = [
-            part * SCALING + jnp.where(t < count, 0.0, masked_score) for t, part in enumerate(sums)
-        ]
-        peak = functools.reduce(jnp.maximum, scores)
-        raised = [jnp.exp(score - peak) for score in scores]
-        inverse = 1.0 / functools.reduce(jnp.add, raised)
-        weights = [part * inverse for part in raised]
-        weights_low = [rounded(part) for part in weights]
-        weight_grad = [swapped(part) for part in sums]
-        dots = functools.reduce(jnp.add, [w * d for w, d in zip(weights_low, weight_grad)])
-        for t in range(window):
-            score_grad = rounded(weights[t] * (weight_grad[t] - dots))
-            coef_ref[frame, t] = jnp.where(is_left, score_grad, swapped(weights_low[t]))
+        for t, parts in enumerate(sums):
+            total = jnp.concatenate(parts, axis=0)
+            sums_ref[t, frame] = total
+            score_ref[t, frame] = total * SCALING + jnp.where(t < count, 0.0, masked_score)
         return carry
 
-    lax.fori_loop(lowest, highest, weigh, 0)
+    lax.fori_loop(lowest, highest, products, 0)
+    flat = (extent * heads, lanes)
+    scores = [score_ref[t].reshape(flat) for t in range(window)]
+    sums = [sums_ref[t].reshape(flat) for t in range(window)]
+    peak = functools.reduce(jnp.maximum, scores)
+    raised = [jnp.exp(score - peak) for score in scores]
+    inverse = 1.0 / functools.reduce(jnp.add, raised)
+    weights = [part * inverse for part in raised]
+    weights_low = [rounded(part) for part in weights]
+    weight_grad = [swapped(part) for part in sums]
+    dots = functools.reduce(jnp.add, [w * d for w, d in zip(weights_low, weight_grad)])
+    for t in range(window):
+        score_grad = rounded(weights[t] * (weight_grad[t] - dots))
+        coef = jnp.where(is_left, score_grad, swapped(weights_low[t]))
+        coef_ref[t] = coef.reshape(extent, heads, lanes)
 
     def gradients(at, carry):
         frame = halo + at
@@ -298,9 +302,9 @@
             span = slice(head * HDIM, (head + 1) * HDIM)
             key_sum, query_sum = None, None
             for t, other in enumerate(others):
-                back = coef_ref[other, place, head : head + 1, :]
+                back = coef_ref[place, other, head : head + 1, :]
                 back = jnp.where(t < count, back, 0.0)
-                ahead = coef_ref[frame, t, head : head + 1, :]
+                ahead = coef_ref[t, frame, head : head + 1, :]
                 key_term = back * x_ref[other, span, :]
                 query_term = ahead * y_ref[other, span, :]
                 key_sum = key_term if t == 0 else key_sum + key_term
@@ -342,7 +346,9 @@
         scratch_shapes=[
             pltpu.VMEM((extent, rows, lanes), jnp.float32),
             pltpu.VMEM((extent, rows, lanes), jnp.float32),
-            pltpu.VMEM((extent, window, heads, lanes), jnp.float32),
+            pltpu.VMEM((window, extent, heads, lanes), jnp.float32),
+            pltpu.VMEM((window, extent, heads, lanes), jnp.float32),
+            pltpu.VMEM((window, extent, heads, lanes), jnp.float32),
             pltpu.VMEM((window, *shape), jnp.bfloat16),
             pltpu.SMEM(bounds.shape, jnp.int32),
             pltpu.SemaphoreType.DMA,
@@ -392,13 +398,17 @@
     space = frame_grads(*space_in)
     packed[1][2:], own[0][2], space = gated(packed[1][2:], own[0][2], space)
     own.append(exchange(packed[1]))
-    beside = [neighbours(sides(blocks)) for blocks in own]
-    back, grads = [], None
-    for blocks, near in zip(own, beside):
-        back.append(exchange(clip_grads(bounds, blocks, near)))
+    ends = [sides(blocks) for blocks in own]
+    beside = [neighbours(ends[0][0], 1), neighbours(ends[0][1], 0)]
+    far = neighbours(ends[1][0], 1)
+    found = list(clip_grads(bounds, own[0], beside))
+    waiting = ends[1][1]
+    back = [exchange(found)]
+    found = clip_grads(bounds, own[1], [far, neighbours(waiting, 0)])
+    back.append(exchange(found))
+    grads = None
     for span, blocks in zip(spans, back):
-        for far in (1, 0):
-            grads = join(blocks, span, tokens, far, grads)
+        grads = join(blocks, span, tokens, grads)
     return turned(*space, *grads)
 
 

time: 61.9 us -> 61.1 us (0.987)
  Pallas kernels: 17.9 us -> 15.6 us
  waiting for transfers between devices: 15.4 us -> 16.8 us
    ppermute x16, waiting for transfers between devices: 15.4 us -> 16.8 us  [swap(): lax.ppermute(block, axis, [(i, j) for i, j in pairs] + [(j, i) for i, j i...]
    pallas_call x4 -> x2, Pallas kernels: 3.44 us -> 2.01 us  [join(): pl.pallas_call(functools.partial(join_kernel, n, span), in_specs=[vmem] *...]
    pallas_call x2, Pallas kernels: 4.16 us -> 3.54 us  [clip_grads(): pl.pallas_call(functools.partial(clip_kernel, window, heads), out_shape=[...]
  transfers between devices with their start and end apart: 16 -> 16, of which waited for: 4 -> 5; matrix products, arithmetic and copies ran while one was open for 0% -> 0% of each run, Pallas kernels for 24% -> 21%
where the time goes in v10:
time: 61.1 us; the launch traced here: 60.8 us
  starting transfers between devices  27.3 us (45%)
  waiting for transfers between devices  16.8 us (27%)
  Pallas kernels  15.6 us (26%)
  between operations  0.78 us (1%)
    ppermute x16, starting transfers between devices, swap(): lax.ppermute(block, axis, [(i, j) for i, j in pairs] + [(j, i) for i, j i...  27.3 us
    ppermute x16, waiting for transfers between devices, swap(): lax.ppermute(block, axis, [(i, j) for i, j in pairs] + [(j, i) for i, j i...  16.8 us
    pallas_call x1, Pallas kernels, frame_grads(): pl.pallas_call(frame_kernel, out_shape=(shape, shape, shape), compiler_pa...  5.59 us
    pallas_call x2, Pallas kernels, split(): pl.pallas_call(functools.partial(split_kernel, n, span), in_specs=[hbm] *...  4.18 us
    pallas_call x2, Pallas kernels, clip_grads(): pl.pallas_call(functools.partial(clip_kernel, window, heads), out_shape=[...  3.54 us
    pallas_call x2, Pallas kernels, join(): pl.pallas_call(functools.partial(join_kernel, n, span), in_specs=[vmem] *...  2.01 us
  transfers between devices with their start and end apart: 16, of which 5 were waited for; matrix products, arithmetic and copies ran while one was open for 0% of the time, Pallas kernels for 21%

profile of v10, /device:TPU:0, one launch (start us, length us, event | category | flops | bytes accessed | tf_op | source)
XLA Modules:
  0.0 60.8 jit_solution(6013898429569856609)
XLA Ops:
  0.6 2.1 %pack.3 = (bf16[2,288,128]{2,1,0:T(8,128)(2,1)}, bf16[2,288,128]{2,1,0:T(8,128)(2,1)}, bf16[2,288,128]{2,1,0:T(8,128)(2,1)}, bf16[2,288,128]{2,1,0:T(8,128)(2,1)}) custom-call(bf16[1,576,256]{2,1,0:T(8,128)(2,1)} %bitcast.18, bf16[1,576,256]{2,1,0:T(8,128)(2,1)} %bitcast.20, bf16[1,576,256]{2,1,0:T(8,128)(2,1)} %bitcast.22, bf16[1,576,256]{2,1,0:T(8,128)(2,1)} %bitcast.24), custom_call_target="tpu_custom_call" | custom-call | tf_op jit(solution)/shard_map/pack/pallas_call | solution.py:114
  2.7 4.1 %collective-permute-start = (bf16[2,288,128]{2,1,0:T(8,128)(2,1)}, bf16[2,288,128]{2,1,0:T(8,128)(2,1)S(1)}, u32[]{:S(2)}, u32[]{:S(2)}) collective-permute-start(bf16[2,288,128]{2,1,0:T(8,128)(2,1)} %get-tuple-element.43), channel_id=1, source_target_pairs={{0,2},{1,3},{2,0},{3,1},{4,6},{5,7},{6,4},{7,5},{8,10},{9,11},{10,... | collective-permute-start | bytes 442376 | tf_op jit(solution)/shard_map/ppermute | solution.py:131
  6.8 1.6 %collective-permute-start.9 = (bf16[2,288,128]{2,1,0:T(8,128)(2,1)}, bf16[2,288,128]{2,1,0:T(8,128)(2,1)S(1)}, u32[]{:S(2)}, u32[]{:S(2)}) collective-permute-start(bf16[2,288,128]{2,1,0:T(8,128)(2,1)} %get-tuple-element.61), channel_id=1, source_target_pairs={{0,1},{2,3},{1,0},{3,2},{4,5},{6,7},{5,4},{7,6},{8,9},{10,11},{9,8... | collective-permute-start | bytes 442376 | tf_op jit(solution)/shard_map/ppermute | solution.py:131
  8.4 0.0 collective-permute-start.10
  8.4 2.1 %pack.2 = (bf16[2,288,128]{2,1,0:T(8,128)(2,1)}, bf16[2,288,128]{2,1,0:T(8,128)(2,1)}, bf16[2,288,128]{2,1,0:T(8,128)(2,1)}, bf16[2,288,128]{2,1,0:T(8,128)(2,1)}) custom-call(bf16[1,576,256]{2,1,0:T(8,128)(2,1)} %bitcast.19, bf16[1,576,256]{2,1,0:T(8,128)(2,1)} %bitcast.21, bf16[1,576,256]{2,1,0:T(8,128)(2,1)} %bitcast.23, bf16[1,576,256]{2,1,0:T(8,128)(2,1)} %bitcast.25), custom_call_target="tpu_custom_call" | custom-call | tf_op jit(solution)/shard_map/pack/pallas_call | solution.py:114
  10.5 1.0 %collective-permute-start.1 = (bf16[2,288,128]{2,1,0:T(8,128)(2,1)}, bf16[2,288,128]{2,1,0:T(8,128)(2,1)S(1)}, u32[]{:S(2)}, u32[]{:S(2)}) collective-permute-start(bf16[2,288,128]{2,1,0:T(8,128)(2,1)} %get-tuple-element.51), channel_id=1, source_target_pairs={{0,1},{2,3},{1,0},{3,2},{4,5},{6,7},{5,4},{7,6},{8,9},{10,11},{9,8... | collective-permute-start | bytes 442376 | tf_op jit(solution)/shard_map/ppermute | solution.py:131
  11.5 0.0 copy-start.4
  11.5 0.0 copy-start.3
  11.5 0.0 copy-start.2
  11.5 0.0 copy-start.1
  11.5 5.6 %space.1 = (bf16[1,576,256]{2,1,0:T(8,128)(2,1)}, bf16[1,576,256]{2,1,0:T(8,128)(2,1)}, bf16[1,576,256]{2,1,0:T(8,128)(2,1)}) custom-call(bf16[1,576,256]{2,1,0:T(8,128)(2,1)} %bitcast.29, bf16[1,576,256]{2,1,0:T(8,128)(2,1)} %bitcast.30, bf16[1,576,256]{2,1,0:T(8,128)(2,1)} %bitcast.31, bf16[1,576,256]{2,1,0:T(8,128)(2,1)} %bitcast.32), custom_call_target="tpu_custom_call" | custom-call | flops 1610612736 | bytes 2064384 | tf_op jit(solution)/shard_map/space/pallas_call | solution.py:65
  17.1 0.0 copy-done.4
  17.1 0.1 select_reduce_fusion.2
  17.2 0.0 collective-permute-done.refs_2_
  17.2 0.0 copy-done.3
  17.2 3.6 %collective-permute-start.2 = (bf16[2,288,128]{2,1,0:T(8,128)(2,1)S(1)}, bf16[2,288,128]{2,1,0:T(8,128)(2,1)S(1)}, u32[]{:S(2)}, u32[]{:S(2)}) collective-permute-start(bf16[2,288,128]{2,1,0:T(8,128)(2,1)S(1)} %copy-done.3), channel_id=1, source_target_pairs={{0,2},{1,3},{2,0},{3,1},{4,6},{5,7},{6,4},{7,5},{8,10},{9,11},{10,... | collective-permute-start | bytes 442376 | tf_op jit(solution)/shard_map/ppermute | solution.py:131
  20.7 0.0 copy-done.2
  20.7 0.0 collective-permute-start.3
  20.7 0.0 collective-permute-done.9.refs_1_
  20.7 0.0 collective-permute-done.10.refs_3_
  20.8 0.0 copy-done.1
  20.8 0.0 copy-start
  20.8 0.1 sides.3
  20.9 0.7 %collective-permute-start.11 = (bf16[3,2,288,128]{3,2,1,0:T(8,128)(2,1)S(1)}, bf16[3,2,288,128]{3,2,1,0:T(8,128)(2,1)S(1)}, u32[]{:S(2)}, u32[]{:S(2)}) collective-permute-start(bf16[3,2,288,128]{3,2,1,0:T(8,128)(2,1)S(1)} %get-tuple-element.64), channel_id=1, source_target_pairs={{4,8},{12,16},{20,24},{8,4},{16,12},{24,20},{5,9},{13,17},{21,25},... | collective-permute-start | bytes 1327112 | tf_op jit(solution)/shard_map/ppermute | solution.py:131
  21.6 3.1 %collective-permute-start.12 = (bf16[3,2,288,128]{3,2,1,0:T(8,128)(2,1)S(1)}, bf16[3,2,288,128]{3,2,1,0:T(8,128)(2,1)S(1)}, u32[]{:S(2)}, u32[]{:S(2)}) collective-permute-start(bf16[3,2,288,128]{3,2,1,0:T(8,128)(2,1)S(1)} %get-tuple-element.65), channel_id=1, source_target_pairs={{0,4},{8,12},{16,20},{24,28},{4,0},{12,8},{20,16},{28,24},{1,5},{9... | collective-permute-start | bytes 1327112 | tf_op jit(solution)/shard_map/ppermute | solution.py:131
  24.7 0.2 select_reduce_fusion.1
  24.9 0.0 collective-permute-done.1.refs_1_
  24.9 6.0 %collective-permute-done.2.refs_2_ = bf16[2,288,128]{2,1,0:T(8,128)(2,1)S(1)} collective-permute-done((bf16[2,288,128]{2,1,0:T(8,128)(2,1)S(1)}, bf16[2,288,128]{2,1,0:T(8,128)(2,1)S(1)}, u32[]{:S(2)}, u32[]{:S(2)}) %collective-permute-start.2) | collective-permute-done | bytes 147488 | tf_op jit(solution)/shard_map/ppermute | solution.py:131
  30.9 0.0 collective-permute-done.3.refs_3_
  30.9 0.0 copy-done
  30.9 0.1 sides.2
  31.0 0.7 %collective-permute-start.4 = (bf16[3,2,288,128]{3,2,1,0:T(8,128)(2,1)S(1)}, bf16[3,2,288,128]{3,2,1,0:T(8,128)(2,1)S(1)}, u32[]{:S(2)}, u32[]{:S(2)}) collective-permute-start(bf16[3,2,288,128]{3,2,1,0:T(8,128)(2,1)S(1)} %get-tuple-element.54), channel_id=1, source_target_pairs={{4,8},{12,16},{20,24},{8,4},{16,12},{24,20},{5,9},{13,17},{21,25},... | collective-permute-start | bytes 1327112 | tf_op jit(solution)/shard_map/ppermute | solution.py:131
  31.7 2.9 %collective-permute-start.5 = (bf16[3,2,288,128]{3,2,1,0:T(8,128)(2,1)S(1)}, bf16[3,2,288,128]{3,2,1,0:T(8,128)(2,1)S(1)}, u32[]{:S(2)}, u32[]{:S(2)}) collective-permute-start(bf16[3,2,288,128]{3,2,1,0:T(8,128)(2,1)S(1)} %get-tuple-element.55), channel_id=1, source_target_pairs={{0,4},{8,12},{16,20},{24,28},{4,0},{12,8},{20,16},{28,24},{1,5},{9... | collective-permute-start | bytes 1327112 | tf_op jit(solution)/shard_map/ppermute | solution.py:131
  34.6 0.0 collective-permute-done.11.refs_4_
  34.6 0.0 collective-permute-done.12.refs_5_
  34.6 1.8 %clips.3 = (bf16[432,128]{1,0:T(8,128)(2,1)S(1)}, bf16[432,128]{1,0:T(8,128)(2,1)S(1)}, bf16[432,128]{1,0:T(8,128)(2,1)S(1)}, bf16[432,128]{1,0:T(8,128)(2,1)S(1)}) custom-call(s32[2,10]{1,0:T(2,128)S(1)} %pad_add_fusion.given_bounds, bf16[2,288,128]{2,1,0:T(8,128)(2,1)S(1)} %copy-done.1, bf16[2,288,128]{2,1,0:T(8,128)(2,1)S(1)} %collective-permute-done.9.refs_1_, ...), custom_call_target="tpu_custom_call" | custom-call | flops 589824000 | bytes 1474560 | tf_op jit(solution)/shard_map/clips/pallas_call | solution.py:341
  36.4 4.9 %collective-permute-start.13 = (bf16[432,128]{1,0:T(8,128)(2,1)S(1)}, bf16[432,128]{1,0:T(8,128)(2,1)S(1)}, u32[]{:S(2)}, u32[]{:S(2)}) collective-permute-start(bf16[432,128]{1,0:T(8,128)(2,1)S(1)} %get-tuple-element.66), channel_id=1, source_target_pairs={{0,2},{1,3},{2,0},{3,1},{4,6},{5,7},{6,4},{7,5},{8,10},{9,11},{10,... | collective-permute-start | bytes 331784 | tf_op jit(solution)/shard_map/ppermute | solution.py:131
  41.3 0.4 collective-permute-start.14
  41.7 0.2 collective-permute-start.15
  41.9 0.0 collective-permute-done.4.refs_4_
  41.9 0.0 collective-permute-done.5.refs_5_
  41.9 1.8 %clips.2 = (bf16[432,128]{1,0:T(8,128)(2,1)S(1)}, bf16[432,128]{1,0:T(8,128)(2,1)S(1)}, bf16[432,128]{1,0:T(8,128)(2,1)S(1)}, bf16[432,128]{1,0:T(8,128)(2,1)S(1)}) custom-call(s32[2,10]{1,0:T(2,128)S(1)} %pad_add_fusion.given_bounds, bf16[2,288,128]{2,1,0:T(8,128)(2,1)S(1)} %copy-done, bf16[2,288,128]{2,1,0:T(8,128)(2,1)S(1)} %collective-permute-done.1.refs_1_, ...), custom_call_target="tpu_custom_call" | custom-call | flops 589824000 | bytes 1474560 | tf_op jit(solution)/shard_map/clips/pallas_call | solution.py:341
  43.7 3.8 %collective-permute-start.6 = (bf16[432,128]{1,0:T(8,128)(2,1)S(1)}, bf16[432,128]{1,0:T(8,128)(2,1)S(1)}, u32[]{:S(2)}, u32[]{:S(2)}) collective-permute-start(bf16[432,128]{1,0:T(8,128)(2,1)S(1)} %get-tuple-element.56), channel_id=1, source_target_pairs={{0,2},{1,3},{2,0},{3,1},{4,6},{5,7},{6,4},{7,5},{8,10},{9,11},{10,... | collective-permute-start | bytes 331784 | tf_op jit(solution)/shard_map/ppermute | solution.py:131
  47.5 0.4 collective-permute-start.7
  48.0 1.6 %collective-permute-done.13.refs_0_ = bf16[432,128]{1,0:T(8,128)(2,1)S(1)} collective-permute-done((bf16[432,128]{1,0:T(8,128)(2,1)S(1)}, bf16[432,128]{1,0:T(8,128)(2,1)S(1)}, u32[]{:S(2)}, u32[]{:S(2)}) %collective-permute-start.13) | collective-permute-done | bytes 110624 | tf_op jit(solution)/shard_map/ppermute | solution.py:131
  49.6 0.0 collective-permute-start.8
  49.6 0.0 collective-permute-done.14.refs_1_
  49.6 1.1 %collective-permute-done.15.refs_3_ = bf16[432,128]{1,0:T(8,128)(2,1)S(1)} collective-permute-done((bf16[432,128]{1,0:T(8,128)(2,1)S(1)}, bf16[432,128]{1,0:T(8,128)(2,1)S(1)}, u32[]{:S(2)}, u32[]{:S(2)}) %collective-permute-start.15) | collective-permute-done | bytes 110624 | tf_op jit(solution)/shard_map/ppermute | solution.py:131
  50.6 1.0 %unpack.2 = (bf16[1,576,256]{2,1,0:T(8,128)(2,1)}, bf16[1,576,256]{2,1,0:T(8,128)(2,1)}, bf16[1,576,256]{2,1,0:T(8,128)(2,1)}) custom-call(bf16[432,128]{1,0:T(8,128)(2,1)S(1)} %collective-permute-done.13.refs_0_, bf16[432,128]{1,0:T(8,128)(2,1)S(1)} %collective-permute-done.14.refs_1_, bf16[432,128]{1,0:T(8,128)(2,1)S(1)} %get-tuple-element.68.refs_2_, ...), custom_call_target="tpu_custom_call" | custom-call | tf_op jit(solution)/shard_map/unpack/pallas_call | solution.py:217
  51.7 7.4 %collective-permute-done.6.refs_0_ = bf16[432,128]{1,0:T(8,128)(2,1)S(1)} collective-permute-done((bf16[432,128]{1,0:T(8,128)(2,1)S(1)}, bf16[432,128]{1,0:T(8,128)(2,1)S(1)}, u32[]{:S(2)}, u32[]{:S(2)}) %collective-permute-start.6) | collective-permute-done | bytes 110624 | tf_op jit(solution)/shard_map/ppermute | solution.py:131
  59.1 0.0 collective-permute-done.7.refs_1_
  59.1 0.8 %collective-permute-done.8.refs_3_ = bf16[432,128]{1,0:T(8,128)(2,1)S(1)} collective-permute-done((bf16[432,128]{1,0:T(8,128)(2,1)S(1)}, bf16[432,128]{1,0:T(8,128)(2,1)S(1)}, u32[]{:S(2)}, u32[]{:S(2)}) %collective-permute-start.8) | collective-permute-done | bytes 110624 | tf_op jit(solution)/shard_map/ppermute | solution.py:131
  59.8 1.0 %unpack.3 = (bf16[1,576,256]{2,1,0:T(8,128)(2,1)}, bf16[1,576,256]{2,1,0:T(8,128)(2,1)}, bf16[1,576,256]{2,1,0:T(8,128)(2,1)}) custom-call(bf16[432,128]{1,0:T(8,128)(2,1)S(1)} %collective-permute-done.6.refs_0_, bf16[432,128]{1,0:T(8,128)(2,1)S(1)} %collective-permute-done.7.refs_1_, ...), custom_call_target="tpu_custom_call", output_to_operand_aliasing={{0}: (4, {}), {1}: (5, {}), {2}: (6, {})} | custom-call | tf_op jit(solution)/shard_map/unpack/pallas_call | solution.py:217
  (4 shorter events, 0.0 us)
Async XLA Ops:
  2.7 14.4 %collective-permute-start = (bf16[2,288,128]{2,1,0:T(8,128)(2,1)}, bf16[2,288,128]{2,1,0:T(8,128)(2,1)S(1)}, u32[]{:S(2)}, u32[]{:S(2)}) collective-permute-start(bf16[2,288,128]{2,1,0:T(8,128)(2,1)} %get-tuple-element.43), channel_id=1, source_target_pairs={{0,2},{1,3},{2,0},{3,1},{4,6},{5,7},{6,4},{7,5},{8,10},{9,11},{10,... | collective-permute-start | bytes 442376 | tf_op jit(solution)/shard_map/ppermute | solution.py:131
  6.8 13.9 %collective-permute-start.9 = (bf16[2,288,128]{2,1,0:T(8,128)(2,1)}, bf16[2,288,128]{2,1,0:T(8,128)(2,1)S(1)}, u32[]{:S(2)}, u32[]{:S(2)}) collective-permute-start(bf16[2,288,128]{2,1,0:T(8,128)(2,1)} %get-tuple-element.61), channel_id=1, source_target_pairs={{0,1},{2,3},{1,0},{3,2},{4,5},{6,7},{5,4},{7,6},{8,9},{10,11},{9,8... | collective-permute-start | bytes 442376 | tf_op jit(solution)/shard_map/ppermute | solution.py:131
  8.4 12.3 %collective-permute-start.10 = (bf16[2,288,128]{2,1,0:T(8,128)(2,1)}, bf16[2,288,128]{2,1,0:T(8,128)(2,1)S(1)}, u32[]{:S(2)}, u32[]{:S(2)}) collective-permute-start(bf16[2,288,128]{2,1,0:T(8,128)(2,1)} %get-tuple-element.63), channel_id=1, source_target_pairs={{0,3},{1,2},{3,0},{2,1},{4,7},{5,6},{7,4},{6,5},{8,11},{9,10},{11,... | collective-permute-start | bytes 442376 | tf_op jit(solution)/shard_map/ppermute | solution.py:131
  10.5 14.4 %collective-permute-start.1 = (bf16[2,288,128]{2,1,0:T(8,128)(2,1)}, bf16[2,288,128]{2,1,0:T(8,128)(2,1)S(1)}, u32[]{:S(2)}, u32[]{:S(2)}) collective-permute-start(bf16[2,288,128]{2,1,0:T(8,128)(2,1)} %get-tuple-element.51), channel_id=1, source_target_pairs={{0,1},{2,3},{1,0},{3,2},{4,5},{6,7},{5,4},{7,6},{8,9},{10,11},{9,8... | collective-permute-start | bytes 442376 | tf_op jit(solution)/shard_map/ppermute | solution.py:131
  11.5 5.6 %copy-start.4 = (s32[16]{0:T(128)S(1)}, s32[16]{0:T(128)}, u32[]{:S(2)}) copy-start(s32[16]{0:T(128)} %param.17) | copy-start | bytes 196
  11.5 5.7 %copy-start.3 = (bf16[2,288,128]{2,1,0:T(8,128)(2,1)S(1)}, bf16[2,288,128]{2,1,0:T(8,128)(2,1)}, u32[]{:S(2)}) copy-start(bf16[2,288,128]{2,1,0:T(8,128)(2,1)} %get-tuple-element.52) | copy-start | bytes 442372
  11.5 9.2 %copy-start.2 = (bf16[2,288,128]{2,1,0:T(8,128)(2,1)S(1)}, bf16[2,288,128]{2,1,0:T(8,128)(2,1)}, u32[]{:S(2)}) copy-start(bf16[2,288,128]{2,1,0:T(8,128)(2,1)} %get-tuple-element.53) | copy-start | bytes 442372
  11.5 9.3 %copy-start.1 = (bf16[2,288,128]{2,1,0:T(8,128)(2,1)S(1)}, bf16[2,288,128]{2,1,0:T(8,128)(2,1)}, u32[]{:S(2)}) copy-start(bf16[2,288,128]{2,1,0:T(8,128)(2,1)} %get-tuple-element.60.refs_0_) | copy-start | bytes 442372
  17.2 13.7 %collective-permute-start.2 = (bf16[2,288,128]{2,1,0:T(8,128)(2,1)S(1)}, bf16[2,288,128]{2,1,0:T(8,128)(2,1)S(1)}, u32[]{:S(2)}, u32[]{:S(2)}) collective-permute-start(bf16[2,288,128]{2,1,0:T(8,128)(2,1)S(1)} %copy-done.3), channel_id=1, source_target_pairs={{0,2},{1,3},{2,0},{3,1},{4,6},{5,7},{6,4},{7,5},{8,10},{9,11},{10,... | collective-permute-start | bytes 442376 | tf_op jit(solution)/shard_map/ppermute | solution.py:131
  20.7 10.2 %collective-permute-start.3 = (bf16[2,288,128]{2,1,0:T(8,128)(2,1)S(1)}, bf16[2,288,128]{2,1,0:T(8,128)(2,1)S(1)}, u32[]{:S(2)}, u32[]{:S(2)}) collective-permute-start(bf16[2,288,128]{2,1,0:T(8,128)(2,1)S(1)} %copy-done.2), channel_id=1, source_target_pairs={{0,3},{1,2},{3,0},{2,1},{4,7},{5,6},{7,4},{6,5},{8,11},{9,10},{11,... | collective-permute-start | bytes 442376 | tf_op jit(solution)/shard_map/ppermute | solution.py:131
  20.8 10.1 %copy-start = (bf16[2,288,128]{2,1,0:T(8,128)(2,1)S(1)}, bf16[2,288,128]{2,1,0:T(8,128)(2,1)}, u32[]{:S(2)}) copy-start(bf16[2,288,128]{2,1,0:T(8,128)(2,1)} %get-tuple-element.50.refs_0_) | copy-start | bytes 442372
  20.9 13.7 %collective-permute-start.11 = (bf16[3,2,288,128]{3,2,1,0:T(8,128)(2,1)S(1)}, bf16[3,2,288,128]{3,2,1,0:T(8,128)(2,1)S(1)}, u32[]{:S(2)}, u32[]{:S(2)}) collective-permute-start(bf16[3,2,288,128]{3,2,1,0:T(8,128)(2,1)S(1)} %get-tuple-element.64), channel_id=1, source_target_pairs={{4,8},{12,16},{20,24},{8,4},{16,12},{24,20},{5,9},{13,17},{21,25},... | collective-permute-start | bytes 1327112 | tf_op jit(solution)/shard_map/ppermute | solution.py:131
  21.6 13.0 %collective-permute-start.12 = (bf16[3,2,288,128]{3,2,1,0:T(8,128)(2,1)S(1)}, bf16[3,2,288,128]{3,2,1,0:T(8,128)(2,1)S(1)}, u32[]{:S(2)}, u32[]{:S(2)}) collective-permute-start(bf16[3,2,288,128]{3,2,1,0:T(8,128)(2,1)S(1)} %get-tuple-element.65), channel_id=1, source_target_pairs={{0,4},{8,12},{16,20},{24,28},{4,0},{12,8},{20,16},{28,24},{1,5},{9... | collective-permute-start | bytes 1327112 | tf_op jit(solution)/shard_map/ppermute | solution.py:131
  31.0 10.9 %collective-permute-start.4 = (bf16[3,2,288,128]{3,2,1,0:T(8,128)(2,1)S(1)}, bf16[3,2,288,128]{3,2,1,0:T(8,128)(2,1)S(1)}, u32[]{:S(2)}, u32[]{:S(2)}) collective-permute-start(bf16[3,2,288,128]{3,2,1,0:T(8,128)(2,1)S(1)} %get-tuple-element.54), channel_id=1, source_target_pairs={{4,8},{12,16},{20,24},{8,4},{16,12},{24,20},{5,9},{13,17},{21,25},... | collective-permute-start | bytes 1327112 | tf_op jit(solution)/shard_map/ppermute | solution.py:131
  31.7 10.2 %collective-permute-start.5 = (bf16[3,2,288,128]{3,2,1,0:T(8,128)(2,1)S(1)}, bf16[3,2,288,128]{3,2,1,0:T(8,128)(2,1)S(1)}, u32[]{:S(2)}, u32[]{:S(2)}) collective-permute-start(bf16[3,2,288,128]{3,2,1,0:T(8,128)(2,1)S(1)} %get-tuple-element.55), channel_id=1, source_target_pairs={{0,4},{8,12},{16,20},{24,28},{4,0},{12,8},{20,16},{28,24},{1,5},{9... | collective-permute-start | bytes 1327112 | tf_op jit(solution)/shard_map/ppermute | solution.py:131
  36.4 13.2 %collective-permute-start.13 = (bf16[432,128]{1,0:T(8,128)(2,1)S(1)}, bf16[432,128]{1,0:T(8,128)(2,1)S(1)}, u32[]{:S(2)}, u32[]{:S(2)}) collective-permute-start(bf16[432,128]{1,0:T(8,128)(2,1)S(1)} %get-tuple-element.66), channel_id=1, source_target_pairs={{0,2},{1,3},{2,0},{3,1},{4,6},{5,7},{6,4},{7,5},{8,10},{9,11},{10,... | collective-permute-start | bytes 331784 | tf_op jit(solution)/shard_map/ppermute | solution.py:131
  41.3 8.3 %collective-permute-start.14 = (bf16[432,128]{1,0:T(8,128)(2,1)S(1)}, bf16[432,128]{1,0:T(8,128)(2,1)S(1)}, u32[]{:S(2)}, u32[]{:S(2)}) collective-permute-start(bf16[432,128]{1,0:T(8,128)(2,1)S(1)} %get-tuple-element.67), channel_id=1, source_target_pairs={{0,3},{1,2},{3,0},{2,1},{4,7},{5,6},{7,4},{6,5},{8,11},{9,10},{11,... | collective-permute-start | bytes 331784 | tf_op jit(solution)/shard_map/ppermute | solution.py:131
  41.7 8.9 %collective-permute-start.15 = (bf16[432,128]{1,0:T(8,128)(2,1)S(1)}, bf16[432,128]{1,0:T(8,128)(2,1)S(1)}, u32[]{:S(2)}, u32[]{:S(2)}) collective-permute-start(bf16[432,128]{1,0:T(8,128)(2,1)S(1)} %get-tuple-element.69), channel_id=1, source_target_pairs={{0,1},{2,3},{1,0},{3,2},{4,5},{6,7},{5,4},{7,6},{8,9},{10,11},{9,8... | collective-permute-start | bytes 331784 | tf_op jit(solution)/shard_map/ppermute | solution.py:131
  43.7 15.3 %collective-permute-start.6 = (bf16[432,128]{1,0:T(8,128)(2,1)S(1)}, bf16[432,128]{1,0:T(8,128)(2,1)S(1)}, u32[]{:S(2)}, u32[]{:S(2)}) collective-permute-start(bf16[432,128]{1,0:T(8,128)(2,1)S(1)} %get-tuple-element.56), channel_id=1, source_target_pairs={{0,2},{1,3},{2,0},{3,1},{4,6},{5,7},{6,4},{7,5},{8,10},{9,11},{10,... | collective-permute-start | bytes 331784 | tf_op jit(solution)/shard_map/ppermute | solution.py:131
  47.5 11.5 %collective-permute-start.7 = (bf16[432,128]{1,0:T(8,128)(2,1)S(1)}, bf16[432,128]{1,0:T(8,128)(2,1)S(1)}, u32[]{:S(2)}, u32[]{:S(2)}) collective-permute-start(bf16[432,128]{1,0:T(8,128)(2,1)S(1)} %get-tuple-element.57), channel_id=1, source_target_pairs={{0,3},{1,2},{3,0},{2,1},{4,7},{5,6},{7,4},{6,5},{8,11},{9,10},{11,... | collective-permute-start | bytes 331784 | tf_op jit(solution)/shard_map/ppermute | solution.py:131
  49.6 10.2 %collective-permute-start.8 = (bf16[432,128]{1,0:T(8,128)(2,1)S(1)}, bf16[432,128]{1,0:T(8,128)(2,1)S(1)}, u32[]{:S(2)}, u32[]{:S(2)}) collective-permute-start(bf16[432,128]{1,0:T(8,128)(2,1)S(1)} %get-tuple-element.59), channel_id=1, source_target_pairs={{0,1},{2,3},{1,0},{3,2},{4,5},{6,7},{5,4},{7,6},{8,9},{10,11},{9,8... | collective-permute-start | bytes 331784 | tf_op jit(solution)/shard_map/ppermute | solution.py:131
